TPU v7x, 256 devices: a whole 4x4x8 slice. The times are simulated.
256 devices in a mesh: section: 4 (over y), seq: 16 (over z, core), tp: 4 (over x).
Axes of the slice: x: 4, y: 4, z: 8, core: 2. Of those that a mesh axis runs over, the one named last changes fastest.
Arguments:
- queries: bfloat16 [4, 6144, 4096], P('section', 'seq', 'tp'), may hold values from -6 to 6
- encoded: bfloat16 [4, 256, 128, 896], P('section', 'seq'), may hold values from -6 to 6
- neighbour: int32 [4, 96, 2], P('section', 'seq'), may hold values from 0 to 15, as said below
- send_rows: int32 [4, 16, 16, 2], P('section', 'seq'), may hold values from 0 to 15
- key_weight: bfloat16 [4, 896, 4096], P('section', None, 'tp'), may hold values from -0.1875 to 0.1875
- value_weight: bfloat16 [4, 896, 4096], P('section', None, 'tp'), may hold values from -0.1875 to 0.1875
- ctx_grad: bfloat16 [4, 6144, 4096], P('section', 'seq', 'tp'), may hold values from -6 to 6
Outputs:
- context: bfloat16 [4, 6144, 4096], P('section', 'seq', 'tp')
- passed_grad: bfloat16 [4, 6144, 4096], P('section', 'seq', 'tp')
- encoded_grad: bfloat16 [4, 256, 128, 896], P('section', 'seq', None, 'tp')
Inputs may be any that keep to these rules, and one draw needn't show every extreme that they name: `neighbour`: among the 12 entries of the spans of one seq device (an aligned block of 6 spans), each device is named at most 2 times, and one device exactly 2 times. send_rows[s, i, d, j] is the row on device i of the neighbour named by the j-th entry (span order, then neighbour order) of device d's spans that names device i; slots past the number of such entries are never read.
All inputs are finite; a program needn't handle non-finite values.
Results may differ from a plain program's by a relative error of at most 0.015.
Values may be sent and summed in bfloat16 or wider, within the bound.
No kernel may reach another device: no remote copies, remote signals or barrier semaphores. Data moves between devices by JAX's collectives and lax.ppermute only.
A program may use at most 128 MiB of HBM per device.

v0:
```python
import math

import jax
import jax.numpy as jnp
from jax import lax
from jax.sharding import PartitionSpec as P

DH = 128
E = 896
SPAN = 64
KNB = 2
NTOK = 128


def shifted(x, axis, by):
    count = lax.axis_size(axis)
    pairs = [(i, i + by) for i in range(count) if 0 <= i + by < count]
    return lax.ppermute(x, axis, pairs)


def body(queries, encoded, neighbour, send_rows, key_weight, value_weight, ctx_grad):
    devices = lax.axis_size("seq")
    capacity = send_rows.shape[3]
    stored = encoded.shape[1]
    sources = neighbour[0].reshape(-1)
    onehot = (sources[:, None] == jnp.arange(devices, dtype=jnp.int32)[None, :]).astype(jnp.int32)
    slot_index = jnp.sum((jnp.cumsum(onehot, axis=0) - onehot) * onehot, axis=1)
    placing = sources * capacity + slot_index
    picked_rows = send_rows[0, 0].reshape(-1)
    encoded_local = encoded[0]
    arrived = lax.all_to_all(
        encoded_local[picked_rows], "seq", split_axis=0, concat_axis=0, tiled=True
    )
    gathered = arrived[placing]
    stacked = gathered.reshape(-1, E)
    keys_all = jnp.dot(stacked, key_weight[0], preferred_element_type=jnp.float32).astype(
        jnp.bfloat16
    )
    values_all = jnp.dot(stacked, value_weight[0], preferred_element_type=jnp.float32).astype(
        jnp.bfloat16
    )
    span_count = queries.shape[1] // SPAN
    heads_local = queries.shape[2] // DH
    query_blocks = queries[0].reshape(span_count, SPAN, heads_local, DH)
    key_blocks = keys_all.reshape(span_count, KNB * NTOK, heads_local, DH)
    value_blocks = values_all.reshape(span_count, KNB * NTOK, heads_local, DH)
    grad_blocks = ctx_grad[0].reshape(span_count, SPAN, heads_local, DH)
    score_scale = 1.0 / math.sqrt(DH)
    scores = (
        jnp.einsum("cqhd,ckhd->chqk", query_blocks, key_blocks, preferred_element_type=jnp.float32)
        * score_scale
    )
    exponent = jnp.exp(scores)
    probs = exponent / jnp.sum(exponent, axis=-1, keepdims=True)
    probs_low = probs.astype(jnp.bfloat16)
    context = jnp.einsum(
        "chqk,ckhd->cqhd", probs_low, value_blocks, preferred_element_type=jnp.float32
    ).astype(jnp.bfloat16)
    prob_grad = jnp.einsum(
        "cqhd,ckhd->chqk", grad_blocks, value_blocks, preferred_element_type=jnp.float32
    )
    row_delta = jnp.sum(probs * prob_grad, axis=-1, keepdims=True)
    dscore = (probs * (prob_grad - row_delta) * score_scale).astype(jnp.bfloat16)
    query_grad = jnp.einsum(
        "chqk,ckhd->cqhd", dscore, key_blocks, preferred_element_type=jnp.float32
    ).astype(jnp.bfloat16)
    key_grad = jnp.einsum(
        "chqk,cqhd->ckhd", dscore, query_blocks, preferred_element_type=jnp.float32
    ).astype(jnp.bfloat16)
    value_grad = jnp.einsum(
        "chqk,cqhd->ckhd", probs_low, grad_blocks, preferred_element_type=jnp.float32
    ).astype(jnp.bfloat16)
    passed = shifted(query_grad.reshape(queries.shape), "section", -1)
    key_rows = key_grad.reshape(-1, heads_local * DH)
    value_rows = value_grad.reshape(-1, heads_local * DH)
    piece_grad = jnp.dot(key_rows, key_weight[0].T, preferred_element_type=jnp.float32)
    piece_grad = piece_grad + jnp.dot(
        value_rows, value_weight[0].T, preferred_element_type=jnp.float32
    )
    piece_grad = piece_grad.reshape(gathered.shape[0], NTOK, E)
    buffer = (
        jnp.zeros((devices * capacity, NTOK, E), jnp.bfloat16)
        .at[placing]
        .set(piece_grad.astype(jnp.bfloat16))
    )
    sent_back = lax.all_to_all(buffer, "seq", split_axis=0, concat_axis=0, tiled=True)
    arrived_grad = lax.psum_scatter(
        sent_back.astype(jnp.float32).astype(jnp.bfloat16), "tp", scatter_dimension=2, tiled=True
    )
    selector = (picked_rows[None, :] == jnp.arange(stored, dtype=jnp.int32)[:, None]).astype(
        jnp.bfloat16
    )
    encoded_grad = jnp.dot(
        selector, arrived_grad.reshape(devices * capacity, -1), preferred_element_type=jnp.float32
    )
    encoded_grad = encoded_grad.reshape(stored, NTOK, -1).astype(jnp.bfloat16)
    return (context.reshape(queries.shape), passed, encoded_grad[None])


def solution(mesh):
    placed = (
        P("section", "seq", "tp"),
        P("section", "seq", None, None),
        P("section", "seq", None),
        P("section", "seq", None, None),
        P("section", None, "tp"),
        P("section", None, "tp"),
        P("section", "seq", "tp"),
    )
    return jax.shard_map(
        body,
        mesh=mesh,
        in_specs=placed,
        out_specs=(
            P("section", "seq", "tp"),
            P("section", "seq", "tp"),
            P("section", "seq", None, "tp"),
        ),
        check_vma=False,
    )
```

profile of v0, /device:TPU:1, one launch (start us, length us, event | category | flops | bytes accessed | tf_op | source)
XLA Modules:
  0.0 545.4 jit_solution(10494996265899042014)
XLA Ops:
  8.2 6.4 %gather_fusion = bf16[32,128,896]{2,1,0:T(8,128)(2,1)} fusion(bf16[16,128,896]{2,1,0:T(8,128)(2,1)} %bitcast.124, s32[1024]{0:T(1024)S(1)} %pad_clamp_fusion.1), kind=kCustom, calls=%fused_computation | custom fusion | bytes 14680192 | tf_op jit(solution)/shard_map/gather | solution.py:32
  14.6 10.1 %all-to-all-start = ((bf16[32,128,896]{2,1,0:T(8,128)(2,1)}), bf16[32,128,896]{2,1,0:T(8,128)(2,1)}, u32[]{:S(2)}, u32[]{:S(2)}) async-start(bf16[32,128,896]{2,1,0:T(8,128)(2,1)} %gather_fusion), calls=%async_computation | async-start | bytes 14680064 | tf_op jit(solution)/shard_map/all_to_all | solution.py:31
  25.2 1.1 copy.102
  26.7 159.0 %all-to-all-done = bf16[32,128,896]{2,1,0:T(8,128)(2,1)} async-done(((bf16[32,128,896]{2,1,0:T(8,128)(2,1)}), bf16[32,128,896]{2,1,0:T(8,128)(2,1)}, u32[]{:S(2)}, u32[]{:S(2)}) %all-to-all-start) | async-done | bytes 7340064 | tf_op jit(solution)/shard_map/all_to_all | solution.py:31
  185.7 5.7 %gather_fusion.1 = bf16[12,128,896]{2,1,0:T(8,128)(2,1)} fusion(bf16[32,128,896]{2,1,0:T(8,128)(2,1)} %all-to-all-done, s32[1024]{0:T(1024)S(1)} %pad_clamp_fusion), kind=kCustom, calls=%fused_computation.1 | custom fusion | bytes 5505072 | tf_op jit(solution)/shard_map/gather | solution.py:34
  191.4 5.4 fusion.18
  199.2 3.6 fusion.17
  203.6 2.9 fusion.9
  206.6 1.3 bitcast_reduce_fusion
  207.9 1.6 copy-done.12
  209.5 3.2 convert_bitcast_fusion
  212.7 24.3 %convert_bitcast_fusion.1 = bf16[6,256,8,128]{3,1,2,0:T(8,128)(2,1)} fusion(f32[6,8,256,64]{2,3,1,0:T(8,128)} %fusion.9, bf16[6,64,8,128]{3,2,1,0:T(8,128)(2,1)S(1)} %bitcast.140, f32[6,8,256,64]{2,3,1,0:T(8,128)} %copy-done.12, f32[6,8,64]{2,1,0:T(8,128)S(1)} %get-tuple-element.18), kind=kOutput, calls=%fused_computation.20 | convolution fusion | flops 209980672 | bytes 10235904 | tf_op jit(solution)/shard_map/chqk,cqhd->ckhd/dot_general | solution.py:67
  237.0 4.1 copy.96
  241.1 2.0 copy.94
  243.2 3.5 fusion.3
  246.7 4.9 add_convert_fusion
  251.6 4.0 broadcast_in_dim.4
  255.6 8.3 %scatter_fusion = bf16[32,128,896]{2,1,0:T(8,128)(2,1)} fusion(bf16[32,128,896]{2,1,0:T(8,128)(2,1)} %broadcast_in_dim.4, s32[12]{0:T(128)S(1)} %fusion.48, bf16[12,128,896]{2,1,0:T(8,128)(2,1)} %bitcast.136), kind=kCustom, calls=%fused_computation.2 | custom fusion | bytes 8257584 | tf_op jit(solution)/shard_map/scatter | solution.py:84
  263.9 169.0 %all_to_all.10 = bf16[32,128,896]{2,1,0:T(8,128)(2,1)} all-to-all(bf16[32,128,896]{2,1,0:T(8,128)(2,1)} %scatter_fusion), channel_id=1, replica_groups=mesh['section'=4,'seq'=16,'tp'=4] {'seq'}, dimensions={0} | all-to-all | bytes 14680064 | tf_op jit(solution)/shard_map/all_to_all | solution.py:86
  432.9 12.1 %copy.97 = bf16[32,128,896]{1,0,2:T(8,128)(2,1)} copy(bf16[32,128,896]{2,1,0:T(8,128)(2,1)} %all_to_all.10) | data formatting | bytes 14680064 | tf_op jit(solution)/shard_map/all_to_all | solution.py:86
  445.0 22.7 %fusion.34 = bf16[6,64,8,128]{3,1,2,0:T(8,128)(2,1)S(1)} fusion(bf16[6,256,8,128]{3,2,1,0:T(8,128)(2,1)} %bitcast.131, f32[6,8,256,64]{2,3,1,0:T(8,128)} %fusion.9, f32[6,8,256,64]{2,3,1,0:T(8,128)} %copy-done.12, f32[6,8,64]{2,1,0:T(8,128)S(1)} %get-tuple-element.18), kind=kOutput, calls=%fused_computation.42 | convolution fusion | flops 208801024 | bytes 10235904 | tf_op jit(solution)/shard_map/chqk,ckhd->cqhd/dot_general | solution.py:64
  468.6 1.3 collective-permute-start
  470.0 3.9 fusion.31
  474.4 1.2 reshape.97
  475.6 13.9 %collective-permute-done = bf16[1,384,1024]{2,1,0:T(8,128)(2,1)S(1)} collective-permute-done((bf16[1,384,1024]{2,1,0:T(8,128)(2,1)S(1)}, bf16[1,384,1024]{2,1,0:T(8,128)(2,1)S(1)}, u32[]{:S(2)}, u32[]{:S(2)}) %collective-permute-start) | collective-permute-done | bytes 786464 | tf_op jit(solution)/shard_map/ppermute | solution.py:18
  489.5 27.5 %reduce-scatter.2.cloned.1.call-done = bf16[32,128,224]{1,0,2:T(8,128)(2,1)} async-done(((bf16[32,128,896]{1,0,2:T(8,128)(2,1)}), bf16[32,128,224]{1,0,2:T(8,128)(2,1)}) %reduce-scatter.2.cloned.1.call-update) | async-done | bytes 1835024 | tf_op jit(solution)/shard_map/reduce_scatter | solution.py:87
  517.0 4.2 copy.98
  521.2 5.0 reshape.101
  526.2 4.0 dot_general.51
  530.2 4.4 copy.99
  534.6 1.9 fusion.30
  536.5 1.2 copy.100
  (49 shorter events, 7.4 us)
Async XLA Ops:
  7.2 184.3 %copy-start = (bf16[1,896,1024]{2,1,0:T(8,128)(2,1)S(1)}, bf16[1,896,1024]{2,1,0:T(8,128)(2,1)}, u32[]{:S(2)}) copy-start(bf16[1,896,1024]{2,1,0:T(8,128)(2,1)} %param.11) | copy-start | bytes 5505028
  14.6 10.2 %copy-start.9 = (s32[1,6,2]{1,2,0:T(2,128)S(1)}, s32[1,6,2]{1,2,0:T(2,128)}, u32[]{:S(2)}) copy-start(s32[1,6,2]{1,2,0:T(2,128)} %param.9) | copy-start | bytes 148
  14.6 10.5 %copy-start.6 = (bf16[1,384,1024]{2,1,0:T(8,128)(2,1)S(1)}, bf16[1,384,1024]{2,1,0:T(8,128)(2,1)}, u32[]{:S(2)}) copy-start(bf16[1,384,1024]{2,1,0:T(8,128)(2,1)} %param.7) | copy-start | bytes 2359300
  14.6 11.6 %copy-start.7 = (bf16[1,384,1024]{2,1,0:T(8,128)(2,1)S(1)}, bf16[1,384,1024]{2,1,0:T(8,128)(2,1)}, u32[]{:S(2)}) copy-start(bf16[1,384,1024]{2,1,0:T(8,128)(2,1)} %param.13) | copy-start | bytes 2359300
  14.6 171.1 %all-to-all-start = ((bf16[32,128,896]{2,1,0:T(8,128)(2,1)}), bf16[32,128,896]{2,1,0:T(8,128)(2,1)}, u32[]{:S(2)}, u32[]{:S(2)}) async-start(bf16[32,128,896]{2,1,0:T(8,128)(2,1)} %gather_fusion), calls=%async_computation | async-start | bytes 14680064 | tf_op jit(solution)/shard_map/all_to_all | solution.py:31
  24.8 492.3 %reduce-scatter.2.cloned.1.call-start = ((), (), s32[]{:S(2)}) async-start(), calls=%async_computation.3 | async-start | bytes 9175040 | tf_op jit(solution)/shard_map/reduce_scatter | solution.py:87
  196.8 1.8 copy-start.5
  196.9 2.3 copy-start.10
  199.2 7.4 %copy-start.3 = (bf16[192,8,8,128]{3,2,1,0:T(8,128)(2,1)}, bf16[192,8,8,128]{3,2,1,0:T(8,128)(2,1)S(1)}, u32[]{:S(2)}) copy-start(bf16[192,8,8,128]{3,2,1,0:T(8,128)(2,1)S(1)} %copy.101) | copy-start | bytes 9437188
  203.6 3.0 copy-start.2
  203.6 3.0 copy-start.8
  207.9 1.6 copy-start.12
  237.0 4.1 copy-start.4
  243.2 3.5 copy-start.11
  468.6 20.9 %collective-permute-start = (bf16[1,384,1024]{2,1,0:T(8,128)(2,1)S(1)}, bf16[1,384,1024]{2,1,0:T(8,128)(2,1)S(1)}, u32[]{:S(2)}, u32[]{:S(2)}) collective-permute-start(bf16[1,384,1024]{2,1,0:T(8,128)(2,1)S(1)} %reshape.98), channel_id=1, source_target_pairs={{64,0},{128,64},{192,128},{65,1},{129,65},{193,129},{66,2},{130,66... | collective-permute-start | bytes 2359304 | tf_op jit(solution)/shard_map/ppermute | solution.py:18
  530.2 8.3 %copy-start.1 = (bf16[1,896,1024]{2,1,0:T(8,128)(2,1)S(1)}, bf16[1,896,1024]{2,1,0:T(8,128)(2,1)}, u32[]{:S(2)}) copy-start(bf16[1,896,1024]{2,1,0:T(8,128)(2,1)} %param.11) | copy-start | bytes 5505028
Sparse Core Ops, SparseCore 0:
  445.1 71.8 reduce-scatter.1
where the time goes:
time: 546 us; the launch traced here: 545 us
  waiting for transfers between devices  200 us (37%)
  blocking collectives  169 us (31%)
  matrix products  77.6 us (14%)
  local copies, waits for them, and re-layouts  72.3 us (13%)
  between operations  14.3 us (3%)
  starting transfers between devices  11.4 us (2%)
    all_to_all x1, blocking collectives, body(): lax.all_to_all(buffer, 'seq', split_axis=0, concat_axis=0, tiled=True)  169 us
    all_to_all x1, waiting for transfers between devices, body(): lax.all_to_all(encoded_local[picked_rows], 'seq', split_axis=0, concat_ax...  159 us
    reduce_scatter x1, waiting for transfers between devices, body(): lax.psum_scatter(sent_back.astype(jnp.float32).astype(jnp.bfloat16), 'tp'...  27.5 us
    dot_general x1, matrix products, body(): jnp.einsum('chqk,cqhd->ckhd', dscore, query_blocks, preferred_element_typ...  24.3 us
    dot_general x1, matrix products, body(): jnp.einsum('chqk,ckhd->cqhd', dscore, key_blocks, preferred_element_type=...  22.7 us
    ppermute x1, waiting for transfers between devices, shifted(): return lax.ppermute(x, axis, pairs)  13.9 us
    all_to_all x1, local copies, waits for them, and re-layouts, body(): lax.all_to_all(buffer, 'seq', split_axis=0, concat_axis=0, tiled=True)  12.1 us
  transfers between devices with their start and end apart: 3, of which 3 were waited for; matrix products, arithmetic and copies ran while one was open for 6% of the time, Pallas kernels for 0%

commit v1 on v0

v1 whole, which is shorter than its diff:
```python
import math

import jax
import jax.numpy as jnp
from jax import lax
from jax.experimental import pallas as pl
from jax.experimental.pallas import tpu as pltpu
from jax.sharding import PartitionSpec as P

DH = 128
E = 896
SPAN = 64
KNB = 2
NTOK = 128
N_SEQ = 16
CHIPS = N_SEQ // 2
CAP = 2
N_TP = 4
SLOTS = N_SEQ * CAP
REQ = 12
STORED = 16
SPANS_DEV = 6
TOKENS_DEV = SPANS_DEV * SPAN
HEADS_DEV = 8
WIDTH = HEADS_DEV * DH
PART = NTOK // N_TP
EQ = E // N_TP
KEYS = KNB * NTOK
GROUPS = ((0, 3), (3, 3))
VMEM = 24 * 1024 * 1024
WIDE_VMEM = 60 * 1024 * 1024
BF16 = jnp.bfloat16
F32 = jnp.float32
SCALE = 1.0 / math.sqrt(DH)
IN_SMEM = pl.BlockSpec(memory_space=pltpu.SMEM)
IN_VMEM = pl.BlockSpec(memory_space=pltpu.VMEM)
ANYWHERE = pl.BlockSpec(memory_space=pl.ANY)


def params(limit=VMEM):
    return pltpu.CompilerParams(vmem_limit_bytes=limit)


def cost(flops, bytes_accessed):
    return pl.CostEstimate(flops=flops, bytes_accessed=bytes_accessed, transcendentals=0)


def dot(a, b):
    return jnp.dot(a, b, preferred_element_type=F32)


def dot_nt(a, b):
    return lax.dot_general(a, b, (((1,), (1,)), ((), ())), preferred_element_type=F32)


def dot_tn(a, b):
    return lax.dot_general(a, b, (((0,), (0,)), ((), ())), preferred_element_type=F32)


def member(shift):
    return lax.rem(lax.axis_index("tp") + shift, N_TP)


def share_kernel(encoded_ref, out_ref, sem):
    start = pl.multiple_of(lax.axis_index("tp") * PART, PART)
    copy = pltpu.make_async_copy(encoded_ref.at[:, pl.ds(start, PART)], out_ref, sem)
    copy.start()
    copy.wait()


def take_share(encoded):
    return pl.pallas_call(
        share_kernel,
        out_shape=jax.ShapeDtypeStruct((STORED, PART, E), BF16),
        in_specs=[ANYWHERE],
        out_specs=IN_VMEM,
        scratch_shapes=[pltpu.SemaphoreType.DMA],
        compiler_params=params(WIDE_VMEM),
        cost_estimate=cost(0, 2_000_000),
        name="take_share",
    )(encoded)


def pack_kernel(rows_ref, sibling_rows_ref, share_ref, sibling_ref, *outs):
    me = lax.axis_index("seq")
    chip, core = me // 2, lax.rem(me, 2)
    for ahead in range(CHIPS):
        device = lax.rem(chip + ahead, CHIPS) * 2 + core
        for j in range(CAP):
            row = jnp.clip(rows_ref[device, j], 0, STORED - 1)
            outs[ahead][j] = share_ref[row]
            row = jnp.clip(sibling_rows_ref[device, j], 0, STORED - 1)
            outs[ahead][CAP + j] = sibling_ref[row]


def pack_rows(rows, sibling_rows, share, sibling):
    return pl.pallas_call(
        pack_kernel,
        out_shape=[jax.ShapeDtypeStruct((2 * CAP, PART, E), BF16)] * CHIPS,
        in_specs=[IN_SMEM, IN_SMEM, IN_VMEM, IN_VMEM],
        out_specs=[IN_VMEM] * CHIPS,
        compiler_params=params(WIDE_VMEM),
        cost_estimate=cost(0, 3_000_000),
        name="pack_rows",
    )(rows, sibling_rows, share, sibling)


def places_of(neighbour_ref):
    me = lax.axis_index("seq")
    chip, core = me // 2, lax.rem(me, 2)
    sources = [neighbour_ref[r // KNB, r % KNB] for r in range(REQ)]
    places = []
    for r in range(REQ):
        earlier = jnp.int32(0)
        for q in range(r):
            earlier = earlier + (sources[q] == sources[r]).astype(jnp.int32)
        away = lax.rem(sources[r] // 2 - chip + CHIPS, CHIPS)
        other = (lax.rem(sources[r], 2) != core).astype(jnp.int32)
        places.append((away, other, jnp.minimum(earlier, CAP - 1)))
    return places


def pick_kernel(neighbour_ref, *refs):
    arrived, outs, table = refs[:CHIPS], refs[CHIPS:-1], refs[-1]
    for at in range(SLOTS):
        table[at] = REQ
    for r, (away, other, slot) in enumerate(places_of(neighbour_ref)):
        table[away * 2 * CAP + other * CAP + slot] = r
    half = GROUPS[0][1] * KNB
    for away in range(CHIPS):
        for block in range(2 * CAP):
            r = table[away * 2 * CAP + block]
            ref = arrived[(CHIPS - away) % CHIPS]

            @pl.when(r < half)
            def _():
                outs[0][r] = ref[block]

            @pl.when((r >= half) & (r < REQ))
            def _():
                outs[1][r - half] = ref[block]


def pick(neighbour, arrived):
    return pl.pallas_call(
        pick_kernel,
        out_shape=[
            jax.ShapeDtypeStruct((spans * KNB, PART, E), BF16) for first, spans in GROUPS
        ],
        in_specs=[IN_SMEM] + [IN_VMEM] * CHIPS,
        out_specs=[IN_VMEM] * len(GROUPS),
        scratch_shapes=[pltpu.SMEM((SLOTS,), jnp.int32)],
        compiler_params=params(),
        cost_estimate=cost(0, 3_000_000),
        name="pick",
    )(neighbour, *arrived)


def attention_kernel(*refs):
    pieces = refs[:N_TP]
    kw_ref, vw_ref, q_ref, g_ref = refs[N_TP : N_TP + 4]
    ctx_ref, qg_ref = refs[-(N_TP + 7) : -(N_TP + 5)]
    outs = refs[-(N_TP + 5) : -5]
    xs, ks, vs, kgs, vgs = refs[-5:]
    for shift in range(N_TP):
        begin = pl.multiple_of(member(shift) * PART, PART)
        for k in range(KNB):
            xs[k, pl.ds(begin, PART), :] = pieces[shift][k]
    x = xs[...].reshape(KEYS, E)
    ks[...] = dot(x, kw_ref[...]).astype(BF16)
    vs[...] = dot(x, vw_ref[...]).astype(BF16)
    cols = [slice(h * DH, (h + 1) * DH) for h in range(HEADS_DEV)]
    scores = [dot_nt(q_ref[:, c], ks[:, c]) for c in cols]
    prob_grads = [dot_nt(g_ref[:, c], vs[:, c]) for c in cols]
    lows, dscores = [], []
    for score, prob_grad in zip(scores, prob_grads):
        exponent = jnp.exp(score * SCALE)
        probs = exponent / jnp.sum(exponent, axis=-1, keepdims=True)
        delta = jnp.sum(probs * prob_grad, axis=-1, keepdims=True)
        lows.append(probs.astype(BF16))
        dscores.append((probs * (prob_grad - delta) * SCALE).astype(BF16))
    for c, low, dscore in zip(cols, lows, dscores):
        kgs[c, :] = dot_tn(q_ref[:, c], dscore).astype(BF16)
        vgs[c, :] = dot_tn(g_ref[:, c], low).astype(BF16)
    for c, low, dscore in zip(cols, lows, dscores):
        ctx_ref[:, c] = dot(low, vs[:, c]).astype(BF16)
        qg_ref[:, c] = dot(dscore, ks[:, c]).astype(BF16)
    for shift in range(N_TP):
        begin = pl.multiple_of(member(shift) * EQ, 16)
        piece = dot(kw_ref[pl.ds(begin, EQ), :], kgs[...])
        piece = (piece + dot(vw_ref[pl.ds(begin, EQ), :], vgs[...])).astype(BF16)
        for k in range(KNB):
            outs[shift][k] = piece[:, k * NTOK : (k + 1) * NTOK]


def attention(pieces, kw, vw, queries, ctx_grad, first, spans, held):
    whole = pl.BlockSpec((E, WIDTH), lambda c: (0, 0))
    span = pl.BlockSpec((SPAN, WIDTH), lambda c: (c + first, 0))
    arrived = pl.BlockSpec((KNB, PART, E), lambda c: (c, 0, 0))
    back = pl.BlockSpec((KNB, EQ, NTOK), lambda c: (c, 0, 0))
    wide = jax.ShapeDtypeStruct((TOKENS_DEV, WIDTH), BF16)
    piece = jax.ShapeDtypeStruct((spans * KNB, EQ, NTOK), BF16)
    at = N_TP + 4
    return pl.pallas_call(
        attention_kernel,
        grid=(spans,),
        out_shape=[wide, wide] + [piece] * N_TP,
        in_specs=[arrived] * N_TP + [whole, whole, span, span] + [ANYWHERE] * len(held),
        out_specs=[span, span] + [back] * N_TP,
        scratch_shapes=[
            pltpu.VMEM((KNB, NTOK, E), BF16),
            pltpu.VMEM((KEYS, WIDTH), BF16),
            pltpu.VMEM((KEYS, WIDTH), BF16),
            pltpu.VMEM((WIDTH, KEYS), BF16),
            pltpu.VMEM((WIDTH, KEYS), BF16),
        ],
        input_output_aliases={at + i: i for i in range(len(held))},
        compiler_params=params(),
        cost_estimate=cost(spans * 2_200_000_000, 5_000_000 + spans * 1_500_000),
        name="attention",
    )(*pieces, kw, vw, queries, ctx_grad, *held)


def sum_kernel(*refs):
    out_ref = refs[-1]
    for r in range(out_ref.shape[0]):
        total = refs[0][r].astype(F32)
        for part in refs[1:-1]:
            total = total + part[r].astype(F32)
        out_ref[r] = total.astype(BF16)


def sum_parts(parts):
    return pl.pallas_call(
        sum_kernel,
        out_shape=jax.ShapeDtypeStruct(parts[0].shape, BF16),
        in_specs=[IN_VMEM] * len(parts),
        out_specs=IN_VMEM,
        compiler_params=params(),
        cost_estimate=cost(0, 2_000_000),
        name="sum_parts",
    )(*parts)


def place_kernel(neighbour_ref, sibling_neighbour_ref, *refs):
    grads, outs, table = refs[:4], refs[4:-1], refs[-1]
    half = GROUPS[0][1] * KNB
    for at in range(SLOTS):
        table[at] = REQ
    for whose, ref in enumerate((neighbour_ref, sibling_neighbour_ref)):
        for r, (away, other, slot) in enumerate(places_of(ref)):
            at = away * 2 * CAP + whose * CAP + slot

            @pl.when(other == 0)
            def _():
                table[at] = r

    for away in range(CHIPS):
        for block in range(2 * CAP):
            r = table[away * 2 * CAP + block]
            low, high = grads[2 * (block // CAP)], grads[2 * (block // CAP) + 1]
            out = outs[away]

            @pl.when(r < half)
            def _():
                out[block] = low[r]

            @pl.when((r >= half) & (r < REQ))
            def _():
                out[block] = high[r - half]

            @pl.when(r >= REQ)
            def _():
                out[block] = jnp.zeros((EQ, NTOK), BF16)


def place(neighbour, sibling_neighbour, grads):
    return pl.pallas_call(
        place_kernel,
        out_shape=[jax.ShapeDtypeStruct((2 * CAP, EQ, NTOK), BF16)] * CHIPS,
        in_specs=[IN_SMEM, IN_SMEM] + [IN_VMEM] * len(grads),
        out_specs=[IN_VMEM] * CHIPS,
        scratch_shapes=[pltpu.SMEM((SLOTS,), jnp.int32)],
        compiler_params=params(),
        cost_estimate=cost(0, 3_000_000),
        name="place",
    )(neighbour, sibling_neighbour, *grads)


def collect_kernel(rows_ref, *refs):
    arrived, (out_ref, acc) = refs[:CHIPS], refs[CHIPS:]
    me = lax.axis_index("seq")
    chip, core = me // 2, lax.rem(me, 2)
    acc[...] = jnp.zeros(acc.shape, F32)
    for behind in range(CHIPS):
        device = lax.rem(chip - behind + CHIPS, CHIPS) * 2
        for block in range(2 * CAP):
            requester = device + (core if block < CAP else 1 - core)
            row = jnp.clip(rows_ref[requester, block % CAP], 0, STORED - 1)
            acc[row] += arrived[behind][block].astype(F32)
    out_ref[...] = acc[...].astype(BF16)


def collect(rows, arrived):
    return pl.pallas_call(
        collect_kernel,
        out_shape=jax.ShapeDtypeStruct((STORED, EQ, NTOK), BF16),
        in_specs=[IN_SMEM] + [IN_VMEM] * CHIPS,
        out_specs=IN_VMEM,
        scratch_shapes=[pltpu.VMEM((STORED, EQ, NTOK), F32)],
        compiler_params=params(),
        cost_estimate=cost(0, 3_000_000),
        name="collect",
    )(rows, *arrived)


def swap(x):
    return lax.ppermute(x, "seq", [(i, i ^ 1) for i in range(N_SEQ)])


def ahead(x, by):
    return lax.ppermute(x, "seq", [(i, (i + 2 * by) % N_SEQ) for i in range(N_SEQ)])


def after(x, *done):
    return lax.optimization_barrier((x,) + done)[0]


def exchange(messages):
    arrived = [messages[0]] + [None] * (CHIPS - 1)
    for by, behind in ((3, 0), (5, 0), (4, 0), (2, 0), (6, 0), (1, 3), (7, 5)):
        message = messages[by]
        if behind:
            message = after(message, arrived[behind])
        arrived[by] = ahead(message, by)
    return arrived


def turn(x, by):
    return lax.ppermute(x, "tp", [(i, (i + by) % N_TP) for i in range(N_TP)])


def section_back(x):
    count = lax.axis_size("section")
    return lax.ppermute(x, "section", [(i, i - 1) for i in range(1, count)])


def deliver_kernel(*refs):
    out_ref = refs[-1]
    at = 0
    for ref in refs[:-1]:
        rows = ref.shape[0]
        out_ref[at : at + rows] = ref[...]
        at += rows


def deliver(parts):
    return pl.pallas_call(
        deliver_kernel,
        out_shape=jax.ShapeDtypeStruct((TOKENS_DEV, WIDTH), BF16),
        in_specs=[IN_VMEM] * len(parts),
        out_specs=IN_VMEM,
        compiler_params=params(),
        cost_estimate=cost(0, 2_000_000),
        name="deliver",
    )(*parts)


def body(queries, encoded, neighbour, send_rows, key_weight, value_weight, ctx_grad):
    sources, rows = neighbour[0], send_rows[0, 0]
    kw, vw = key_weight[0], value_weight[0]
    share = take_share(encoded[0])
    sibling_sources = swap(sources)
    sibling_rows = after(swap(rows), sibling_sources)
    arrived = exchange(pack_rows(rows, sibling_rows, share, swap(share)))
    picked = pick(sources, arrived)
    whole = []
    for own in picked:
        if whole:
            own = after(own, whole[0][-1])
        whole.append([own] + [turn(own, -shift) for shift in range(1, N_TP)])
    held = ()
    grads = []
    for group, (first, spans) in enumerate(GROUPS):
        *held, first_piece, second, third, fourth = attention(
            whole[group], kw, vw, queries[0], ctx_grad[0], first, spans, held
        )
        turned = [turn(x, by) for by, x in ((1, second), (2, third), (3, fourth))]
        grads.append(sum_parts([first_piece] + turned))
    context, query_grad = held
    passed = section_back(query_grad)
    messages = place(sources, sibling_sources, grads + [swap(grad) for grad in grads])
    returned = exchange(messages)
    encoded_grad = jnp.swapaxes(collect(rows, returned), 1, 2)
    passed = deliver([after(passed, returned[3])])
    return (context[None], passed[None], encoded_grad[None])


def solution(mesh):
    placed = (
        P("section", "seq", "tp"),
        P("section", "seq", None, None),
        P("section", "seq", None),
        P("section", "seq", None, None),
        P("section", None, "tp"),
        P("section", None, "tp"),
        P("section", "seq", "tp"),
    )
    return jax.shard_map(
        body,
        mesh=mesh,
        in_specs=placed,
        out_specs=(
            P("section", "seq", "tp"),
            P("section", "seq", "tp"),
            P("section", "seq", None, "tp"),
        ),
        check_vma=False,
    )
```

time: 546 us -> 179 us (0.33)
  blocking collectives: 169 us -> 0 us
  waiting for transfers between devices: 200 us -> 69.8 us
  matrix products: 77.6 us -> 0 us
  local copies, waits for them, and re-layouts: 72.3 us -> 2.91 us
  starting transfers between devices: 11.4 us -> 70.5 us
  Pallas kernels: 0 us -> 33.6 us
  between operations: 14.3 us -> 0.78 us
    all_to_all x1 -> x0, blocking collectives: 169 us -> none  [body(): lax.all_to_all(buffer, 'seq', split_axis=0, concat_axis=0, tiled=True)]
    all_to_all x1 -> x0, waiting for transfers between devices: 159 us -> none  [body(): lax.all_to_all(encoded_local[picked_rows], 'seq', split_axis=0, concat_ax...]
    dot_general x11 -> x0, matrix products: 77.6 us -> none  [the longest x1 24.3 us: body(): jnp.einsum('chqk,cqhd->ckhd', dscore, query_blocks, preferred_element_typ...]
    ppermute x1 -> x32, starting transfers between devices: 1.29 us -> 70.5 us  [the longest x14 35.6 us: ahead(): lax.ppermute(x, 'seq', [(i, (i + 2 * by) % N_SEQ) for i in range(N_SEQ)])]
    ppermute x1 -> x32, waiting for transfers between devices: 13.9 us -> 69.8 us  [the longest x14 53.2 us: ahead(): lax.ppermute(x, 'seq', [(i, (i + 2 * by) % N_SEQ) for i in range(N_SEQ)])]
    pallas_call x0 -> x10, Pallas kernels: none -> 33.6 us  [the longest x2 21.7 us: attention(): pl.pallas_call(attention_kernel, grid=(spans,), out_shape=[wide, wide] +...]
    reduce_scatter x1 -> x0, waiting for transfers between devices: 27.5 us -> none  [body(): lax.psum_scatter(sent_back.astype(jnp.float32).astype(jnp.bfloat16), 'tp'...]
    gather x2 -> x0, local copies, waits for them, and re-layouts: 12.1 us -> none  [the longest x1 6.45 us: body(): encoded_local[picked_rows]]
  transfers between devices with their start and end apart: 3 -> 32, of which waited for: 3 -> 17; matrix products, arithmetic and copies ran while one was open for 6% -> 0% of each run, Pallas kernels for 0% -> 14%
where the time goes in v1:
time: 179 us; the launch traced here: 178 us
  starting transfers between devices  70.5 us (39%)
  waiting for transfers between devices  69.8 us (39%)
  Pallas kernels  33.6 us (19%)
  local copies, waits for them, and re-layouts  2.91 us (2%)
    ppermute x14, waiting for transfers between devices, ahead(): lax.ppermute(x, 'seq', [(i, (i + 2 * by) % N_SEQ) for i in range(N_SEQ)])  53.2 us
    ppermute x14, starting transfers between devices, ahead(): lax.ppermute(x, 'seq', [(i, (i + 2 * by) % N_SEQ) for i in range(N_SEQ)])  35.6 us
    pallas_call x2, Pallas kernels, attention(): pl.pallas_call(attention_kernel, grid=(spans,), out_shape=[wide, wide] +...  21.7 us
    ppermute x12, starting transfers between devices, turn(): return lax.ppermute(x, 'tp', [(i, (i + by) % N_TP) for i in range(N_TP)])  17.4 us
    ppermute x5, starting transfers between devices, swap(): return lax.ppermute(x, 'seq', [(i, i ^ 1) for i in range(N_SEQ)])  16.2 us
    ppermute x12, waiting for transfers between devices, turn(): return lax.ppermute(x, 'tp', [(i, (i + by) % N_TP) for i in range(N_TP)])  13.6 us
  transfers between devices with their start and end apart: 32, of which 17 were waited for; matrix products, arithmetic and copies ran while one was open for 0% of the time, Pallas kernels for 14%

profile of v1, /device:TPU:1, one launch (start us, length us, event | category | flops | bytes accessed | tf_op | source)
XLA Modules:
  0.0 177.6 jit_solution(14452498578828969572)
XLA Ops:
  0.7 2.2 %take_share.1.share_ref = bf16[16,32,896]{2,1,0:T(8,128)(2,1)} custom-call(bf16[16,128,896]{2,1,0:T(8,128)(2,1)} %bitcast.20), custom_call_target="tpu_custom_call" | custom-call | bytes 2000000 | tf_op jit(solution)/shard_map/take_share/pallas_call | solution.py:72
  2.9 3.3 %collective-permute-start.2 = (bf16[16,32,896]{2,1,0:T(8,128)(2,1)}, bf16[16,32,896]{2,1,0:T(8,128)(2,1)}, u32[]{:S(2)}, u32[]{:S(2)}) collective-permute-start(bf16[16,32,896]{2,1,0:T(8,128)(2,1)} %take_share.1.share_ref), channel_id=1, source_target_pairs={{0,4},{4,0},{8,12},{12,8},{16,20},{20,16},{24,28},{28,24},{32,36},... | collective-permute-start | bytes 2752520 | tf_op jit(solution)/shard_map/ppermute | solution.py:318
  9.0 2.8 %pack_rows.1 = (bf16[4,32,896]{2,1,0:T(8,128)(2,1)}, bf16[4,32,896]{2,1,0:T(8,128)(2,1)}, bf16[4,32,896]{2,1,0:T(8,128)(2,1)}, bf16[4,32,896]{2,1,0:T(8,128)(2,1...) custom-call(s32[16,2]{1,0:T(8,128)} %copy-done.1, ...), custom_call_target="tpu_custom_call" | custom-call | bytes 3000000 | tf_op jit(solution)/shard_map/pack_rows/pallas_call | solution.py:97
  11.8 2.6 %collective-permute-start.3 = (bf16[4,32,896]{2,1,0:T(8,128)(2,1)}, bf16[4,32,896]{2,1,0:T(8,128)(2,1)S(1)}, u32[]{:S(2)}, u32[]{:S(2)}) collective-permute-start(bf16[4,32,896]{2,1,0:T(8,128)(2,1)} %get-tuple-element.43), channel_id=1, source_target_pairs={{0,24},{4,28},{8,32},{12,36},{16,40},{20,44},{24,48},{28,52},{32,5... | collective-permute-start | bytes 688136 | tf_op jit(solution)/shard_map/ppermute | solution.py:322
  14.4 2.2 %collective-permute-start.7 = (bf16[4,32,896]{2,1,0:T(8,128)(2,1)}, bf16[4,32,896]{2,1,0:T(8,128)(2,1)S(1)}, u32[]{:S(2)}, u32[]{:S(2)}) collective-permute-start(bf16[4,32,896]{2,1,0:T(8,128)(2,1)} %get-tuple-element.47), channel_id=1, source_target_pairs={{0,40},{4,44},{8,48},{12,52},{16,56},{20,60},{24,0},{28,4},{32,8},... | collective-permute-start | bytes 688136 | tf_op jit(solution)/shard_map/ppermute | solution.py:322
  17.8 4.9 %collective-permute-start.6 = (bf16[4,32,896]{2,1,0:T(8,128)(2,1)}, bf16[4,32,896]{2,1,0:T(8,128)(2,1)S(1)}, u32[]{:S(2)}, u32[]{:S(2)}) collective-permute-start(bf16[4,32,896]{2,1,0:T(8,128)(2,1)} %get-tuple-element.46), channel_id=1, source_target_pairs={{0,32},{4,36},{8,40},{12,44},{16,48},{20,52},{24,56},{28,60},{32,0... | collective-permute-start | bytes 688136 | tf_op jit(solution)/shard_map/ppermute | solution.py:322
  22.7 2.4 %collective-permute-start.8 = (bf16[4,32,896]{2,1,0:T(8,128)(2,1)}, bf16[4,32,896]{2,1,0:T(8,128)(2,1)S(1)}, u32[]{:S(2)}, u32[]{:S(2)}) collective-permute-start(bf16[4,32,896]{2,1,0:T(8,128)(2,1)} %get-tuple-element.48), channel_id=1, source_target_pairs={{0,48},{4,52},{8,56},{12,60},{16,0},{20,4},{24,8},{28,12},{32,16},... | collective-permute-start | bytes 688136 | tf_op jit(solution)/shard_map/ppermute | solution.py:322
  25.0 3.6 %collective-permute-done.3.refs_3_ = bf16[4,32,896]{2,1,0:T(8,128)(2,1)S(1)} collective-permute-done((bf16[4,32,896]{2,1,0:T(8,128)(2,1)}, bf16[4,32,896]{2,1,0:T(8,128)(2,1)S(1)}, u32[]{:S(2)}, u32[]{:S(2)}) %collective-permute-start.3) | collective-permute-done | bytes 229408 | tf_op jit(solution)/shard_map/ppermute | solution.py:322
  28.6 3.8 %collective-permute-start.4 = (bf16[4,32,896]{2,1,0:T(8,128)(2,1)}, bf16[4,32,896]{2,1,0:T(8,128)(2,1)S(1)}, u32[]{:S(2)}, u32[]{:S(2)}) collective-permute-start(bf16[4,32,896]{2,1,0:T(8,128)(2,1)} %get-tuple-element.44), channel_id=1, source_target_pairs={{0,8},{4,12},{8,16},{12,20},{16,24},{20,28},{24,32},{28,36},{32,40... | collective-permute-start | bytes 688136 | tf_op jit(solution)/shard_map/ppermute | solution.py:322
  32.5 8.1 %collective-permute-done.5.refs_2_ = bf16[4,32,896]{2,1,0:T(8,128)(2,1)S(1)} collective-permute-done((bf16[4,32,896]{2,1,0:T(8,128)(2,1)}, bf16[4,32,896]{2,1,0:T(8,128)(2,1)S(1)}, u32[]{:S(2)}, u32[]{:S(2)}) %collective-permute-start.5) | collective-permute-done | bytes 229408 | tf_op jit(solution)/shard_map/ppermute | solution.py:322
  40.6 8.9 %collective-permute-done.6.refs_4_ = bf16[4,32,896]{2,1,0:T(8,128)(2,1)S(1)} collective-permute-done((bf16[4,32,896]{2,1,0:T(8,128)(2,1)}, bf16[4,32,896]{2,1,0:T(8,128)(2,1)S(1)}, u32[]{:S(2)}, u32[]{:S(2)}) %collective-permute-start.6) | collective-permute-done | bytes 229408 | tf_op jit(solution)/shard_map/ppermute | solution.py:322
  49.5 3.1 %collective-permute-done.8.refs_6_ = bf16[4,32,896]{2,1,0:T(8,128)(2,1)S(1)} collective-permute-done((bf16[4,32,896]{2,1,0:T(8,128)(2,1)}, bf16[4,32,896]{2,1,0:T(8,128)(2,1)S(1)}, u32[]{:S(2)}, u32[]{:S(2)}) %collective-permute-start.8) | collective-permute-done | bytes 229408 | tf_op jit(solution)/shard_map/ppermute | solution.py:322
  52.6 3.5 %collective-permute-done.4.refs_1_ = bf16[4,32,896]{2,1,0:T(8,128)(2,1)S(1)} collective-permute-done((bf16[4,32,896]{2,1,0:T(8,128)(2,1)}, bf16[4,32,896]{2,1,0:T(8,128)(2,1)S(1)}, u32[]{:S(2)}, u32[]{:S(2)}) %collective-permute-start.4) | collective-permute-done | bytes 229408 | tf_op jit(solution)/shard_map/ppermute | solution.py:322
  61.2 2.5 %collective-permute-start.15 = (bf16[6,32,896]{2,1,0:T(8,128)(2,1)S(1)}, bf16[6,32,896]{2,1,0:T(8,128)(2,1)S(1)}, u32[]{:S(2)}, u32[]{:S(2)}) collective-permute-start(bf16[6,32,896]{2,1,0:T(8,128)(2,1)S(1)} %get-tuple-element.52.refs_0_), channel_id=1, source_target_pairs={{0,2},{1,3},{2,0},{3,1},{4,6},{5,7},{6,4},{7,5},{8,10},{9,11},{10,... | collective-permute-start | bytes 1032200 | tf_op jit(solution)/shard_map/ppermute | solution.py:340
  64.8 5.0 %collective-permute-done.10.refs_3_ = bf16[6,32,896]{2,1,0:T(8,128)(2,1)S(1)} collective-permute-done((bf16[6,32,896]{2,1,0:T(8,128)(2,1)S(1)}, bf16[6,32,896]{2,1,0:T(8,128)(2,1)S(1)}, u32[]{:S(2)}, u32[]{:S(2)}) %collective-permute-start.10) | collective-permute-done | bytes 344096 | tf_op jit(solution)/shard_map/ppermute | solution.py:340
  69.9 2.4 %collective-permute-start.12 = (bf16[6,32,896]{2,1,0:T(8,128)(2,1)S(1)}, bf16[6,32,896]{2,1,0:T(8,128)(2,1)S(1)}, u32[]{:S(2)}, u32[]{:S(2)}) collective-permute-start(bf16[6,32,896]{2,1,0:T(8,128)(2,1)S(1)} %get-tuple-element.53.refs_0_), channel_id=1, source_target_pairs={{0,2},{1,3},{2,0},{3,1},{4,6},{5,7},{6,4},{7,5},{8,10},{9,11},{10,... | collective-permute-start | bytes 1032200 | tf_op jit(solution)/shard_map/ppermute | solution.py:340
  73.5 4.8 %collective-permute-done.15.refs_2_ = bf16[6,32,896]{2,1,0:T(8,128)(2,1)S(1)} collective-permute-done((bf16[6,32,896]{2,1,0:T(8,128)(2,1)S(1)}, bf16[6,32,896]{2,1,0:T(8,128)(2,1)S(1)}, u32[]{:S(2)}, u32[]{:S(2)}) %collective-permute-start.15) | collective-permute-done | bytes 344096 | tf_op jit(solution)/shard_map/ppermute | solution.py:340
  80.7 10.8 %attention.2 = (bf16[384,1024]{1,0:T(8,128)(2,1)}, bf16[384,1024]{1,0:T(8,128)(2,1)S(1)}, bf16[6,224,128]{2,1,0:T(8,128)(2,1)S(1)}, bf16[6,224,128]{2,1,0:T(8,12...) custom-call(bf16[6,32,896]{2,1,0:T(8,128)(2,1)S(1)} %get-tuple-element.52.refs_0_, ...), custom_call_target="tpu_custom_call" | custom-call | flops 6600000000 | bytes 9500000 | tf_op jit(solution)/shard_map/attention/pallas_call | solution.py:204
  92.4 4.3 %collective-permute-start.18 = (bf16[6,224,128]{2,1,0:T(8,128)(2,1)S(1)}, bf16[6,224,128]{2,1,0:T(8,128)(2,1)S(1)}, u32[]{:S(2)}, u32[]{:S(2)}) collective-permute-start(bf16[6,224,128]{2,1,0:T(8,128)(2,1)S(1)} %get-tuple-element.60), channel_id=1, source_target_pairs={{0,2},{1,3},{2,0},{3,1},{4,6},{5,7},{6,4},{7,5},{8,10},{9,11},{10,... | collective-permute-start | bytes 1032200 | tf_op jit(solution)/shard_map/ppermute | solution.py:340
  96.7 10.9 %attention.3 = (bf16[384,1024]{1,0:T(8,128)(2,1)}, bf16[384,1024]{1,0:T(8,128)(2,1)S(1)}, bf16[6,224,128]{2,1,0:T(8,128)(2,1)S(1)}, bf16[6,224,128]{2,1,0:T(8,12...) custom-call(bf16[6,32,896]{2,1,0:T(8,128)(2,1)S(1)} %get-tuple-eleme, ...), custom_call_target="tpu_custom_call", output_to_operand_aliasing={{0}: (8, {}), {1}: (9, {})} | custom-call | flops 6600000000 | bytes 9500000 | tf_op jit(solution)/shard_map/attention/pallas_call | solution.py:204
  109.0 2.4 %collective-permute-start.22 = (bf16[6,224,128]{2,1,0:T(8,128)(2,1)S(1)}, bf16[6,224,128]{2,1,0:T(8,128)(2,1)S(1)}, u32[]{:S(2)}, u32[]{:S(2)}) collective-permute-start(bf16[6,224,128]{2,1,0:T(8,128)(2,1)S(1)} %get-tuple-element.65), channel_id=1, source_target_pairs={{0,3},{1,0},{2,1},{3,2},{4,7},{5,4},{6,5},{7,6},{8,11},{9,8},{10,9... | collective-permute-start | bytes 1032200 | tf_op jit(solution)/shard_map/ppermute | solution.py:340
  112.9 6.1 %collective-permute-start.23 = (bf16[6,224,128]{2,1,0:T(8,128)(2,1)S(1)}, bf16[6,224,128]{2,1,0:T(8,128)(2,1)S(1)}, u32[]{:S(2)}, u32[]{:S(2)}) collective-permute-start(bf16[6,224,128]{2,1,0:T(8,128)(2,1)S(1)} %sum_parts.2.refs_0_), channel_id=1, source_target_pairs={{0,4},{4,0},{8,12},{12,8},{16,20},{20,16},{24,28},{28,24},{32,36},... | collective-permute-start | bytes 1032200 | tf_op jit(solution)/shard_map/ppermute | solution.py:318
  119.0 2.8 %collective-permute-done.21.refs_2_ = bf16[6,224,128]{2,1,0:T(8,128)(2,1)S(1)} collective-permute-done((bf16[6,224,128]{2,1,0:T(8,128)(2,1)S(1)}, bf16[6,224,128]{2,1,0:T(8,128)(2,1)S(1)}, u32[]{:S(2)}, u32[]{:S(2)}) %collective-permute-start.21) | collective-permute-done | bytes 344096 | tf_op jit(solution)/shard_map/ppermute | solution.py:340
  122.0 6.2 %collective-permute-start.24 = (bf16[6,224,128]{2,1,0:T(8,128)(2,1)S(1)}, bf16[6,224,128]{2,1,0:T(8,128)(2,1)S(1)}, u32[]{:S(2)}, u32[]{:S(2)}) collective-permute-start(bf16[6,224,128]{2,1,0:T(8,128)(2,1)S(1)} %sum_parts.3.refs_1_), channel_id=1, source_target_pairs={{0,4},{4,0},{8,12},{12,8},{16,20},{20,16},{24,28},{28,24},{32,36},... | collective-permute-start | bytes 1032200 | tf_op jit(solution)/shard_map/ppermute | solution.py:318
  131.5 4.4 %collective-permute-start.25 = (bf16[4,224,128]{2,1,0:T(8,128)(2,1)S(1)}, bf16[4,224,128]{2,1,0:T(8,128)(2,1)S(1)}, u32[]{:S(2)}, u32[]{:S(2)}) collective-permute-start(bf16[4,224,128]{2,1,0:T(8,128)(2,1)S(1)} %get-tuple-element.66), channel_id=1, source_target_pairs={{0,24},{4,28},{8,32},{12,36},{16,40},{20,44},{24,48},{28,52},{32,5... | collective-permute-start | bytes 688136 | tf_op jit(solution)/shard_map/ppermute | solution.py:322
  137.3 3.6 %collective-permute-start.28 = (bf16[4,224,128]{2,1,0:T(8,128)(2,1)S(1)}, bf16[4,224,128]{2,1,0:T(8,128)(2,1)S(1)}, u32[]{:S(2)}, u32[]{:S(2)}) collective-permute-start(bf16[4,224,128]{2,1,0:T(8,128)(2,1)S(1)} %get-tuple-element.72), channel_id=1, source_target_pairs={{0,32},{4,36},{8,40},{12,44},{16,48},{20,52},{24,56},{28,60},{32,0... | collective-permute-start | bytes 688136 | tf_op jit(solution)/shard_map/ppermute | solution.py:322
  141.0 9.9 %collective-permute-done.25.refs_3_ = bf16[4,224,128]{2,1,0:T(8,128)(2,1)S(1)} collective-permute-done((bf16[4,224,128]{2,1,0:T(8,128)(2,1)S(1)}, bf16[4,224,128]{2,1,0:T(8,128)(2,1)S(1)}, u32[]{:S(2)}, u32[]{:S(2)}) %collective-permute-start.25) | collective-permute-done | bytes 229408 | tf_op jit(solution)/shard_map/ppermute | solution.py:322
  150.9 9.2 %collective-permute-start.26 = (bf16[4,224,128]{2,1,0:T(8,128)(2,1)S(1)}, bf16[4,224,128]{2,1,0:T(8,128)(2,1)S(1)}, u32[]{:S(2)}, u32[]{:S(2)}) collective-permute-start(bf16[4,224,128]{2,1,0:T(8,128)(2,1)S(1)} %get-tuple-element.70), channel_id=1, source_target_pairs={{0,8},{4,12},{8,16},{12,20},{16,24},{20,28},{24,32},{28,36},{32,40... | collective-permute-start | bytes 688136 | tf_op jit(solution)/shard_map/ppermute | solution.py:322
  161.0 7.1 %collective-permute-done.28.refs_4_ = bf16[4,224,128]{2,1,0:T(8,128)(2,1)S(1)} collective-permute-done((bf16[4,224,128]{2,1,0:T(8,128)(2,1)S(1)}, bf16[4,224,128]{2,1,0:T(8,128)(2,1)S(1)}, u32[]{:S(2)}, u32[]{:S(2)}) %collective-permute-start.28) | collective-permute-done | bytes 229408 | tf_op jit(solution)/shard_map/ppermute | solution.py:322
  168.1 5.2 %collective-permute-done.30.refs_6_ = bf16[4,224,128]{2,1,0:T(8,128)(2,1)S(1)} collective-permute-done((bf16[4,224,128]{2,1,0:T(8,128)(2,1)S(1)}, bf16[4,224,128]{2,1,0:T(8,128)(2,1)S(1)}, u32[]{:S(2)}, u32[]{:S(2)}) %collective-permute-start.30) | collective-permute-done | bytes 229408 | tf_op jit(solution)/shard_map/ppermute | solution.py:322
  173.3 2.1 %collective-permute-done.26.refs_1_ = bf16[4,224,128]{2,1,0:T(8,128)(2,1)S(1)} collective-permute-done((bf16[4,224,128]{2,1,0:T(8,128)(2,1)S(1)}, bf16[4,224,128]{2,1,0:T(8,128)(2,1)S(1)}, u32[]{:S(2)}, u32[]{:S(2)}) %collective-permute-start.26) | collective-permute-done | bytes 229408 | tf_op jit(solution)/shard_map/ppermute | solution.py:322
  175.4 2.2 %collect.1 = bf16[16,224,128]{2,1,0:T(8,128)(2,1)} custom-call(s32[16,2]{1,0:T(8,128)S(1)} %copy-done.2, bf16[4,224,128]{2,1,0:T(8,128)(2,1)S(1)} %get-tuple-element.68.refs_0_, bf16[4,224,128]{2,1,0:T(8,128)(2,1)S(1)} %collective-permute-done.26.refs_1_, bf16[4,224,128]{2,1,0:T(8,128)(2,1)S(1)} %collective-permute-done.27.refs_2_, ...), custom_call_target="tpu_custom_call" | custom-call | bytes 3000000 | tf_op jit(solution)/shard_map/collect/pallas_call | solution.py:305
  (64 shorter events, 23.4 us)
Async XLA Ops:
  2.9 5.8 %collective-permute-start.2 = (bf16[16,32,896]{2,1,0:T(8,128)(2,1)}, bf16[16,32,896]{2,1,0:T(8,128)(2,1)}, u32[]{:S(2)}, u32[]{:S(2)}) collective-permute-start(bf16[16,32,896]{2,1,0:T(8,128)(2,1)} %take_share.1.share_ref), channel_id=1, source_target_pairs={{0,4},{4,0},{8,12},{12,8},{16,20},{20,16},{24,28},{28,24},{32,36},... | collective-permute-start | bytes 2752520 | tf_op jit(solution)/shard_map/ppermute | solution.py:318
  6.3 2.0 %collective-permute-start = (s32[16,2]{1,0:T(8,128)S(1)}, s32[16,2]{1,0:T(8,128)S(1)}, u32[]{:S(2)}, u32[]{:S(2)}) collective-permute-start(s32[16,2]{1,0:T(8,128)S(1)} %copy.14.rows_ref), channel_id=1, source_target_pairs={{0,4},{4,0},{8,12},{12,8},{16,20},{20,16},{24,28},{28,24},{32,36},... | collective-permute-start | bytes 392 | tf_op jit(solution)/shard_map/ppermute | solution.py:318
  6.5 1.9 %collective-permute-start.1 = (s32[6,2]{1,0:T(8,128)S(1)}, s32[6,2]{1,0:T(8,128)S(1)}, u32[]{:S(2)}, u32[]{:S(2)}) collective-permute-start(s32[6,2]{1,0:T(8,128)S(1)} %copy.15.neighbour_ref), channel_id=1, source_target_pairs={{0,4},{4,0},{8,12},{12,8},{16,20},{20,16},{24,28},{28,24},{32,36},... | collective-permute-start | bytes 152 | tf_op jit(solution)/shard_map/ppermute | solution.py:318
  11.8 16.8 %collective-permute-start.3 = (bf16[4,32,896]{2,1,0:T(8,128)(2,1)}, bf16[4,32,896]{2,1,0:T(8,128)(2,1)S(1)}, u32[]{:S(2)}, u32[]{:S(2)}) collective-permute-start(bf16[4,32,896]{2,1,0:T(8,128)(2,1)} %get-tuple-element.43), channel_id=1, source_target_pairs={{0,24},{4,28},{8,32},{12,36},{16,40},{20,44},{24,48},{28,52},{32,5... | collective-permute-start | bytes 688136 | tf_op jit(solution)/shard_map/ppermute | solution.py:322
  14.4 18.0 %collective-permute-start.7 = (bf16[4,32,896]{2,1,0:T(8,128)(2,1)}, bf16[4,32,896]{2,1,0:T(8,128)(2,1)S(1)}, u32[]{:S(2)}, u32[]{:S(2)}) collective-permute-start(bf16[4,32,896]{2,1,0:T(8,128)(2,1)} %get-tuple-element.47), channel_id=1, source_target_pairs={{0,40},{4,44},{8,48},{12,52},{16,56},{20,60},{24,0},{28,4},{32,8},... | collective-permute-start | bytes 688136 | tf_op jit(solution)/shard_map/ppermute | solution.py:322
  16.6 24.0 %collective-permute-start.5 = (bf16[4,32,896]{2,1,0:T(8,128)(2,1)}, bf16[4,32,896]{2,1,0:T(8,128)(2,1)S(1)}, u32[]{:S(2)}, u32[]{:S(2)}) collective-permute-start(bf16[4,32,896]{2,1,0:T(8,128)(2,1)} %get-tuple-element.45), channel_id=1, source_target_pairs={{0,16},{4,20},{8,24},{12,28},{16,32},{20,36},{24,40},{28,44},{32,4... | collective-permute-start | bytes 688136 | tf_op jit(solution)/shard_map/ppermute | solution.py:322
  17.8 31.7 %collective-permute-start.6 = (bf16[4,32,896]{2,1,0:T(8,128)(2,1)}, bf16[4,32,896]{2,1,0:T(8,128)(2,1)S(1)}, u32[]{:S(2)}, u32[]{:S(2)}) collective-permute-start(bf16[4,32,896]{2,1,0:T(8,128)(2,1)} %get-tuple-element.46), channel_id=1, source_target_pairs={{0,32},{4,36},{8,40},{12,44},{16,48},{20,52},{24,56},{28,60},{32,0... | collective-permute-start | bytes 688136 | tf_op jit(solution)/shard_map/ppermute | solution.py:322
  22.7 29.9 %collective-permute-start.8 = (bf16[4,32,896]{2,1,0:T(8,128)(2,1)}, bf16[4,32,896]{2,1,0:T(8,128)(2,1)S(1)}, u32[]{:S(2)}, u32[]{:S(2)}) collective-permute-start(bf16[4,32,896]{2,1,0:T(8,128)(2,1)} %get-tuple-element.48), channel_id=1, source_target_pairs={{0,48},{4,52},{8,56},{12,60},{16,0},{20,4},{24,8},{28,12},{32,16},... | collective-permute-start | bytes 688136 | tf_op jit(solution)/shard_map/ppermute | solution.py:322
  28.6 27.4 %collective-permute-start.4 = (bf16[4,32,896]{2,1,0:T(8,128)(2,1)}, bf16[4,32,896]{2,1,0:T(8,128)(2,1)S(1)}, u32[]{:S(2)}, u32[]{:S(2)}) collective-permute-start(bf16[4,32,896]{2,1,0:T(8,128)(2,1)} %get-tuple-element.44), channel_id=1, source_target_pairs={{0,8},{4,12},{8,16},{12,20},{16,24},{20,28},{24,32},{28,36},{32,40... | collective-permute-start | bytes 688136 | tf_op jit(solution)/shard_map/ppermute | solution.py:322
  32.5 25.2 %collective-permute-start.9 = (bf16[4,32,896]{2,1,0:T(8,128)(2,1)}, bf16[4,32,896]{2,1,0:T(8,128)(2,1)S(1)}, u32[]{:S(2)}, u32[]{:S(2)}) collective-permute-start(bf16[4,32,896]{2,1,0:T(8,128)(2,1)} %get-tuple-element.50), channel_id=1, source_target_pairs={{0,56},{4,60},{8,0},{12,4},{16,8},{20,12},{24,16},{28,20},{32,24},... | collective-permute-start | bytes 688136 | tf_op jit(solution)/shard_map/ppermute | solution.py:322
  59.9 9.9 %collective-permute-start.10 = (bf16[6,32,896]{2,1,0:T(8,128)(2,1)S(1)}, bf16[6,32,896]{2,1,0:T(8,128)(2,1)S(1)}, u32[]{:S(2)}, u32[]{:S(2)}) collective-permute-start(bf16[6,32,896]{2,1,0:T(8,128)(2,1)S(1)} %get-tuple-element.52.refs_0_), channel_id=1, source_target_pairs={{0,1},{1,2},{2,3},{3,0},{4,5},{5,6},{6,7},{7,4},{8,9},{9,10},{10,1... | collective-permute-start | bytes 1032200 | tf_op jit(solution)/shard_map/ppermute | solution.py:340
  61.2 17.1 %collective-permute-start.15 = (bf16[6,32,896]{2,1,0:T(8,128)(2,1)S(1)}, bf16[6,32,896]{2,1,0:T(8,128)(2,1)S(1)}, u32[]{:S(2)}, u32[]{:S(2)}) collective-permute-start(bf16[6,32,896]{2,1,0:T(8,128)(2,1)S(1)} %get-tuple-element.52.refs_0_), channel_id=1, source_target_pairs={{0,2},{1,3},{2,0},{3,1},{4,6},{5,7},{6,4},{7,5},{8,10},{9,11},{10,... | collective-permute-start | bytes 1032200 | tf_op jit(solution)/shard_map/ppermute | solution.py:340
  63.7 15.6 %collective-permute-start.14 = (bf16[6,32,896]{2,1,0:T(8,128)(2,1)S(1)}, bf16[6,32,896]{2,1,0:T(8,128)(2,1)S(1)}, u32[]{:S(2)}, u32[]{:S(2)}) collective-permute-start(bf16[6,32,896]{2,1,0:T(8,128)(2,1)S(1)} %get-tuple-element.52.refs_0_), channel_id=1, source_target_pairs={{0,3},{1,0},{2,1},{3,2},{4,7},{5,4},{6,5},{7,6},{8,11},{9,8},{10,9... | collective-permute-start | bytes 1032200 | tf_op jit(solution)/shard_map/ppermute | solution.py:340
  69.9 26.8 %collective-permute-start.13 = (bf16[6,32,896]{2,1,0:T(8,128)(2,1)S(1)}, bf16[6,32,896]{2,1,0:T(8,128)(2,1)S(1)}, u32[]{:S(2)}, u32[]{:S(2)}) collective-permute-start(bf16[6,32,896]{2,1,0:T(8,128)(2,1)S(1)} %get-tuple-element.53.refs_0_), channel_id=1, source_target_pairs={{0,1},{1,2},{2,3},{3,0},{4,5},{5,6},{6,7},{7,4},{8,9},{9,10},{10,1... | collective-permute-start | bytes 1032200 | tf_op jit(solution)/shard_map/ppermute | solution.py:340
  69.9 26.8 %collective-permute-start.12 = (bf16[6,32,896]{2,1,0:T(8,128)(2,1)S(1)}, bf16[6,32,896]{2,1,0:T(8,128)(2,1)S(1)}, u32[]{:S(2)}, u32[]{:S(2)}) collective-permute-start(bf16[6,32,896]{2,1,0:T(8,128)(2,1)S(1)} %get-tuple-element.53.refs_0_), channel_id=1, source_target_pairs={{0,2},{1,3},{2,0},{3,1},{4,6},{5,7},{6,4},{7,5},{8,10},{9,11},{10,... | collective-permute-start | bytes 1032200 | tf_op jit(solution)/shard_map/ppermute | solution.py:340
  72.3 24.4 %collective-permute-start.11 = (bf16[6,32,896]{2,1,0:T(8,128)(2,1)S(1)}, bf16[6,32,896]{2,1,0:T(8,128)(2,1)S(1)}, u32[]{:S(2)}, u32[]{:S(2)}) collective-permute-start(bf16[6,32,896]{2,1,0:T(8,128)(2,1)S(1)} %get-tuple-element.53.refs_0_), channel_id=1, source_target_pairs={{0,3},{1,0},{2,1},{3,2},{4,7},{5,4},{6,5},{7,6},{8,11},{9,8},{10,9... | collective-permute-start | bytes 1032200 | tf_op jit(solution)/shard_map/ppermute | solution.py:340
  91.6 17.5 %collective-permute-start.17 = (bf16[6,224,128]{2,1,0:T(8,128)(2,1)S(1)}, bf16[6,224,128]{2,1,0:T(8,128)(2,1)S(1)}, u32[]{:S(2)}, u32[]{:S(2)}) collective-permute-start(bf16[6,224,128]{2,1,0:T(8,128)(2,1)S(1)} %get-tuple-element.59), channel_id=1, source_target_pairs={{0,1},{1,2},{2,3},{3,0},{4,5},{5,6},{6,7},{7,4},{8,9},{9,10},{10,1... | collective-permute-start | bytes 1032200 | tf_op jit(solution)/shard_map/ppermute | solution.py:340
  92.4 19.1 %collective-permute-start.18 = (bf16[6,224,128]{2,1,0:T(8,128)(2,1)S(1)}, bf16[6,224,128]{2,1,0:T(8,128)(2,1)S(1)}, u32[]{:S(2)}, u32[]{:S(2)}) collective-permute-start(bf16[6,224,128]{2,1,0:T(8,128)(2,1)S(1)} %get-tuple-element.60), channel_id=1, source_target_pairs={{0,2},{1,3},{2,0},{3,1},{4,6},{5,7},{6,4},{7,5},{8,10},{9,11},{10,... | collective-permute-start | bytes 1032200 | tf_op jit(solution)/shard_map/ppermute | solution.py:340
  96.7 16.0 %collective-permute-start.19 = (bf16[6,224,128]{2,1,0:T(8,128)(2,1)S(1)}, bf16[6,224,128]{2,1,0:T(8,128)(2,1)S(1)}, u32[]{:S(2)}, u32[]{:S(2)}) collective-permute-start(bf16[6,224,128]{2,1,0:T(8,128)(2,1)S(1)} %get-tuple-element.61), channel_id=1, source_target_pairs={{0,3},{1,0},{2,1},{3,2},{4,7},{5,4},{6,5},{7,6},{8,11},{9,8},{10,9... | collective-permute-start | bytes 1032200 | tf_op jit(solution)/shard_map/ppermute | solution.py:340
  107.6 11.4 %collective-permute-start.20 = (bf16[6,224,128]{2,1,0:T(8,128)(2,1)S(1)}, bf16[6,224,128]{2,1,0:T(8,128)(2,1)S(1)}, u32[]{:S(2)}, u32[]{:S(2)}) collective-permute-start(bf16[6,224,128]{2,1,0:T(8,128)(2,1)S(1)} %get-tuple-element.63), channel_id=1, source_target_pairs={{0,1},{1,2},{2,3},{3,0},{4,5},{5,6},{6,7},{7,4},{8,9},{9,10},{10,1... | collective-permute-start | bytes 1032200 | tf_op jit(solution)/shard_map/ppermute | solution.py:340
  109.0 12.8 %collective-permute-start.21 = (bf16[6,224,128]{2,1,0:T(8,128)(2,1)S(1)}, bf16[6,224,128]{2,1,0:T(8,128)(2,1)S(1)}, u32[]{:S(2)}, u32[]{:S(2)}) collective-permute-start(bf16[6,224,128]{2,1,0:T(8,128)(2,1)S(1)} %get-tuple-element.64), channel_id=1, source_target_pairs={{0,2},{1,3},{2,0},{3,1},{4,6},{5,7},{6,4},{7,5},{8,10},{9,11},{10,... | collective-permute-start | bytes 1032200 | tf_op jit(solution)/shard_map/ppermute | solution.py:340
  109.0 12.8 %collective-permute-start.22 = (bf16[6,224,128]{2,1,0:T(8,128)(2,1)S(1)}, bf16[6,224,128]{2,1,0:T(8,128)(2,1)S(1)}, u32[]{:S(2)}, u32[]{:S(2)}) collective-permute-start(bf16[6,224,128]{2,1,0:T(8,128)(2,1)S(1)} %get-tuple-element.65), channel_id=1, source_target_pairs={{0,3},{1,0},{2,1},{3,2},{4,7},{5,4},{6,5},{7,6},{8,11},{9,8},{10,9... | collective-permute-start | bytes 1032200 | tf_op jit(solution)/shard_map/ppermute | solution.py:340
  111.4 48.6 %collective-permute-start.16 = (bf16[384,1024]{1,0:T(8,128)(2,1)S(1)}, bf16[384,1024]{1,0:T(8,128)(2,1)S(1)}, u32[]{:S(2)}, u32[]{:S(2)}) collective-permute-start(bf16[384,1024]{1,0:T(8,128)(2,1)S(1)} %get-tuple-element.57), channel_id=1, source_target_pairs={{64,0},{128,64},{192,128},{65,1},{129,65},{193,129},{66,2},{130,66... | collective-permute-start | bytes 2359304 | tf_op jit(solution)/shard_map/ppermute | solution.py:345
  112.9 15.3 %collective-permute-start.23 = (bf16[6,224,128]{2,1,0:T(8,128)(2,1)S(1)}, bf16[6,224,128]{2,1,0:T(8,128)(2,1)S(1)}, u32[]{:S(2)}, u32[]{:S(2)}) collective-permute-start(bf16[6,224,128]{2,1,0:T(8,128)(2,1)S(1)} %sum_parts.2.refs_0_), channel_id=1, source_target_pairs={{0,4},{4,0},{8,12},{12,8},{16,20},{20,16},{24,28},{28,24},{32,36},... | collective-permute-start | bytes 1032200 | tf_op jit(solution)/shard_map/ppermute | solution.py:318
  122.0 7.5 %collective-permute-start.24 = (bf16[6,224,128]{2,1,0:T(8,128)(2,1)S(1)}, bf16[6,224,128]{2,1,0:T(8,128)(2,1)S(1)}, u32[]{:S(2)}, u32[]{:S(2)}) collective-permute-start(bf16[6,224,128]{2,1,0:T(8,128)(2,1)S(1)} %sum_parts.3.refs_1_), channel_id=1, source_target_pairs={{0,4},{4,0},{8,12},{12,8},{16,20},{20,16},{24,28},{28,24},{32,36},... | collective-permute-start | bytes 1032200 | tf_op jit(solution)/shard_map/ppermute | solution.py:318
  131.5 19.3 %collective-permute-start.25 = (bf16[4,224,128]{2,1,0:T(8,128)(2,1)S(1)}, bf16[4,224,128]{2,1,0:T(8,128)(2,1)S(1)}, u32[]{:S(2)}, u32[]{:S(2)}) collective-permute-start(bf16[4,224,128]{2,1,0:T(8,128)(2,1)S(1)} %get-tuple-element.66), channel_id=1, source_target_pairs={{0,24},{4,28},{8,32},{12,36},{16,40},{20,44},{24,48},{28,52},{32,5... | collective-permute-start | bytes 688136 | tf_op jit(solution)/shard_map/ppermute | solution.py:322
  136.0 14.9 %collective-permute-start.29 = (bf16[4,224,128]{2,1,0:T(8,128)(2,1)S(1)}, bf16[4,224,128]{2,1,0:T(8,128)(2,1)S(1)}, u32[]{:S(2)}, u32[]{:S(2)}) collective-permute-start(bf16[4,224,128]{2,1,0:T(8,128)(2,1)S(1)} %get-tuple-element.73), channel_id=1, source_target_pairs={{0,40},{4,44},{8,48},{12,52},{16,56},{20,60},{24,0},{28,4},{32,8},... | collective-permute-start | bytes 688136 | tf_op jit(solution)/shard_map/ppermute | solution.py:322
  136.1 24.9 %collective-permute-start.27 = (bf16[4,224,128]{2,1,0:T(8,128)(2,1)S(1)}, bf16[4,224,128]{2,1,0:T(8,128)(2,1)S(1)}, u32[]{:S(2)}, u32[]{:S(2)}) collective-permute-start(bf16[4,224,128]{2,1,0:T(8,128)(2,1)S(1)} %get-tuple-element.71), channel_id=1, source_target_pairs={{0,16},{4,20},{8,24},{12,28},{16,32},{20,36},{24,40},{28,44},{32,4... | collective-permute-start | bytes 688136 | tf_op jit(solution)/shard_map/ppermute | solution.py:322
  137.3 30.8 %collective-permute-start.28 = (bf16[4,224,128]{2,1,0:T(8,128)(2,1)S(1)}, bf16[4,224,128]{2,1,0:T(8,128)(2,1)S(1)}, u32[]{:S(2)}, u32[]{:S(2)}) collective-permute-start(bf16[4,224,128]{2,1,0:T(8,128)(2,1)S(1)} %get-tuple-element.72), channel_id=1, source_target_pairs={{0,32},{4,36},{8,40},{12,44},{16,48},{20,52},{24,56},{28,60},{32,0... | collective-permute-start | bytes 688136 | tf_op jit(solution)/shard_map/ppermute | solution.py:322
  150.9 22.4 %collective-permute-start.30 = (bf16[4,224,128]{2,1,0:T(8,128)(2,1)S(1)}, bf16[4,224,128]{2,1,0:T(8,128)(2,1)S(1)}, u32[]{:S(2)}, u32[]{:S(2)}) collective-permute-start(bf16[4,224,128]{2,1,0:T(8,128)(2,1)S(1)} %get-tuple-element.74), channel_id=1, source_target_pairs={{0,48},{4,52},{8,56},{12,60},{16,0},{20,4},{24,8},{28,12},{32,16},... | collective-permute-start | bytes 688136 | tf_op jit(solution)/shard_map/ppermute | solution.py:322
  150.9 24.5 %collective-permute-start.26 = (bf16[4,224,128]{2,1,0:T(8,128)(2,1)S(1)}, bf16[4,224,128]{2,1,0:T(8,128)(2,1)S(1)}, u32[]{:S(2)}, u32[]{:S(2)}) collective-permute-start(bf16[4,224,128]{2,1,0:T(8,128)(2,1)S(1)} %get-tuple-element.70), channel_id=1, source_target_pairs={{0,8},{4,12},{8,16},{12,20},{16,24},{20,28},{24,32},{28,36},{32,40... | collective-permute-start | bytes 688136 | tf_op jit(solution)/shard_map/ppermute | solution.py:322
  160.0 15.4 %collective-permute-start.31 = (bf16[4,224,128]{2,1,0:T(8,128)(2,1)S(1)}, bf16[4,224,128]{2,1,0:T(8,128)(2,1)S(1)}, u32[]{:S(2)}, u32[]{:S(2)}) collective-permute-start(bf16[4,224,128]{2,1,0:T(8,128)(2,1)S(1)} %get-tuple-element.76), channel_id=1, source_target_pairs={{0,56},{4,60},{8,0},{12,4},{16,8},{20,12},{24,16},{28,20},{32,24},... | collective-permute-start | bytes 688136 | tf_op jit(solution)/shard_map/ppermute | solution.py:322
  (10 other events, 300.1 us)

commit v2 on v1

--- a/solution.py
+++ b/solution.py
@@ -27,8 +27,11 @@
 EQ = E // N_TP
 KEYS = KNB * NTOK
 GROUPS = ((0, 3), (3, 3))
-VMEM = 24 * 1024 * 1024
+VMEM = 16 * 1024 * 1024
 WIDE_VMEM = 60 * 1024 * 1024
+STREAMS = 4
+FAR = (0, 3, 5, 4, 2)
+NEAR = (6, 1, 7)
 BF16 = jnp.bfloat16
 F32 = jnp.float32
 SCALE = 1.0 / math.sqrt(DH)
@@ -61,11 +64,21 @@
     return lax.rem(lax.axis_index("tp") + shift, N_TP)
 
 
-def share_kernel(encoded_ref, out_ref, sem):
+def share_kernel(encoded_ref, out_ref, buffer, in_sems, out_sems):
     start = pl.multiple_of(lax.axis_index("tp") * PART, PART)
-    copy = pltpu.make_async_copy(encoded_ref.at[:, pl.ds(start, PART)], out_ref, sem)
-    copy.start()
-    copy.wait()
+    reads, writes = [], []
+    for n in range(STREAMS):
+        rows = pl.ds(n * (STORED // STREAMS), STORED // STREAMS)
+        source = encoded_ref.at[rows, pl.ds(start, PART)]
+        reads.append(pltpu.make_async_copy(source, buffer.at[rows], in_sems.at[n]))
+        writes.append(pltpu.make_async_copy(buffer.at[rows], out_ref.at[rows], out_sems.at[n]))
+    for read in reads:
+        read.start()
+    for read, write in zip(reads, writes):
+        read.wait()
+        write.start()
+    for write in writes:
+        write.wait()
 
 
 def take_share(encoded):
@@ -73,32 +86,55 @@
         share_kernel,
         out_shape=jax.ShapeDtypeStruct((STORED, PART, E), BF16),
         in_specs=[ANYWHERE],
-        out_specs=IN_VMEM,
-        scratch_shapes=[pltpu.SemaphoreType.DMA],
+        out_specs=ANYWHERE,
+        scratch_shapes=[
+            pltpu.VMEM((STORED, PART, E), BF16),
+            pltpu.SemaphoreType.DMA((STREAMS,)),
+            pltpu.SemaphoreType.DMA((STREAMS,)),
+        ],
         compiler_params=params(WIDE_VMEM),
         cost_estimate=cost(0, 2_000_000),
         name="take_share",
     )(encoded)
 
 
-def pack_kernel(rows_ref, sibling_rows_ref, share_ref, sibling_ref, *outs):
+def pack_kernel(rows_ref, sibling_rows_ref, share_ref, sibling_ref, *refs):
+    outs, (held, messages, in_sems, out_sems) = refs[:CHIPS], refs[CHIPS:]
+    reads = [
+        pltpu.make_async_copy(ref, held.at[whose], in_sems.at[whose])
+        for whose, ref in enumerate((share_ref, sibling_ref))
+    ]
+    for read in reads:
+        read.start()
+    for read in reads:
+        read.wait()
     me = lax.axis_index("seq")
     chip, core = me // 2, lax.rem(me, 2)
-    for ahead in range(CHIPS):
-        device = lax.rem(chip + ahead, CHIPS) * 2 + core
-        for j in range(CAP):
-            row = jnp.clip(rows_ref[device, j], 0, STORED - 1)
-            outs[ahead][j] = share_ref[row]
-            row = jnp.clip(sibling_rows_ref[device, j], 0, STORED - 1)
-            outs[ahead][CAP + j] = sibling_ref[row]
+    writes = []
+    for by in (3, 5, 4, 2, 6, 1, 7, 0):
+        device = lax.rem(chip + by, CHIPS) * 2 + core
+        for whose, table in enumerate((rows_ref, sibling_rows_ref)):
+            for j in range(CAP):
+                row = jnp.clip(table[device, j], 0, STORED - 1)
+                messages[by, whose * CAP + j] = held[whose, row]
+        writes.append(pltpu.make_async_copy(messages.at[by], outs[by], out_sems.at[by]))
+        writes[-1].start()
+    for write in writes:
+        write.wait()
 
 
 def pack_rows(rows, sibling_rows, share, sibling):
     return pl.pallas_call(
         pack_kernel,
         out_shape=[jax.ShapeDtypeStruct((2 * CAP, PART, E), BF16)] * CHIPS,
-        in_specs=[IN_SMEM, IN_SMEM, IN_VMEM, IN_VMEM],
-        out_specs=[IN_VMEM] * CHIPS,
+        in_specs=[IN_SMEM, IN_SMEM, ANYWHERE, ANYWHERE],
+        out_specs=[ANYWHERE] * CHIPS,
+        scratch_shapes=[
+            pltpu.VMEM((2, STORED, PART, E), BF16),
+            pltpu.VMEM((CHIPS, 2 * CAP, PART, E), BF16),
+            pltpu.SemaphoreType.DMA((2,)),
+            pltpu.SemaphoreType.DMA((CHIPS,)),
+        ],
         compiler_params=params(WIDE_VMEM),
         cost_estimate=cost(0, 3_000_000),
         name="pack_rows",
@@ -121,16 +157,20 @@
 
 
 def pick_kernel(neighbour_ref, *refs):
-    arrived, outs, table = refs[:CHIPS], refs[CHIPS:-1], refs[-1]
+    arrived, outs, (table, local, sem) = refs[:CHIPS], refs[CHIPS:-3], refs[-3:]
+    copy = pltpu.make_async_copy(arrived[0], local, sem)
+    copy.start()
     for at in range(SLOTS):
         table[at] = REQ
     for r, (away, other, slot) in enumerate(places_of(neighbour_ref)):
         table[away * 2 * CAP + other * CAP + slot] = r
     half = GROUPS[0][1] * KNB
-    for away in range(CHIPS):
+    for away in (1, 2, 3, 4, 5, 6, 7, 0):
+        if away == 0:
+            copy.wait()
         for block in range(2 * CAP):
             r = table[away * 2 * CAP + block]
-            ref = arrived[(CHIPS - away) % CHIPS]
+            ref = arrived[CHIPS - away] if away else local
 
             @pl.when(r < half)
             def _():
@@ -147,9 +187,13 @@
         out_shape=[
             jax.ShapeDtypeStruct((spans * KNB, PART, E), BF16) for first, spans in GROUPS
         ],
-        in_specs=[IN_SMEM] + [IN_VMEM] * CHIPS,
+        in_specs=[IN_SMEM, ANYWHERE] + [IN_VMEM] * (CHIPS - 1),
         out_specs=[IN_VMEM] * len(GROUPS),
-        scratch_shapes=[pltpu.SMEM((SLOTS,), jnp.int32)],
+        scratch_shapes=[
+            pltpu.SMEM((SLOTS,), jnp.int32),
+            pltpu.VMEM((2 * CAP, PART, E), BF16),
+            pltpu.SemaphoreType.DMA,
+        ],
         compiler_params=params(),
         cost_estimate=cost(0, 3_000_000),
         name="pick",
@@ -287,31 +331,48 @@
     )(neighbour, sibling_neighbour, *grads)
 
 
-def collect_kernel(rows_ref, *refs):
-    arrived, (out_ref, acc) = refs[:CHIPS], refs[CHIPS:]
+def add_arrived(rows_ref, arrived, acc):
     me = lax.axis_index("seq")
     chip, core = me // 2, lax.rem(me, 2)
-    acc[...] = jnp.zeros(acc.shape, F32)
-    for behind in range(CHIPS):
+    for behind, ref in arrived:
         device = lax.rem(chip - behind + CHIPS, CHIPS) * 2
         for block in range(2 * CAP):
             requester = device + (core if block < CAP else 1 - core)
             row = jnp.clip(rows_ref[requester, block % CAP], 0, STORED - 1)
-            acc[row] += arrived[behind][block].astype(F32)
-    out_ref[...] = acc[...].astype(BF16)
+            acc[row] += ref[block].astype(F32)
+
+
+def collect_far_kernel(rows_ref, *refs):
+    acc = refs[-1]
+    acc[...] = jnp.zeros(acc.shape, F32)
+    add_arrived(rows_ref, list(zip(FAR, refs[:-1])), acc)
+
+
+def collect_near_kernel(rows_ref, acc, *refs):
+    add_arrived(rows_ref, list(zip(NEAR, refs[:-1])), acc)
+    refs[-1][...] = acc[...].astype(BF16)
 
 
 def collect(rows, arrived):
-    return pl.pallas_call(
-        collect_kernel,
-        out_shape=jax.ShapeDtypeStruct((STORED, EQ, NTOK), BF16),
-        in_specs=[IN_SMEM] + [IN_VMEM] * CHIPS,
+    shape = (STORED, EQ, NTOK)
+    far = pl.pallas_call(
+        collect_far_kernel,
+        out_shape=jax.ShapeDtypeStruct(shape, F32),
+        in_specs=[IN_SMEM] + [IN_VMEM] * len(FAR),
         out_specs=IN_VMEM,
-        scratch_shapes=[pltpu.VMEM((STORED, EQ, NTOK), F32)],
-        compiler_params=params(),
-        cost_estimate=cost(0, 3_000_000),
-        name="collect",
-    )(rows, *arrived)
+        compiler_params=params(),
+        cost_estimate=cost(0, 5_000_000),
+        name="collect_far",
+    )(rows, *[arrived[by] for by in FAR])
+    return pl.pallas_call(
+        collect_near_kernel,
+        out_shape=jax.ShapeDtypeStruct(shape, BF16),
+        in_specs=[IN_SMEM] + [IN_VMEM] * (1 + len(NEAR)),
+        out_specs=IN_VMEM,
+        compiler_params=params(),
+        cost_estimate=cost(0, 5_000_000),
+        name="collect_near",
+    )(rows, far, *[arrived[by] for by in NEAR])
 
 
 def swap(x):

time: 179 us -> 180 us (level)
  transfers between devices with their start and end apart: 32 -> 32, of which waited for: 17 -> 18; matrix products, arithmetic and copies ran while one was open for 0% -> 0% of each run, Pallas kernels for 14% -> 15%
where the time goes in v2:
time: 180 us; the launch traced here: 178 us
  starting transfers between devices  70.5 us (39%)
  waiting for transfers between devices  68.8 us (38%)
  Pallas kernels  35.3 us (20%)
  local copies, waits for them, and re-layouts  2.91 us (2%)
    ppermute x14, waiting for transfers between devices, ahead(): lax.ppermute(x, 'seq', [(i, (i + 2 * by) % N_SEQ) for i in range(N_SEQ)])  52.2 us
    ppermute x14, starting transfers between devices, ahead(): lax.ppermute(x, 'seq', [(i, (i + 2 * by) % N_SEQ) for i in range(N_SEQ)])  35.6 us
    pallas_call x2, Pallas kernels, attention(): pl.pallas_call(attention_kernel, grid=(spans,), out_shape=[wide, wide] +...  21.7 us
    ppermute x12, starting transfers between devices, turn(): return lax.ppermute(x, 'tp', [(i, (i + by) % N_TP) for i in range(N_TP)])  17.4 us
    ppermute x5, starting transfers between devices, swap(): return lax.ppermute(x, 'seq', [(i, i ^ 1) for i in range(N_SEQ)])  16.2 us
    ppermute x12, waiting for transfers between devices, turn(): return lax.ppermute(x, 'tp', [(i, (i + by) % N_TP) for i in range(N_TP)])  13.6 us
    pallas_call x1, Pallas kernels, pack_rows(): pl.pallas_call(pack_kernel, out_shape=[jax.ShapeDtypeStruct((2 * CAP, PAR...  3.7 us
  transfers between devices with their start and end apart: 32, of which 18 were waited for; matrix products, arithmetic and copies ran while one was open for 0% of the time, Pallas kernels for 15%

profile of v2, /device:TPU:1, one launch (start us, length us, event | category | flops | bytes accessed | tf_op | source)
XLA Modules:
  0.0 178.3 jit_solution(11781094400238738492)
XLA Ops:
  0.7 2.1 %take_share.1.share_ref = bf16[16,32,896]{2,1,0:T(8,128)(2,1)} custom-call(bf16[16,128,896]{2,1,0:T(8,128)(2,1)} %bitcast.20), custom_call_target="tpu_custom_call" | custom-call | bytes 2000000 | tf_op jit(solution)/shard_map/take_share/pallas_call | solution.py:85
  2.8 3.3 %collective-permute-start.2 = (bf16[16,32,896]{2,1,0:T(8,128)(2,1)}, bf16[16,32,896]{2,1,0:T(8,128)(2,1)}, u32[]{:S(2)}, u32[]{:S(2)}) collective-permute-start(bf16[16,32,896]{2,1,0:T(8,128)(2,1)} %take_share.1.share_ref), channel_id=1, source_target_pairs={{0,4},{4,0},{8,12},{12,8},{16,20},{20,16},{24,28},{28,24},{32,36},... | collective-permute-start | bytes 2752520 | tf_op jit(solution)/shard_map/ppermute | solution.py:379
  8.9 3.7 %pack_rows.1 = (bf16[4,32,896]{2,1,0:T(8,128)(2,1)}, bf16[4,32,896]{2,1,0:T(8,128)(2,1)}, bf16[4,32,896]{2,1,0:T(8,128)(2,1)}, bf16[4,32,896]{2,1,0:T(8,128)(2,1...) custom-call(s32[16,2]{1,0:T(8,128)} %copy-done.1, ...), custom_call_target="tpu_custom_call" | custom-call | bytes 3000000 | tf_op jit(solution)/shard_map/pack_rows/pallas_call | solution.py:127
  12.6 2.7 %collective-permute-start.3 = (bf16[4,32,896]{2,1,0:T(8,128)(2,1)}, bf16[4,32,896]{2,1,0:T(8,128)(2,1)S(1)}, u32[]{:S(2)}, u32[]{:S(2)}) collective-permute-start(bf16[4,32,896]{2,1,0:T(8,128)(2,1)} %get-tuple-element.43), channel_id=1, source_target_pairs={{0,24},{4,28},{8,32},{12,36},{16,40},{20,44},{24,48},{28,52},{32,5... | collective-permute-start | bytes 688136 | tf_op jit(solution)/shard_map/ppermute | solution.py:383
  15.3 2.2 %collective-permute-start.7 = (bf16[4,32,896]{2,1,0:T(8,128)(2,1)}, bf16[4,32,896]{2,1,0:T(8,128)(2,1)S(1)}, u32[]{:S(2)}, u32[]{:S(2)}) collective-permute-start(bf16[4,32,896]{2,1,0:T(8,128)(2,1)} %get-tuple-element.47), channel_id=1, source_target_pairs={{0,40},{4,44},{8,48},{12,52},{16,56},{20,60},{24,0},{28,4},{32,8},... | collective-permute-start | bytes 688136 | tf_op jit(solution)/shard_map/ppermute | solution.py:383
  18.7 4.8 %collective-permute-start.6 = (bf16[4,32,896]{2,1,0:T(8,128)(2,1)}, bf16[4,32,896]{2,1,0:T(8,128)(2,1)S(1)}, u32[]{:S(2)}, u32[]{:S(2)}) collective-permute-start(bf16[4,32,896]{2,1,0:T(8,128)(2,1)} %get-tuple-element.46), channel_id=1, source_target_pairs={{0,32},{4,36},{8,40},{12,44},{16,48},{20,52},{24,56},{28,60},{32,0... | collective-permute-start | bytes 688136 | tf_op jit(solution)/shard_map/ppermute | solution.py:383
  23.5 2.4 %collective-permute-start.8 = (bf16[4,32,896]{2,1,0:T(8,128)(2,1)}, bf16[4,32,896]{2,1,0:T(8,128)(2,1)S(1)}, u32[]{:S(2)}, u32[]{:S(2)}) collective-permute-start(bf16[4,32,896]{2,1,0:T(8,128)(2,1)} %get-tuple-element.48), channel_id=1, source_target_pairs={{0,48},{4,52},{8,56},{12,60},{16,0},{20,4},{24,8},{28,12},{32,16},... | collective-permute-start | bytes 688136 | tf_op jit(solution)/shard_map/ppermute | solution.py:383
  25.9 3.6 %collective-permute-done.3.refs_3_ = bf16[4,32,896]{2,1,0:T(8,128)(2,1)S(1)} collective-permute-done((bf16[4,32,896]{2,1,0:T(8,128)(2,1)}, bf16[4,32,896]{2,1,0:T(8,128)(2,1)S(1)}, u32[]{:S(2)}, u32[]{:S(2)}) %collective-permute-start.3) | collective-permute-done | bytes 229408 | tf_op jit(solution)/shard_map/ppermute | solution.py:383
  29.5 3.8 %collective-permute-start.4 = (bf16[4,32,896]{2,1,0:T(8,128)(2,1)}, bf16[4,32,896]{2,1,0:T(8,128)(2,1)S(1)}, u32[]{:S(2)}, u32[]{:S(2)}) collective-permute-start(bf16[4,32,896]{2,1,0:T(8,128)(2,1)} %get-tuple-element.44), channel_id=1, source_target_pairs={{0,8},{4,12},{8,16},{12,20},{16,24},{20,28},{24,32},{28,36},{32,40... | collective-permute-start | bytes 688136 | tf_op jit(solution)/shard_map/ppermute | solution.py:383
  33.3 8.1 %collective-permute-done.5.refs_2_ = bf16[4,32,896]{2,1,0:T(8,128)(2,1)S(1)} collective-permute-done((bf16[4,32,896]{2,1,0:T(8,128)(2,1)}, bf16[4,32,896]{2,1,0:T(8,128)(2,1)S(1)}, u32[]{:S(2)}, u32[]{:S(2)}) %collective-permute-start.5) | collective-permute-done | bytes 229408 | tf_op jit(solution)/shard_map/ppermute | solution.py:383
  41.4 8.8 %collective-permute-done.6.refs_4_ = bf16[4,32,896]{2,1,0:T(8,128)(2,1)S(1)} collective-permute-done((bf16[4,32,896]{2,1,0:T(8,128)(2,1)}, bf16[4,32,896]{2,1,0:T(8,128)(2,1)S(1)}, u32[]{:S(2)}, u32[]{:S(2)}) %collective-permute-start.6) | collective-permute-done | bytes 229408 | tf_op jit(solution)/shard_map/ppermute | solution.py:383
  50.3 3.4 %collective-permute-done.8.refs_6_ = bf16[4,32,896]{2,1,0:T(8,128)(2,1)S(1)} collective-permute-done((bf16[4,32,896]{2,1,0:T(8,128)(2,1)}, bf16[4,32,896]{2,1,0:T(8,128)(2,1)S(1)}, u32[]{:S(2)}, u32[]{:S(2)}) %collective-permute-start.8) | collective-permute-done | bytes 229408 | tf_op jit(solution)/shard_map/ppermute | solution.py:383
  53.7 3.2 %collective-permute-done.4.refs_1_ = bf16[4,32,896]{2,1,0:T(8,128)(2,1)S(1)} collective-permute-done((bf16[4,32,896]{2,1,0:T(8,128)(2,1)}, bf16[4,32,896]{2,1,0:T(8,128)(2,1)S(1)}, u32[]{:S(2)}, u32[]{:S(2)}) %collective-permute-start.4) | collective-permute-done | bytes 229408 | tf_op jit(solution)/shard_map/ppermute | solution.py:383
  62.4 2.5 %collective-permute-start.15 = (bf16[6,32,896]{2,1,0:T(8,128)(2,1)S(1)}, bf16[6,32,896]{2,1,0:T(8,128)(2,1)S(1)}, u32[]{:S(2)}, u32[]{:S(2)}) collective-permute-start(bf16[6,32,896]{2,1,0:T(8,128)(2,1)S(1)} %get-tuple-element.52.refs_0_), channel_id=1, source_target_pairs={{0,2},{1,3},{2,0},{3,1},{4,6},{5,7},{6,4},{7,5},{8,10},{9,11},{10,... | collective-permute-start | bytes 1032200 | tf_op jit(solution)/shard_map/ppermute | solution.py:401
  66.0 5.0 %collective-permute-done.10.refs_3_ = bf16[6,32,896]{2,1,0:T(8,128)(2,1)S(1)} collective-permute-done((bf16[6,32,896]{2,1,0:T(8,128)(2,1)S(1)}, bf16[6,32,896]{2,1,0:T(8,128)(2,1)S(1)}, u32[]{:S(2)}, u32[]{:S(2)}) %collective-permute-start.10) | collective-permute-done | bytes 344096 | tf_op jit(solution)/shard_map/ppermute | solution.py:401
  71.1 2.4 %collective-permute-start.12 = (bf16[6,32,896]{2,1,0:T(8,128)(2,1)S(1)}, bf16[6,32,896]{2,1,0:T(8,128)(2,1)S(1)}, u32[]{:S(2)}, u32[]{:S(2)}) collective-permute-start(bf16[6,32,896]{2,1,0:T(8,128)(2,1)S(1)} %get-tuple-element.53.refs_0_), channel_id=1, source_target_pairs={{0,2},{1,3},{2,0},{3,1},{4,6},{5,7},{6,4},{7,5},{8,10},{9,11},{10,... | collective-permute-start | bytes 1032200 | tf_op jit(solution)/shard_map/ppermute | solution.py:401
  74.7 4.8 %collective-permute-done.15.refs_2_ = bf16[6,32,896]{2,1,0:T(8,128)(2,1)S(1)} collective-permute-done((bf16[6,32,896]{2,1,0:T(8,128)(2,1)S(1)}, bf16[6,32,896]{2,1,0:T(8,128)(2,1)S(1)}, u32[]{:S(2)}, u32[]{:S(2)}) %collective-permute-start.15) | collective-permute-done | bytes 344096 | tf_op jit(solution)/shard_map/ppermute | solution.py:401
  81.9 10.8 %attention.2 = (bf16[384,1024]{1,0:T(8,128)(2,1)}, bf16[384,1024]{1,0:T(8,128)(2,1)S(1)}, bf16[6,224,128]{2,1,0:T(8,128)(2,1)S(1)}, bf16[6,224,128]{2,1,0:T(8,12...) custom-call(bf16[6,32,896]{2,1,0:T(8,128)(2,1)S(1)} %get-tuple-element.52.refs_0_, ...), custom_call_target="tpu_custom_call" | custom-call | flops 6600000000 | bytes 9500000 | tf_op jit(solution)/shard_map/attention/pallas_call | solution.py:248
  93.6 4.3 %collective-permute-start.18 = (bf16[6,224,128]{2,1,0:T(8,128)(2,1)S(1)}, bf16[6,224,128]{2,1,0:T(8,128)(2,1)S(1)}, u32[]{:S(2)}, u32[]{:S(2)}) collective-permute-start(bf16[6,224,128]{2,1,0:T(8,128)(2,1)S(1)} %get-tuple-element.60), channel_id=1, source_target_pairs={{0,2},{1,3},{2,0},{3,1},{4,6},{5,7},{6,4},{7,5},{8,10},{9,11},{10,... | collective-permute-start | bytes 1032200 | tf_op jit(solution)/shard_map/ppermute | solution.py:401
  97.9 10.9 %attention.3 = (bf16[384,1024]{1,0:T(8,128)(2,1)}, bf16[384,1024]{1,0:T(8,128)(2,1)S(1)}, bf16[6,224,128]{2,1,0:T(8,128)(2,1)S(1)}, bf16[6,224,128]{2,1,0:T(8,12...) custom-call(bf16[6,32,896]{2,1,0:T(8,128)(2,1)S(1)} %get-tuple-eleme, ...), custom_call_target="tpu_custom_call", output_to_operand_aliasing={{0}: (8, {}), {1}: (9, {})} | custom-call | flops 6600000000 | bytes 9500000 | tf_op jit(solution)/shard_map/attention/pallas_call | solution.py:248
  110.2 2.4 %collective-permute-start.22 = (bf16[6,224,128]{2,1,0:T(8,128)(2,1)S(1)}, bf16[6,224,128]{2,1,0:T(8,128)(2,1)S(1)}, u32[]{:S(2)}, u32[]{:S(2)}) collective-permute-start(bf16[6,224,128]{2,1,0:T(8,128)(2,1)S(1)} %get-tuple-element.65), channel_id=1, source_target_pairs={{0,3},{1,0},{2,1},{3,2},{4,7},{5,4},{6,5},{7,6},{8,11},{9,8},{10,9... | collective-permute-start | bytes 1032200 | tf_op jit(solution)/shard_map/ppermute | solution.py:401
  114.1 6.1 %collective-permute-start.23 = (bf16[6,224,128]{2,1,0:T(8,128)(2,1)S(1)}, bf16[6,224,128]{2,1,0:T(8,128)(2,1)S(1)}, u32[]{:S(2)}, u32[]{:S(2)}) collective-permute-start(bf16[6,224,128]{2,1,0:T(8,128)(2,1)S(1)} %sum_parts.2.refs_0_), channel_id=1, source_target_pairs={{0,4},{4,0},{8,12},{12,8},{16,20},{20,16},{24,28},{28,24},{32,36},... | collective-permute-start | bytes 1032200 | tf_op jit(solution)/shard_map/ppermute | solution.py:379
  120.2 2.8 %collective-permute-done.21.refs_2_ = bf16[6,224,128]{2,1,0:T(8,128)(2,1)S(1)} collective-permute-done((bf16[6,224,128]{2,1,0:T(8,128)(2,1)S(1)}, bf16[6,224,128]{2,1,0:T(8,128)(2,1)S(1)}, u32[]{:S(2)}, u32[]{:S(2)}) %collective-permute-start.21) | collective-permute-done | bytes 344096 | tf_op jit(solution)/shard_map/ppermute | solution.py:401
  123.2 6.2 %collective-permute-start.24 = (bf16[6,224,128]{2,1,0:T(8,128)(2,1)S(1)}, bf16[6,224,128]{2,1,0:T(8,128)(2,1)S(1)}, u32[]{:S(2)}, u32[]{:S(2)}) collective-permute-start(bf16[6,224,128]{2,1,0:T(8,128)(2,1)S(1)} %sum_parts.3.refs_1_), channel_id=1, source_target_pairs={{0,4},{4,0},{8,12},{12,8},{16,20},{20,16},{24,28},{28,24},{32,36},... | collective-permute-start | bytes 1032200 | tf_op jit(solution)/shard_map/ppermute | solution.py:379
  130.7 2.0 %place.1 = (bf16[4,224,128]{2,1,0:T(8,128)(2,1)S(1)}, bf16[4,224,128]{2,1,0:T(8,128)(2,1)S(1)}, bf16[4,224,128]{2,1,0:T(8,128)(2,1)S(1)}, bf16[4,224,128]{2,1,0:...) custom-call(s32[6,2]{1,0:T(8,128)S(1)} %copy.15.neighbour_ref, ...), custom_call_target="tpu_custom_call" | custom-call | bytes 3000000 | tf_op jit(solution)/shard_map/place/pallas_call | solution.py:322
  132.7 4.4 %collective-permute-start.25 = (bf16[4,224,128]{2,1,0:T(8,128)(2,1)S(1)}, bf16[4,224,128]{2,1,0:T(8,128)(2,1)S(1)}, u32[]{:S(2)}, u32[]{:S(2)}) collective-permute-start(bf16[4,224,128]{2,1,0:T(8,128)(2,1)S(1)} %get-tuple-element.66), channel_id=1, source_target_pairs={{0,24},{4,28},{8,32},{12,36},{16,40},{20,44},{24,48},{28,52},{32,5... | collective-permute-start | bytes 688136 | tf_op jit(solution)/shard_map/ppermute | solution.py:383
  137.3 4.6 %collective-permute-start.27 = (bf16[4,224,128]{2,1,0:T(8,128)(2,1)S(1)}, bf16[4,224,128]{2,1,0:T(8,128)(2,1)S(1)}, u32[]{:S(2)}, u32[]{:S(2)}) collective-permute-start(bf16[4,224,128]{2,1,0:T(8,128)(2,1)S(1)} %get-tuple-element.70), channel_id=1, source_target_pairs={{0,32},{4,36},{8,40},{12,44},{16,48},{20,52},{24,56},{28,60},{32,0... | collective-permute-start | bytes 688136 | tf_op jit(solution)/shard_map/ppermute | solution.py:383
  142.1 9.9 %collective-permute-done.25.refs_1_ = bf16[4,224,128]{2,1,0:T(8,128)(2,1)S(1)} collective-permute-done((bf16[4,224,128]{2,1,0:T(8,128)(2,1)S(1)}, bf16[4,224,128]{2,1,0:T(8,128)(2,1)S(1)}, u32[]{:S(2)}, u32[]{:S(2)}) %collective-permute-start.25) | collective-permute-done | bytes 229408 | tf_op jit(solution)/shard_map/ppermute | solution.py:383
  152.0 9.1 %collective-permute-start.30 = (bf16[4,224,128]{2,1,0:T(8,128)(2,1)S(1)}, bf16[4,224,128]{2,1,0:T(8,128)(2,1)S(1)}, u32[]{:S(2)}, u32[]{:S(2)}) collective-permute-start(bf16[4,224,128]{2,1,0:T(8,128)(2,1)S(1)} %get-tuple-element.74), channel_id=1, source_target_pairs={{0,8},{4,12},{8,16},{12,20},{16,24},{20,28},{24,32},{28,36},{32,40... | collective-permute-start | bytes 688136 | tf_op jit(solution)/shard_map/ppermute | solution.py:383
  163.3 8.8 %collective-permute-done.28.refs_4_ = bf16[4,224,128]{2,1,0:T(8,128)(2,1)S(1)} collective-permute-done((bf16[4,224,128]{2,1,0:T(8,128)(2,1)S(1)}, bf16[4,224,128]{2,1,0:T(8,128)(2,1)S(1)}, u32[]{:S(2)}, u32[]{:S(2)}) %collective-permute-start.28) | collective-permute-done | bytes 229408 | tf_op jit(solution)/shard_map/ppermute | solution.py:383
  174.5 2.0 %collective-permute-done.30.refs_1_ = bf16[4,224,128]{2,1,0:T(8,128)(2,1)S(1)} collective-permute-done((bf16[4,224,128]{2,1,0:T(8,128)(2,1)S(1)}, bf16[4,224,128]{2,1,0:T(8,128)(2,1)S(1)}, u32[]{:S(2)}, u32[]{:S(2)}) %collective-permute-start.30) | collective-permute-done | bytes 229408 | tf_op jit(solution)/shard_map/ppermute | solution.py:383
  176.5 1.8 %collect_near.1 = bf16[16,224,128]{2,1,0:T(8,128)(2,1)} custom-call(s32[16,2]{1,0:T(8,128)S(1)} %copy-done.2, f32[16,224,128]{2,1,0:T(8,128)S(1)} %collect_far.1.acc, bf16[4,224,128]{2,1,0:T(8,128)(2,1)S(1)} %collective-permute-done.29.refs_0_, bf16[4,224,128]{2,1,0:T(8,128)(2,1)S(1)} %collective-permute-done.30.refs_1_, ...), custom_call_target="tpu_custom_call" | custom-call | bytes 5000000 | tf_op jit(solution)/shard_map/collect_near/pallas_call | solution.py:367
  (65 shorter events, 24.5 us)
Async XLA Ops:
  2.8 5.8 %collective-permute-start.2 = (bf16[16,32,896]{2,1,0:T(8,128)(2,1)}, bf16[16,32,896]{2,1,0:T(8,128)(2,1)}, u32[]{:S(2)}, u32[]{:S(2)}) collective-permute-start(bf16[16,32,896]{2,1,0:T(8,128)(2,1)} %take_share.1.share_ref), channel_id=1, source_target_pairs={{0,4},{4,0},{8,12},{12,8},{16,20},{20,16},{24,28},{28,24},{32,36},... | collective-permute-start | bytes 2752520 | tf_op jit(solution)/shard_map/ppermute | solution.py:379
  6.2 2.0 %collective-permute-start = (s32[16,2]{1,0:T(8,128)S(1)}, s32[16,2]{1,0:T(8,128)S(1)}, u32[]{:S(2)}, u32[]{:S(2)}) collective-permute-start(s32[16,2]{1,0:T(8,128)S(1)} %copy.14.rows_ref), channel_id=1, source_target_pairs={{0,4},{4,0},{8,12},{12,8},{16,20},{20,16},{24,28},{28,24},{32,36},... | collective-permute-start | bytes 392 | tf_op jit(solution)/shard_map/ppermute | solution.py:379
  6.4 1.9 %collective-permute-start.1 = (s32[6,2]{1,0:T(8,128)S(1)}, s32[6,2]{1,0:T(8,128)S(1)}, u32[]{:S(2)}, u32[]{:S(2)}) collective-permute-start(s32[6,2]{1,0:T(8,128)S(1)} %copy.15.neighbour_ref), channel_id=1, source_target_pairs={{0,4},{4,0},{8,12},{12,8},{16,20},{20,16},{24,28},{28,24},{32,36},... | collective-permute-start | bytes 152 | tf_op jit(solution)/shard_map/ppermute | solution.py:379
  12.6 16.9 %collective-permute-start.3 = (bf16[4,32,896]{2,1,0:T(8,128)(2,1)}, bf16[4,32,896]{2,1,0:T(8,128)(2,1)S(1)}, u32[]{:S(2)}, u32[]{:S(2)}) collective-permute-start(bf16[4,32,896]{2,1,0:T(8,128)(2,1)} %get-tuple-element.43), channel_id=1, source_target_pairs={{0,24},{4,28},{8,32},{12,36},{16,40},{20,44},{24,48},{28,52},{32,5... | collective-permute-start | bytes 688136 | tf_op jit(solution)/shard_map/ppermute | solution.py:383
  15.3 18.0 %collective-permute-start.7 = (bf16[4,32,896]{2,1,0:T(8,128)(2,1)}, bf16[4,32,896]{2,1,0:T(8,128)(2,1)S(1)}, u32[]{:S(2)}, u32[]{:S(2)}) collective-permute-start(bf16[4,32,896]{2,1,0:T(8,128)(2,1)} %get-tuple-element.47), channel_id=1, source_target_pairs={{0,40},{4,44},{8,48},{12,52},{16,56},{20,60},{24,0},{28,4},{32,8},... | collective-permute-start | bytes 688136 | tf_op jit(solution)/shard_map/ppermute | solution.py:383
  17.5 23.9 %collective-permute-start.5 = (bf16[4,32,896]{2,1,0:T(8,128)(2,1)}, bf16[4,32,896]{2,1,0:T(8,128)(2,1)S(1)}, u32[]{:S(2)}, u32[]{:S(2)}) collective-permute-start(bf16[4,32,896]{2,1,0:T(8,128)(2,1)} %get-tuple-element.45), channel_id=1, source_target_pairs={{0,16},{4,20},{8,24},{12,28},{16,32},{20,36},{24,40},{28,44},{32,4... | collective-permute-start | bytes 688136 | tf_op jit(solution)/shard_map/ppermute | solution.py:383
  18.7 31.6 %collective-permute-start.6 = (bf16[4,32,896]{2,1,0:T(8,128)(2,1)}, bf16[4,32,896]{2,1,0:T(8,128)(2,1)S(1)}, u32[]{:S(2)}, u32[]{:S(2)}) collective-permute-start(bf16[4,32,896]{2,1,0:T(8,128)(2,1)} %get-tuple-element.46), channel_id=1, source_target_pairs={{0,32},{4,36},{8,40},{12,44},{16,48},{20,52},{24,56},{28,60},{32,0... | collective-permute-start | bytes 688136 | tf_op jit(solution)/shard_map/ppermute | solution.py:383
  23.5 30.2 %collective-permute-start.8 = (bf16[4,32,896]{2,1,0:T(8,128)(2,1)}, bf16[4,32,896]{2,1,0:T(8,128)(2,1)S(1)}, u32[]{:S(2)}, u32[]{:S(2)}) collective-permute-start(bf16[4,32,896]{2,1,0:T(8,128)(2,1)} %get-tuple-element.48), channel_id=1, source_target_pairs={{0,48},{4,52},{8,56},{12,60},{16,0},{20,4},{24,8},{28,12},{32,16},... | collective-permute-start | bytes 688136 | tf_op jit(solution)/shard_map/ppermute | solution.py:383
  29.5 27.4 %collective-permute-start.4 = (bf16[4,32,896]{2,1,0:T(8,128)(2,1)}, bf16[4,32,896]{2,1,0:T(8,128)(2,1)S(1)}, u32[]{:S(2)}, u32[]{:S(2)}) collective-permute-start(bf16[4,32,896]{2,1,0:T(8,128)(2,1)} %get-tuple-element.44), channel_id=1, source_target_pairs={{0,8},{4,12},{8,16},{12,20},{16,24},{20,28},{24,32},{28,36},{32,40... | collective-permute-start | bytes 688136 | tf_op jit(solution)/shard_map/ppermute | solution.py:383
  33.3 25.2 %collective-permute-start.9 = (bf16[4,32,896]{2,1,0:T(8,128)(2,1)}, bf16[4,32,896]{2,1,0:T(8,128)(2,1)S(1)}, u32[]{:S(2)}, u32[]{:S(2)}) collective-permute-start(bf16[4,32,896]{2,1,0:T(8,128)(2,1)} %get-tuple-element.50), channel_id=1, source_target_pairs={{0,56},{4,60},{8,0},{12,4},{16,8},{20,12},{24,16},{28,20},{32,24},... | collective-permute-start | bytes 688136 | tf_op jit(solution)/shard_map/ppermute | solution.py:383
  61.1 9.9 %collective-permute-start.10 = (bf16[6,32,896]{2,1,0:T(8,128)(2,1)S(1)}, bf16[6,32,896]{2,1,0:T(8,128)(2,1)S(1)}, u32[]{:S(2)}, u32[]{:S(2)}) collective-permute-start(bf16[6,32,896]{2,1,0:T(8,128)(2,1)S(1)} %get-tuple-element.52.refs_0_), channel_id=1, source_target_pairs={{0,1},{1,2},{2,3},{3,0},{4,5},{5,6},{6,7},{7,4},{8,9},{9,10},{10,1... | collective-permute-start | bytes 1032200 | tf_op jit(solution)/shard_map/ppermute | solution.py:401
  62.4 17.1 %collective-permute-start.15 = (bf16[6,32,896]{2,1,0:T(8,128)(2,1)S(1)}, bf16[6,32,896]{2,1,0:T(8,128)(2,1)S(1)}, u32[]{:S(2)}, u32[]{:S(2)}) collective-permute-start(bf16[6,32,896]{2,1,0:T(8,128)(2,1)S(1)} %get-tuple-element.52.refs_0_), channel_id=1, source_target_pairs={{0,2},{1,3},{2,0},{3,1},{4,6},{5,7},{6,4},{7,5},{8,10},{9,11},{10,... | collective-permute-start | bytes 1032200 | tf_op jit(solution)/shard_map/ppermute | solution.py:401
  64.9 15.6 %collective-permute-start.14 = (bf16[6,32,896]{2,1,0:T(8,128)(2,1)S(1)}, bf16[6,32,896]{2,1,0:T(8,128)(2,1)S(1)}, u32[]{:S(2)}, u32[]{:S(2)}) collective-permute-start(bf16[6,32,896]{2,1,0:T(8,128)(2,1)S(1)} %get-tuple-element.52.refs_0_), channel_id=1, source_target_pairs={{0,3},{1,0},{2,1},{3,2},{4,7},{5,4},{6,5},{7,6},{8,11},{9,8},{10,9... | collective-permute-start | bytes 1032200 | tf_op jit(solution)/shard_map/ppermute | solution.py:401
  71.1 26.8 %collective-permute-start.13 = (bf16[6,32,896]{2,1,0:T(8,128)(2,1)S(1)}, bf16[6,32,896]{2,1,0:T(8,128)(2,1)S(1)}, u32[]{:S(2)}, u32[]{:S(2)}) collective-permute-start(bf16[6,32,896]{2,1,0:T(8,128)(2,1)S(1)} %get-tuple-element.53.refs_0_), channel_id=1, source_target_pairs={{0,1},{1,2},{2,3},{3,0},{4,5},{5,6},{6,7},{7,4},{8,9},{9,10},{10,1... | collective-permute-start | bytes 1032200 | tf_op jit(solution)/shard_map/ppermute | solution.py:401
  71.1 26.8 %collective-permute-start.12 = (bf16[6,32,896]{2,1,0:T(8,128)(2,1)S(1)}, bf16[6,32,896]{2,1,0:T(8,128)(2,1)S(1)}, u32[]{:S(2)}, u32[]{:S(2)}) collective-permute-start(bf16[6,32,896]{2,1,0:T(8,128)(2,1)S(1)} %get-tuple-element.53.refs_0_), channel_id=1, source_target_pairs={{0,2},{1,3},{2,0},{3,1},{4,6},{5,7},{6,4},{7,5},{8,10},{9,11},{10,... | collective-permute-start | bytes 1032200 | tf_op jit(solution)/shard_map/ppermute | solution.py:401
  73.5 24.3 %collective-permute-start.11 = (bf16[6,32,896]{2,1,0:T(8,128)(2,1)S(1)}, bf16[6,32,896]{2,1,0:T(8,128)(2,1)S(1)}, u32[]{:S(2)}, u32[]{:S(2)}) collective-permute-start(bf16[6,32,896]{2,1,0:T(8,128)(2,1)S(1)} %get-tuple-element.53.refs_0_), channel_id=1, source_target_pairs={{0,3},{1,0},{2,1},{3,2},{4,7},{5,4},{6,5},{7,6},{8,11},{9,8},{10,9... | collective-permute-start | bytes 1032200 | tf_op jit(solution)/shard_map/ppermute | solution.py:401
  92.8 17.4 %collective-permute-start.17 = (bf16[6,224,128]{2,1,0:T(8,128)(2,1)S(1)}, bf16[6,224,128]{2,1,0:T(8,128)(2,1)S(1)}, u32[]{:S(2)}, u32[]{:S(2)}) collective-permute-start(bf16[6,224,128]{2,1,0:T(8,128)(2,1)S(1)} %get-tuple-element.59), channel_id=1, source_target_pairs={{0,1},{1,2},{2,3},{3,0},{4,5},{5,6},{6,7},{7,4},{8,9},{9,10},{10,1... | collective-permute-start | bytes 1032200 | tf_op jit(solution)/shard_map/ppermute | solution.py:401
  93.6 19.0 %collective-permute-start.18 = (bf16[6,224,128]{2,1,0:T(8,128)(2,1)S(1)}, bf16[6,224,128]{2,1,0:T(8,128)(2,1)S(1)}, u32[]{:S(2)}, u32[]{:S(2)}) collective-permute-start(bf16[6,224,128]{2,1,0:T(8,128)(2,1)S(1)} %get-tuple-element.60), channel_id=1, source_target_pairs={{0,2},{1,3},{2,0},{3,1},{4,6},{5,7},{6,4},{7,5},{8,10},{9,11},{10,... | collective-permute-start | bytes 1032200 | tf_op jit(solution)/shard_map/ppermute | solution.py:401
  97.8 16.0 %collective-permute-start.19 = (bf16[6,224,128]{2,1,0:T(8,128)(2,1)S(1)}, bf16[6,224,128]{2,1,0:T(8,128)(2,1)S(1)}, u32[]{:S(2)}, u32[]{:S(2)}) collective-permute-start(bf16[6,224,128]{2,1,0:T(8,128)(2,1)S(1)} %get-tuple-element.61), channel_id=1, source_target_pairs={{0,3},{1,0},{2,1},{3,2},{4,7},{5,4},{6,5},{7,6},{8,11},{9,8},{10,9... | collective-permute-start | bytes 1032200 | tf_op jit(solution)/shard_map/ppermute | solution.py:401
  108.8 11.4 %collective-permute-start.20 = (bf16[6,224,128]{2,1,0:T(8,128)(2,1)S(1)}, bf16[6,224,128]{2,1,0:T(8,128)(2,1)S(1)}, u32[]{:S(2)}, u32[]{:S(2)}) collective-permute-start(bf16[6,224,128]{2,1,0:T(8,128)(2,1)S(1)} %get-tuple-element.63), channel_id=1, source_target_pairs={{0,1},{1,2},{2,3},{3,0},{4,5},{5,6},{6,7},{7,4},{8,9},{9,10},{10,1... | collective-permute-start | bytes 1032200 | tf_op jit(solution)/shard_map/ppermute | solution.py:401
  110.2 12.8 %collective-permute-start.21 = (bf16[6,224,128]{2,1,0:T(8,128)(2,1)S(1)}, bf16[6,224,128]{2,1,0:T(8,128)(2,1)S(1)}, u32[]{:S(2)}, u32[]{:S(2)}) collective-permute-start(bf16[6,224,128]{2,1,0:T(8,128)(2,1)S(1)} %get-tuple-element.64), channel_id=1, source_target_pairs={{0,2},{1,3},{2,0},{3,1},{4,6},{5,7},{6,4},{7,5},{8,10},{9,11},{10,... | collective-permute-start | bytes 1032200 | tf_op jit(solution)/shard_map/ppermute | solution.py:401
  110.2 12.8 %collective-permute-start.22 = (bf16[6,224,128]{2,1,0:T(8,128)(2,1)S(1)}, bf16[6,224,128]{2,1,0:T(8,128)(2,1)S(1)}, u32[]{:S(2)}, u32[]{:S(2)}) collective-permute-start(bf16[6,224,128]{2,1,0:T(8,128)(2,1)S(1)} %get-tuple-element.65), channel_id=1, source_target_pairs={{0,3},{1,0},{2,1},{3,2},{4,7},{5,4},{6,5},{7,6},{8,11},{9,8},{10,9... | collective-permute-start | bytes 1032200 | tf_op jit(solution)/shard_map/ppermute | solution.py:401
  112.6 48.5 %collective-permute-start.16 = (bf16[384,1024]{1,0:T(8,128)(2,1)S(1)}, bf16[384,1024]{1,0:T(8,128)(2,1)S(1)}, u32[]{:S(2)}, u32[]{:S(2)}) collective-permute-start(bf16[384,1024]{1,0:T(8,128)(2,1)S(1)} %get-tuple-element.57), channel_id=1, source_target_pairs={{64,0},{128,64},{192,128},{65,1},{129,65},{193,129},{66,2},{130,66... | collective-permute-start | bytes 2359304 | tf_op jit(solution)/shard_map/ppermute | solution.py:406
  114.1 15.4 %collective-permute-start.23 = (bf16[6,224,128]{2,1,0:T(8,128)(2,1)S(1)}, bf16[6,224,128]{2,1,0:T(8,128)(2,1)S(1)}, u32[]{:S(2)}, u32[]{:S(2)}) collective-permute-start(bf16[6,224,128]{2,1,0:T(8,128)(2,1)S(1)} %sum_parts.2.refs_0_), channel_id=1, source_target_pairs={{0,4},{4,0},{8,12},{12,8},{16,20},{20,16},{24,28},{28,24},{32,36},... | collective-permute-start | bytes 1032200 | tf_op jit(solution)/shard_map/ppermute | solution.py:379
  123.2 7.5 %collective-permute-start.24 = (bf16[6,224,128]{2,1,0:T(8,128)(2,1)S(1)}, bf16[6,224,128]{2,1,0:T(8,128)(2,1)S(1)}, u32[]{:S(2)}, u32[]{:S(2)}) collective-permute-start(bf16[6,224,128]{2,1,0:T(8,128)(2,1)S(1)} %sum_parts.3.refs_1_), channel_id=1, source_target_pairs={{0,4},{4,0},{8,12},{12,8},{16,20},{20,16},{24,28},{28,24},{32,36},... | collective-permute-start | bytes 1032200 | tf_op jit(solution)/shard_map/ppermute | solution.py:379
  132.7 19.3 %collective-permute-start.25 = (bf16[4,224,128]{2,1,0:T(8,128)(2,1)S(1)}, bf16[4,224,128]{2,1,0:T(8,128)(2,1)S(1)}, u32[]{:S(2)}, u32[]{:S(2)}) collective-permute-start(bf16[4,224,128]{2,1,0:T(8,128)(2,1)S(1)} %get-tuple-element.66), channel_id=1, source_target_pairs={{0,24},{4,28},{8,32},{12,36},{16,40},{20,44},{24,48},{28,52},{32,5... | collective-permute-start | bytes 688136 | tf_op jit(solution)/shard_map/ppermute | solution.py:383
  137.1 14.9 %collective-permute-start.26 = (bf16[4,224,128]{2,1,0:T(8,128)(2,1)S(1)}, bf16[4,224,128]{2,1,0:T(8,128)(2,1)S(1)}, u32[]{:S(2)}, u32[]{:S(2)}) collective-permute-start(bf16[4,224,128]{2,1,0:T(8,128)(2,1)S(1)} %get-tuple-element.69), channel_id=1, source_target_pairs={{0,40},{4,44},{8,48},{12,52},{16,56},{20,60},{24,0},{28,4},{32,8},... | collective-permute-start | bytes 688136 | tf_op jit(solution)/shard_map/ppermute | solution.py:383
  137.3 26.0 %collective-permute-start.27 = (bf16[4,224,128]{2,1,0:T(8,128)(2,1)S(1)}, bf16[4,224,128]{2,1,0:T(8,128)(2,1)S(1)}, u32[]{:S(2)}, u32[]{:S(2)}) collective-permute-start(bf16[4,224,128]{2,1,0:T(8,128)(2,1)S(1)} %get-tuple-element.70), channel_id=1, source_target_pairs={{0,32},{4,36},{8,40},{12,44},{16,48},{20,52},{24,56},{28,60},{32,0... | collective-permute-start | bytes 688136 | tf_op jit(solution)/shard_map/ppermute | solution.py:383
  141.8 30.2 %collective-permute-start.28 = (bf16[4,224,128]{2,1,0:T(8,128)(2,1)S(1)}, bf16[4,224,128]{2,1,0:T(8,128)(2,1)S(1)}, u32[]{:S(2)}, u32[]{:S(2)}) collective-permute-start(bf16[4,224,128]{2,1,0:T(8,128)(2,1)S(1)} %get-tuple-element.71), channel_id=1, source_target_pairs={{0,16},{4,20},{8,24},{12,28},{16,32},{20,36},{24,40},{28,44},{32,4... | collective-permute-start | bytes 688136 | tf_op jit(solution)/shard_map/ppermute | solution.py:383
  152.0 22.5 %collective-permute-start.29 = (bf16[4,224,128]{2,1,0:T(8,128)(2,1)S(1)}, bf16[4,224,128]{2,1,0:T(8,128)(2,1)S(1)}, u32[]{:S(2)}, u32[]{:S(2)}) collective-permute-start(bf16[4,224,128]{2,1,0:T(8,128)(2,1)S(1)} %get-tuple-element.72), channel_id=1, source_target_pairs={{0,48},{4,52},{8,56},{12,60},{16,0},{20,4},{24,8},{28,12},{32,16},... | collective-permute-start | bytes 688136 | tf_op jit(solution)/shard_map/ppermute | solution.py:383
  152.0 24.5 %collective-permute-start.30 = (bf16[4,224,128]{2,1,0:T(8,128)(2,1)S(1)}, bf16[4,224,128]{2,1,0:T(8,128)(2,1)S(1)}, u32[]{:S(2)}, u32[]{:S(2)}) collective-permute-start(bf16[4,224,128]{2,1,0:T(8,128)(2,1)S(1)} %get-tuple-element.74), channel_id=1, source_target_pairs={{0,8},{4,12},{8,16},{12,20},{16,24},{20,28},{24,32},{28,36},{32,40... | collective-permute-start | bytes 688136 | tf_op jit(solution)/shard_map/ppermute | solution.py:383
  161.1 15.4 %collective-permute-start.31 = (bf16[4,224,128]{2,1,0:T(8,128)(2,1)S(1)}, bf16[4,224,128]{2,1,0:T(8,128)(2,1)S(1)}, u32[]{:S(2)}, u32[]{:S(2)}) collective-permute-start(bf16[4,224,128]{2,1,0:T(8,128)(2,1)S(1)} %get-tuple-element.76), channel_id=1, source_target_pairs={{0,56},{4,60},{8,0},{12,4},{16,8},{20,12},{24,16},{28,20},{32,24},... | collective-permute-start | bytes 688136 | tf_op jit(solution)/shard_map/ppermute | solution.py:383
  (10 other events, 299.0 us)

commit v3 on v1

--- a/solution.py
+++ b/solution.py
@@ -1,3 +1,4 @@
+import functools
 import math
 
 import jax
@@ -27,6 +28,8 @@
 EQ = E // N_TP
 KEYS = KNB * NTOK
 GROUPS = ((0, 3), (3, 3))
+HALVES = 2
+ROWS = PART // HALVES
 VMEM = 24 * 1024 * 1024
 WIDE_VMEM = 60 * 1024 * 1024
 BF16 = jnp.bfloat16
@@ -134,18 +137,20 @@
 
             @pl.when(r < half)
             def _():
-                outs[0][r] = ref[block]
+                for n in range(HALVES):
+                    outs[0][n, r] = ref[block, n * ROWS : (n + 1) * ROWS]
 
             @pl.when((r >= half) & (r < REQ))
             def _():
-                outs[1][r - half] = ref[block]
+                for n in range(HALVES):
+                    outs[1][n, r - half] = ref[block, n * ROWS : (n + 1) * ROWS]
 
 
 def pick(neighbour, arrived):
     return pl.pallas_call(
         pick_kernel,
         out_shape=[
-            jax.ShapeDtypeStruct((spans * KNB, PART, E), BF16) for first, spans in GROUPS
+            jax.ShapeDtypeStruct((HALVES, spans * KNB, ROWS, E), BF16) for first, spans in GROUPS
         ],
         in_specs=[IN_SMEM] + [IN_VMEM] * CHIPS,
         out_specs=[IN_VMEM] * len(GROUPS),
@@ -156,22 +161,33 @@
     )(neighbour, *arrived)
 
 
-def attention_kernel(*refs):
-    pieces = refs[:N_TP]
-    kw_ref, vw_ref, q_ref, g_ref = refs[N_TP : N_TP + 4]
-    ctx_ref, qg_ref = refs[-(N_TP + 7) : -(N_TP + 5)]
-    outs = refs[-(N_TP + 5) : -5]
-    xs, ks, vs, kgs, vgs = refs[-5:]
-    for shift in range(N_TP):
-        begin = pl.multiple_of(member(shift) * PART, PART)
-        for k in range(KNB):
-            xs[k, pl.ds(begin, PART), :] = pieces[shift][k]
-    x = xs[...].reshape(KEYS, E)
-    ks[...] = dot(x, kw_ref[...]).astype(BF16)
-    vs[...] = dot(x, vw_ref[...]).astype(BF16)
+def attention_kernel(hops, *refs):
+    pieces = refs[:hops]
+    kw_ref, vw_ref, q_ref, g_ref = refs[hops : hops + 4]
+    ctx_ref, qg_ref = refs[-(N_TP + 8) : -(N_TP + 6)]
+    outs = refs[-(N_TP + 6) : -6]
+    xs, ks, vs, kgs, vgs, backs = refs[-6:]
+    step = pl.program_id(0)
+
+    @pl.when(step == 0)
+    def _():
+        order = (0, 1, 2, 3) if hops == N_TP else (0, 1, 2, 2, 3)
+        for n, shift in enumerate(order):
+            ref = pieces[n]
+            halves = [n - 2] if len(ref.shape) == 3 else range(HALVES)
+            for half in halves:
+                begin = pl.multiple_of(member(shift) * PART + half * ROWS, ROWS)
+                for r in range(ref.shape[-3]):
+                    piece = ref[r] if len(ref.shape) == 3 else ref[half, r]
+                    xs[r, pl.ds(begin, ROWS), :] = piece
+        x = xs[...].reshape(-1, E)
+        ks[...] = dot(x, kw_ref[...]).astype(BF16)
+        vs[...] = dot(x, vw_ref[...]).astype(BF16)
+
+    mine = pl.ds(pl.multiple_of(step * KEYS, KEYS), KEYS)
     cols = [slice(h * DH, (h + 1) * DH) for h in range(HEADS_DEV)]
-    scores = [dot_nt(q_ref[:, c], ks[:, c]) for c in cols]
-    prob_grads = [dot_nt(g_ref[:, c], vs[:, c]) for c in cols]
+    scores = [dot_nt(q_ref[:, c], ks[mine, c]) for c in cols]
+    prob_grads = [dot_nt(g_ref[:, c], vs[mine, c]) for c in cols]
     lows, dscores = [], []
     for score, prob_grad in zip(scores, prob_grads):
         exponent = jnp.exp(score * SCALE)
@@ -183,38 +199,37 @@
         kgs[c, :] = dot_tn(q_ref[:, c], dscore).astype(BF16)
         vgs[c, :] = dot_tn(g_ref[:, c], low).astype(BF16)
     for c, low, dscore in zip(cols, lows, dscores):
-        ctx_ref[:, c] = dot(low, vs[:, c]).astype(BF16)
-        qg_ref[:, c] = dot(dscore, ks[:, c]).astype(BF16)
+        ctx_ref[:, c] = dot(low, vs[mine, c]).astype(BF16)
+        qg_ref[:, c] = dot(dscore, ks[mine, c]).astype(BF16)
+    backs[...] = (dot(kw_ref[...], kgs[...]) + dot(vw_ref[...], vgs[...])).astype(BF16)
     for shift in range(N_TP):
         begin = pl.multiple_of(member(shift) * EQ, 16)
-        piece = dot(kw_ref[pl.ds(begin, EQ), :], kgs[...])
-        piece = (piece + dot(vw_ref[pl.ds(begin, EQ), :], vgs[...])).astype(BF16)
         for k in range(KNB):
-            outs[shift][k] = piece[:, k * NTOK : (k + 1) * NTOK]
+            outs[shift][k] = backs[pl.ds(begin, EQ), k * NTOK : (k + 1) * NTOK]
 
 
 def attention(pieces, kw, vw, queries, ctx_grad, first, spans, held):
     whole = pl.BlockSpec((E, WIDTH), lambda c: (0, 0))
     span = pl.BlockSpec((SPAN, WIDTH), lambda c: (c + first, 0))
-    arrived = pl.BlockSpec((KNB, PART, E), lambda c: (c, 0, 0))
     back = pl.BlockSpec((KNB, EQ, NTOK), lambda c: (c, 0, 0))
     wide = jax.ShapeDtypeStruct((TOKENS_DEV, WIDTH), BF16)
     piece = jax.ShapeDtypeStruct((spans * KNB, EQ, NTOK), BF16)
-    at = N_TP + 4
-    return pl.pallas_call(
-        attention_kernel,
+    hops = len(pieces)
+    return pl.pallas_call(
+        functools.partial(attention_kernel, hops),
         grid=(spans,),
         out_shape=[wide, wide] + [piece] * N_TP,
-        in_specs=[arrived] * N_TP + [whole, whole, span, span] + [ANYWHERE] * len(held),
+        in_specs=[IN_VMEM] * hops + [whole, whole, span, span] + [ANYWHERE] * len(held),
         out_specs=[span, span] + [back] * N_TP,
         scratch_shapes=[
-            pltpu.VMEM((KNB, NTOK, E), BF16),
-            pltpu.VMEM((KEYS, WIDTH), BF16),
-            pltpu.VMEM((KEYS, WIDTH), BF16),
+            pltpu.VMEM((spans * KNB, NTOK, E), BF16),
+            pltpu.VMEM((spans * KEYS, WIDTH), BF16),
+            pltpu.VMEM((spans * KEYS, WIDTH), BF16),
             pltpu.VMEM((WIDTH, KEYS), BF16),
             pltpu.VMEM((WIDTH, KEYS), BF16),
+            pltpu.VMEM((E, KEYS), BF16),
         ],
-        input_output_aliases={at + i: i for i in range(len(held))},
+        input_output_aliases={hops + 4 + i: i for i in range(len(held))},
         compiler_params=params(),
         cost_estimate=cost(spans * 2_200_000_000, 5_000_000 + spans * 1_500_000),
         name="attention",
@@ -374,11 +389,11 @@
     sibling_rows = after(swap(rows), sibling_sources)
     arrived = exchange(pack_rows(rows, sibling_rows, share, swap(share)))
     picked = pick(sources, arrived)
-    whole = []
-    for own in picked:
-        if whole:
-            own = after(own, whole[0][-1])
-        whole.append([own] + [turn(own, -shift) for shift in range(1, N_TP)])
+    low, high = turn(picked[0], 1), turn(picked[0], -1)
+    across = [turn(low[0], 1), turn(high[1], -1)]
+    whole = [[picked[0], high] + across + [low]]
+    own = after(picked[1], low, high)
+    whole.append([own] + [turn(own, -shift) for shift in range(1, N_TP)])
     held = ()
     grads = []
     for group, (first, spans) in enumerate(GROUPS):

time: 179 us -> 177 us (0.989)
  waiting for transfers between devices: 69.8 us -> 64.8 us
  starting transfers between devices: 70.5 us -> 75.1 us
    ppermute x12 -> x13, waiting for transfers between devices: 13.6 us -> 8.19 us  [turn(): return lax.ppermute(x, 'tp', [(i, (i + by) % N_TP) for i in range(N_TP)])]
    ppermute x5, starting transfers between devices: 16.2 us -> 20.3 us  [swap(): return lax.ppermute(x, 'seq', [(i, i ^ 1) for i in range(N_SEQ)])]
    ppermute x12 -> x13, starting transfers between devices: 17.4 us -> 17.3 us  [turn(): return lax.ppermute(x, 'tp', [(i, (i + by) % N_TP) for i in range(N_TP)])]
  transfers between devices with their start and end apart: 32 -> 33, of which waited for: 17 -> 17; matrix products, arithmetic and copies ran while one was open for 0% -> 0% of each run, Pallas kernels for 14% -> 14%
where the time goes in v3:
time: 177 us
  starting transfers between devices  75.1 us (42%)
  waiting for transfers between devices  64.8 us (37%)
  Pallas kernels  33.2 us (19%)
  local copies, waits for them, and re-layouts  2.93 us (2%)
    ppermute x14, waiting for transfers between devices, ahead(): lax.ppermute(x, 'seq', [(i, (i + 2 * by) % N_SEQ) for i in range(N_SEQ)])  53.6 us
    ppermute x14, starting transfers between devices, ahead(): lax.ppermute(x, 'seq', [(i, (i + 2 * by) % N_SEQ) for i in range(N_SEQ)])  36.2 us
    pallas_call x2, Pallas kernels, attention(): pl.pallas_call(functools.partial(attention_kernel, hops), grid=(spans,),...  21.5 us
    ppermute x5, starting transfers between devices, swap(): return lax.ppermute(x, 'seq', [(i, i ^ 1) for i in range(N_SEQ)])  20.3 us
    ppermute x13, starting transfers between devices, turn(): return lax.ppermute(x, 'tp', [(i, (i + by) % N_TP) for i in range(N_TP)])  17.3 us
    ppermute x13, waiting for transfers between devices, turn(): return lax.ppermute(x, 'tp', [(i, (i + by) % N_TP) for i in range(N_TP)])  8.19 us
  transfers between devices with their start and end apart: 33, of which 17 were waited for; matrix products, arithmetic and copies ran while one was open for 0% of the time, Pallas kernels for 14%

profile of v3, /device:TPU:1, one launch (start us, length us, event | category | flops | bytes accessed | tf_op | source)
XLA Modules:
  0.0 176.8 jit_solution(5235551090339830651)
XLA Ops:
  0.7 2.2 %take_share.1.share_ref = bf16[16,32,896]{2,1,0:T(8,128)(2,1)} custom-call(bf16[16,128,896]{2,1,0:T(8,128)(2,1)} %bitcast.24), custom_call_target="tpu_custom_call" | custom-call | bytes 2000000 | tf_op jit(solution)/shard_map/take_share/pallas_call | solution.py:75
  2.9 3.3 %collective-permute-start.2 = (bf16[16,32,896]{2,1,0:T(8,128)(2,1)}, bf16[16,32,896]{2,1,0:T(8,128)(2,1)}, u32[]{:S(2)}, u32[]{:S(2)}) collective-permute-start(bf16[16,32,896]{2,1,0:T(8,128)(2,1)} %take_share.1.share_ref), channel_id=1, source_target_pairs={{0,4},{4,0},{8,12},{12,8},{16,20},{20,16},{24,28},{28,24},{32,36},... | collective-permute-start | bytes 2752520 | tf_op jit(solution)/shard_map/ppermute | solution.py:333
  9.0 2.9 %pack_rows.1 = (bf16[4,32,896]{2,1,0:T(8,128)(2,1)}, bf16[4,32,896]{2,1,0:T(8,128)(2,1)}, bf16[4,32,896]{2,1,0:T(8,128)(2,1)}, bf16[4,32,896]{2,1,0:T(8,128)(2,1...) custom-call(s32[16,2]{1,0:T(8,128)} %copy-done.1, ...), custom_call_target="tpu_custom_call" | custom-call | bytes 3000000 | tf_op jit(solution)/shard_map/pack_rows/pallas_call | solution.py:100
  11.8 2.6 %collective-permute-start.3 = (bf16[4,32,896]{2,1,0:T(8,128)(2,1)}, bf16[4,32,896]{2,1,0:T(8,128)(2,1)S(1)}, u32[]{:S(2)}, u32[]{:S(2)}) collective-permute-start(bf16[4,32,896]{2,1,0:T(8,128)(2,1)} %get-tuple-element.43), channel_id=1, source_target_pairs={{0,24},{4,28},{8,32},{12,36},{16,40},{20,44},{24,48},{28,52},{32,5... | collective-permute-start | bytes 688136 | tf_op jit(solution)/shard_map/ppermute | solution.py:337
  14.4 2.2 %collective-permute-start.7 = (bf16[4,32,896]{2,1,0:T(8,128)(2,1)}, bf16[4,32,896]{2,1,0:T(8,128)(2,1)S(1)}, u32[]{:S(2)}, u32[]{:S(2)}) collective-permute-start(bf16[4,32,896]{2,1,0:T(8,128)(2,1)} %get-tuple-element.47), channel_id=1, source_target_pairs={{0,40},{4,44},{8,48},{12,52},{16,56},{20,60},{24,0},{28,4},{32,8},... | collective-permute-start | bytes 688136 | tf_op jit(solution)/shard_map/ppermute | solution.py:337
  17.8 4.9 %collective-permute-start.6 = (bf16[4,32,896]{2,1,0:T(8,128)(2,1)}, bf16[4,32,896]{2,1,0:T(8,128)(2,1)S(1)}, u32[]{:S(2)}, u32[]{:S(2)}) collective-permute-start(bf16[4,32,896]{2,1,0:T(8,128)(2,1)} %get-tuple-element.46), channel_id=1, source_target_pairs={{0,32},{4,36},{8,40},{12,44},{16,48},{20,52},{24,56},{28,60},{32,0... | collective-permute-start | bytes 688136 | tf_op jit(solution)/shard_map/ppermute | solution.py:337
  22.6 2.4 %collective-permute-start.8 = (bf16[4,32,896]{2,1,0:T(8,128)(2,1)}, bf16[4,32,896]{2,1,0:T(8,128)(2,1)S(1)}, u32[]{:S(2)}, u32[]{:S(2)}) collective-permute-start(bf16[4,32,896]{2,1,0:T(8,128)(2,1)} %get-tuple-element.48), channel_id=1, source_target_pairs={{0,48},{4,52},{8,56},{12,60},{16,0},{20,4},{24,8},{28,12},{32,16},... | collective-permute-start | bytes 688136 | tf_op jit(solution)/shard_map/ppermute | solution.py:337
  25.0 3.6 %collective-permute-done.3.refs_3_ = bf16[4,32,896]{2,1,0:T(8,128)(2,1)S(1)} collective-permute-done((bf16[4,32,896]{2,1,0:T(8,128)(2,1)}, bf16[4,32,896]{2,1,0:T(8,128)(2,1)S(1)}, u32[]{:S(2)}, u32[]{:S(2)}) %collective-permute-start.3) | collective-permute-done | bytes 229408 | tf_op jit(solution)/shard_map/ppermute | solution.py:337
  28.6 3.8 %collective-permute-start.4 = (bf16[4,32,896]{2,1,0:T(8,128)(2,1)}, bf16[4,32,896]{2,1,0:T(8,128)(2,1)S(1)}, u32[]{:S(2)}, u32[]{:S(2)}) collective-permute-start(bf16[4,32,896]{2,1,0:T(8,128)(2,1)} %get-tuple-element.44), channel_id=1, source_target_pairs={{0,8},{4,12},{8,16},{12,20},{16,24},{20,28},{24,32},{28,36},{32,40... | collective-permute-start | bytes 688136 | tf_op jit(solution)/shard_map/ppermute | solution.py:337
  32.5 8.1 %collective-permute-done.5.refs_2_ = bf16[4,32,896]{2,1,0:T(8,128)(2,1)S(1)} collective-permute-done((bf16[4,32,896]{2,1,0:T(8,128)(2,1)}, bf16[4,32,896]{2,1,0:T(8,128)(2,1)S(1)}, u32[]{:S(2)}, u32[]{:S(2)}) %collective-permute-start.5) | collective-permute-done | bytes 229408 | tf_op jit(solution)/shard_map/ppermute | solution.py:337
  40.6 8.9 %collective-permute-done.6.refs_4_ = bf16[4,32,896]{2,1,0:T(8,128)(2,1)S(1)} collective-permute-done((bf16[4,32,896]{2,1,0:T(8,128)(2,1)}, bf16[4,32,896]{2,1,0:T(8,128)(2,1)S(1)}, u32[]{:S(2)}, u32[]{:S(2)}) %collective-permute-start.6) | collective-permute-done | bytes 229408 | tf_op jit(solution)/shard_map/ppermute | solution.py:337
  49.5 2.9 %collective-permute-done.8.refs_6_ = bf16[4,32,896]{2,1,0:T(8,128)(2,1)S(1)} collective-permute-done((bf16[4,32,896]{2,1,0:T(8,128)(2,1)}, bf16[4,32,896]{2,1,0:T(8,128)(2,1)S(1)}, u32[]{:S(2)}, u32[]{:S(2)}) %collective-permute-start.8) | collective-permute-done | bytes 229408 | tf_op jit(solution)/shard_map/ppermute | solution.py:337
  52.4 3.7 %collective-permute-done.4.refs_1_ = bf16[4,32,896]{2,1,0:T(8,128)(2,1)S(1)} collective-permute-done((bf16[4,32,896]{2,1,0:T(8,128)(2,1)}, bf16[4,32,896]{2,1,0:T(8,128)(2,1)S(1)}, u32[]{:S(2)}, u32[]{:S(2)}) %collective-permute-start.4) | collective-permute-done | bytes 229408 | tf_op jit(solution)/shard_map/ppermute | solution.py:337
  59.9 2.6 %collective-permute-start.11 = (bf16[2,6,16,896]{3,2,1,0:T(8,128)(2,1)S(1)}, bf16[2,6,16,896]{3,2,1,0:T(8,128)(2,1)S(1)}, u32[]{:S(2)}, u32[]{:S(2)}) collective-permute-start(bf16[2,6,16,896]{3,2,1,0:T(8,128)(2,1)S(1)} %get-tuple-element.52.refs_0_), channel_id=1, source_target_pairs={{0,3},{1,0},{2,1},{3,2},{4,7},{5,4},{6,5},{7,6},{8,11},{9,8},{10,9... | collective-permute-start | bytes 1032200 | tf_op jit(solution)/shard_map/ppermute | solution.py:355
  62.5 6.4 %collective-permute-done.11.refs_1_ = bf16[2,6,16,896]{3,2,1,0:T(8,128)(2,1)S(1)} collective-permute-done((bf16[2,6,16,896]{3,2,1,0:T(8,128)(2,1)S(1)}, bf16[2,6,16,896]{3,2,1,0:T(8,128)(2,1)S(1)}, u32[]{:S(2)}, u32[]{:S(2)}) %collective-permute-start.11) | collective-permute-done | bytes 344096 | tf_op jit(solution)/shard_map/ppermute | solution.py:355
  69.0 3.5 %collective-permute-start.16 = (bf16[6,16,896]{2,1,0:T(8,128)(2,1)S(1)}, bf16[6,16,896]{2,1,0:T(8,128)(2,1)S(1)}, u32[]{:S(2)}, u32[]{:S(2)}) collective-permute-start(bf16[6,16,896]{2,1,0:T(8,128)(2,1)S(1)} %slice_bitcast_fusion), channel_id=1, source_target_pairs={{0,3},{1,0},{2,1},{3,2},{4,7},{5,4},{6,5},{7,6},{8,11},{9,8},{10,9... | collective-permute-start | bytes 516104 | tf_op jit(solution)/shard_map/ppermute | solution.py:355
  72.6 3.8 %collective-permute-start.13 = (bf16[2,6,16,896]{3,2,1,0:T(8,128)(2,1)S(1)}, bf16[2,6,16,896]{3,2,1,0:T(8,128)(2,1)S(1)}, u32[]{:S(2)}, u32[]{:S(2)}) collective-permute-start(bf16[2,6,16,896]{3,2,1,0:T(8,128)(2,1)S(1)} %get-tuple-element.53.refs_0_), channel_id=1, source_target_pairs={{0,2},{1,3},{2,0},{3,1},{4,6},{5,7},{6,4},{7,5},{8,10},{9,11},{10,... | collective-permute-start | bytes 1032200 | tf_op jit(solution)/shard_map/ppermute | solution.py:355
  79.5 10.8 %attention.2 = (bf16[384,1024]{1,0:T(8,128)(2,1)}, bf16[384,1024]{1,0:T(8,128)(2,1)S(1)}, bf16[6,224,128]{2,1,0:T(8,128)(2,1)S(1)}, bf16[6,224,128]{2,1,0:T(8,12...) custom-call(bf16[2,6,16,896]{3,2,1,0:T(8,128)(2,1)S(1)} %get-tuple-element.52.refs_0_, ...), custom_call_target="tpu_custom_call" | custom-call | flops 6600000000 | bytes 9500000 | tf_op jit(solution)/shard_map/attention/pallas_call | solution.py:218
  93.1 10.7 %attention.3 = (bf16[384,1024]{1,0:T(8,128)(2,1)}, bf16[384,1024]{1,0:T(8,128)(2,1)S(1)}, bf16[6,224,128]{2,1,0:T(8,128)(2,1)S(1)}, bf16[6,224,128]{2,1,0:T(8,12...) custom-call(bf16[2,6,16,896]{3,2,1,0:T(8,128)(2,1)S(1)} %get-tuple-e, ...), custom_call_target="tpu_custom_call", output_to_operand_aliasing={{0}: (8, {}), {1}: (9, {})} | custom-call | flops 6600000000 | bytes 9500000 | tf_op jit(solution)/shard_map/attention/pallas_call | solution.py:218
  104.5 1.9 %collective-permute-start.22 = (bf16[6,224,128]{2,1,0:T(8,128)(2,1)S(1)}, bf16[6,224,128]{2,1,0:T(8,128)(2,1)S(1)}, u32[]{:S(2)}, u32[]{:S(2)}) collective-permute-start(bf16[6,224,128]{2,1,0:T(8,128)(2,1)S(1)} %get-tuple-element.64), channel_id=1, source_target_pairs={{0,2},{1,3},{2,0},{3,1},{4,6},{5,7},{6,4},{7,5},{8,10},{9,11},{10,... | collective-permute-start | bytes 1032200 | tf_op jit(solution)/shard_map/ppermute | solution.py:355
  106.5 1.9 %collective-permute-start.23 = (bf16[6,224,128]{2,1,0:T(8,128)(2,1)S(1)}, bf16[6,224,128]{2,1,0:T(8,128)(2,1)S(1)}, u32[]{:S(2)}, u32[]{:S(2)}) collective-permute-start(bf16[6,224,128]{2,1,0:T(8,128)(2,1)S(1)} %get-tuple-element.65), channel_id=1, source_target_pairs={{0,3},{1,0},{2,1},{3,2},{4,7},{5,4},{6,5},{7,6},{8,11},{9,8},{10,9... | collective-permute-start | bytes 1032200 | tf_op jit(solution)/shard_map/ppermute | solution.py:355
  109.8 9.4 %collective-permute-start.24 = (bf16[6,224,128]{2,1,0:T(8,128)(2,1)S(1)}, bf16[6,224,128]{2,1,0:T(8,128)(2,1)S(1)}, u32[]{:S(2)}, u32[]{:S(2)}) collective-permute-start(bf16[6,224,128]{2,1,0:T(8,128)(2,1)S(1)} %sum_parts.2.refs_0_), channel_id=1, source_target_pairs={{0,4},{4,0},{8,12},{12,8},{16,20},{20,16},{24,28},{28,24},{32,36},... | collective-permute-start | bytes 1032200 | tf_op jit(solution)/shard_map/ppermute | solution.py:333
  119.6 7.0 %collective-permute-start.25 = (bf16[6,224,128]{2,1,0:T(8,128)(2,1)S(1)}, bf16[6,224,128]{2,1,0:T(8,128)(2,1)S(1)}, u32[]{:S(2)}, u32[]{:S(2)}) collective-permute-start(bf16[6,224,128]{2,1,0:T(8,128)(2,1)S(1)} %sum_parts.3.refs_1_), channel_id=1, source_target_pairs={{0,4},{4,0},{8,12},{12,8},{16,20},{20,16},{24,28},{28,24},{32,36},... | collective-permute-start | bytes 1032200 | tf_op jit(solution)/shard_map/ppermute | solution.py:333
  127.8 1.8 %place.1 = (bf16[4,224,128]{2,1,0:T(8,128)(2,1)S(1)}, bf16[4,224,128]{2,1,0:T(8,128)(2,1)S(1)}, bf16[4,224,128]{2,1,0:T(8,128)(2,1)S(1)}, bf16[4,224,128]{2,1,0:...) custom-call(s32[6,2]{1,0:T(8,128)S(1)} %copy.15.neighbour_ref, ...), custom_call_target="tpu_custom_call" | custom-call | bytes 3000000 | tf_op jit(solution)/shard_map/place/pallas_call | solution.py:293
  129.7 4.5 %collective-permute-start.26 = (bf16[4,224,128]{2,1,0:T(8,128)(2,1)S(1)}, bf16[4,224,128]{2,1,0:T(8,128)(2,1)S(1)}, u32[]{:S(2)}, u32[]{:S(2)}) collective-permute-start(bf16[4,224,128]{2,1,0:T(8,128)(2,1)S(1)} %get-tuple-element.66), channel_id=1, source_target_pairs={{0,24},{4,28},{8,32},{12,36},{16,40},{20,44},{24,48},{28,52},{32,5... | collective-permute-start | bytes 688136 | tf_op jit(solution)/shard_map/ppermute | solution.py:337
  135.8 3.1 %collective-permute-start.29 = (bf16[4,224,128]{2,1,0:T(8,128)(2,1)S(1)}, bf16[4,224,128]{2,1,0:T(8,128)(2,1)S(1)}, u32[]{:S(2)}, u32[]{:S(2)}) collective-permute-start(bf16[4,224,128]{2,1,0:T(8,128)(2,1)S(1)} %get-tuple-element.72), channel_id=1, source_target_pairs={{0,32},{4,36},{8,40},{12,44},{16,48},{20,52},{24,56},{28,60},{32,0... | collective-permute-start | bytes 688136 | tf_op jit(solution)/shard_map/ppermute | solution.py:337
  138.9 9.7 %collective-permute-done.26.refs_3_ = bf16[4,224,128]{2,1,0:T(8,128)(2,1)S(1)} collective-permute-done((bf16[4,224,128]{2,1,0:T(8,128)(2,1)S(1)}, bf16[4,224,128]{2,1,0:T(8,128)(2,1)S(1)}, u32[]{:S(2)}, u32[]{:S(2)}) %collective-permute-start.26) | collective-permute-done | bytes 229408 | tf_op jit(solution)/shard_map/ppermute | solution.py:337
  148.6 10.0 %collective-permute-start.27 = (bf16[4,224,128]{2,1,0:T(8,128)(2,1)S(1)}, bf16[4,224,128]{2,1,0:T(8,128)(2,1)S(1)}, u32[]{:S(2)}, u32[]{:S(2)}) collective-permute-start(bf16[4,224,128]{2,1,0:T(8,128)(2,1)S(1)} %get-tuple-element.70), channel_id=1, source_target_pairs={{0,8},{4,12},{8,16},{12,20},{16,24},{20,28},{24,32},{28,36},{32,40... | collective-permute-start | bytes 688136 | tf_op jit(solution)/shard_map/ppermute | solution.py:337
  159.5 7.1 %collective-permute-done.29.refs_4_ = bf16[4,224,128]{2,1,0:T(8,128)(2,1)S(1)} collective-permute-done((bf16[4,224,128]{2,1,0:T(8,128)(2,1)S(1)}, bf16[4,224,128]{2,1,0:T(8,128)(2,1)S(1)}, u32[]{:S(2)}, u32[]{:S(2)}) %collective-permute-start.29) | collective-permute-done | bytes 229408 | tf_op jit(solution)/shard_map/ppermute | solution.py:337
  166.6 4.6 %collective-permute-done.31.refs_6_ = bf16[4,224,128]{2,1,0:T(8,128)(2,1)S(1)} collective-permute-done((bf16[4,224,128]{2,1,0:T(8,128)(2,1)S(1)}, bf16[4,224,128]{2,1,0:T(8,128)(2,1)S(1)}, u32[]{:S(2)}, u32[]{:S(2)}) %collective-permute-start.31) | collective-permute-done | bytes 229408 | tf_op jit(solution)/shard_map/ppermute | solution.py:337
  171.2 3.2 %collective-permute-done.27.refs_1_ = bf16[4,224,128]{2,1,0:T(8,128)(2,1)S(1)} collective-permute-done((bf16[4,224,128]{2,1,0:T(8,128)(2,1)S(1)}, bf16[4,224,128]{2,1,0:T(8,128)(2,1)S(1)}, u32[]{:S(2)}, u32[]{:S(2)}) %collective-permute-start.27) | collective-permute-done | bytes 229408 | tf_op jit(solution)/shard_map/ppermute | solution.py:337
  174.6 2.2 %collect.1 = bf16[16,224,128]{2,1,0:T(8,128)(2,1)} custom-call(s32[16,2]{1,0:T(8,128)S(1)} %copy-done.2, bf16[4,224,128]{2,1,0:T(8,128)(2,1)S(1)} %get-tuple-element.68.refs_0_, bf16[4,224,128]{2,1,0:T(8,128)(2,1)S(1)} %collective-permute-done.27.refs_1_, bf16[4,224,128]{2,1,0:T(8,128)(2,1)S(1)} %collective-permute-done.28.refs_2_, ...), custom_call_target="tpu_custom_call" | custom-call | bytes 3000000 | tf_op jit(solution)/shard_map/collect/pallas_call | solution.py:320
  (68 shorter events, 20.5 us)
Async XLA Ops:
  2.9 5.8 %collective-permute-start.2 = (bf16[16,32,896]{2,1,0:T(8,128)(2,1)}, bf16[16,32,896]{2,1,0:T(8,128)(2,1)}, u32[]{:S(2)}, u32[]{:S(2)}) collective-permute-start(bf16[16,32,896]{2,1,0:T(8,128)(2,1)} %take_share.1.share_ref), channel_id=1, source_target_pairs={{0,4},{4,0},{8,12},{12,8},{16,20},{20,16},{24,28},{28,24},{32,36},... | collective-permute-start | bytes 2752520 | tf_op jit(solution)/shard_map/ppermute | solution.py:333
  6.3 2.0 %collective-permute-start = (s32[16,2]{1,0:T(8,128)S(1)}, s32[16,2]{1,0:T(8,128)S(1)}, u32[]{:S(2)}, u32[]{:S(2)}) collective-permute-start(s32[16,2]{1,0:T(8,128)S(1)} %copy.14.rows_ref), channel_id=1, source_target_pairs={{0,4},{4,0},{8,12},{12,8},{16,20},{20,16},{24,28},{28,24},{32,36},... | collective-permute-start | bytes 392 | tf_op jit(solution)/shard_map/ppermute | solution.py:333
  11.8 16.8 %collective-permute-start.3 = (bf16[4,32,896]{2,1,0:T(8,128)(2,1)}, bf16[4,32,896]{2,1,0:T(8,128)(2,1)S(1)}, u32[]{:S(2)}, u32[]{:S(2)}) collective-permute-start(bf16[4,32,896]{2,1,0:T(8,128)(2,1)} %get-tuple-element.43), channel_id=1, source_target_pairs={{0,24},{4,28},{8,32},{12,36},{16,40},{20,44},{24,48},{28,52},{32,5... | collective-permute-start | bytes 688136 | tf_op jit(solution)/shard_map/ppermute | solution.py:337
  14.4 18.0 %collective-permute-start.7 = (bf16[4,32,896]{2,1,0:T(8,128)(2,1)}, bf16[4,32,896]{2,1,0:T(8,128)(2,1)S(1)}, u32[]{:S(2)}, u32[]{:S(2)}) collective-permute-start(bf16[4,32,896]{2,1,0:T(8,128)(2,1)} %get-tuple-element.47), channel_id=1, source_target_pairs={{0,40},{4,44},{8,48},{12,52},{16,56},{20,60},{24,0},{28,4},{32,8},... | collective-permute-start | bytes 688136 | tf_op jit(solution)/shard_map/ppermute | solution.py:337
  16.6 24.0 %collective-permute-start.5 = (bf16[4,32,896]{2,1,0:T(8,128)(2,1)}, bf16[4,32,896]{2,1,0:T(8,128)(2,1)S(1)}, u32[]{:S(2)}, u32[]{:S(2)}) collective-permute-start(bf16[4,32,896]{2,1,0:T(8,128)(2,1)} %get-tuple-element.45), channel_id=1, source_target_pairs={{0,16},{4,20},{8,24},{12,28},{16,32},{20,36},{24,40},{28,44},{32,4... | collective-permute-start | bytes 688136 | tf_op jit(solution)/shard_map/ppermute | solution.py:337
  17.8 31.7 %collective-permute-start.6 = (bf16[4,32,896]{2,1,0:T(8,128)(2,1)}, bf16[4,32,896]{2,1,0:T(8,128)(2,1)S(1)}, u32[]{:S(2)}, u32[]{:S(2)}) collective-permute-start(bf16[4,32,896]{2,1,0:T(8,128)(2,1)} %get-tuple-element.46), channel_id=1, source_target_pairs={{0,32},{4,36},{8,40},{12,44},{16,48},{20,52},{24,56},{28,60},{32,0... | collective-permute-start | bytes 688136 | tf_op jit(solution)/shard_map/ppermute | solution.py:337
  22.6 29.7 %collective-permute-start.8 = (bf16[4,32,896]{2,1,0:T(8,128)(2,1)}, bf16[4,32,896]{2,1,0:T(8,128)(2,1)S(1)}, u32[]{:S(2)}, u32[]{:S(2)}) collective-permute-start(bf16[4,32,896]{2,1,0:T(8,128)(2,1)} %get-tuple-element.48), channel_id=1, source_target_pairs={{0,48},{4,52},{8,56},{12,60},{16,0},{20,4},{24,8},{28,12},{32,16},... | collective-permute-start | bytes 688136 | tf_op jit(solution)/shard_map/ppermute | solution.py:337
  28.6 27.4 %collective-permute-start.4 = (bf16[4,32,896]{2,1,0:T(8,128)(2,1)}, bf16[4,32,896]{2,1,0:T(8,128)(2,1)S(1)}, u32[]{:S(2)}, u32[]{:S(2)}) collective-permute-start(bf16[4,32,896]{2,1,0:T(8,128)(2,1)} %get-tuple-element.44), channel_id=1, source_target_pairs={{0,8},{4,12},{8,16},{12,20},{16,24},{20,28},{24,32},{28,36},{32,40... | collective-permute-start | bytes 688136 | tf_op jit(solution)/shard_map/ppermute | solution.py:337
  32.5 25.2 %collective-permute-start.9 = (bf16[4,32,896]{2,1,0:T(8,128)(2,1)}, bf16[4,32,896]{2,1,0:T(8,128)(2,1)S(1)}, u32[]{:S(2)}, u32[]{:S(2)}) collective-permute-start(bf16[4,32,896]{2,1,0:T(8,128)(2,1)} %get-tuple-element.50), channel_id=1, source_target_pairs={{0,56},{4,60},{8,0},{12,4},{16,8},{20,12},{24,16},{28,20},{32,24},... | collective-permute-start | bytes 688136 | tf_op jit(solution)/shard_map/ppermute | solution.py:337
  59.9 9.0 %collective-permute-start.11 = (bf16[2,6,16,896]{3,2,1,0:T(8,128)(2,1)S(1)}, bf16[2,6,16,896]{3,2,1,0:T(8,128)(2,1)S(1)}, u32[]{:S(2)}, u32[]{:S(2)}) collective-permute-start(bf16[2,6,16,896]{3,2,1,0:T(8,128)(2,1)S(1)} %get-tuple-element.52.refs_0_), channel_id=1, source_target_pairs={{0,3},{1,0},{2,1},{3,2},{4,7},{5,4},{6,5},{7,6},{8,11},{9,8},{10,9... | collective-permute-start | bytes 1032200 | tf_op jit(solution)/shard_map/ppermute | solution.py:355
  62.5 10.0 %collective-permute-start.10 = (bf16[2,6,16,896]{3,2,1,0:T(8,128)(2,1)S(1)}, bf16[2,6,16,896]{3,2,1,0:T(8,128)(2,1)S(1)}, u32[]{:S(2)}, u32[]{:S(2)}) collective-permute-start(bf16[2,6,16,896]{3,2,1,0:T(8,128)(2,1)S(1)} %get-tuple-element.52.refs_0_), channel_id=1, source_target_pairs={{0,1},{1,2},{2,3},{3,0},{4,5},{5,6},{6,7},{7,4},{8,9},{9,10},{10,1... | collective-permute-start | bytes 1032200 | tf_op jit(solution)/shard_map/ppermute | solution.py:355
  69.0 7.5 %collective-permute-start.16 = (bf16[6,16,896]{2,1,0:T(8,128)(2,1)S(1)}, bf16[6,16,896]{2,1,0:T(8,128)(2,1)S(1)}, u32[]{:S(2)}, u32[]{:S(2)}) collective-permute-start(bf16[6,16,896]{2,1,0:T(8,128)(2,1)S(1)} %slice_bitcast_fusion), channel_id=1, source_target_pairs={{0,3},{1,0},{2,1},{3,2},{4,7},{5,4},{6,5},{7,6},{8,11},{9,8},{10,9... | collective-permute-start | bytes 516104 | tf_op jit(solution)/shard_map/ppermute | solution.py:355
  72.5 5.5 %collective-permute-start.15 = (bf16[6,16,896]{2,1,0:T(8,128)(2,1)S(1)}, bf16[6,16,896]{2,1,0:T(8,128)(2,1)S(1)}, u32[]{:S(2)}, u32[]{:S(2)}) collective-permute-start(bf16[6,16,896]{2,1,0:T(8,128)(2,1)S(1)} %slice_bitcast_fusion.1), channel_id=1, source_target_pairs={{0,1},{1,2},{2,3},{3,0},{4,5},{5,6},{6,7},{7,4},{8,9},{9,10},{10,1... | collective-permute-start | bytes 516104 | tf_op jit(solution)/shard_map/ppermute | solution.py:355
  72.6 18.9 %collective-permute-start.14 = (bf16[2,6,16,896]{3,2,1,0:T(8,128)(2,1)S(1)}, bf16[2,6,16,896]{3,2,1,0:T(8,128)(2,1)S(1)}, u32[]{:S(2)}, u32[]{:S(2)}) collective-permute-start(bf16[2,6,16,896]{3,2,1,0:T(8,128)(2,1)S(1)} %get-tuple-element.53.refs_0_), channel_id=1, source_target_pairs={{0,1},{1,2},{2,3},{3,0},{4,5},{5,6},{6,7},{7,4},{8,9},{9,10},{10,1... | collective-permute-start | bytes 1032200 | tf_op jit(solution)/shard_map/ppermute | solution.py:355
  72.6 20.4 %collective-permute-start.13 = (bf16[2,6,16,896]{3,2,1,0:T(8,128)(2,1)S(1)}, bf16[2,6,16,896]{3,2,1,0:T(8,128)(2,1)S(1)}, u32[]{:S(2)}, u32[]{:S(2)}) collective-permute-start(bf16[2,6,16,896]{3,2,1,0:T(8,128)(2,1)S(1)} %get-tuple-element.53.refs_0_), channel_id=1, source_target_pairs={{0,2},{1,3},{2,0},{3,1},{4,6},{5,7},{6,4},{7,5},{8,10},{9,11},{10,... | collective-permute-start | bytes 1032200 | tf_op jit(solution)/shard_map/ppermute | solution.py:355
  76.4 16.7 %collective-permute-start.12 = (bf16[2,6,16,896]{3,2,1,0:T(8,128)(2,1)S(1)}, bf16[2,6,16,896]{3,2,1,0:T(8,128)(2,1)S(1)}, u32[]{:S(2)}, u32[]{:S(2)}) collective-permute-start(bf16[2,6,16,896]{3,2,1,0:T(8,128)(2,1)S(1)} %get-tuple-element.53.refs_0_), channel_id=1, source_target_pairs={{0,3},{1,0},{2,1},{3,2},{4,7},{5,4},{6,5},{7,6},{8,11},{9,8},{10,9... | collective-permute-start | bytes 1032200 | tf_op jit(solution)/shard_map/ppermute | solution.py:355
  90.3 16.2 %collective-permute-start.18 = (bf16[6,224,128]{2,1,0:T(8,128)(2,1)S(1)}, bf16[6,224,128]{2,1,0:T(8,128)(2,1)S(1)}, u32[]{:S(2)}, u32[]{:S(2)}) collective-permute-start(bf16[6,224,128]{2,1,0:T(8,128)(2,1)S(1)} %get-tuple-element.59), channel_id=1, source_target_pairs={{0,1},{1,2},{2,3},{3,0},{4,5},{5,6},{6,7},{7,4},{8,9},{9,10},{10,1... | collective-permute-start | bytes 1032200 | tf_op jit(solution)/shard_map/ppermute | solution.py:355
  90.4 18.0 %collective-permute-start.19 = (bf16[6,224,128]{2,1,0:T(8,128)(2,1)S(1)}, bf16[6,224,128]{2,1,0:T(8,128)(2,1)S(1)}, u32[]{:S(2)}, u32[]{:S(2)}) collective-permute-start(bf16[6,224,128]{2,1,0:T(8,128)(2,1)S(1)} %get-tuple-element.60), channel_id=1, source_target_pairs={{0,2},{1,3},{2,0},{3,1},{4,6},{5,7},{6,4},{7,5},{8,10},{9,11},{10,... | collective-permute-start | bytes 1032200 | tf_op jit(solution)/shard_map/ppermute | solution.py:355
  91.5 18.2 %collective-permute-start.20 = (bf16[6,224,128]{2,1,0:T(8,128)(2,1)S(1)}, bf16[6,224,128]{2,1,0:T(8,128)(2,1)S(1)}, u32[]{:S(2)}, u32[]{:S(2)}) collective-permute-start(bf16[6,224,128]{2,1,0:T(8,128)(2,1)S(1)} %get-tuple-element.61), channel_id=1, source_target_pairs={{0,3},{1,0},{2,1},{3,2},{4,7},{5,4},{6,5},{7,6},{8,11},{9,8},{10,9... | collective-permute-start | bytes 1032200 | tf_op jit(solution)/shard_map/ppermute | solution.py:355
  103.8 15.5 %collective-permute-start.21 = (bf16[6,224,128]{2,1,0:T(8,128)(2,1)S(1)}, bf16[6,224,128]{2,1,0:T(8,128)(2,1)S(1)}, u32[]{:S(2)}, u32[]{:S(2)}) collective-permute-start(bf16[6,224,128]{2,1,0:T(8,128)(2,1)S(1)} %get-tuple-element.63), channel_id=1, source_target_pairs={{0,1},{1,2},{2,3},{3,0},{4,5},{5,6},{6,7},{7,4},{8,9},{9,10},{10,1... | collective-permute-start | bytes 1032200 | tf_op jit(solution)/shard_map/ppermute | solution.py:355
  104.5 14.9 %collective-permute-start.22 = (bf16[6,224,128]{2,1,0:T(8,128)(2,1)S(1)}, bf16[6,224,128]{2,1,0:T(8,128)(2,1)S(1)}, u32[]{:S(2)}, u32[]{:S(2)}) collective-permute-start(bf16[6,224,128]{2,1,0:T(8,128)(2,1)S(1)} %get-tuple-element.64), channel_id=1, source_target_pairs={{0,2},{1,3},{2,0},{3,1},{4,6},{5,7},{6,4},{7,5},{8,10},{9,11},{10,... | collective-permute-start | bytes 1032200 | tf_op jit(solution)/shard_map/ppermute | solution.py:355
  106.5 12.9 %collective-permute-start.23 = (bf16[6,224,128]{2,1,0:T(8,128)(2,1)S(1)}, bf16[6,224,128]{2,1,0:T(8,128)(2,1)S(1)}, u32[]{:S(2)}, u32[]{:S(2)}) collective-permute-start(bf16[6,224,128]{2,1,0:T(8,128)(2,1)S(1)} %get-tuple-element.65), channel_id=1, source_target_pairs={{0,3},{1,0},{2,1},{3,2},{4,7},{5,4},{6,5},{7,6},{8,11},{9,8},{10,9... | collective-permute-start | bytes 1032200 | tf_op jit(solution)/shard_map/ppermute | solution.py:355
  108.4 50.2 %collective-permute-start.17 = (bf16[384,1024]{1,0:T(8,128)(2,1)S(1)}, bf16[384,1024]{1,0:T(8,128)(2,1)S(1)}, u32[]{:S(2)}, u32[]{:S(2)}) collective-permute-start(bf16[384,1024]{1,0:T(8,128)(2,1)S(1)} %get-tuple-element.57), channel_id=1, source_target_pairs={{64,0},{128,64},{192,128},{65,1},{129,65},{193,129},{66,2},{130,66... | collective-permute-start | bytes 2359304 | tf_op jit(solution)/shard_map/ppermute | solution.py:360
  109.8 16.7 %collective-permute-start.24 = (bf16[6,224,128]{2,1,0:T(8,128)(2,1)S(1)}, bf16[6,224,128]{2,1,0:T(8,128)(2,1)S(1)}, u32[]{:S(2)}, u32[]{:S(2)}) collective-permute-start(bf16[6,224,128]{2,1,0:T(8,128)(2,1)S(1)} %sum_parts.2.refs_0_), channel_id=1, source_target_pairs={{0,4},{4,0},{8,12},{12,8},{16,20},{20,16},{24,28},{28,24},{32,36},... | collective-permute-start | bytes 1032200 | tf_op jit(solution)/shard_map/ppermute | solution.py:333
  119.6 8.2 %collective-permute-start.25 = (bf16[6,224,128]{2,1,0:T(8,128)(2,1)S(1)}, bf16[6,224,128]{2,1,0:T(8,128)(2,1)S(1)}, u32[]{:S(2)}, u32[]{:S(2)}) collective-permute-start(bf16[6,224,128]{2,1,0:T(8,128)(2,1)S(1)} %sum_parts.3.refs_1_), channel_id=1, source_target_pairs={{0,4},{4,0},{8,12},{12,8},{16,20},{20,16},{24,28},{28,24},{32,36},... | collective-permute-start | bytes 1032200 | tf_op jit(solution)/shard_map/ppermute | solution.py:333
  129.7 18.9 %collective-permute-start.26 = (bf16[4,224,128]{2,1,0:T(8,128)(2,1)S(1)}, bf16[4,224,128]{2,1,0:T(8,128)(2,1)S(1)}, u32[]{:S(2)}, u32[]{:S(2)}) collective-permute-start(bf16[4,224,128]{2,1,0:T(8,128)(2,1)S(1)} %get-tuple-element.66), channel_id=1, source_target_pairs={{0,24},{4,28},{8,32},{12,36},{16,40},{20,44},{24,48},{28,52},{32,5... | collective-permute-start | bytes 688136 | tf_op jit(solution)/shard_map/ppermute | solution.py:337
  134.1 14.5 %collective-permute-start.30 = (bf16[4,224,128]{2,1,0:T(8,128)(2,1)S(1)}, bf16[4,224,128]{2,1,0:T(8,128)(2,1)S(1)}, u32[]{:S(2)}, u32[]{:S(2)}) collective-permute-start(bf16[4,224,128]{2,1,0:T(8,128)(2,1)S(1)} %get-tuple-element.73), channel_id=1, source_target_pairs={{0,40},{4,44},{8,48},{12,52},{16,56},{20,60},{24,0},{28,4},{32,8},... | collective-permute-start | bytes 688136 | tf_op jit(solution)/shard_map/ppermute | solution.py:337
  134.2 25.3 %collective-permute-start.28 = (bf16[4,224,128]{2,1,0:T(8,128)(2,1)S(1)}, bf16[4,224,128]{2,1,0:T(8,128)(2,1)S(1)}, u32[]{:S(2)}, u32[]{:S(2)}) collective-permute-start(bf16[4,224,128]{2,1,0:T(8,128)(2,1)S(1)} %get-tuple-element.71), channel_id=1, source_target_pairs={{0,16},{4,20},{8,24},{12,28},{16,32},{20,36},{24,40},{28,44},{32,4... | collective-permute-start | bytes 688136 | tf_op jit(solution)/shard_map/ppermute | solution.py:337
  135.8 30.8 %collective-permute-start.29 = (bf16[4,224,128]{2,1,0:T(8,128)(2,1)S(1)}, bf16[4,224,128]{2,1,0:T(8,128)(2,1)S(1)}, u32[]{:S(2)}, u32[]{:S(2)}) collective-permute-start(bf16[4,224,128]{2,1,0:T(8,128)(2,1)S(1)} %get-tuple-element.72), channel_id=1, source_target_pairs={{0,32},{4,36},{8,40},{12,44},{16,48},{20,52},{24,56},{28,60},{32,0... | collective-permute-start | bytes 688136 | tf_op jit(solution)/shard_map/ppermute | solution.py:337
  148.6 22.6 %collective-permute-start.31 = (bf16[4,224,128]{2,1,0:T(8,128)(2,1)S(1)}, bf16[4,224,128]{2,1,0:T(8,128)(2,1)S(1)}, u32[]{:S(2)}, u32[]{:S(2)}) collective-permute-start(bf16[4,224,128]{2,1,0:T(8,128)(2,1)S(1)} %get-tuple-element.74), channel_id=1, source_target_pairs={{0,48},{4,52},{8,56},{12,60},{16,0},{20,4},{24,8},{28,12},{32,16},... | collective-permute-start | bytes 688136 | tf_op jit(solution)/shard_map/ppermute | solution.py:337
  148.6 25.8 %collective-permute-start.27 = (bf16[4,224,128]{2,1,0:T(8,128)(2,1)S(1)}, bf16[4,224,128]{2,1,0:T(8,128)(2,1)S(1)}, u32[]{:S(2)}, u32[]{:S(2)}) collective-permute-start(bf16[4,224,128]{2,1,0:T(8,128)(2,1)S(1)} %get-tuple-element.70), channel_id=1, source_target_pairs={{0,8},{4,12},{8,16},{12,20},{16,24},{20,28},{24,32},{28,36},{32,40... | collective-permute-start | bytes 688136 | tf_op jit(solution)/shard_map/ppermute | solution.py:337
  158.6 16.0 %collective-permute-start.32 = (bf16[4,224,128]{2,1,0:T(8,128)(2,1)S(1)}, bf16[4,224,128]{2,1,0:T(8,128)(2,1)S(1)}, u32[]{:S(2)}, u32[]{:S(2)}) collective-permute-start(bf16[4,224,128]{2,1,0:T(8,128)(2,1)S(1)} %get-tuple-element.76), channel_id=1, source_target_pairs={{0,56},{4,60},{8,0},{12,4},{16,8},{20,12},{24,16},{28,20},{32,24},... | collective-permute-start | bytes 688136 | tf_op jit(solution)/shard_map/ppermute | solution.py:337
  (11 other events, 299.9 us)

commit v4 on v3

--- a/solution.py
+++ b/solution.py
@@ -161,9 +161,33 @@
     )(neighbour, *arrived)
 
 
-def attention_kernel(hops, *refs):
-    pieces = refs[:hops]
-    kw_ref, vw_ref, q_ref, g_ref = refs[hops : hops + 4]
+def project_kernel(count, *refs):
+    pieces, (kw_ref, vw_ref) = refs[:count], refs[count : count + 2]
+    outs = refs[count + 2 :]
+    for n, piece in enumerate(pieces):
+        x = piece[...].reshape(-1, E)
+        for w_ref, out in ((kw_ref, outs[2 * n]), (vw_ref, outs[2 * n + 1])):
+            out[...] = dot(x, w_ref[...]).astype(BF16).reshape(out.shape)
+
+
+def project(pieces, kw, vw):
+    outs = [jax.ShapeDtypeStruct(piece.shape[:-1] + (WIDTH,), BF16) for piece in pieces]
+    results = pl.pallas_call(
+        functools.partial(project_kernel, len(pieces)),
+        out_shape=[out for out in outs for _ in range(2)],
+        in_specs=[IN_VMEM] * (len(pieces) + 2),
+        out_specs=[IN_VMEM] * (2 * len(pieces)),
+        compiler_params=params(),
+        cost_estimate=cost(1_500_000_000, 6_000_000),
+        name="project",
+    )(*pieces, kw, vw)
+    return [results[2 * n : 2 * n + 2] for n in range(len(pieces))]
+
+
+def attention_kernel(known, raw, *refs):
+    ready, arrived = refs[: 2 * len(known)], refs[2 * len(known) : 2 * len(known) + len(raw)]
+    at = 2 * len(known) + len(raw)
+    kw_ref, vw_ref, q_ref, g_ref = refs[at : at + 4]
     ctx_ref, qg_ref = refs[-(N_TP + 8) : -(N_TP + 6)]
     outs = refs[-(N_TP + 6) : -6]
     xs, ks, vs, kgs, vgs, backs = refs[-6:]
@@ -171,18 +195,27 @@
 
     @pl.when(step == 0)
     def _():
-        order = (0, 1, 2, 3) if hops == N_TP else (0, 1, 2, 2, 3)
-        for n, shift in enumerate(order):
-            ref = pieces[n]
-            halves = [n - 2] if len(ref.shape) == 3 else range(HALVES)
+        def rows_of(shift, half, r):
+            begin = r * NTOK + member(shift) * PART + half * ROWS
+            return pl.ds(pl.multiple_of(begin, ROWS), ROWS)
+
+        requests = ks.shape[0] // NTOK
+        for n, shift in enumerate(known):
+            for half in range(HALVES):
+                for r in range(requests):
+                    ks[rows_of(shift, half, r), :] = ready[2 * n][half, r]
+                    vs[rows_of(shift, half, r), :] = ready[2 * n + 1][half, r]
+        spots = []
+        for ref, (shift, halves) in zip(arrived, raw):
             for half in halves:
-                begin = pl.multiple_of(member(shift) * PART + half * ROWS, ROWS)
-                for r in range(ref.shape[-3]):
-                    piece = ref[r] if len(ref.shape) == 3 else ref[half, r]
-                    xs[r, pl.ds(begin, ROWS), :] = piece
-        x = xs[...].reshape(-1, E)
-        ks[...] = dot(x, kw_ref[...]).astype(BF16)
-        vs[...] = dot(x, vw_ref[...]).astype(BF16)
+                for r in range(requests):
+                    piece = ref[r] if len(halves) == 1 else ref[half, r]
+                    xs[len(spots) * ROWS : (len(spots) + 1) * ROWS, :] = piece
+                    spots.append(rows_of(shift, half, r))
+        for w_ref, out in ((kw_ref, ks), (vw_ref, vs)):
+            found = dot(xs[...], w_ref[...]).astype(BF16)
+            for n, spot in enumerate(spots):
+                out[spot, :] = found[n * ROWS : (n + 1) * ROWS]
 
     mine = pl.ds(pl.multiple_of(step * KEYS, KEYS), KEYS)
     cols = [slice(h * DH, (h + 1) * DH) for h in range(HEADS_DEV)]
@@ -208,32 +241,39 @@
             outs[shift][k] = backs[pl.ds(begin, EQ), k * NTOK : (k + 1) * NTOK]
 
 
-def attention(pieces, kw, vw, queries, ctx_grad, first, spans, held):
+def attention(known, raw, kw, vw, queries, ctx_grad, first, spans, held):
     whole = pl.BlockSpec((E, WIDTH), lambda c: (0, 0))
     span = pl.BlockSpec((SPAN, WIDTH), lambda c: (c + first, 0))
     back = pl.BlockSpec((KNB, EQ, NTOK), lambda c: (c, 0, 0))
     wide = jax.ShapeDtypeStruct((TOKENS_DEV, WIDTH), BF16)
     piece = jax.ShapeDtypeStruct((spans * KNB, EQ, NTOK), BF16)
-    hops = len(pieces)
-    return pl.pallas_call(
-        functools.partial(attention_kernel, hops),
+    ready = [x for shift, pair in known for x in pair]
+    arrived = [x for shift, halves, x in raw]
+    at = len(ready) + len(arrived)
+    raw_rows = sum(len(halves) for shift, halves, x in raw) * spans * KNB * ROWS
+    return pl.pallas_call(
+        functools.partial(
+            attention_kernel,
+            [shift for shift, pair in known],
+            [(shift, halves) for shift, halves, x in raw],
+        ),
         grid=(spans,),
         out_shape=[wide, wide] + [piece] * N_TP,
-        in_specs=[IN_VMEM] * hops + [whole, whole, span, span] + [ANYWHERE] * len(held),
+        in_specs=[IN_VMEM] * at + [whole, whole, span, span] + [ANYWHERE] * len(held),
         out_specs=[span, span] + [back] * N_TP,
         scratch_shapes=[
-            pltpu.VMEM((spans * KNB, NTOK, E), BF16),
+            pltpu.VMEM((raw_rows, E), BF16),
             pltpu.VMEM((spans * KEYS, WIDTH), BF16),
             pltpu.VMEM((spans * KEYS, WIDTH), BF16),
             pltpu.VMEM((WIDTH, KEYS), BF16),
             pltpu.VMEM((WIDTH, KEYS), BF16),
             pltpu.VMEM((E, KEYS), BF16),
         ],
-        input_output_aliases={hops + 4 + i: i for i in range(len(held))},
+        input_output_aliases={at + 4 + i: i for i in range(len(held))},
         compiler_params=params(),
         cost_estimate=cost(spans * 2_200_000_000, 5_000_000 + spans * 1_500_000),
         name="attention",
-    )(*pieces, kw, vw, queries, ctx_grad, *held)
+    )(*ready, *arrived, kw, vw, queries, ctx_grad, *held)
 
 
 def sum_kernel(*refs):
@@ -390,15 +430,25 @@
     arrived = exchange(pack_rows(rows, sibling_rows, share, swap(share)))
     picked = pick(sources, arrived)
     low, high = turn(picked[0], 1), turn(picked[0], -1)
-    across = [turn(low[0], 1), turn(high[1], -1)]
-    whole = [[picked[0], high] + across + [low]]
+    own_first, own_second = project(picked, kw, vw)
+    across = [turn(after(low, *own_first)[0], 1), turn(after(high, *own_first)[1], -1)]
     own = after(picked[1], low, high)
-    whole.append([own] + [turn(own, -shift) for shift in range(1, N_TP)])
+    others = [turn(own, -shift) for shift in range(1, N_TP)]
+    next_first, last_first = project([high, low], kw, vw)
+    both = tuple(range(HALVES))
+    known = [
+        [(0, own_first), (1, next_first), (3, last_first)],
+        [(0, own_second)],
+    ]
+    raw = [
+        [(2, (half,), x) for half, x in enumerate(across)],
+        [(shift, both, x) for shift, x in enumerate(others, 1)],
+    ]
     held = ()
     grads = []
     for group, (first, spans) in enumerate(GROUPS):
         *held, first_piece, second, third, fourth = attention(
-            whole[group], kw, vw, queries[0], ctx_grad[0], first, spans, held
+            known[group], raw[group], kw, vw, queries[0], ctx_grad[0], first, spans, held
         )
         turned = [turn(x, by) for by, x in ((1, second), (2, third), (3, fourth))]
         grads.append(sum_parts([first_piece] + turned))

time: 177 us -> 180 us (1.017)
    pallas_call x2 -> x4, Pallas kernels: 21.5 us -> 22.9 us  [the longest x2 19.2 us: attention(): pl.pallas_call(functools.partial(attention_kernel, [shift for shift, pair...]
    unnamed x20 -> x22, local copies, waits for them, and re-layouts: 2.73 us -> 3.83 us
  transfers between devices with their start and end apart: 33 -> 33, of which waited for: 17 -> 18; matrix products, arithmetic and copies ran while one was open for 0% -> 0% of each run, Pallas kernels for 14% -> 14%
where the time goes in v4:
time: 180 us
  starting transfers between devices  75.3 us (42%)
  waiting for transfers between devices  65.5 us (36%)
  Pallas kernels  34.4 us (19%)
  local copies, waits for them, and re-layouts  4.04 us (2%)
    ppermute x14, waiting for transfers between devices, ahead(): lax.ppermute(x, 'seq', [(i, (i + 2 * by) % N_SEQ) for i in range(N_SEQ)])  55.3 us
    ppermute x14, starting transfers between devices, ahead(): lax.ppermute(x, 'seq', [(i, (i + 2 * by) % N_SEQ) for i in range(N_SEQ)])  35.5 us
    ppermute x5, starting transfers between devices, swap(): return lax.ppermute(x, 'seq', [(i, i ^ 1) for i in range(N_SEQ)])  20.9 us
    pallas_call x2, Pallas kernels, attention(): pl.pallas_call(functools.partial(attention_kernel, [shift for shift, pair...  19.2 us
    ppermute x13, starting transfers between devices, turn(): return lax.ppermute(x, 'tp', [(i, (i + by) % N_TP) for i in range(N_TP)])  17.6 us
    ppermute x13, waiting for transfers between devices, turn(): return lax.ppermute(x, 'tp', [(i, (i + by) % N_TP) for i in range(N_TP)])  7.4 us
    unnamed x22, local copies, waits for them, and re-layouts  3.83 us
    pallas_call x2, Pallas kernels, project(): pl.pallas_call(functools.partial(project_kernel, len(pieces)), out_shape=...  3.67 us
  transfers between devices with their start and end apart: 33, of which 18 were waited for; matrix products, arithmetic and copies ran while one was open for 0% of the time, Pallas kernels for 14%

profile of v4, /device:TPU:1, one launch (start us, length us, event | category | flops | bytes accessed | tf_op | source)
XLA Modules:
  0.0 180.1 jit_solution(10265991527473732579)
XLA Ops:
  0.7 2.1 %take_share.1.share_ref = bf16[16,32,896]{2,1,0:T(8,128)(2,1)} custom-call(bf16[16,128,896]{2,1,0:T(8,128)(2,1)} %bitcast.28), custom_call_target="tpu_custom_call" | custom-call | bytes 2000000 | tf_op jit(solution)/shard_map/take_share/pallas_call | solution.py:75
  2.8 3.3 %collective-permute-start.2 = (bf16[16,32,896]{2,1,0:T(8,128)(2,1)}, bf16[16,32,896]{2,1,0:T(8,128)(2,1)S(1)}, u32[]{:S(2)}, u32[]{:S(2)}) collective-permute-start(bf16[16,32,896]{2,1,0:T(8,128)(2,1)} %take_share.1.share_ref), channel_id=1, source_target_pairs={{0,4},{4,0},{8,12},{12,8},{16,20},{20,16},{24,28},{28,24},{32,36},... | collective-permute-start | bytes 2752520 | tf_op jit(solution)/shard_map/ppermute | solution.py:373
  9.8 2.9 %pack_rows.1 = (bf16[4,32,896]{2,1,0:T(8,128)(2,1)}, bf16[4,32,896]{2,1,0:T(8,128)(2,1)}, bf16[4,32,896]{2,1,0:T(8,128)(2,1)}, bf16[4,32,896]{2,1,0:T(8,128)(2,1...) custom-call(s32[16,2]{1,0:T(8,128)} %copy-done.1, ...), custom_call_target="tpu_custom_call" | custom-call | bytes 3000000 | tf_op jit(solution)/shard_map/pack_rows/pallas_call | solution.py:100
  12.6 2.6 %collective-permute-start.3 = (bf16[4,32,896]{2,1,0:T(8,128)(2,1)}, bf16[4,32,896]{2,1,0:T(8,128)(2,1)S(1)}, u32[]{:S(2)}, u32[]{:S(2)}) collective-permute-start(bf16[4,32,896]{2,1,0:T(8,128)(2,1)} %get-tuple-element.53), channel_id=1, source_target_pairs={{0,24},{4,28},{8,32},{12,36},{16,40},{20,44},{24,48},{28,52},{32,5... | collective-permute-start | bytes 688136 | tf_op jit(solution)/shard_map/ppermute | solution.py:377
  15.2 2.2 %collective-permute-start.7 = (bf16[4,32,896]{2,1,0:T(8,128)(2,1)}, bf16[4,32,896]{2,1,0:T(8,128)(2,1)S(1)}, u32[]{:S(2)}, u32[]{:S(2)}) collective-permute-start(bf16[4,32,896]{2,1,0:T(8,128)(2,1)} %get-tuple-element.57), channel_id=1, source_target_pairs={{0,40},{4,44},{8,48},{12,52},{16,56},{20,60},{24,0},{28,4},{32,8},... | collective-permute-start | bytes 688136 | tf_op jit(solution)/shard_map/ppermute | solution.py:377
  18.6 4.9 %collective-permute-start.6 = (bf16[4,32,896]{2,1,0:T(8,128)(2,1)}, bf16[4,32,896]{2,1,0:T(8,128)(2,1)S(1)}, u32[]{:S(2)}, u32[]{:S(2)}) collective-permute-start(bf16[4,32,896]{2,1,0:T(8,128)(2,1)} %get-tuple-element.56), channel_id=1, source_target_pairs={{0,32},{4,36},{8,40},{12,44},{16,48},{20,52},{24,56},{28,60},{32,0... | collective-permute-start | bytes 688136 | tf_op jit(solution)/shard_map/ppermute | solution.py:377
  23.5 2.4 %collective-permute-start.8 = (bf16[4,32,896]{2,1,0:T(8,128)(2,1)}, bf16[4,32,896]{2,1,0:T(8,128)(2,1)S(1)}, u32[]{:S(2)}, u32[]{:S(2)}) collective-permute-start(bf16[4,32,896]{2,1,0:T(8,128)(2,1)} %get-tuple-element.58), channel_id=1, source_target_pairs={{0,48},{4,52},{8,56},{12,60},{16,0},{20,4},{24,8},{28,12},{32,16},... | collective-permute-start | bytes 688136 | tf_op jit(solution)/shard_map/ppermute | solution.py:377
  25.9 3.6 %collective-permute-done.3.refs_3_ = bf16[4,32,896]{2,1,0:T(8,128)(2,1)S(1)} collective-permute-done((bf16[4,32,896]{2,1,0:T(8,128)(2,1)}, bf16[4,32,896]{2,1,0:T(8,128)(2,1)S(1)}, u32[]{:S(2)}, u32[]{:S(2)}) %collective-permute-start.3) | collective-permute-done | bytes 229408 | tf_op jit(solution)/shard_map/ppermute | solution.py:377
  29.5 3.8 %collective-permute-start.4 = (bf16[4,32,896]{2,1,0:T(8,128)(2,1)}, bf16[4,32,896]{2,1,0:T(8,128)(2,1)S(1)}, u32[]{:S(2)}, u32[]{:S(2)}) collective-permute-start(bf16[4,32,896]{2,1,0:T(8,128)(2,1)} %get-tuple-element.54), channel_id=1, source_target_pairs={{0,8},{4,12},{8,16},{12,20},{16,24},{20,28},{24,32},{28,36},{32,40... | collective-permute-start | bytes 688136 | tf_op jit(solution)/shard_map/ppermute | solution.py:377
  33.3 8.1 %collective-permute-done.5.refs_2_ = bf16[4,32,896]{2,1,0:T(8,128)(2,1)S(1)} collective-permute-done((bf16[4,32,896]{2,1,0:T(8,128)(2,1)}, bf16[4,32,896]{2,1,0:T(8,128)(2,1)S(1)}, u32[]{:S(2)}, u32[]{:S(2)}) %collective-permute-start.5) | collective-permute-done | bytes 229408 | tf_op jit(solution)/shard_map/ppermute | solution.py:377
  41.4 8.9 %collective-permute-done.6.refs_4_ = bf16[4,32,896]{2,1,0:T(8,128)(2,1)S(1)} collective-permute-done((bf16[4,32,896]{2,1,0:T(8,128)(2,1)}, bf16[4,32,896]{2,1,0:T(8,128)(2,1)S(1)}, u32[]{:S(2)}, u32[]{:S(2)}) %collective-permute-start.6) | collective-permute-done | bytes 229408 | tf_op jit(solution)/shard_map/ppermute | solution.py:377
  50.3 2.9 %collective-permute-done.8.refs_6_ = bf16[4,32,896]{2,1,0:T(8,128)(2,1)S(1)} collective-permute-done((bf16[4,32,896]{2,1,0:T(8,128)(2,1)}, bf16[4,32,896]{2,1,0:T(8,128)(2,1)S(1)}, u32[]{:S(2)}, u32[]{:S(2)}) %collective-permute-start.8) | collective-permute-done | bytes 229408 | tf_op jit(solution)/shard_map/ppermute | solution.py:377
  53.3 3.6 %collective-permute-done.4.refs_1_ = bf16[4,32,896]{2,1,0:T(8,128)(2,1)S(1)} collective-permute-done((bf16[4,32,896]{2,1,0:T(8,128)(2,1)}, bf16[4,32,896]{2,1,0:T(8,128)(2,1)S(1)}, u32[]{:S(2)}, u32[]{:S(2)}) %collective-permute-start.4) | collective-permute-done | bytes 229408 | tf_op jit(solution)/shard_map/ppermute | solution.py:377
  60.8 2.6 %collective-permute-start.11 = (bf16[2,6,16,896]{3,2,1,0:T(8,128)(2,1)S(1)}, bf16[2,6,16,896]{3,2,1,0:T(8,128)(2,1)S(1)}, u32[]{:S(2)}, u32[]{:S(2)}) collective-permute-start(bf16[2,6,16,896]{3,2,1,0:T(8,128)(2,1)S(1)} %get-tuple-element.61.refs_0_), channel_id=1, source_target_pairs={{0,3},{1,0},{2,1},{3,2},{4,7},{5,4},{6,5},{7,6},{8,11},{9,8},{10,9... | collective-permute-start | bytes 1032200 | tf_op jit(solution)/shard_map/ppermute | solution.py:395
  66.7 3.1 %collective-permute-done.11.refs_0_ = bf16[2,6,16,896]{3,2,1,0:T(8,128)(2,1)S(1)} collective-permute-done((bf16[2,6,16,896]{3,2,1,0:T(8,128)(2,1)S(1)}, bf16[2,6,16,896]{3,2,1,0:T(8,128)(2,1)S(1)}, u32[]{:S(2)}, u32[]{:S(2)}) %collective-permute-start.11) | collective-permute-done | bytes 344096 | tf_op jit(solution)/shard_map/ppermute | solution.py:395
  69.8 3.1 %collective-permute-done.10.refs_1_ = bf16[2,6,16,896]{3,2,1,0:T(8,128)(2,1)S(1)} collective-permute-done((bf16[2,6,16,896]{3,2,1,0:T(8,128)(2,1)S(1)}, bf16[2,6,16,896]{3,2,1,0:T(8,128)(2,1)S(1)}, u32[]{:S(2)}, u32[]{:S(2)}) %collective-permute-start.10) | collective-permute-done | bytes 344096 | tf_op jit(solution)/shard_map/ppermute | solution.py:395
  73.0 2.7 %collective-permute-start.16 = (bf16[6,16,896]{2,1,0:T(8,128)(2,1)S(1)}, bf16[6,16,896]{2,1,0:T(8,128)(2,1)S(1)}, u32[]{:S(2)}, u32[]{:S(2)}) collective-permute-start(bf16[6,16,896]{2,1,0:T(8,128)(2,1)S(1)} %slice_bitcast_fusion), channel_id=1, source_target_pairs={{0,3},{1,0},{2,1},{3,2},{4,7},{5,4},{6,5},{7,6},{8,11},{9,8},{10,9... | collective-permute-start | bytes 516104 | tf_op jit(solution)/shard_map/ppermute | solution.py:395
  80.2 8.9 %attention.2 = (bf16[384,1024]{1,0:T(8,128)(2,1)}, bf16[384,1024]{1,0:T(8,128)(2,1)S(1)}, bf16[6,224,128]{2,1,0:T(8,128)(2,1)S(1)}, bf16[6,224,128]{2,1,0:T(8,12...) custom-call(bf16[2,6,16,1024]{3,2,1,0:T(8,128)(2,1)S(1)} %get-tuple-element.66.refs_0_, ...), custom_call_target="tpu_custom_call" | custom-call | flops 6600000000 | bytes 9500000 | tf_op jit(solution)/shard_map/attention/pallas_call | solution.py:254
  91.5 2.1 %collective-permute-start.20 = (bf16[6,224,128]{2,1,0:T(8,128)(2,1)S(1)}, bf16[6,224,128]{2,1,0:T(8,128)(2,1)S(1)}, u32[]{:S(2)}, u32[]{:S(2)}) collective-permute-start(bf16[6,224,128]{2,1,0:T(8,128)(2,1)S(1)} %get-tuple-element.81), channel_id=1, source_target_pairs={{0,3},{1,0},{2,1},{3,2},{4,7},{5,4},{6,5},{7,6},{8,11},{9,8},{10,9... | collective-permute-start | bytes 1032200 | tf_op jit(solution)/shard_map/ppermute | solution.py:395
  93.7 10.4 %attention.3 = (bf16[384,1024]{1,0:T(8,128)(2,1)}, bf16[384,1024]{1,0:T(8,128)(2,1)S(1)}, bf16[6,224,128]{2,1,0:T(8,128)(2,1)S(1)}, bf16[6,224,128]{2,1,0:T(8,12...) custom-call(bf16[2,6,16,1024]{3,2,1,0:T(8,128)(2,1)S(1)} %get-tuple-, ...), custom_call_target="tpu_custom_call", output_to_operand_aliasing={{0}: (9, {}), {1}: (10, {})} | custom-call | flops 6600000000 | bytes 9500000 | tf_op jit(solution)/shard_map/attention/pallas_call | solution.py:254
  104.9 4.3 %collective-permute-start.22 = (bf16[6,224,128]{2,1,0:T(8,128)(2,1)S(1)}, bf16[6,224,128]{2,1,0:T(8,128)(2,1)S(1)}, u32[]{:S(2)}, u32[]{:S(2)}) collective-permute-start(bf16[6,224,128]{2,1,0:T(8,128)(2,1)S(1)} %get-tuple-element.84), channel_id=1, source_target_pairs={{0,2},{1,3},{2,0},{3,1},{4,6},{5,7},{6,4},{7,5},{8,10},{9,11},{10,... | collective-permute-start | bytes 1032200 | tf_op jit(solution)/shard_map/ppermute | solution.py:395
  110.7 10.4 %collective-permute-start.24 = (bf16[6,224,128]{2,1,0:T(8,128)(2,1)S(1)}, bf16[6,224,128]{2,1,0:T(8,128)(2,1)S(1)}, u32[]{:S(2)}, u32[]{:S(2)}) collective-permute-start(bf16[6,224,128]{2,1,0:T(8,128)(2,1)S(1)} %sum_parts.2.refs_0_), channel_id=1, source_target_pairs={{0,4},{4,0},{8,12},{12,8},{16,20},{20,16},{24,28},{28,24},{32,36},... | collective-permute-start | bytes 1032200 | tf_op jit(solution)/shard_map/ppermute | solution.py:373
  122.4 6.6 %collective-permute-start.25 = (bf16[6,224,128]{2,1,0:T(8,128)(2,1)S(1)}, bf16[6,224,128]{2,1,0:T(8,128)(2,1)S(1)}, u32[]{:S(2)}, u32[]{:S(2)}) collective-permute-start(bf16[6,224,128]{2,1,0:T(8,128)(2,1)S(1)} %sum_parts.3.refs_1_), channel_id=1, source_target_pairs={{0,4},{4,0},{8,12},{12,8},{16,20},{20,16},{24,28},{28,24},{32,36},... | collective-permute-start | bytes 1032200 | tf_op jit(solution)/shard_map/ppermute | solution.py:373
  132.0 4.4 %collective-permute-start.26 = (bf16[4,224,128]{2,1,0:T(8,128)(2,1)S(1)}, bf16[4,224,128]{2,1,0:T(8,128)(2,1)S(1)}, u32[]{:S(2)}, u32[]{:S(2)}) collective-permute-start(bf16[4,224,128]{2,1,0:T(8,128)(2,1)S(1)} %get-tuple-element.86), channel_id=1, source_target_pairs={{0,24},{4,28},{8,32},{12,36},{16,40},{20,44},{24,48},{28,52},{32,5... | collective-permute-start | bytes 688136 | tf_op jit(solution)/shard_map/ppermute | solution.py:377
  137.4 4.1 %collective-permute-start.29 = (bf16[4,224,128]{2,1,0:T(8,128)(2,1)S(1)}, bf16[4,224,128]{2,1,0:T(8,128)(2,1)S(1)}, u32[]{:S(2)}, u32[]{:S(2)}) collective-permute-start(bf16[4,224,128]{2,1,0:T(8,128)(2,1)S(1)} %get-tuple-element.92), channel_id=1, source_target_pairs={{0,32},{4,36},{8,40},{12,44},{16,48},{20,52},{24,56},{28,60},{32,0... | collective-permute-start | bytes 688136 | tf_op jit(solution)/shard_map/ppermute | solution.py:377
  141.5 9.4 %collective-permute-done.26.refs_3_ = bf16[4,224,128]{2,1,0:T(8,128)(2,1)S(1)} collective-permute-done((bf16[4,224,128]{2,1,0:T(8,128)(2,1)S(1)}, bf16[4,224,128]{2,1,0:T(8,128)(2,1)S(1)}, u32[]{:S(2)}, u32[]{:S(2)}) %collective-permute-start.26) | collective-permute-done | bytes 229408 | tf_op jit(solution)/shard_map/ppermute | solution.py:377
  150.9 9.1 %collective-permute-start.27 = (bf16[4,224,128]{2,1,0:T(8,128)(2,1)S(1)}, bf16[4,224,128]{2,1,0:T(8,128)(2,1)S(1)}, u32[]{:S(2)}, u32[]{:S(2)}) collective-permute-start(bf16[4,224,128]{2,1,0:T(8,128)(2,1)S(1)} %get-tuple-element.90), channel_id=1, source_target_pairs={{0,8},{4,12},{8,16},{12,20},{16,24},{20,28},{24,32},{28,36},{32,40... | collective-permute-start | bytes 688136 | tf_op jit(solution)/shard_map/ppermute | solution.py:377
  160.9 7.0 %collective-permute-done.29.refs_4_ = bf16[4,224,128]{2,1,0:T(8,128)(2,1)S(1)} collective-permute-done((bf16[4,224,128]{2,1,0:T(8,128)(2,1)S(1)}, bf16[4,224,128]{2,1,0:T(8,128)(2,1)S(1)}, u32[]{:S(2)}, u32[]{:S(2)}) %collective-permute-start.29) | collective-permute-done | bytes 229408 | tf_op jit(solution)/shard_map/ppermute | solution.py:377
  167.9 4.6 %collective-permute-done.31.refs_6_ = bf16[4,224,128]{2,1,0:T(8,128)(2,1)S(1)} collective-permute-done((bf16[4,224,128]{2,1,0:T(8,128)(2,1)S(1)}, bf16[4,224,128]{2,1,0:T(8,128)(2,1)S(1)}, u32[]{:S(2)}, u32[]{:S(2)}) %collective-permute-start.31) | collective-permute-done | bytes 229408 | tf_op jit(solution)/shard_map/ppermute | solution.py:377
  172.5 2.5 %collective-permute-done.27.refs_1_ = bf16[4,224,128]{2,1,0:T(8,128)(2,1)S(1)} collective-permute-done((bf16[4,224,128]{2,1,0:T(8,128)(2,1)S(1)}, bf16[4,224,128]{2,1,0:T(8,128)(2,1)S(1)}, u32[]{:S(2)}, u32[]{:S(2)}) %collective-permute-start.27) | collective-permute-done | bytes 229408 | tf_op jit(solution)/shard_map/ppermute | solution.py:377
  175.0 2.9 %collective-permute-done.32.refs_7_ = bf16[4,224,128]{2,1,0:T(8,128)(2,1)S(1)} collective-permute-done((bf16[4,224,128]{2,1,0:T(8,128)(2,1)S(1)}, bf16[4,224,128]{2,1,0:T(8,128)(2,1)S(1)}, u32[]{:S(2)}, u32[]{:S(2)}) %collective-permute-start.32) | collective-permute-done | bytes 229408 | tf_op jit(solution)/shard_map/ppermute | solution.py:377
  178.0 2.2 %collect.1 = bf16[16,224,128]{2,1,0:T(8,128)(2,1)} custom-call(s32[16,2]{1,0:T(8,128)S(1)} %copy-done.2, bf16[4,224,128]{2,1,0:T(8,128)(2,1)S(1)} %get-tuple-element.88.refs_0_, bf16[4,224,128]{2,1,0:T(8,128)(2,1)S(1)} %collective-permute-done.27.refs_1_, bf16[4,224,128]{2,1,0:T(8,128)(2,1)S(1)} %collective-permute-done.28.refs_2_, ...), custom_call_target="tpu_custom_call" | custom-call | bytes 3000000 | tf_op jit(solution)/shard_map/collect/pallas_call | solution.py:360
  (72 shorter events, 27.7 us)
Async XLA Ops:
  2.8 5.6 %collective-permute-start.2 = (bf16[16,32,896]{2,1,0:T(8,128)(2,1)}, bf16[16,32,896]{2,1,0:T(8,128)(2,1)S(1)}, u32[]{:S(2)}, u32[]{:S(2)}) collective-permute-start(bf16[16,32,896]{2,1,0:T(8,128)(2,1)} %take_share.1.share_ref), channel_id=1, source_target_pairs={{0,4},{4,0},{8,12},{12,8},{16,20},{20,16},{24,28},{28,24},{32,36},... | collective-permute-start | bytes 2752520 | tf_op jit(solution)/shard_map/ppermute | solution.py:373
  6.2 2.0 %collective-permute-start = (s32[16,2]{1,0:T(8,128)S(1)}, s32[16,2]{1,0:T(8,128)S(1)}, u32[]{:S(2)}, u32[]{:S(2)}) collective-permute-start(s32[16,2]{1,0:T(8,128)S(1)} %copy.14.rows_ref), channel_id=1, source_target_pairs={{0,4},{4,0},{8,12},{12,8},{16,20},{20,16},{24,28},{28,24},{32,36},... | collective-permute-start | bytes 392 | tf_op jit(solution)/shard_map/ppermute | solution.py:373
  12.6 16.8 %collective-permute-start.3 = (bf16[4,32,896]{2,1,0:T(8,128)(2,1)}, bf16[4,32,896]{2,1,0:T(8,128)(2,1)S(1)}, u32[]{:S(2)}, u32[]{:S(2)}) collective-permute-start(bf16[4,32,896]{2,1,0:T(8,128)(2,1)} %get-tuple-element.53), channel_id=1, source_target_pairs={{0,24},{4,28},{8,32},{12,36},{16,40},{20,44},{24,48},{28,52},{32,5... | collective-permute-start | bytes 688136 | tf_op jit(solution)/shard_map/ppermute | solution.py:377
  15.2 18.0 %collective-permute-start.7 = (bf16[4,32,896]{2,1,0:T(8,128)(2,1)}, bf16[4,32,896]{2,1,0:T(8,128)(2,1)S(1)}, u32[]{:S(2)}, u32[]{:S(2)}) collective-permute-start(bf16[4,32,896]{2,1,0:T(8,128)(2,1)} %get-tuple-element.57), channel_id=1, source_target_pairs={{0,40},{4,44},{8,48},{12,52},{16,56},{20,60},{24,0},{28,4},{32,8},... | collective-permute-start | bytes 688136 | tf_op jit(solution)/shard_map/ppermute | solution.py:377
  17.4 24.0 %collective-permute-start.5 = (bf16[4,32,896]{2,1,0:T(8,128)(2,1)}, bf16[4,32,896]{2,1,0:T(8,128)(2,1)S(1)}, u32[]{:S(2)}, u32[]{:S(2)}) collective-permute-start(bf16[4,32,896]{2,1,0:T(8,128)(2,1)} %get-tuple-element.55), channel_id=1, source_target_pairs={{0,16},{4,20},{8,24},{12,28},{16,32},{20,36},{24,40},{28,44},{32,4... | collective-permute-start | bytes 688136 | tf_op jit(solution)/shard_map/ppermute | solution.py:377
  18.6 31.7 %collective-permute-start.6 = (bf16[4,32,896]{2,1,0:T(8,128)(2,1)}, bf16[4,32,896]{2,1,0:T(8,128)(2,1)S(1)}, u32[]{:S(2)}, u32[]{:S(2)}) collective-permute-start(bf16[4,32,896]{2,1,0:T(8,128)(2,1)} %get-tuple-element.56), channel_id=1, source_target_pairs={{0,32},{4,36},{8,40},{12,44},{16,48},{20,52},{24,56},{28,60},{32,0... | collective-permute-start | bytes 688136 | tf_op jit(solution)/shard_map/ppermute | solution.py:377
  23.5 29.8 %collective-permute-start.8 = (bf16[4,32,896]{2,1,0:T(8,128)(2,1)}, bf16[4,32,896]{2,1,0:T(8,128)(2,1)S(1)}, u32[]{:S(2)}, u32[]{:S(2)}) collective-permute-start(bf16[4,32,896]{2,1,0:T(8,128)(2,1)} %get-tuple-element.58), channel_id=1, source_target_pairs={{0,48},{4,52},{8,56},{12,60},{16,0},{20,4},{24,8},{28,12},{32,16},... | collective-permute-start | bytes 688136 | tf_op jit(solution)/shard_map/ppermute | solution.py:377
  29.5 27.4 %collective-permute-start.4 = (bf16[4,32,896]{2,1,0:T(8,128)(2,1)}, bf16[4,32,896]{2,1,0:T(8,128)(2,1)S(1)}, u32[]{:S(2)}, u32[]{:S(2)}) collective-permute-start(bf16[4,32,896]{2,1,0:T(8,128)(2,1)} %get-tuple-element.54), channel_id=1, source_target_pairs={{0,8},{4,12},{8,16},{12,20},{16,24},{20,28},{24,32},{28,36},{32,40... | collective-permute-start | bytes 688136 | tf_op jit(solution)/shard_map/ppermute | solution.py:377
  33.3 25.2 %collective-permute-start.9 = (bf16[4,32,896]{2,1,0:T(8,128)(2,1)}, bf16[4,32,896]{2,1,0:T(8,128)(2,1)S(1)}, u32[]{:S(2)}, u32[]{:S(2)}) collective-permute-start(bf16[4,32,896]{2,1,0:T(8,128)(2,1)} %get-tuple-element.60), channel_id=1, source_target_pairs={{0,56},{4,60},{8,0},{12,4},{16,8},{20,12},{24,16},{28,20},{32,24},... | collective-permute-start | bytes 688136 | tf_op jit(solution)/shard_map/ppermute | solution.py:377
  60.8 9.0 %collective-permute-start.11 = (bf16[2,6,16,896]{3,2,1,0:T(8,128)(2,1)S(1)}, bf16[2,6,16,896]{3,2,1,0:T(8,128)(2,1)S(1)}, u32[]{:S(2)}, u32[]{:S(2)}) collective-permute-start(bf16[2,6,16,896]{3,2,1,0:T(8,128)(2,1)S(1)} %get-tuple-element.61.refs_0_), channel_id=1, source_target_pairs={{0,3},{1,0},{2,1},{3,2},{4,7},{5,4},{6,5},{7,6},{8,11},{9,8},{10,9... | collective-permute-start | bytes 1032200 | tf_op jit(solution)/shard_map/ppermute | solution.py:395
  63.3 9.6 %collective-permute-start.10 = (bf16[2,6,16,896]{3,2,1,0:T(8,128)(2,1)S(1)}, bf16[2,6,16,896]{3,2,1,0:T(8,128)(2,1)S(1)}, u32[]{:S(2)}, u32[]{:S(2)}) collective-permute-start(bf16[2,6,16,896]{3,2,1,0:T(8,128)(2,1)S(1)} %get-tuple-element.61.refs_0_), channel_id=1, source_target_pairs={{0,1},{1,2},{2,3},{3,0},{4,5},{5,6},{6,7},{7,4},{8,9},{9,10},{10,1... | collective-permute-start | bytes 1032200 | tf_op jit(solution)/shard_map/ppermute | solution.py:395
  72.9 7.3 %collective-permute-start.15 = (bf16[6,16,896]{2,1,0:T(8,128)(2,1)S(1)}, bf16[6,16,896]{2,1,0:T(8,128)(2,1)S(1)}, u32[]{:S(2)}, u32[]{:S(2)}) collective-permute-start(bf16[6,16,896]{2,1,0:T(8,128)(2,1)S(1)} %slice_bitcast_fusion.1), channel_id=1, source_target_pairs={{0,1},{1,2},{2,3},{3,0},{4,5},{5,6},{6,7},{7,4},{8,9},{9,10},{10,1... | collective-permute-start | bytes 516104 | tf_op jit(solution)/shard_map/ppermute | solution.py:395
  73.0 7.2 %collective-permute-start.16 = (bf16[6,16,896]{2,1,0:T(8,128)(2,1)S(1)}, bf16[6,16,896]{2,1,0:T(8,128)(2,1)S(1)}, u32[]{:S(2)}, u32[]{:S(2)}) collective-permute-start(bf16[6,16,896]{2,1,0:T(8,128)(2,1)S(1)} %slice_bitcast_fusion), channel_id=1, source_target_pairs={{0,3},{1,0},{2,1},{3,2},{4,7},{5,4},{6,5},{7,6},{8,11},{9,8},{10,9... | collective-permute-start | bytes 516104 | tf_op jit(solution)/shard_map/ppermute | solution.py:395
  75.7 15.8 %collective-permute-start.14 = (bf16[2,6,16,896]{3,2,1,0:T(8,128)(2,1)S(1)}, bf16[2,6,16,896]{3,2,1,0:T(8,128)(2,1)S(1)}, u32[]{:S(2)}, u32[]{:S(2)}) collective-permute-start(bf16[2,6,16,896]{3,2,1,0:T(8,128)(2,1)S(1)} %get-tuple-element.65.refs_1_), channel_id=1, source_target_pairs={{0,1},{1,2},{2,3},{3,0},{4,5},{5,6},{6,7},{7,4},{8,9},{9,10},{10,1... | collective-permute-start | bytes 1032200 | tf_op jit(solution)/shard_map/ppermute | solution.py:395
  75.7 17.9 %collective-permute-start.13 = (bf16[2,6,16,896]{3,2,1,0:T(8,128)(2,1)S(1)}, bf16[2,6,16,896]{3,2,1,0:T(8,128)(2,1)S(1)}, u32[]{:S(2)}, u32[]{:S(2)}) collective-permute-start(bf16[2,6,16,896]{3,2,1,0:T(8,128)(2,1)S(1)} %get-tuple-element.65.refs_1_), channel_id=1, source_target_pairs={{0,2},{1,3},{2,0},{3,1},{4,6},{5,7},{6,4},{7,5},{8,10},{9,11},{10,... | collective-permute-start | bytes 1032200 | tf_op jit(solution)/shard_map/ppermute | solution.py:395
  76.9 16.9 %collective-permute-start.12 = (bf16[2,6,16,896]{3,2,1,0:T(8,128)(2,1)S(1)}, bf16[2,6,16,896]{3,2,1,0:T(8,128)(2,1)S(1)}, u32[]{:S(2)}, u32[]{:S(2)}) collective-permute-start(bf16[2,6,16,896]{3,2,1,0:T(8,128)(2,1)S(1)} %get-tuple-element.65.refs_1_), channel_id=1, source_target_pairs={{0,3},{1,0},{2,1},{3,2},{4,7},{5,4},{6,5},{7,6},{8,11},{9,8},{10,9... | collective-permute-start | bytes 1032200 | tf_op jit(solution)/shard_map/ppermute | solution.py:395
  89.1 20.1 %collective-permute-start.18 = (bf16[6,224,128]{2,1,0:T(8,128)(2,1)S(1)}, bf16[6,224,128]{2,1,0:T(8,128)(2,1)S(1)}, u32[]{:S(2)}, u32[]{:S(2)}) collective-permute-start(bf16[6,224,128]{2,1,0:T(8,128)(2,1)S(1)} %get-tuple-element.79), channel_id=1, source_target_pairs={{0,1},{1,2},{2,3},{3,0},{4,5},{5,6},{6,7},{7,4},{8,9},{9,10},{10,1... | collective-permute-start | bytes 1032200 | tf_op jit(solution)/shard_map/ppermute | solution.py:395
  89.7 19.5 %collective-permute-start.19 = (bf16[6,224,128]{2,1,0:T(8,128)(2,1)S(1)}, bf16[6,224,128]{2,1,0:T(8,128)(2,1)S(1)}, u32[]{:S(2)}, u32[]{:S(2)}) collective-permute-start(bf16[6,224,128]{2,1,0:T(8,128)(2,1)S(1)} %get-tuple-element.80), channel_id=1, source_target_pairs={{0,2},{1,3},{2,0},{3,1},{4,6},{5,7},{6,4},{7,5},{8,10},{9,11},{10,... | collective-permute-start | bytes 1032200 | tf_op jit(solution)/shard_map/ppermute | solution.py:395
  91.5 19.0 %collective-permute-start.20 = (bf16[6,224,128]{2,1,0:T(8,128)(2,1)S(1)}, bf16[6,224,128]{2,1,0:T(8,128)(2,1)S(1)}, u32[]{:S(2)}, u32[]{:S(2)}) collective-permute-start(bf16[6,224,128]{2,1,0:T(8,128)(2,1)S(1)} %get-tuple-element.81), channel_id=1, source_target_pairs={{0,3},{1,0},{2,1},{3,2},{4,7},{5,4},{6,5},{7,6},{8,11},{9,8},{10,9... | collective-permute-start | bytes 1032200 | tf_op jit(solution)/shard_map/ppermute | solution.py:395
  104.1 17.1 %collective-permute-start.21 = (bf16[6,224,128]{2,1,0:T(8,128)(2,1)S(1)}, bf16[6,224,128]{2,1,0:T(8,128)(2,1)S(1)}, u32[]{:S(2)}, u32[]{:S(2)}) collective-permute-start(bf16[6,224,128]{2,1,0:T(8,128)(2,1)S(1)} %get-tuple-element.83), channel_id=1, source_target_pairs={{0,1},{1,2},{2,3},{3,0},{4,5},{5,6},{6,7},{7,4},{8,9},{9,10},{10,1... | collective-permute-start | bytes 1032200 | tf_op jit(solution)/shard_map/ppermute | solution.py:395
  104.9 17.3 %collective-permute-start.22 = (bf16[6,224,128]{2,1,0:T(8,128)(2,1)S(1)}, bf16[6,224,128]{2,1,0:T(8,128)(2,1)S(1)}, u32[]{:S(2)}, u32[]{:S(2)}) collective-permute-start(bf16[6,224,128]{2,1,0:T(8,128)(2,1)S(1)} %get-tuple-element.84), channel_id=1, source_target_pairs={{0,2},{1,3},{2,0},{3,1},{4,6},{5,7},{6,4},{7,5},{8,10},{9,11},{10,... | collective-permute-start | bytes 1032200 | tf_op jit(solution)/shard_map/ppermute | solution.py:395
  109.2 13.0 %collective-permute-start.23 = (bf16[6,224,128]{2,1,0:T(8,128)(2,1)S(1)}, bf16[6,224,128]{2,1,0:T(8,128)(2,1)S(1)}, u32[]{:S(2)}, u32[]{:S(2)}) collective-permute-start(bf16[6,224,128]{2,1,0:T(8,128)(2,1)S(1)} %get-tuple-element.85), channel_id=1, source_target_pairs={{0,3},{1,0},{2,1},{3,2},{4,7},{5,4},{6,5},{7,6},{8,11},{9,8},{10,9... | collective-permute-start | bytes 1032200 | tf_op jit(solution)/shard_map/ppermute | solution.py:395
  109.2 50.8 %collective-permute-start.17 = (bf16[384,1024]{1,0:T(8,128)(2,1)S(1)}, bf16[384,1024]{1,0:T(8,128)(2,1)S(1)}, u32[]{:S(2)}, u32[]{:S(2)}) collective-permute-start(bf16[384,1024]{1,0:T(8,128)(2,1)S(1)} %get-tuple-element.77), channel_id=1, source_target_pairs={{64,0},{128,64},{192,128},{65,1},{129,65},{193,129},{66,2},{130,66... | collective-permute-start | bytes 2359304 | tf_op jit(solution)/shard_map/ppermute | solution.py:400
  110.7 18.2 %collective-permute-start.24 = (bf16[6,224,128]{2,1,0:T(8,128)(2,1)S(1)}, bf16[6,224,128]{2,1,0:T(8,128)(2,1)S(1)}, u32[]{:S(2)}, u32[]{:S(2)}) collective-permute-start(bf16[6,224,128]{2,1,0:T(8,128)(2,1)S(1)} %sum_parts.2.refs_0_), channel_id=1, source_target_pairs={{0,4},{4,0},{8,12},{12,8},{16,20},{20,16},{24,28},{28,24},{32,36},... | collective-permute-start | bytes 1032200 | tf_op jit(solution)/shard_map/ppermute | solution.py:373
  122.4 7.9 %collective-permute-start.25 = (bf16[6,224,128]{2,1,0:T(8,128)(2,1)S(1)}, bf16[6,224,128]{2,1,0:T(8,128)(2,1)S(1)}, u32[]{:S(2)}, u32[]{:S(2)}) collective-permute-start(bf16[6,224,128]{2,1,0:T(8,128)(2,1)S(1)} %sum_parts.3.refs_1_), channel_id=1, source_target_pairs={{0,4},{4,0},{8,12},{12,8},{16,20},{20,16},{24,28},{28,24},{32,36},... | collective-permute-start | bytes 1032200 | tf_op jit(solution)/shard_map/ppermute | solution.py:373
  132.0 18.9 %collective-permute-start.26 = (bf16[4,224,128]{2,1,0:T(8,128)(2,1)S(1)}, bf16[4,224,128]{2,1,0:T(8,128)(2,1)S(1)}, u32[]{:S(2)}, u32[]{:S(2)}) collective-permute-start(bf16[4,224,128]{2,1,0:T(8,128)(2,1)S(1)} %get-tuple-element.86), channel_id=1, source_target_pairs={{0,24},{4,28},{8,32},{12,36},{16,40},{20,44},{24,48},{28,52},{32,5... | collective-permute-start | bytes 688136 | tf_op jit(solution)/shard_map/ppermute | solution.py:377
  136.4 14.5 %collective-permute-start.30 = (bf16[4,224,128]{2,1,0:T(8,128)(2,1)S(1)}, bf16[4,224,128]{2,1,0:T(8,128)(2,1)S(1)}, u32[]{:S(2)}, u32[]{:S(2)}) collective-permute-start(bf16[4,224,128]{2,1,0:T(8,128)(2,1)S(1)} %get-tuple-element.93), channel_id=1, source_target_pairs={{0,40},{4,44},{8,48},{12,52},{16,56},{20,60},{24,0},{28,4},{32,8},... | collective-permute-start | bytes 688136 | tf_op jit(solution)/shard_map/ppermute | solution.py:377
  136.6 24.3 %collective-permute-start.28 = (bf16[4,224,128]{2,1,0:T(8,128)(2,1)S(1)}, bf16[4,224,128]{2,1,0:T(8,128)(2,1)S(1)}, u32[]{:S(2)}, u32[]{:S(2)}) collective-permute-start(bf16[4,224,128]{2,1,0:T(8,128)(2,1)S(1)} %get-tuple-element.91), channel_id=1, source_target_pairs={{0,16},{4,20},{8,24},{12,28},{16,32},{20,36},{24,40},{28,44},{32,4... | collective-permute-start | bytes 688136 | tf_op jit(solution)/shard_map/ppermute | solution.py:377
  137.4 30.5 %collective-permute-start.29 = (bf16[4,224,128]{2,1,0:T(8,128)(2,1)S(1)}, bf16[4,224,128]{2,1,0:T(8,128)(2,1)S(1)}, u32[]{:S(2)}, u32[]{:S(2)}) collective-permute-start(bf16[4,224,128]{2,1,0:T(8,128)(2,1)S(1)} %get-tuple-element.92), channel_id=1, source_target_pairs={{0,32},{4,36},{8,40},{12,44},{16,48},{20,52},{24,56},{28,60},{32,0... | collective-permute-start | bytes 688136 | tf_op jit(solution)/shard_map/ppermute | solution.py:377
  150.9 21.6 %collective-permute-start.31 = (bf16[4,224,128]{2,1,0:T(8,128)(2,1)S(1)}, bf16[4,224,128]{2,1,0:T(8,128)(2,1)S(1)}, u32[]{:S(2)}, u32[]{:S(2)}) collective-permute-start(bf16[4,224,128]{2,1,0:T(8,128)(2,1)S(1)} %get-tuple-element.94), channel_id=1, source_target_pairs={{0,48},{4,52},{8,56},{12,60},{16,0},{20,4},{24,8},{28,12},{32,16},... | collective-permute-start | bytes 688136 | tf_op jit(solution)/shard_map/ppermute | solution.py:377
  150.9 24.1 %collective-permute-start.27 = (bf16[4,224,128]{2,1,0:T(8,128)(2,1)S(1)}, bf16[4,224,128]{2,1,0:T(8,128)(2,1)S(1)}, u32[]{:S(2)}, u32[]{:S(2)}) collective-permute-start(bf16[4,224,128]{2,1,0:T(8,128)(2,1)S(1)} %get-tuple-element.90), channel_id=1, source_target_pairs={{0,8},{4,12},{8,16},{12,20},{16,24},{20,28},{24,32},{28,36},{32,40... | collective-permute-start | bytes 688136 | tf_op jit(solution)/shard_map/ppermute | solution.py:377
  160.0 18.0 %collective-permute-start.32 = (bf16[4,224,128]{2,1,0:T(8,128)(2,1)S(1)}, bf16[4,224,128]{2,1,0:T(8,128)(2,1)S(1)}, u32[]{:S(2)}, u32[]{:S(2)}) collective-permute-start(bf16[4,224,128]{2,1,0:T(8,128)(2,1)S(1)} %get-tuple-element.96), channel_id=1, source_target_pairs={{0,56},{4,60},{8,0},{12,4},{16,8},{20,12},{24,16},{28,20},{32,24},... | collective-permute-start | bytes 688136 | tf_op jit(solution)/shard_map/ppermute | solution.py:377
  (12 other events, 146.4 us)

commit v5 on v4

--- a/solution.py
+++ b/solution.py
@@ -431,7 +431,7 @@
     picked = pick(sources, arrived)
     low, high = turn(picked[0], 1), turn(picked[0], -1)
     own_first, own_second = project(picked, kw, vw)
-    across = [turn(after(low, *own_first)[0], 1), turn(after(high, *own_first)[1], -1)]
+    across = [turn(low[0], 1), turn(after(high, *own_first)[1], -1)]
     own = after(picked[1], low, high)
     others = [turn(own, -shift) for shift in range(1, N_TP)]
     next_first, last_first = project([high, low], kw, vw)

time: 180 us -> 177 us (0.983)
  waiting for transfers between devices: 65.5 us -> 61.1 us
    ppermute x14, waiting for transfers between devices: 55.3 us -> 52.9 us  [ahead(): lax.ppermute(x, 'seq', [(i, (i + 2 * by) % N_SEQ) for i in range(N_SEQ)])]
    ppermute x13, waiting for transfers between devices: 7.4 us -> 5.29 us  [turn(): return lax.ppermute(x, 'tp', [(i, (i + by) % N_TP) for i in range(N_TP)])]
  transfers between devices with their start and end apart: 33 -> 33, of which waited for: 18 -> 16; matrix products, arithmetic and copies ran while one was open for 0% -> 0% of each run, Pallas kernels for 14% -> 15%
where the time goes in v5:
time: 177 us; the launch traced here: 176 us
  starting transfers between devices  75.2 us (42%)
  waiting for transfers between devices  61.1 us (35%)
  Pallas kernels  34.5 us (19%)
  local copies, waits for them, and re-layouts  4.04 us (2%)
    ppermute x14, waiting for transfers between devices, ahead(): lax.ppermute(x, 'seq', [(i, (i + 2 * by) % N_SEQ) for i in range(N_SEQ)])  52.9 us
    ppermute x14, starting transfers between devices, ahead(): lax.ppermute(x, 'seq', [(i, (i + 2 * by) % N_SEQ) for i in range(N_SEQ)])  35.8 us
    ppermute x5, starting transfers between devices, swap(): return lax.ppermute(x, 'seq', [(i, i ^ 1) for i in range(N_SEQ)])  20.2 us
    pallas_call x2, Pallas kernels, attention(): pl.pallas_call(functools.partial(attention_kernel, [shift for shift, pair...  19.3 us
    ppermute x13, starting transfers between devices, turn(): return lax.ppermute(x, 'tp', [(i, (i + by) % N_TP) for i in range(N_TP)])  18 us
    ppermute x13, waiting for transfers between devices, turn(): return lax.ppermute(x, 'tp', [(i, (i + by) % N_TP) for i in range(N_TP)])  5.29 us
    unnamed x22, local copies, waits for them, and re-layouts  3.83 us
    pallas_call x2, Pallas kernels, project(): pl.pallas_call(functools.partial(project_kernel, len(pieces)), out_shape=...  3.67 us
  transfers between devices with their start and end apart: 33, of which 16 were waited for; matrix products, arithmetic and copies ran while one was open for 0% of the time, Pallas kernels for 15%

profile of v5, /device:TPU:1, one launch (start us, length us, event | category | flops | bytes accessed | tf_op | source)
XLA Modules:
  0.0 175.7 jit_solution(439895788692292760)
XLA Ops:
  0.7 2.1 %take_share.1.share_ref = bf16[16,32,896]{2,1,0:T(8,128)(2,1)} custom-call(bf16[16,128,896]{2,1,0:T(8,128)(2,1)} %bitcast.28), custom_call_target="tpu_custom_call" | custom-call | bytes 2000000 | tf_op jit(solution)/shard_map/take_share/pallas_call | solution.py:75
  2.8 3.3 %collective-permute-start.2 = (bf16[16,32,896]{2,1,0:T(8,128)(2,1)}, bf16[16,32,896]{2,1,0:T(8,128)(2,1)S(1)}, u32[]{:S(2)}, u32[]{:S(2)}) collective-permute-start(bf16[16,32,896]{2,1,0:T(8,128)(2,1)} %take_share.1.share_ref), channel_id=1, source_target_pairs={{0,4},{4,0},{8,12},{12,8},{16,20},{20,16},{24,28},{28,24},{32,36},... | collective-permute-start | bytes 2752520 | tf_op jit(solution)/shard_map/ppermute | solution.py:373
  9.8 2.9 %pack_rows.1 = (bf16[4,32,896]{2,1,0:T(8,128)(2,1)}, bf16[4,32,896]{2,1,0:T(8,128)(2,1)}, bf16[4,32,896]{2,1,0:T(8,128)(2,1)}, bf16[4,32,896]{2,1,0:T(8,128)(2,1...) custom-call(s32[16,2]{1,0:T(8,128)} %copy-done.1, ...), custom_call_target="tpu_custom_call" | custom-call | bytes 3000000 | tf_op jit(solution)/shard_map/pack_rows/pallas_call | solution.py:100
  12.6 2.6 %collective-permute-start.3 = (bf16[4,32,896]{2,1,0:T(8,128)(2,1)}, bf16[4,32,896]{2,1,0:T(8,128)(2,1)S(1)}, u32[]{:S(2)}, u32[]{:S(2)}) collective-permute-start(bf16[4,32,896]{2,1,0:T(8,128)(2,1)} %get-tuple-element.52), channel_id=1, source_target_pairs={{0,24},{4,28},{8,32},{12,36},{16,40},{20,44},{24,48},{28,52},{32,5... | collective-permute-start | bytes 688136 | tf_op jit(solution)/shard_map/ppermute | solution.py:377
  15.2 2.2 %collective-permute-start.7 = (bf16[4,32,896]{2,1,0:T(8,128)(2,1)}, bf16[4,32,896]{2,1,0:T(8,128)(2,1)S(1)}, u32[]{:S(2)}, u32[]{:S(2)}) collective-permute-start(bf16[4,32,896]{2,1,0:T(8,128)(2,1)} %get-tuple-element.56), channel_id=1, source_target_pairs={{0,40},{4,44},{8,48},{12,52},{16,56},{20,60},{24,0},{28,4},{32,8},... | collective-permute-start | bytes 688136 | tf_op jit(solution)/shard_map/ppermute | solution.py:377
  18.6 4.9 %collective-permute-start.6 = (bf16[4,32,896]{2,1,0:T(8,128)(2,1)}, bf16[4,32,896]{2,1,0:T(8,128)(2,1)S(1)}, u32[]{:S(2)}, u32[]{:S(2)}) collective-permute-start(bf16[4,32,896]{2,1,0:T(8,128)(2,1)} %get-tuple-element.55), channel_id=1, source_target_pairs={{0,32},{4,36},{8,40},{12,44},{16,48},{20,52},{24,56},{28,60},{32,0... | collective-permute-start | bytes 688136 | tf_op jit(solution)/shard_map/ppermute | solution.py:377
  23.5 2.4 %collective-permute-start.8 = (bf16[4,32,896]{2,1,0:T(8,128)(2,1)}, bf16[4,32,896]{2,1,0:T(8,128)(2,1)S(1)}, u32[]{:S(2)}, u32[]{:S(2)}) collective-permute-start(bf16[4,32,896]{2,1,0:T(8,128)(2,1)} %get-tuple-element.57), channel_id=1, source_target_pairs={{0,48},{4,52},{8,56},{12,60},{16,0},{20,4},{24,8},{28,12},{32,16},... | collective-permute-start | bytes 688136 | tf_op jit(solution)/shard_map/ppermute | solution.py:377
  25.9 3.6 %collective-permute-done.3.refs_3_ = bf16[4,32,896]{2,1,0:T(8,128)(2,1)S(1)} collective-permute-done((bf16[4,32,896]{2,1,0:T(8,128)(2,1)}, bf16[4,32,896]{2,1,0:T(8,128)(2,1)S(1)}, u32[]{:S(2)}, u32[]{:S(2)}) %collective-permute-start.3) | collective-permute-done | bytes 229408 | tf_op jit(solution)/shard_map/ppermute | solution.py:377
  29.5 3.8 %collective-permute-start.4 = (bf16[4,32,896]{2,1,0:T(8,128)(2,1)}, bf16[4,32,896]{2,1,0:T(8,128)(2,1)S(1)}, u32[]{:S(2)}, u32[]{:S(2)}) collective-permute-start(bf16[4,32,896]{2,1,0:T(8,128)(2,1)} %get-tuple-element.53), channel_id=1, source_target_pairs={{0,8},{4,12},{8,16},{12,20},{16,24},{20,28},{24,32},{28,36},{32,40... | collective-permute-start | bytes 688136 | tf_op jit(solution)/shard_map/ppermute | solution.py:377
  33.3 8.1 %collective-permute-done.5.refs_2_ = bf16[4,32,896]{2,1,0:T(8,128)(2,1)S(1)} collective-permute-done((bf16[4,32,896]{2,1,0:T(8,128)(2,1)}, bf16[4,32,896]{2,1,0:T(8,128)(2,1)S(1)}, u32[]{:S(2)}, u32[]{:S(2)}) %collective-permute-start.5) | collective-permute-done | bytes 229408 | tf_op jit(solution)/shard_map/ppermute | solution.py:377
  41.4 8.9 %collective-permute-done.6.refs_4_ = bf16[4,32,896]{2,1,0:T(8,128)(2,1)S(1)} collective-permute-done((bf16[4,32,896]{2,1,0:T(8,128)(2,1)}, bf16[4,32,896]{2,1,0:T(8,128)(2,1)S(1)}, u32[]{:S(2)}, u32[]{:S(2)}) %collective-permute-start.6) | collective-permute-done | bytes 229408 | tf_op jit(solution)/shard_map/ppermute | solution.py:377
  50.3 2.9 %collective-permute-done.8.refs_6_ = bf16[4,32,896]{2,1,0:T(8,128)(2,1)S(1)} collective-permute-done((bf16[4,32,896]{2,1,0:T(8,128)(2,1)}, bf16[4,32,896]{2,1,0:T(8,128)(2,1)S(1)}, u32[]{:S(2)}, u32[]{:S(2)}) %collective-permute-start.8) | collective-permute-done | bytes 229408 | tf_op jit(solution)/shard_map/ppermute | solution.py:377
  53.3 3.6 %collective-permute-done.4.refs_1_ = bf16[4,32,896]{2,1,0:T(8,128)(2,1)S(1)} collective-permute-done((bf16[4,32,896]{2,1,0:T(8,128)(2,1)}, bf16[4,32,896]{2,1,0:T(8,128)(2,1)S(1)}, u32[]{:S(2)}, u32[]{:S(2)}) %collective-permute-start.4) | collective-permute-done | bytes 229408 | tf_op jit(solution)/shard_map/ppermute | solution.py:377
  65.0 1.8 %project.2 = (bf16[2,6,16,1024]{3,2,1,0:T(8,128)(2,1)S(1)}, bf16[2,6,16,1024]{3,2,1,0:T(8,128)(2,1)S(1)}, bf16[2,6,16,1024]{3,2,1,0:T(8,128)(2,1)S(1)}, bf16[2,6,16,1024]{3,2,1,0:T(8,128)(2,1)S(1)}) custom-call(bf16[2,6,16,896]{3,2,1,0:T(8,128)(2,1)S(1)} %get-tuple-element.60.refs_0_, bf16[2,6,16,896]{3,2,1,0:T(8,128)(2,1)S(1)} %get-tuple-element.64.refs_1_, ...), custom_call_target="tpu_custom_call" | custom-call | flops 1500000000 | bytes 6000000 | tf_op jit(solution)/shard_map/project/pallas_call | solution.py:175
  66.9 3.8 %collective-permute-done.10.refs_1_ = bf16[2,6,16,896]{3,2,1,0:T(8,128)(2,1)S(1)} collective-permute-done((bf16[2,6,16,896]{3,2,1,0:T(8,128)(2,1)S(1)}, bf16[2,6,16,896]{3,2,1,0:T(8,128)(2,1)S(1)}, u32[]{:S(2)}, u32[]{:S(2)}) %collective-permute-start.10) | collective-permute-done | bytes 344096 | tf_op jit(solution)/shard_map/ppermute | solution.py:395
  70.9 2.9 %collective-permute-start.16 = (bf16[6,16,896]{2,1,0:T(8,128)(2,1)S(1)}, bf16[6,16,896]{2,1,0:T(8,128)(2,1)S(1)}, u32[]{:S(2)}, u32[]{:S(2)}) collective-permute-start(bf16[6,16,896]{2,1,0:T(8,128)(2,1)S(1)} %slice_bitcast_fusion.1), channel_id=1, source_target_pairs={{0,3},{1,0},{2,1},{3,2},{4,7},{5,4},{6,5},{7,6},{8,11},{9,8},{10,9... | collective-permute-start | bytes 516104 | tf_op jit(solution)/shard_map/ppermute | solution.py:395
  76.5 1.8 %project.3 = (bf16[2,6,16,1024]{3,2,1,0:T(8,128)(2,1)S(1)}, bf16[2,6,16,1024]{3,2,1,0:T(8,128)(2,1)S(1)}, bf16[2,6,16,1024]{3,2,1,0:T(8,128)(2,1)S(1)}, bf16[2,6,16,1024]{3,2,1,0:T(8,128)(2,1)S(1)}) custom-call(bf16[2,6,16,896]{3,2,1,0:T(8,128)(2,1)S(1)} %collective-permute-done.11.refs_0_, bf16[2,6,16,896]{3,2,1,0:T(8,128)(2,1)S(1)} %collective-permute-done.10.refs_1_, ...), custom_call_target="tpu_custom_call" | custom-call | flops 1500000000 | bytes 6000000 | tf_op jit(solution)/shard_map/project/pallas_call | solution.py:175
  78.3 8.9 %attention.2 = (bf16[384,1024]{1,0:T(8,128)(2,1)}, bf16[384,1024]{1,0:T(8,128)(2,1)S(1)}, bf16[6,224,128]{2,1,0:T(8,128)(2,1)S(1)}, bf16[6,224,128]{2,1,0:T(8,12...) custom-call(bf16[2,6,16,1024]{3,2,1,0:T(8,128)(2,1)S(1)} %get-tuple-element.65.refs_0_, ...), custom_call_target="tpu_custom_call" | custom-call | flops 6600000000 | bytes 9500000 | tf_op jit(solution)/shard_map/attention/pallas_call | solution.py:254
  89.6 2.1 %collective-permute-start.20 = (bf16[6,224,128]{2,1,0:T(8,128)(2,1)S(1)}, bf16[6,224,128]{2,1,0:T(8,128)(2,1)S(1)}, u32[]{:S(2)}, u32[]{:S(2)}) collective-permute-start(bf16[6,224,128]{2,1,0:T(8,128)(2,1)S(1)} %get-tuple-element.79), channel_id=1, source_target_pairs={{0,3},{1,0},{2,1},{3,2},{4,7},{5,4},{6,5},{7,6},{8,11},{9,8},{10,9... | collective-permute-start | bytes 1032200 | tf_op jit(solution)/shard_map/ppermute | solution.py:395
  92.2 10.4 %attention.3 = (bf16[384,1024]{1,0:T(8,128)(2,1)}, bf16[384,1024]{1,0:T(8,128)(2,1)S(1)}, bf16[6,224,128]{2,1,0:T(8,128)(2,1)S(1)}, bf16[6,224,128]{2,1,0:T(8,12...) custom-call(bf16[2,6,16,1024]{3,2,1,0:T(8,128)(2,1)S(1)} %get-tuple-, ...), custom_call_target="tpu_custom_call", output_to_operand_aliasing={{0}: (9, {}), {1}: (10, {})} | custom-call | flops 6600000000 | bytes 9500000 | tf_op jit(solution)/shard_map/attention/pallas_call | solution.py:254
  103.8 3.9 %collective-permute-start.22 = (bf16[6,224,128]{2,1,0:T(8,128)(2,1)S(1)}, bf16[6,224,128]{2,1,0:T(8,128)(2,1)S(1)}, u32[]{:S(2)}, u32[]{:S(2)}) collective-permute-start(bf16[6,224,128]{2,1,0:T(8,128)(2,1)S(1)} %get-tuple-element.82), channel_id=1, source_target_pairs={{0,2},{1,3},{2,0},{3,1},{4,6},{5,7},{6,4},{7,5},{8,10},{9,11},{10,... | collective-permute-start | bytes 1032200 | tf_op jit(solution)/shard_map/ppermute | solution.py:395
  109.2 9.6 %collective-permute-start.24 = (bf16[6,224,128]{2,1,0:T(8,128)(2,1)S(1)}, bf16[6,224,128]{2,1,0:T(8,128)(2,1)S(1)}, u32[]{:S(2)}, u32[]{:S(2)}) collective-permute-start(bf16[6,224,128]{2,1,0:T(8,128)(2,1)S(1)} %sum_parts.2.refs_0_), channel_id=1, source_target_pairs={{0,4},{4,0},{8,12},{12,8},{16,20},{20,16},{24,28},{28,24},{32,36},... | collective-permute-start | bytes 1032200 | tf_op jit(solution)/shard_map/ppermute | solution.py:373
  119.9 6.6 %collective-permute-start.25 = (bf16[6,224,128]{2,1,0:T(8,128)(2,1)S(1)}, bf16[6,224,128]{2,1,0:T(8,128)(2,1)S(1)}, u32[]{:S(2)}, u32[]{:S(2)}) collective-permute-start(bf16[6,224,128]{2,1,0:T(8,128)(2,1)S(1)} %sum_parts.3.refs_1_), channel_id=1, source_target_pairs={{0,4},{4,0},{8,12},{12,8},{16,20},{20,16},{24,28},{28,24},{32,36},... | collective-permute-start | bytes 1032200 | tf_op jit(solution)/shard_map/ppermute | solution.py:373
  127.9 1.8 %place.1 = (bf16[4,224,128]{2,1,0:T(8,128)(2,1)S(1)}, bf16[4,224,128]{2,1,0:T(8,128)(2,1)S(1)}, bf16[4,224,128]{2,1,0:T(8,128)(2,1)S(1)}, bf16[4,224,128]{2,1,0:...) custom-call(s32[6,2]{1,0:T(8,128)S(1)} %copy.15.neighbour_ref, ...), custom_call_target="tpu_custom_call" | custom-call | bytes 3000000 | tf_op jit(solution)/shard_map/place/pallas_call | solution.py:333
  129.7 4.5 %collective-permute-start.26 = (bf16[4,224,128]{2,1,0:T(8,128)(2,1)S(1)}, bf16[4,224,128]{2,1,0:T(8,128)(2,1)S(1)}, u32[]{:S(2)}, u32[]{:S(2)}) collective-permute-start(bf16[4,224,128]{2,1,0:T(8,128)(2,1)S(1)} %get-tuple-element.84), channel_id=1, source_target_pairs={{0,24},{4,28},{8,32},{12,36},{16,40},{20,44},{24,48},{28,52},{32,5... | collective-permute-start | bytes 688136 | tf_op jit(solution)/shard_map/ppermute | solution.py:377
  135.4 3.5 %collective-permute-start.29 = (bf16[4,224,128]{2,1,0:T(8,128)(2,1)S(1)}, bf16[4,224,128]{2,1,0:T(8,128)(2,1)S(1)}, u32[]{:S(2)}, u32[]{:S(2)}) collective-permute-start(bf16[4,224,128]{2,1,0:T(8,128)(2,1)S(1)} %get-tuple-element.90), channel_id=1, source_target_pairs={{0,32},{4,36},{8,40},{12,44},{16,48},{20,52},{24,56},{28,60},{32,0... | collective-permute-start | bytes 688136 | tf_op jit(solution)/shard_map/ppermute | solution.py:377
  138.9 9.7 %collective-permute-done.26.refs_3_ = bf16[4,224,128]{2,1,0:T(8,128)(2,1)S(1)} collective-permute-done((bf16[4,224,128]{2,1,0:T(8,128)(2,1)S(1)}, bf16[4,224,128]{2,1,0:T(8,128)(2,1)S(1)}, u32[]{:S(2)}, u32[]{:S(2)}) %collective-permute-start.26) | collective-permute-done | bytes 229408 | tf_op jit(solution)/shard_map/ppermute | solution.py:377
  148.5 9.5 %collective-permute-start.27 = (bf16[4,224,128]{2,1,0:T(8,128)(2,1)S(1)}, bf16[4,224,128]{2,1,0:T(8,128)(2,1)S(1)}, u32[]{:S(2)}, u32[]{:S(2)}) collective-permute-start(bf16[4,224,128]{2,1,0:T(8,128)(2,1)S(1)} %get-tuple-element.88), channel_id=1, source_target_pairs={{0,8},{4,12},{8,16},{12,20},{16,24},{20,28},{24,32},{28,36},{32,40... | collective-permute-start | bytes 688136 | tf_op jit(solution)/shard_map/ppermute | solution.py:377
  159.0 7.1 %collective-permute-done.29.refs_4_ = bf16[4,224,128]{2,1,0:T(8,128)(2,1)S(1)} collective-permute-done((bf16[4,224,128]{2,1,0:T(8,128)(2,1)S(1)}, bf16[4,224,128]{2,1,0:T(8,128)(2,1)S(1)}, u32[]{:S(2)}, u32[]{:S(2)}) %collective-permute-start.29) | collective-permute-done | bytes 229408 | tf_op jit(solution)/shard_map/ppermute | solution.py:377
  166.2 4.8 %collective-permute-done.31.refs_6_ = bf16[4,224,128]{2,1,0:T(8,128)(2,1)S(1)} collective-permute-done((bf16[4,224,128]{2,1,0:T(8,128)(2,1)S(1)}, bf16[4,224,128]{2,1,0:T(8,128)(2,1)S(1)}, u32[]{:S(2)}, u32[]{:S(2)}) %collective-permute-start.31) | collective-permute-done | bytes 229408 | tf_op jit(solution)/shard_map/ppermute | solution.py:377
  171.0 2.5 %collective-permute-done.27.refs_1_ = bf16[4,224,128]{2,1,0:T(8,128)(2,1)S(1)} collective-permute-done((bf16[4,224,128]{2,1,0:T(8,128)(2,1)S(1)}, bf16[4,224,128]{2,1,0:T(8,128)(2,1)S(1)}, u32[]{:S(2)}, u32[]{:S(2)}) %collective-permute-start.27) | collective-permute-done | bytes 229408 | tf_op jit(solution)/shard_map/ppermute | solution.py:377
  173.5 2.2 %collect.1 = bf16[16,224,128]{2,1,0:T(8,128)(2,1)} custom-call(s32[16,2]{1,0:T(8,128)S(1)} %copy-done.2, bf16[4,224,128]{2,1,0:T(8,128)(2,1)S(1)} %get-tuple-element.86.refs_0_, bf16[4,224,128]{2,1,0:T(8,128)(2,1)S(1)} %collective-permute-done.27.refs_1_, bf16[4,224,128]{2,1,0:T(8,128)(2,1)S(1)} %collective-permute-done.28.refs_2_, ...), custom_call_target="tpu_custom_call" | custom-call | bytes 3000000 | tf_op jit(solution)/shard_map/collect/pallas_call | solution.py:360
  (72 shorter events, 26.0 us)
Async XLA Ops:
  2.8 5.6 %collective-permute-start.2 = (bf16[16,32,896]{2,1,0:T(8,128)(2,1)}, bf16[16,32,896]{2,1,0:T(8,128)(2,1)S(1)}, u32[]{:S(2)}, u32[]{:S(2)}) collective-permute-start(bf16[16,32,896]{2,1,0:T(8,128)(2,1)} %take_share.1.share_ref), channel_id=1, source_target_pairs={{0,4},{4,0},{8,12},{12,8},{16,20},{20,16},{24,28},{28,24},{32,36},... | collective-permute-start | bytes 2752520 | tf_op jit(solution)/shard_map/ppermute | solution.py:373
  6.2 2.0 %collective-permute-start = (s32[16,2]{1,0:T(8,128)S(1)}, s32[16,2]{1,0:T(8,128)S(1)}, u32[]{:S(2)}, u32[]{:S(2)}) collective-permute-start(s32[16,2]{1,0:T(8,128)S(1)} %copy.14.rows_ref), channel_id=1, source_target_pairs={{0,4},{4,0},{8,12},{12,8},{16,20},{20,16},{24,28},{28,24},{32,36},... | collective-permute-start | bytes 392 | tf_op jit(solution)/shard_map/ppermute | solution.py:373
  12.6 16.8 %collective-permute-start.3 = (bf16[4,32,896]{2,1,0:T(8,128)(2,1)}, bf16[4,32,896]{2,1,0:T(8,128)(2,1)S(1)}, u32[]{:S(2)}, u32[]{:S(2)}) collective-permute-start(bf16[4,32,896]{2,1,0:T(8,128)(2,1)} %get-tuple-element.52), channel_id=1, source_target_pairs={{0,24},{4,28},{8,32},{12,36},{16,40},{20,44},{24,48},{28,52},{32,5... | collective-permute-start | bytes 688136 | tf_op jit(solution)/shard_map/ppermute | solution.py:377
  15.2 18.0 %collective-permute-start.7 = (bf16[4,32,896]{2,1,0:T(8,128)(2,1)}, bf16[4,32,896]{2,1,0:T(8,128)(2,1)S(1)}, u32[]{:S(2)}, u32[]{:S(2)}) collective-permute-start(bf16[4,32,896]{2,1,0:T(8,128)(2,1)} %get-tuple-element.56), channel_id=1, source_target_pairs={{0,40},{4,44},{8,48},{12,52},{16,56},{20,60},{24,0},{28,4},{32,8},... | collective-permute-start | bytes 688136 | tf_op jit(solution)/shard_map/ppermute | solution.py:377
  17.4 24.0 %collective-permute-start.5 = (bf16[4,32,896]{2,1,0:T(8,128)(2,1)}, bf16[4,32,896]{2,1,0:T(8,128)(2,1)S(1)}, u32[]{:S(2)}, u32[]{:S(2)}) collective-permute-start(bf16[4,32,896]{2,1,0:T(8,128)(2,1)} %get-tuple-element.54), channel_id=1, source_target_pairs={{0,16},{4,20},{8,24},{12,28},{16,32},{20,36},{24,40},{28,44},{32,4... | collective-permute-start | bytes 688136 | tf_op jit(solution)/shard_map/ppermute | solution.py:377
  18.6 31.7 %collective-permute-start.6 = (bf16[4,32,896]{2,1,0:T(8,128)(2,1)}, bf16[4,32,896]{2,1,0:T(8,128)(2,1)S(1)}, u32[]{:S(2)}, u32[]{:S(2)}) collective-permute-start(bf16[4,32,896]{2,1,0:T(8,128)(2,1)} %get-tuple-element.55), channel_id=1, source_target_pairs={{0,32},{4,36},{8,40},{12,44},{16,48},{20,52},{24,56},{28,60},{32,0... | collective-permute-start | bytes 688136 | tf_op jit(solution)/shard_map/ppermute | solution.py:377
  23.5 29.8 %collective-permute-start.8 = (bf16[4,32,896]{2,1,0:T(8,128)(2,1)}, bf16[4,32,896]{2,1,0:T(8,128)(2,1)S(1)}, u32[]{:S(2)}, u32[]{:S(2)}) collective-permute-start(bf16[4,32,896]{2,1,0:T(8,128)(2,1)} %get-tuple-element.57), channel_id=1, source_target_pairs={{0,48},{4,52},{8,56},{12,60},{16,0},{20,4},{24,8},{28,12},{32,16},... | collective-permute-start | bytes 688136 | tf_op jit(solution)/shard_map/ppermute | solution.py:377
  29.5 27.4 %collective-permute-start.4 = (bf16[4,32,896]{2,1,0:T(8,128)(2,1)}, bf16[4,32,896]{2,1,0:T(8,128)(2,1)S(1)}, u32[]{:S(2)}, u32[]{:S(2)}) collective-permute-start(bf16[4,32,896]{2,1,0:T(8,128)(2,1)} %get-tuple-element.53), channel_id=1, source_target_pairs={{0,8},{4,12},{8,16},{12,20},{16,24},{20,28},{24,32},{28,36},{32,40... | collective-permute-start | bytes 688136 | tf_op jit(solution)/shard_map/ppermute | solution.py:377
  33.3 25.2 %collective-permute-start.9 = (bf16[4,32,896]{2,1,0:T(8,128)(2,1)}, bf16[4,32,896]{2,1,0:T(8,128)(2,1)S(1)}, u32[]{:S(2)}, u32[]{:S(2)}) collective-permute-start(bf16[4,32,896]{2,1,0:T(8,128)(2,1)} %get-tuple-element.59), channel_id=1, source_target_pairs={{0,56},{4,60},{8,0},{12,4},{16,8},{20,12},{24,16},{28,20},{32,24},... | collective-permute-start | bytes 688136 | tf_op jit(solution)/shard_map/ppermute | solution.py:377
  60.8 9.9 %collective-permute-start.10 = (bf16[2,6,16,896]{3,2,1,0:T(8,128)(2,1)S(1)}, bf16[2,6,16,896]{3,2,1,0:T(8,128)(2,1)S(1)}, u32[]{:S(2)}, u32[]{:S(2)}) collective-permute-start(bf16[2,6,16,896]{3,2,1,0:T(8,128)(2,1)S(1)} %get-tuple-element.60.refs_0_), channel_id=1, source_target_pairs={{0,1},{1,2},{2,3},{3,0},{4,5},{5,6},{6,7},{7,4},{8,9},{9,10},{10,1... | collective-permute-start | bytes 1032200 | tf_op jit(solution)/shard_map/ppermute | solution.py:395
  62.1 8.8 %collective-permute-start.11 = (bf16[2,6,16,896]{3,2,1,0:T(8,128)(2,1)S(1)}, bf16[2,6,16,896]{3,2,1,0:T(8,128)(2,1)S(1)}, u32[]{:S(2)}, u32[]{:S(2)}) collective-permute-start(bf16[2,6,16,896]{3,2,1,0:T(8,128)(2,1)S(1)} %get-tuple-element.60.refs_0_), channel_id=1, source_target_pairs={{0,3},{1,0},{2,1},{3,2},{4,7},{5,4},{6,5},{7,6},{8,11},{9,8},{10,9... | collective-permute-start | bytes 1032200 | tf_op jit(solution)/shard_map/ppermute | solution.py:395
  70.7 7.6 %collective-permute-start.15 = (bf16[6,16,896]{2,1,0:T(8,128)(2,1)S(1)}, bf16[6,16,896]{2,1,0:T(8,128)(2,1)S(1)}, u32[]{:S(2)}, u32[]{:S(2)}) collective-permute-start(bf16[6,16,896]{2,1,0:T(8,128)(2,1)S(1)} %slice_bitcast_fusion), channel_id=1, source_target_pairs={{0,1},{1,2},{2,3},{3,0},{4,5},{5,6},{6,7},{7,4},{8,9},{9,10},{10,1... | collective-permute-start | bytes 516104 | tf_op jit(solution)/shard_map/ppermute | solution.py:395
  70.9 7.4 %collective-permute-start.16 = (bf16[6,16,896]{2,1,0:T(8,128)(2,1)S(1)}, bf16[6,16,896]{2,1,0:T(8,128)(2,1)S(1)}, u32[]{:S(2)}, u32[]{:S(2)}) collective-permute-start(bf16[6,16,896]{2,1,0:T(8,128)(2,1)S(1)} %slice_bitcast_fusion.1), channel_id=1, source_target_pairs={{0,3},{1,0},{2,1},{3,2},{4,7},{5,4},{6,5},{7,6},{8,11},{9,8},{10,9... | collective-permute-start | bytes 516104 | tf_op jit(solution)/shard_map/ppermute | solution.py:395
  73.8 15.8 %collective-permute-start.14 = (bf16[2,6,16,896]{3,2,1,0:T(8,128)(2,1)S(1)}, bf16[2,6,16,896]{3,2,1,0:T(8,128)(2,1)S(1)}, u32[]{:S(2)}, u32[]{:S(2)}) collective-permute-start(bf16[2,6,16,896]{3,2,1,0:T(8,128)(2,1)S(1)} %get-tuple-element.64.refs_1_), channel_id=1, source_target_pairs={{0,1},{1,2},{2,3},{3,0},{4,5},{5,6},{6,7},{7,4},{8,9},{9,10},{10,1... | collective-permute-start | bytes 1032200 | tf_op jit(solution)/shard_map/ppermute | solution.py:395
  73.8 17.9 %collective-permute-start.13 = (bf16[2,6,16,896]{3,2,1,0:T(8,128)(2,1)S(1)}, bf16[2,6,16,896]{3,2,1,0:T(8,128)(2,1)S(1)}, u32[]{:S(2)}, u32[]{:S(2)}) collective-permute-start(bf16[2,6,16,896]{3,2,1,0:T(8,128)(2,1)S(1)} %get-tuple-element.64.refs_1_), channel_id=1, source_target_pairs={{0,2},{1,3},{2,0},{3,1},{4,6},{5,7},{6,4},{7,5},{8,10},{9,11},{10,... | collective-permute-start | bytes 1032200 | tf_op jit(solution)/shard_map/ppermute | solution.py:395
  75.1 17.1 %collective-permute-start.12 = (bf16[2,6,16,896]{3,2,1,0:T(8,128)(2,1)S(1)}, bf16[2,6,16,896]{3,2,1,0:T(8,128)(2,1)S(1)}, u32[]{:S(2)}, u32[]{:S(2)}) collective-permute-start(bf16[2,6,16,896]{3,2,1,0:T(8,128)(2,1)S(1)} %get-tuple-element.64.refs_1_), channel_id=1, source_target_pairs={{0,3},{1,0},{2,1},{3,2},{4,7},{5,4},{6,5},{7,6},{8,11},{9,8},{10,9... | collective-permute-start | bytes 1032200 | tf_op jit(solution)/shard_map/ppermute | solution.py:395
  87.2 20.5 %collective-permute-start.18 = (bf16[6,224,128]{2,1,0:T(8,128)(2,1)S(1)}, bf16[6,224,128]{2,1,0:T(8,128)(2,1)S(1)}, u32[]{:S(2)}, u32[]{:S(2)}) collective-permute-start(bf16[6,224,128]{2,1,0:T(8,128)(2,1)S(1)} %get-tuple-element.77), channel_id=1, source_target_pairs={{0,1},{1,2},{2,3},{3,0},{4,5},{5,6},{6,7},{7,4},{8,9},{9,10},{10,1... | collective-permute-start | bytes 1032200 | tf_op jit(solution)/shard_map/ppermute | solution.py:395
  87.8 19.9 %collective-permute-start.19 = (bf16[6,224,128]{2,1,0:T(8,128)(2,1)S(1)}, bf16[6,224,128]{2,1,0:T(8,128)(2,1)S(1)}, u32[]{:S(2)}, u32[]{:S(2)}) collective-permute-start(bf16[6,224,128]{2,1,0:T(8,128)(2,1)S(1)} %get-tuple-element.78), channel_id=1, source_target_pairs={{0,2},{1,3},{2,0},{3,1},{4,6},{5,7},{6,4},{7,5},{8,10},{9,11},{10,... | collective-permute-start | bytes 1032200 | tf_op jit(solution)/shard_map/ppermute | solution.py:395
  89.6 19.4 %collective-permute-start.20 = (bf16[6,224,128]{2,1,0:T(8,128)(2,1)S(1)}, bf16[6,224,128]{2,1,0:T(8,128)(2,1)S(1)}, u32[]{:S(2)}, u32[]{:S(2)}) collective-permute-start(bf16[6,224,128]{2,1,0:T(8,128)(2,1)S(1)} %get-tuple-element.79), channel_id=1, source_target_pairs={{0,3},{1,0},{2,1},{3,2},{4,7},{5,4},{6,5},{7,6},{8,11},{9,8},{10,9... | collective-permute-start | bytes 1032200 | tf_op jit(solution)/shard_map/ppermute | solution.py:395
  102.6 16.3 %collective-permute-start.21 = (bf16[6,224,128]{2,1,0:T(8,128)(2,1)S(1)}, bf16[6,224,128]{2,1,0:T(8,128)(2,1)S(1)}, u32[]{:S(2)}, u32[]{:S(2)}) collective-permute-start(bf16[6,224,128]{2,1,0:T(8,128)(2,1)S(1)} %get-tuple-element.81), channel_id=1, source_target_pairs={{0,1},{1,2},{2,3},{3,0},{4,5},{5,6},{6,7},{7,4},{8,9},{9,10},{10,1... | collective-permute-start | bytes 1032200 | tf_op jit(solution)/shard_map/ppermute | solution.py:395
  103.8 16.0 %collective-permute-start.22 = (bf16[6,224,128]{2,1,0:T(8,128)(2,1)S(1)}, bf16[6,224,128]{2,1,0:T(8,128)(2,1)S(1)}, u32[]{:S(2)}, u32[]{:S(2)}) collective-permute-start(bf16[6,224,128]{2,1,0:T(8,128)(2,1)S(1)} %get-tuple-element.82), channel_id=1, source_target_pairs={{0,2},{1,3},{2,0},{3,1},{4,6},{5,7},{6,4},{7,5},{8,10},{9,11},{10,... | collective-permute-start | bytes 1032200 | tf_op jit(solution)/shard_map/ppermute | solution.py:395
  107.7 12.1 %collective-permute-start.23 = (bf16[6,224,128]{2,1,0:T(8,128)(2,1)S(1)}, bf16[6,224,128]{2,1,0:T(8,128)(2,1)S(1)}, u32[]{:S(2)}, u32[]{:S(2)}) collective-permute-start(bf16[6,224,128]{2,1,0:T(8,128)(2,1)S(1)} %get-tuple-element.83), channel_id=1, source_target_pairs={{0,3},{1,0},{2,1},{3,2},{4,7},{5,4},{6,5},{7,6},{8,11},{9,8},{10,9... | collective-permute-start | bytes 1032200 | tf_op jit(solution)/shard_map/ppermute | solution.py:395
  107.7 50.4 %collective-permute-start.17 = (bf16[384,1024]{1,0:T(8,128)(2,1)S(1)}, bf16[384,1024]{1,0:T(8,128)(2,1)S(1)}, u32[]{:S(2)}, u32[]{:S(2)}) collective-permute-start(bf16[384,1024]{1,0:T(8,128)(2,1)S(1)} %get-tuple-element.75), channel_id=1, source_target_pairs={{64,0},{128,64},{192,128},{65,1},{129,65},{193,129},{66,2},{130,66... | collective-permute-start | bytes 2359304 | tf_op jit(solution)/shard_map/ppermute | solution.py:400
  109.2 17.4 %collective-permute-start.24 = (bf16[6,224,128]{2,1,0:T(8,128)(2,1)S(1)}, bf16[6,224,128]{2,1,0:T(8,128)(2,1)S(1)}, u32[]{:S(2)}, u32[]{:S(2)}) collective-permute-start(bf16[6,224,128]{2,1,0:T(8,128)(2,1)S(1)} %sum_parts.2.refs_0_), channel_id=1, source_target_pairs={{0,4},{4,0},{8,12},{12,8},{16,20},{20,16},{24,28},{28,24},{32,36},... | collective-permute-start | bytes 1032200 | tf_op jit(solution)/shard_map/ppermute | solution.py:373
  119.9 7.9 %collective-permute-start.25 = (bf16[6,224,128]{2,1,0:T(8,128)(2,1)S(1)}, bf16[6,224,128]{2,1,0:T(8,128)(2,1)S(1)}, u32[]{:S(2)}, u32[]{:S(2)}) collective-permute-start(bf16[6,224,128]{2,1,0:T(8,128)(2,1)S(1)} %sum_parts.3.refs_1_), channel_id=1, source_target_pairs={{0,4},{4,0},{8,12},{12,8},{16,20},{20,16},{24,28},{28,24},{32,36},... | collective-permute-start | bytes 1032200 | tf_op jit(solution)/shard_map/ppermute | solution.py:373
  129.7 18.9 %collective-permute-start.26 = (bf16[4,224,128]{2,1,0:T(8,128)(2,1)S(1)}, bf16[4,224,128]{2,1,0:T(8,128)(2,1)S(1)}, u32[]{:S(2)}, u32[]{:S(2)}) collective-permute-start(bf16[4,224,128]{2,1,0:T(8,128)(2,1)S(1)} %get-tuple-element.84), channel_id=1, source_target_pairs={{0,24},{4,28},{8,32},{12,36},{16,40},{20,44},{24,48},{28,52},{32,5... | collective-permute-start | bytes 688136 | tf_op jit(solution)/shard_map/ppermute | solution.py:377
  134.1 14.4 %collective-permute-start.30 = (bf16[4,224,128]{2,1,0:T(8,128)(2,1)S(1)}, bf16[4,224,128]{2,1,0:T(8,128)(2,1)S(1)}, u32[]{:S(2)}, u32[]{:S(2)}) collective-permute-start(bf16[4,224,128]{2,1,0:T(8,128)(2,1)S(1)} %get-tuple-element.91), channel_id=1, source_target_pairs={{0,40},{4,44},{8,48},{12,52},{16,56},{20,60},{24,0},{28,4},{32,8},... | collective-permute-start | bytes 688136 | tf_op jit(solution)/shard_map/ppermute | solution.py:377
  134.2 24.8 %collective-permute-start.28 = (bf16[4,224,128]{2,1,0:T(8,128)(2,1)S(1)}, bf16[4,224,128]{2,1,0:T(8,128)(2,1)S(1)}, u32[]{:S(2)}, u32[]{:S(2)}) collective-permute-start(bf16[4,224,128]{2,1,0:T(8,128)(2,1)S(1)} %get-tuple-element.89), channel_id=1, source_target_pairs={{0,16},{4,20},{8,24},{12,28},{16,32},{20,36},{24,40},{28,44},{32,4... | collective-permute-start | bytes 688136 | tf_op jit(solution)/shard_map/ppermute | solution.py:377
  135.4 30.8 %collective-permute-start.29 = (bf16[4,224,128]{2,1,0:T(8,128)(2,1)S(1)}, bf16[4,224,128]{2,1,0:T(8,128)(2,1)S(1)}, u32[]{:S(2)}, u32[]{:S(2)}) collective-permute-start(bf16[4,224,128]{2,1,0:T(8,128)(2,1)S(1)} %get-tuple-element.90), channel_id=1, source_target_pairs={{0,32},{4,36},{8,40},{12,44},{16,48},{20,52},{24,56},{28,60},{32,0... | collective-permute-start | bytes 688136 | tf_op jit(solution)/shard_map/ppermute | solution.py:377
  148.5 22.4 %collective-permute-start.31 = (bf16[4,224,128]{2,1,0:T(8,128)(2,1)S(1)}, bf16[4,224,128]{2,1,0:T(8,128)(2,1)S(1)}, u32[]{:S(2)}, u32[]{:S(2)}) collective-permute-start(bf16[4,224,128]{2,1,0:T(8,128)(2,1)S(1)} %get-tuple-element.92), channel_id=1, source_target_pairs={{0,48},{4,52},{8,56},{12,60},{16,0},{20,4},{24,8},{28,12},{32,16},... | collective-permute-start | bytes 688136 | tf_op jit(solution)/shard_map/ppermute | solution.py:377
  148.5 24.9 %collective-permute-start.27 = (bf16[4,224,128]{2,1,0:T(8,128)(2,1)S(1)}, bf16[4,224,128]{2,1,0:T(8,128)(2,1)S(1)}, u32[]{:S(2)}, u32[]{:S(2)}) collective-permute-start(bf16[4,224,128]{2,1,0:T(8,128)(2,1)S(1)} %get-tuple-element.88), channel_id=1, source_target_pairs={{0,8},{4,12},{8,16},{12,20},{16,24},{20,28},{24,32},{28,36},{32,40... | collective-permute-start | bytes 688136 | tf_op jit(solution)/shard_map/ppermute | solution.py:377
  158.1 15.4 %collective-permute-start.32 = (bf16[4,224,128]{2,1,0:T(8,128)(2,1)S(1)}, bf16[4,224,128]{2,1,0:T(8,128)(2,1)S(1)}, u32[]{:S(2)}, u32[]{:S(2)}) collective-permute-start(bf16[4,224,128]{2,1,0:T(8,128)(2,1)S(1)} %get-tuple-element.94), channel_id=1, source_target_pairs={{0,56},{4,60},{8,0},{12,4},{16,8},{20,12},{24,16},{28,20},{32,24},... | collective-permute-start | bytes 688136 | tf_op jit(solution)/shard_map/ppermute | solution.py:377
  (12 other events, 144.9 us)

commit v6 on v3

--- a/solution.py
+++ b/solution.py
@@ -392,7 +392,7 @@
     low, high = turn(picked[0], 1), turn(picked[0], -1)
     across = [turn(low[0], 1), turn(high[1], -1)]
     whole = [[picked[0], high] + across + [low]]
-    own = after(picked[1], low, high)
+    own = after(picked[1], low, high, across[0])
     whole.append([own] + [turn(own, -shift) for shift in range(1, N_TP)])
     held = ()
     grads = []

time: 177 us -> 178 us (level)
    ppermute x14, starting transfers between devices: 36.2 us -> 45.5 us  [ahead(): lax.ppermute(x, 'seq', [(i, (i + 2 * by) % N_SEQ) for i in range(N_SEQ)])]
    ppermute x13, waiting for transfers between devices: 8.19 us -> 16.6 us  [turn(): return lax.ppermute(x, 'tp', [(i, (i + by) % N_TP) for i in range(N_TP)])]
    ppermute x5, starting transfers between devices: 20.3 us -> 12.9 us  [swap(): return lax.ppermute(x, 'seq', [(i, i ^ 1) for i in range(N_SEQ)])]
    ppermute x14, waiting for transfers between devices: 53.6 us -> 46.3 us  [ahead(): lax.ppermute(x, 'seq', [(i, (i + 2 * by) % N_SEQ) for i in range(N_SEQ)])]
  transfers between devices with their start and end apart: 33 -> 33, of which waited for: 17 -> 18; matrix products, arithmetic and copies ran while one was open for 0% -> 0% of each run, Pallas kernels for 14% -> 14%
where the time goes in v6:
time: 178 us
  starting transfers between devices  75.2 us (42%)
  waiting for transfers between devices  65.9 us (37%)
  Pallas kernels  33.2 us (19%)
  local copies, waits for them, and re-layouts  2.93 us (2%)
    ppermute x14, waiting for transfers between devices, ahead(): lax.ppermute(x, 'seq', [(i, (i + 2 * by) % N_SEQ) for i in range(N_SEQ)])  46.3 us
    ppermute x14, starting transfers between devices, ahead(): lax.ppermute(x, 'seq', [(i, (i + 2 * by) % N_SEQ) for i in range(N_SEQ)])  45.5 us
    pallas_call x2, Pallas kernels, attention(): pl.pallas_call(functools.partial(attention_kernel, hops), grid=(spans,),...  21.5 us
    ppermute x13, waiting for transfers between devices, turn(): return lax.ppermute(x, 'tp', [(i, (i + by) % N_TP) for i in range(N_TP)])  16.6 us
    ppermute x13, starting transfers between devices, turn(): return lax.ppermute(x, 'tp', [(i, (i + by) % N_TP) for i in range(N_TP)])  15.5 us
    ppermute x5, starting transfers between devices, swap(): return lax.ppermute(x, 'seq', [(i, i ^ 1) for i in range(N_SEQ)])  12.9 us
  transfers between devices with their start and end apart: 33, of which 18 were waited for; matrix products, arithmetic and copies ran while one was open for 0% of the time, Pallas kernels for 14%

profile of v6, /device:TPU:1, one launch (start us, length us, event | category | flops | bytes accessed | tf_op | source)
XLA Modules:
  0.0 178.1 jit_solution(13838158398521142640)
XLA Ops:
  0.7 2.2 %take_share.1.share_ref = bf16[16,32,896]{2,1,0:T(8,128)(2,1)} custom-call(bf16[16,128,896]{2,1,0:T(8,128)(2,1)} %bitcast.24), custom_call_target="tpu_custom_call" | custom-call | bytes 2000000 | tf_op jit(solution)/shard_map/take_share/pallas_call | solution.py:75
  2.9 3.3 %collective-permute-start.2 = (bf16[16,32,896]{2,1,0:T(8,128)(2,1)}, bf16[16,32,896]{2,1,0:T(8,128)(2,1)}, u32[]{:S(2)}, u32[]{:S(2)}) collective-permute-start(bf16[16,32,896]{2,1,0:T(8,128)(2,1)} %take_share.1.share_ref), channel_id=1, source_target_pairs={{0,4},{4,0},{8,12},{12,8},{16,20},{20,16},{24,28},{28,24},{32,36},... | collective-permute-start | bytes 2752520 | tf_op jit(solution)/shard_map/ppermute | solution.py:333
  9.0 2.9 %pack_rows.1 = (bf16[4,32,896]{2,1,0:T(8,128)(2,1)}, bf16[4,32,896]{2,1,0:T(8,128)(2,1)}, bf16[4,32,896]{2,1,0:T(8,128)(2,1)}, bf16[4,32,896]{2,1,0:T(8,128)(2,1...) custom-call(s32[16,2]{1,0:T(8,128)} %copy-done.1, ...), custom_call_target="tpu_custom_call" | custom-call | bytes 3000000 | tf_op jit(solution)/shard_map/pack_rows/pallas_call | solution.py:100
  11.8 2.6 %collective-permute-start.3 = (bf16[4,32,896]{2,1,0:T(8,128)(2,1)}, bf16[4,32,896]{2,1,0:T(8,128)(2,1)S(1)}, u32[]{:S(2)}, u32[]{:S(2)}) collective-permute-start(bf16[4,32,896]{2,1,0:T(8,128)(2,1)} %get-tuple-element.43), channel_id=1, source_target_pairs={{0,24},{4,28},{8,32},{12,36},{16,40},{20,44},{24,48},{28,52},{32,5... | collective-permute-start | bytes 688136 | tf_op jit(solution)/shard_map/ppermute | solution.py:337
  14.4 2.2 %collective-permute-start.7 = (bf16[4,32,896]{2,1,0:T(8,128)(2,1)}, bf16[4,32,896]{2,1,0:T(8,128)(2,1)S(1)}, u32[]{:S(2)}, u32[]{:S(2)}) collective-permute-start(bf16[4,32,896]{2,1,0:T(8,128)(2,1)} %get-tuple-element.47), channel_id=1, source_target_pairs={{0,40},{4,44},{8,48},{12,52},{16,56},{20,60},{24,0},{28,4},{32,8},... | collective-permute-start | bytes 688136 | tf_op jit(solution)/shard_map/ppermute | solution.py:337
  17.8 4.9 %collective-permute-start.6 = (bf16[4,32,896]{2,1,0:T(8,128)(2,1)}, bf16[4,32,896]{2,1,0:T(8,128)(2,1)S(1)}, u32[]{:S(2)}, u32[]{:S(2)}) collective-permute-start(bf16[4,32,896]{2,1,0:T(8,128)(2,1)} %get-tuple-element.46), channel_id=1, source_target_pairs={{0,32},{4,36},{8,40},{12,44},{16,48},{20,52},{24,56},{28,60},{32,0... | collective-permute-start | bytes 688136 | tf_op jit(solution)/shard_map/ppermute | solution.py:337
  22.6 2.4 %collective-permute-start.8 = (bf16[4,32,896]{2,1,0:T(8,128)(2,1)}, bf16[4,32,896]{2,1,0:T(8,128)(2,1)S(1)}, u32[]{:S(2)}, u32[]{:S(2)}) collective-permute-start(bf16[4,32,896]{2,1,0:T(8,128)(2,1)} %get-tuple-element.48), channel_id=1, source_target_pairs={{0,48},{4,52},{8,56},{12,60},{16,0},{20,4},{24,8},{28,12},{32,16},... | collective-permute-start | bytes 688136 | tf_op jit(solution)/shard_map/ppermute | solution.py:337
  25.0 3.6 %collective-permute-done.3.refs_3_ = bf16[4,32,896]{2,1,0:T(8,128)(2,1)S(1)} collective-permute-done((bf16[4,32,896]{2,1,0:T(8,128)(2,1)}, bf16[4,32,896]{2,1,0:T(8,128)(2,1)S(1)}, u32[]{:S(2)}, u32[]{:S(2)}) %collective-permute-start.3) | collective-permute-done | bytes 229408 | tf_op jit(solution)/shard_map/ppermute | solution.py:337
  28.6 3.8 %collective-permute-start.4 = (bf16[4,32,896]{2,1,0:T(8,128)(2,1)}, bf16[4,32,896]{2,1,0:T(8,128)(2,1)S(1)}, u32[]{:S(2)}, u32[]{:S(2)}) collective-permute-start(bf16[4,32,896]{2,1,0:T(8,128)(2,1)} %get-tuple-element.44), channel_id=1, source_target_pairs={{0,8},{4,12},{8,16},{12,20},{16,24},{20,28},{24,32},{28,36},{32,40... | collective-permute-start | bytes 688136 | tf_op jit(solution)/shard_map/ppermute | solution.py:337
  32.5 8.1 %collective-permute-done.5.refs_2_ = bf16[4,32,896]{2,1,0:T(8,128)(2,1)S(1)} collective-permute-done((bf16[4,32,896]{2,1,0:T(8,128)(2,1)}, bf16[4,32,896]{2,1,0:T(8,128)(2,1)S(1)}, u32[]{:S(2)}, u32[]{:S(2)}) %collective-permute-start.5) | collective-permute-done | bytes 229408 | tf_op jit(solution)/shard_map/ppermute | solution.py:337
  40.6 8.9 %collective-permute-done.6.refs_4_ = bf16[4,32,896]{2,1,0:T(8,128)(2,1)S(1)} collective-permute-done((bf16[4,32,896]{2,1,0:T(8,128)(2,1)}, bf16[4,32,896]{2,1,0:T(8,128)(2,1)S(1)}, u32[]{:S(2)}, u32[]{:S(2)}) %collective-permute-start.6) | collective-permute-done | bytes 229408 | tf_op jit(solution)/shard_map/ppermute | solution.py:337
  49.5 2.9 %collective-permute-done.8.refs_6_ = bf16[4,32,896]{2,1,0:T(8,128)(2,1)S(1)} collective-permute-done((bf16[4,32,896]{2,1,0:T(8,128)(2,1)}, bf16[4,32,896]{2,1,0:T(8,128)(2,1)S(1)}, u32[]{:S(2)}, u32[]{:S(2)}) %collective-permute-start.8) | collective-permute-done | bytes 229408 | tf_op jit(solution)/shard_map/ppermute | solution.py:337
  52.4 3.7 %collective-permute-done.4.refs_1_ = bf16[4,32,896]{2,1,0:T(8,128)(2,1)S(1)} collective-permute-done((bf16[4,32,896]{2,1,0:T(8,128)(2,1)}, bf16[4,32,896]{2,1,0:T(8,128)(2,1)S(1)}, u32[]{:S(2)}, u32[]{:S(2)}) %collective-permute-start.4) | collective-permute-done | bytes 229408 | tf_op jit(solution)/shard_map/ppermute | solution.py:337
  62.7 7.2 %collective-permute-done.10.refs_4_ = bf16[2,6,16,896]{3,2,1,0:T(8,128)(2,1)S(1)} collective-permute-done((bf16[2,6,16,896]{3,2,1,0:T(8,128)(2,1)S(1)}, bf16[2,6,16,896]{3,2,1,0:T(8,128)(2,1)S(1)}, u32[]{:S(2)}, u32[]{:S(2)}) %collective-permute-start.10) | collective-permute-done | bytes 344096 | tf_op jit(solution)/shard_map/ppermute | solution.py:355
  70.0 2.7 %collective-permute-start.16 = (bf16[6,16,896]{2,1,0:T(8,128)(2,1)S(1)}, bf16[6,16,896]{2,1,0:T(8,128)(2,1)S(1)}, u32[]{:S(2)}, u32[]{:S(2)}) collective-permute-start(bf16[6,16,896]{2,1,0:T(8,128)(2,1)S(1)} %slice_bitcast_fusion), channel_id=1, source_target_pairs={{0,3},{1,0},{2,1},{3,2},{4,7},{5,4},{6,5},{7,6},{8,11},{9,8},{10,9... | collective-permute-start | bytes 516104 | tf_op jit(solution)/shard_map/ppermute | solution.py:355
  72.7 2.7 %collective-permute-done.12.refs_2_ = bf16[6,16,896]{2,1,0:T(8,128)(2,1)S(1)} collective-permute-done((bf16[6,16,896]{2,1,0:T(8,128)(2,1)S(1)}, bf16[6,16,896]{2,1,0:T(8,128)(2,1)S(1)}, u32[]{:S(2)}, u32[]{:S(2)}) %collective-permute-start.12) | collective-permute-done | bytes 172064 | tf_op jit(solution)/shard_map/ppermute | solution.py:355
  79.6 10.8 %attention.2 = (bf16[384,1024]{1,0:T(8,128)(2,1)}, bf16[384,1024]{1,0:T(8,128)(2,1)S(1)}, bf16[6,224,128]{2,1,0:T(8,128)(2,1)S(1)}, bf16[6,224,128]{2,1,0:T(8,12...) custom-call(bf16[2,6,16,896]{3,2,1,0:T(8,128)(2,1)S(1)} %get-tuple-element.52.refs_0_, ...), custom_call_target="tpu_custom_call" | custom-call | flops 6600000000 | bytes 9500000 | tf_op jit(solution)/shard_map/attention/pallas_call | solution.py:218
  91.1 1.9 %collective-permute-start.19 = (bf16[6,224,128]{2,1,0:T(8,128)(2,1)S(1)}, bf16[6,224,128]{2,1,0:T(8,128)(2,1)S(1)}, u32[]{:S(2)}, u32[]{:S(2)}) collective-permute-start(bf16[6,224,128]{2,1,0:T(8,128)(2,1)S(1)} %get-tuple-element.60), channel_id=1, source_target_pairs={{0,2},{1,3},{2,0},{3,1},{4,6},{5,7},{6,4},{7,5},{8,10},{9,11},{10,... | collective-permute-start | bytes 1032200 | tf_op jit(solution)/shard_map/ppermute | solution.py:355
  93.0 2.0 %collective-permute-start.20 = (bf16[6,224,128]{2,1,0:T(8,128)(2,1)S(1)}, bf16[6,224,128]{2,1,0:T(8,128)(2,1)S(1)}, u32[]{:S(2)}, u32[]{:S(2)}) collective-permute-start(bf16[6,224,128]{2,1,0:T(8,128)(2,1)S(1)} %get-tuple-element.61), channel_id=1, source_target_pairs={{0,3},{1,0},{2,1},{3,2},{4,7},{5,4},{6,5},{7,6},{8,11},{9,8},{10,9... | collective-permute-start | bytes 1032200 | tf_op jit(solution)/shard_map/ppermute | solution.py:355
  94.9 10.7 %attention.3 = (bf16[384,1024]{1,0:T(8,128)(2,1)}, bf16[384,1024]{1,0:T(8,128)(2,1)S(1)}, bf16[6,224,128]{2,1,0:T(8,128)(2,1)S(1)}, bf16[6,224,128]{2,1,0:T(8,12...) custom-call(bf16[2,6,16,896]{3,2,1,0:T(8,128)(2,1)S(1)} %get-tuple-e, ...), custom_call_target="tpu_custom_call", output_to_operand_aliasing={{0}: (8, {}), {1}: (9, {})} | custom-call | flops 6600000000 | bytes 9500000 | tf_op jit(solution)/shard_map/attention/pallas_call | solution.py:218
  105.8 2.6 %collective-permute-start.22 = (bf16[6,224,128]{2,1,0:T(8,128)(2,1)S(1)}, bf16[6,224,128]{2,1,0:T(8,128)(2,1)S(1)}, u32[]{:S(2)}, u32[]{:S(2)}) collective-permute-start(bf16[6,224,128]{2,1,0:T(8,128)(2,1)S(1)} %get-tuple-element.64), channel_id=1, source_target_pairs={{0,2},{1,3},{2,0},{3,1},{4,6},{5,7},{6,4},{7,5},{8,10},{9,11},{10,... | collective-permute-start | bytes 1032200 | tf_op jit(solution)/shard_map/ppermute | solution.py:355
  109.9 5.3 %collective-permute-start.24 = (bf16[6,224,128]{2,1,0:T(8,128)(2,1)S(1)}, bf16[6,224,128]{2,1,0:T(8,128)(2,1)S(1)}, u32[]{:S(2)}, u32[]{:S(2)}) collective-permute-start(bf16[6,224,128]{2,1,0:T(8,128)(2,1)S(1)} %sum_parts.2.refs_0_), channel_id=1, source_target_pairs={{0,4},{4,0},{8,12},{12,8},{16,20},{20,16},{24,28},{28,24},{32,36},... | collective-permute-start | bytes 1032200 | tf_op jit(solution)/shard_map/ppermute | solution.py:333
  115.2 5.5 %collective-permute-done.22.refs_2_ = bf16[6,224,128]{2,1,0:T(8,128)(2,1)S(1)} collective-permute-done((bf16[6,224,128]{2,1,0:T(8,128)(2,1)S(1)}, bf16[6,224,128]{2,1,0:T(8,128)(2,1)S(1)}, u32[]{:S(2)}, u32[]{:S(2)}) %collective-permute-start.22) | collective-permute-done | bytes 344096 | tf_op jit(solution)/shard_map/ppermute | solution.py:355
  122.1 3.7 %collective-permute-start.25 = (bf16[6,224,128]{2,1,0:T(8,128)(2,1)S(1)}, bf16[6,224,128]{2,1,0:T(8,128)(2,1)S(1)}, u32[]{:S(2)}, u32[]{:S(2)}) collective-permute-start(bf16[6,224,128]{2,1,0:T(8,128)(2,1)S(1)} %sum_parts.3.refs_1_), channel_id=1, source_target_pairs={{0,4},{4,0},{8,12},{12,8},{16,20},{20,16},{24,28},{28,24},{32,36},... | collective-permute-start | bytes 1032200 | tf_op jit(solution)/shard_map/ppermute | solution.py:333
  128.9 4.3 %collective-permute-start.26 = (bf16[4,224,128]{2,1,0:T(8,128)(2,1)S(1)}, bf16[4,224,128]{2,1,0:T(8,128)(2,1)S(1)}, u32[]{:S(2)}, u32[]{:S(2)}) collective-permute-start(bf16[4,224,128]{2,1,0:T(8,128)(2,1)S(1)} %get-tuple-element.66), channel_id=1, source_target_pairs={{0,24},{4,28},{8,32},{12,36},{16,40},{20,44},{24,48},{28,52},{32,5... | collective-permute-start | bytes 688136 | tf_op jit(solution)/shard_map/ppermute | solution.py:337
  134.2 5.0 %collective-permute-start.29 = (bf16[4,224,128]{2,1,0:T(8,128)(2,1)S(1)}, bf16[4,224,128]{2,1,0:T(8,128)(2,1)S(1)}, u32[]{:S(2)}, u32[]{:S(2)}) collective-permute-start(bf16[4,224,128]{2,1,0:T(8,128)(2,1)S(1)} %get-tuple-element.72), channel_id=1, source_target_pairs={{0,32},{4,36},{8,40},{12,44},{16,48},{20,52},{24,56},{28,60},{32,0... | collective-permute-start | bytes 688136 | tf_op jit(solution)/shard_map/ppermute | solution.py:337
  139.2 3.9 %collective-permute-done.26.refs_3_ = bf16[4,224,128]{2,1,0:T(8,128)(2,1)S(1)} collective-permute-done((bf16[4,224,128]{2,1,0:T(8,128)(2,1)S(1)}, bf16[4,224,128]{2,1,0:T(8,128)(2,1)S(1)}, u32[]{:S(2)}, u32[]{:S(2)}) %collective-permute-start.26) | collective-permute-done | bytes 229408 | tf_op jit(solution)/shard_map/ppermute | solution.py:337
  143.0 10.0 %collective-permute-start.31 = (bf16[4,224,128]{2,1,0:T(8,128)(2,1)S(1)}, bf16[4,224,128]{2,1,0:T(8,128)(2,1)S(1)}, u32[]{:S(2)}, u32[]{:S(2)}) collective-permute-start(bf16[4,224,128]{2,1,0:T(8,128)(2,1)S(1)} %get-tuple-element.74), channel_id=1, source_target_pairs={{0,48},{4,52},{8,56},{12,60},{16,0},{20,4},{24,8},{28,12},{32,16},... | collective-permute-start | bytes 688136 | tf_op jit(solution)/shard_map/ppermute | solution.py:337
  153.0 8.3 %collective-permute-start.27 = (bf16[4,224,128]{2,1,0:T(8,128)(2,1)S(1)}, bf16[4,224,128]{2,1,0:T(8,128)(2,1)S(1)}, u32[]{:S(2)}, u32[]{:S(2)}) collective-permute-start(bf16[4,224,128]{2,1,0:T(8,128)(2,1)S(1)} %get-tuple-element.70), channel_id=1, source_target_pairs={{0,8},{4,12},{8,16},{12,20},{16,24},{20,28},{24,32},{28,36},{32,40... | collective-permute-start | bytes 688136 | tf_op jit(solution)/shard_map/ppermute | solution.py:337
  162.9 8.1 %collective-permute-done.31.refs_6_ = bf16[4,224,128]{2,1,0:T(8,128)(2,1)S(1)} collective-permute-done((bf16[4,224,128]{2,1,0:T(8,128)(2,1)S(1)}, bf16[4,224,128]{2,1,0:T(8,128)(2,1)S(1)}, u32[]{:S(2)}, u32[]{:S(2)}) %collective-permute-start.31) | collective-permute-done | bytes 229408 | tf_op jit(solution)/shard_map/ppermute | solution.py:337
  171.9 4.0 %collective-permute-done.32.refs_7_ = bf16[4,224,128]{2,1,0:T(8,128)(2,1)S(1)} collective-permute-done((bf16[4,224,128]{2,1,0:T(8,128)(2,1)S(1)}, bf16[4,224,128]{2,1,0:T(8,128)(2,1)S(1)}, u32[]{:S(2)}, u32[]{:S(2)}) %collective-permute-start.32) | collective-permute-done | bytes 229408 | tf_op jit(solution)/shard_map/ppermute | solution.py:337
  175.9 2.2 %collect.1 = bf16[16,224,128]{2,1,0:T(8,128)(2,1)} custom-call(s32[16,2]{1,0:T(8,128)S(1)} %copy-done.2, bf16[4,224,128]{2,1,0:T(8,128)(2,1)S(1)} %get-tuple-element.68.refs_0_, bf16[4,224,128]{2,1,0:T(8,128)(2,1)S(1)} %collective-permute-done.27.refs_1_, bf16[4,224,128]{2,1,0:T(8,128)(2,1)S(1)} %collective-permute-done.28.refs_2_, ...), custom_call_target="tpu_custom_call" | custom-call | bytes 3000000 | tf_op jit(solution)/shard_map/collect/pallas_call | solution.py:320
  (68 shorter events, 25.0 us)
Async XLA Ops:
  2.9 5.8 %collective-permute-start.2 = (bf16[16,32,896]{2,1,0:T(8,128)(2,1)}, bf16[16,32,896]{2,1,0:T(8,128)(2,1)}, u32[]{:S(2)}, u32[]{:S(2)}) collective-permute-start(bf16[16,32,896]{2,1,0:T(8,128)(2,1)} %take_share.1.share_ref), channel_id=1, source_target_pairs={{0,4},{4,0},{8,12},{12,8},{16,20},{20,16},{24,28},{28,24},{32,36},... | collective-permute-start | bytes 2752520 | tf_op jit(solution)/shard_map/ppermute | solution.py:333
  6.3 2.0 %collective-permute-start = (s32[16,2]{1,0:T(8,128)S(1)}, s32[16,2]{1,0:T(8,128)S(1)}, u32[]{:S(2)}, u32[]{:S(2)}) collective-permute-start(s32[16,2]{1,0:T(8,128)S(1)} %copy.14.rows_ref), channel_id=1, source_target_pairs={{0,4},{4,0},{8,12},{12,8},{16,20},{20,16},{24,28},{28,24},{32,36},... | collective-permute-start | bytes 392 | tf_op jit(solution)/shard_map/ppermute | solution.py:333
  11.8 16.8 %collective-permute-start.3 = (bf16[4,32,896]{2,1,0:T(8,128)(2,1)}, bf16[4,32,896]{2,1,0:T(8,128)(2,1)S(1)}, u32[]{:S(2)}, u32[]{:S(2)}) collective-permute-start(bf16[4,32,896]{2,1,0:T(8,128)(2,1)} %get-tuple-element.43), channel_id=1, source_target_pairs={{0,24},{4,28},{8,32},{12,36},{16,40},{20,44},{24,48},{28,52},{32,5... | collective-permute-start | bytes 688136 | tf_op jit(solution)/shard_map/ppermute | solution.py:337
  14.4 18.0 %collective-permute-start.7 = (bf16[4,32,896]{2,1,0:T(8,128)(2,1)}, bf16[4,32,896]{2,1,0:T(8,128)(2,1)S(1)}, u32[]{:S(2)}, u32[]{:S(2)}) collective-permute-start(bf16[4,32,896]{2,1,0:T(8,128)(2,1)} %get-tuple-element.47), channel_id=1, source_target_pairs={{0,40},{4,44},{8,48},{12,52},{16,56},{20,60},{24,0},{28,4},{32,8},... | collective-permute-start | bytes 688136 | tf_op jit(solution)/shard_map/ppermute | solution.py:337
  16.6 24.0 %collective-permute-start.5 = (bf16[4,32,896]{2,1,0:T(8,128)(2,1)}, bf16[4,32,896]{2,1,0:T(8,128)(2,1)S(1)}, u32[]{:S(2)}, u32[]{:S(2)}) collective-permute-start(bf16[4,32,896]{2,1,0:T(8,128)(2,1)} %get-tuple-element.45), channel_id=1, source_target_pairs={{0,16},{4,20},{8,24},{12,28},{16,32},{20,36},{24,40},{28,44},{32,4... | collective-permute-start | bytes 688136 | tf_op jit(solution)/shard_map/ppermute | solution.py:337
  17.8 31.7 %collective-permute-start.6 = (bf16[4,32,896]{2,1,0:T(8,128)(2,1)}, bf16[4,32,896]{2,1,0:T(8,128)(2,1)S(1)}, u32[]{:S(2)}, u32[]{:S(2)}) collective-permute-start(bf16[4,32,896]{2,1,0:T(8,128)(2,1)} %get-tuple-element.46), channel_id=1, source_target_pairs={{0,32},{4,36},{8,40},{12,44},{16,48},{20,52},{24,56},{28,60},{32,0... | collective-permute-start | bytes 688136 | tf_op jit(solution)/shard_map/ppermute | solution.py:337
  22.6 29.7 %collective-permute-start.8 = (bf16[4,32,896]{2,1,0:T(8,128)(2,1)}, bf16[4,32,896]{2,1,0:T(8,128)(2,1)S(1)}, u32[]{:S(2)}, u32[]{:S(2)}) collective-permute-start(bf16[4,32,896]{2,1,0:T(8,128)(2,1)} %get-tuple-element.48), channel_id=1, source_target_pairs={{0,48},{4,52},{8,56},{12,60},{16,0},{20,4},{24,8},{28,12},{32,16},... | collective-permute-start | bytes 688136 | tf_op jit(solution)/shard_map/ppermute | solution.py:337
  28.6 27.4 %collective-permute-start.4 = (bf16[4,32,896]{2,1,0:T(8,128)(2,1)}, bf16[4,32,896]{2,1,0:T(8,128)(2,1)S(1)}, u32[]{:S(2)}, u32[]{:S(2)}) collective-permute-start(bf16[4,32,896]{2,1,0:T(8,128)(2,1)} %get-tuple-element.44), channel_id=1, source_target_pairs={{0,8},{4,12},{8,16},{12,20},{16,24},{20,28},{24,32},{28,36},{32,40... | collective-permute-start | bytes 688136 | tf_op jit(solution)/shard_map/ppermute | solution.py:337
  32.5 25.2 %collective-permute-start.9 = (bf16[4,32,896]{2,1,0:T(8,128)(2,1)}, bf16[4,32,896]{2,1,0:T(8,128)(2,1)S(1)}, u32[]{:S(2)}, u32[]{:S(2)}) collective-permute-start(bf16[4,32,896]{2,1,0:T(8,128)(2,1)} %get-tuple-element.50), channel_id=1, source_target_pairs={{0,56},{4,60},{8,0},{12,4},{16,8},{20,12},{24,16},{28,20},{32,24},... | collective-permute-start | bytes 688136 | tf_op jit(solution)/shard_map/ppermute | solution.py:337
  59.9 9.9 %collective-permute-start.10 = (bf16[2,6,16,896]{3,2,1,0:T(8,128)(2,1)S(1)}, bf16[2,6,16,896]{3,2,1,0:T(8,128)(2,1)S(1)}, u32[]{:S(2)}, u32[]{:S(2)}) collective-permute-start(bf16[2,6,16,896]{3,2,1,0:T(8,128)(2,1)S(1)} %get-tuple-element.52.refs_0_), channel_id=1, source_target_pairs={{0,1},{1,2},{2,3},{3,0},{4,5},{5,6},{6,7},{7,4},{8,9},{9,10},{10,1... | collective-permute-start | bytes 1032200 | tf_op jit(solution)/shard_map/ppermute | solution.py:355
  61.2 8.8 %collective-permute-start.11 = (bf16[2,6,16,896]{3,2,1,0:T(8,128)(2,1)S(1)}, bf16[2,6,16,896]{3,2,1,0:T(8,128)(2,1)S(1)}, u32[]{:S(2)}, u32[]{:S(2)}) collective-permute-start(bf16[2,6,16,896]{3,2,1,0:T(8,128)(2,1)S(1)} %get-tuple-element.52.refs_0_), channel_id=1, source_target_pairs={{0,3},{1,0},{2,1},{3,2},{4,7},{5,4},{6,5},{7,6},{8,11},{9,8},{10,9... | collective-permute-start | bytes 1032200 | tf_op jit(solution)/shard_map/ppermute | solution.py:355
  69.9 5.5 %collective-permute-start.12 = (bf16[6,16,896]{2,1,0:T(8,128)(2,1)S(1)}, bf16[6,16,896]{2,1,0:T(8,128)(2,1)S(1)}, u32[]{:S(2)}, u32[]{:S(2)}) collective-permute-start(bf16[6,16,896]{2,1,0:T(8,128)(2,1)S(1)} %slice_bitcast_fusion.1), channel_id=1, source_target_pairs={{0,1},{1,2},{2,3},{3,0},{4,5},{5,6},{6,7},{7,4},{8,9},{9,10},{10,1... | collective-permute-start | bytes 516104 | tf_op jit(solution)/shard_map/ppermute | solution.py:355
  70.0 8.1 %collective-permute-start.16 = (bf16[6,16,896]{2,1,0:T(8,128)(2,1)S(1)}, bf16[6,16,896]{2,1,0:T(8,128)(2,1)S(1)}, u32[]{:S(2)}, u32[]{:S(2)}) collective-permute-start(bf16[6,16,896]{2,1,0:T(8,128)(2,1)S(1)} %slice_bitcast_fusion), channel_id=1, source_target_pairs={{0,3},{1,0},{2,1},{3,2},{4,7},{5,4},{6,5},{7,6},{8,11},{9,8},{10,9... | collective-permute-start | bytes 516104 | tf_op jit(solution)/shard_map/ppermute | solution.py:355
  75.4 17.5 %collective-permute-start.15 = (bf16[2,6,16,896]{3,2,1,0:T(8,128)(2,1)S(1)}, bf16[2,6,16,896]{3,2,1,0:T(8,128)(2,1)S(1)}, u32[]{:S(2)}, u32[]{:S(2)}) collective-permute-start(bf16[2,6,16,896]{3,2,1,0:T(8,128)(2,1)S(1)} %get-tuple-element.53.refs_0_), channel_id=1, source_target_pairs={{0,1},{1,2},{2,3},{3,0},{4,5},{5,6},{6,7},{7,4},{8,9},{9,10},{10,1... | collective-permute-start | bytes 1032200 | tf_op jit(solution)/shard_map/ppermute | solution.py:355
  75.4 19.5 %collective-permute-start.14 = (bf16[2,6,16,896]{3,2,1,0:T(8,128)(2,1)S(1)}, bf16[2,6,16,896]{3,2,1,0:T(8,128)(2,1)S(1)}, u32[]{:S(2)}, u32[]{:S(2)}) collective-permute-start(bf16[2,6,16,896]{3,2,1,0:T(8,128)(2,1)S(1)} %get-tuple-element.53.refs_0_), channel_id=1, source_target_pairs={{0,2},{1,3},{2,0},{3,1},{4,6},{5,7},{6,4},{7,5},{8,10},{9,11},{10,... | collective-permute-start | bytes 1032200 | tf_op jit(solution)/shard_map/ppermute | solution.py:355
  76.7 18.3 %collective-permute-start.13 = (bf16[2,6,16,896]{3,2,1,0:T(8,128)(2,1)S(1)}, bf16[2,6,16,896]{3,2,1,0:T(8,128)(2,1)S(1)}, u32[]{:S(2)}, u32[]{:S(2)}) collective-permute-start(bf16[2,6,16,896]{3,2,1,0:T(8,128)(2,1)S(1)} %get-tuple-element.53.refs_0_), channel_id=1, source_target_pairs={{0,3},{1,0},{2,1},{3,2},{4,7},{5,4},{6,5},{7,6},{8,11},{9,8},{10,9... | collective-permute-start | bytes 1032200 | tf_op jit(solution)/shard_map/ppermute | solution.py:355
  90.4 18.0 %collective-permute-start.18 = (bf16[6,224,128]{2,1,0:T(8,128)(2,1)S(1)}, bf16[6,224,128]{2,1,0:T(8,128)(2,1)S(1)}, u32[]{:S(2)}, u32[]{:S(2)}) collective-permute-start(bf16[6,224,128]{2,1,0:T(8,128)(2,1)S(1)} %get-tuple-element.59), channel_id=1, source_target_pairs={{0,1},{1,2},{2,3},{3,0},{4,5},{5,6},{6,7},{7,4},{8,9},{9,10},{10,1... | collective-permute-start | bytes 1032200 | tf_op jit(solution)/shard_map/ppermute | solution.py:355
  91.1 17.4 %collective-permute-start.19 = (bf16[6,224,128]{2,1,0:T(8,128)(2,1)S(1)}, bf16[6,224,128]{2,1,0:T(8,128)(2,1)S(1)}, u32[]{:S(2)}, u32[]{:S(2)}) collective-permute-start(bf16[6,224,128]{2,1,0:T(8,128)(2,1)S(1)} %get-tuple-element.60), channel_id=1, source_target_pairs={{0,2},{1,3},{2,0},{3,1},{4,6},{5,7},{6,4},{7,5},{8,10},{9,11},{10,... | collective-permute-start | bytes 1032200 | tf_op jit(solution)/shard_map/ppermute | solution.py:355
  93.0 16.8 %collective-permute-start.20 = (bf16[6,224,128]{2,1,0:T(8,128)(2,1)S(1)}, bf16[6,224,128]{2,1,0:T(8,128)(2,1)S(1)}, u32[]{:S(2)}, u32[]{:S(2)}) collective-permute-start(bf16[6,224,128]{2,1,0:T(8,128)(2,1)S(1)} %get-tuple-element.61), channel_id=1, source_target_pairs={{0,3},{1,0},{2,1},{3,2},{4,7},{5,4},{6,5},{7,6},{8,11},{9,8},{10,9... | collective-permute-start | bytes 1032200 | tf_op jit(solution)/shard_map/ppermute | solution.py:355
  105.7 9.6 %collective-permute-start.21 = (bf16[6,224,128]{2,1,0:T(8,128)(2,1)S(1)}, bf16[6,224,128]{2,1,0:T(8,128)(2,1)S(1)}, u32[]{:S(2)}, u32[]{:S(2)}) collective-permute-start(bf16[6,224,128]{2,1,0:T(8,128)(2,1)S(1)} %get-tuple-element.63), channel_id=1, source_target_pairs={{0,1},{1,2},{2,3},{3,0},{4,5},{5,6},{6,7},{7,4},{8,9},{9,10},{10,1... | collective-permute-start | bytes 1032200 | tf_op jit(solution)/shard_map/ppermute | solution.py:355
  105.8 15.0 %collective-permute-start.22 = (bf16[6,224,128]{2,1,0:T(8,128)(2,1)S(1)}, bf16[6,224,128]{2,1,0:T(8,128)(2,1)S(1)}, u32[]{:S(2)}, u32[]{:S(2)}) collective-permute-start(bf16[6,224,128]{2,1,0:T(8,128)(2,1)S(1)} %get-tuple-element.64), channel_id=1, source_target_pairs={{0,2},{1,3},{2,0},{3,1},{4,6},{5,7},{6,4},{7,5},{8,10},{9,11},{10,... | collective-permute-start | bytes 1032200 | tf_op jit(solution)/shard_map/ppermute | solution.py:355
  108.4 13.6 %collective-permute-start.23 = (bf16[6,224,128]{2,1,0:T(8,128)(2,1)S(1)}, bf16[6,224,128]{2,1,0:T(8,128)(2,1)S(1)}, u32[]{:S(2)}, u32[]{:S(2)}) collective-permute-start(bf16[6,224,128]{2,1,0:T(8,128)(2,1)S(1)} %get-tuple-element.65), channel_id=1, source_target_pairs={{0,3},{1,0},{2,1},{3,2},{4,7},{5,4},{6,5},{7,6},{8,11},{9,8},{10,9... | collective-permute-start | bytes 1032200 | tf_op jit(solution)/shard_map/ppermute | solution.py:355
  108.5 52.8 %collective-permute-start.17 = (bf16[384,1024]{1,0:T(8,128)(2,1)S(1)}, bf16[384,1024]{1,0:T(8,128)(2,1)S(1)}, u32[]{:S(2)}, u32[]{:S(2)}) collective-permute-start(bf16[384,1024]{1,0:T(8,128)(2,1)S(1)} %get-tuple-element.57), channel_id=1, source_target_pairs={{64,0},{128,64},{192,128},{65,1},{129,65},{193,129},{66,2},{130,66... | collective-permute-start | bytes 2359304 | tf_op jit(solution)/shard_map/ppermute | solution.py:360
  109.9 15.9 %collective-permute-start.24 = (bf16[6,224,128]{2,1,0:T(8,128)(2,1)S(1)}, bf16[6,224,128]{2,1,0:T(8,128)(2,1)S(1)}, u32[]{:S(2)}, u32[]{:S(2)}) collective-permute-start(bf16[6,224,128]{2,1,0:T(8,128)(2,1)S(1)} %sum_parts.2.refs_0_), channel_id=1, source_target_pairs={{0,4},{4,0},{8,12},{12,8},{16,20},{20,16},{24,28},{28,24},{32,36},... | collective-permute-start | bytes 1032200 | tf_op jit(solution)/shard_map/ppermute | solution.py:333
  122.1 5.0 %collective-permute-start.25 = (bf16[6,224,128]{2,1,0:T(8,128)(2,1)S(1)}, bf16[6,224,128]{2,1,0:T(8,128)(2,1)S(1)}, u32[]{:S(2)}, u32[]{:S(2)}) collective-permute-start(bf16[6,224,128]{2,1,0:T(8,128)(2,1)S(1)} %sum_parts.3.refs_1_), channel_id=1, source_target_pairs={{0,4},{4,0},{8,12},{12,8},{16,20},{20,16},{24,28},{28,24},{32,36},... | collective-permute-start | bytes 1032200 | tf_op jit(solution)/shard_map/ppermute | solution.py:333
  128.9 14.1 %collective-permute-start.26 = (bf16[4,224,128]{2,1,0:T(8,128)(2,1)S(1)}, bf16[4,224,128]{2,1,0:T(8,128)(2,1)S(1)}, u32[]{:S(2)}, u32[]{:S(2)}) collective-permute-start(bf16[4,224,128]{2,1,0:T(8,128)(2,1)S(1)} %get-tuple-element.66), channel_id=1, source_target_pairs={{0,24},{4,28},{8,32},{12,36},{16,40},{20,44},{24,48},{28,52},{32,5... | collective-permute-start | bytes 688136 | tf_op jit(solution)/shard_map/ppermute | solution.py:337
  133.3 19.7 %collective-permute-start.30 = (bf16[4,224,128]{2,1,0:T(8,128)(2,1)S(1)}, bf16[4,224,128]{2,1,0:T(8,128)(2,1)S(1)}, u32[]{:S(2)}, u32[]{:S(2)}) collective-permute-start(bf16[4,224,128]{2,1,0:T(8,128)(2,1)S(1)} %get-tuple-element.73), channel_id=1, source_target_pairs={{0,40},{4,44},{8,48},{12,52},{16,56},{20,60},{24,0},{28,4},{32,8},... | collective-permute-start | bytes 688136 | tf_op jit(solution)/shard_map/ppermute | solution.py:337
  133.5 28.7 %collective-permute-start.28 = (bf16[4,224,128]{2,1,0:T(8,128)(2,1)S(1)}, bf16[4,224,128]{2,1,0:T(8,128)(2,1)S(1)}, u32[]{:S(2)}, u32[]{:S(2)}) collective-permute-start(bf16[4,224,128]{2,1,0:T(8,128)(2,1)S(1)} %get-tuple-element.71), channel_id=1, source_target_pairs={{0,16},{4,20},{8,24},{12,28},{16,32},{20,36},{24,40},{28,44},{32,4... | collective-permute-start | bytes 688136 | tf_op jit(solution)/shard_map/ppermute | solution.py:337
  134.2 28.7 %collective-permute-start.29 = (bf16[4,224,128]{2,1,0:T(8,128)(2,1)S(1)}, bf16[4,224,128]{2,1,0:T(8,128)(2,1)S(1)}, u32[]{:S(2)}, u32[]{:S(2)}) collective-permute-start(bf16[4,224,128]{2,1,0:T(8,128)(2,1)S(1)} %get-tuple-element.72), channel_id=1, source_target_pairs={{0,32},{4,36},{8,40},{12,44},{16,48},{20,52},{24,56},{28,60},{32,0... | collective-permute-start | bytes 688136 | tf_op jit(solution)/shard_map/ppermute | solution.py:337
  143.0 28.0 %collective-permute-start.31 = (bf16[4,224,128]{2,1,0:T(8,128)(2,1)S(1)}, bf16[4,224,128]{2,1,0:T(8,128)(2,1)S(1)}, u32[]{:S(2)}, u32[]{:S(2)}) collective-permute-start(bf16[4,224,128]{2,1,0:T(8,128)(2,1)S(1)} %get-tuple-element.74), channel_id=1, source_target_pairs={{0,48},{4,52},{8,56},{12,60},{16,0},{20,4},{24,8},{28,12},{32,16},... | collective-permute-start | bytes 688136 | tf_op jit(solution)/shard_map/ppermute | solution.py:337
  153.0 18.9 %collective-permute-start.27 = (bf16[4,224,128]{2,1,0:T(8,128)(2,1)S(1)}, bf16[4,224,128]{2,1,0:T(8,128)(2,1)S(1)}, u32[]{:S(2)}, u32[]{:S(2)}) collective-permute-start(bf16[4,224,128]{2,1,0:T(8,128)(2,1)S(1)} %get-tuple-element.70), channel_id=1, source_target_pairs={{0,8},{4,12},{8,16},{12,20},{16,24},{20,28},{24,32},{28,36},{32,40... | collective-permute-start | bytes 688136 | tf_op jit(solution)/shard_map/ppermute | solution.py:337
  161.3 14.6 %collective-permute-start.32 = (bf16[4,224,128]{2,1,0:T(8,128)(2,1)S(1)}, bf16[4,224,128]{2,1,0:T(8,128)(2,1)S(1)}, u32[]{:S(2)}, u32[]{:S(2)}) collective-permute-start(bf16[4,224,128]{2,1,0:T(8,128)(2,1)S(1)} %get-tuple-element.76), channel_id=1, source_target_pairs={{0,56},{4,60},{8,0},{12,4},{16,8},{20,12},{24,16},{28,20},{32,24},... | collective-permute-start | bytes 688136 | tf_op jit(solution)/shard_map/ppermute | solution.py:337
  (11 other events, 299.0 us)

commit v7 on v6

--- a/solution.py
+++ b/solution.py
@@ -15,6 +15,8 @@
 NTOK = 128
 N_SEQ = 16
 CHIPS = N_SEQ // 2
+ACROSS = CHIPS // 2
+SENT = tuple(by for by in range(CHIPS) if by != ACROSS)
 CAP = 2
 N_TP = 4
 SLOTS = N_SEQ * CAP
@@ -84,6 +86,27 @@
     )(encoded)
 
 
+def message_blocks(by):
+    return 3 * CAP if by in (1, CHIPS - 1) else 2 * CAP
+
+
+def outgoing(refs, by, block):
+    if len(refs) == CHIPS:
+        return refs[by].at[block]
+    if by != ACROSS:
+        return refs[SENT.index(by)].at[block]
+    relay = 1 if block < CAP else CHIPS - 1
+    return refs[SENT.index(relay)].at[2 * CAP + block % CAP]
+
+
+def incoming(refs, by, block):
+    if len(refs) == CHIPS:
+        return refs[by].at[block]
+    if by != ACROSS:
+        return refs[SENT.index(by)].at[block]
+    return refs[len(SENT) + block // CAP].at[block % CAP]
+
+
 def pack_kernel(rows_ref, sibling_rows_ref, share_ref, sibling_ref, *outs):
     me = lax.axis_index("seq")
     chip, core = me // 2, lax.rem(me, 2)
@@ -91,17 +114,17 @@
         device = lax.rem(chip + ahead, CHIPS) * 2 + core
         for j in range(CAP):
             row = jnp.clip(rows_ref[device, j], 0, STORED - 1)
-            outs[ahead][j] = share_ref[row]
+            outgoing(outs, ahead, j)[...] = share_ref[row]
             row = jnp.clip(sibling_rows_ref[device, j], 0, STORED - 1)
-            outs[ahead][CAP + j] = sibling_ref[row]
+            outgoing(outs, ahead, CAP + j)[...] = sibling_ref[row]
 
 
 def pack_rows(rows, sibling_rows, share, sibling):
     return pl.pallas_call(
         pack_kernel,
-        out_shape=[jax.ShapeDtypeStruct((2 * CAP, PART, E), BF16)] * CHIPS,
+        out_shape=[jax.ShapeDtypeStruct((message_blocks(by), PART, E), BF16) for by in SENT],
         in_specs=[IN_SMEM, IN_SMEM, IN_VMEM, IN_VMEM],
-        out_specs=[IN_VMEM] * CHIPS,
+        out_specs=[IN_VMEM] * len(SENT),
         compiler_params=params(WIDE_VMEM),
         cost_estimate=cost(0, 3_000_000),
         name="pack_rows",
@@ -124,7 +147,8 @@
 
 
 def pick_kernel(neighbour_ref, *refs):
-    arrived, outs, table = refs[:CHIPS], refs[CHIPS:-1], refs[-1]
+    count = len(SENT) + 2
+    arrived, outs, table = refs[:count], refs[count:-1], refs[-1]
     for at in range(SLOTS):
         table[at] = REQ
     for r, (away, other, slot) in enumerate(places_of(neighbour_ref)):
@@ -133,17 +157,17 @@
     for away in range(CHIPS):
         for block in range(2 * CAP):
             r = table[away * 2 * CAP + block]
-            ref = arrived[(CHIPS - away) % CHIPS]
+            ref = incoming(arrived, (CHIPS - away) % CHIPS, block)
 
             @pl.when(r < half)
             def _():
                 for n in range(HALVES):
-                    outs[0][n, r] = ref[block, n * ROWS : (n + 1) * ROWS]
+                    outs[0][n, r] = ref[n * ROWS : (n + 1) * ROWS]
 
             @pl.when((r >= half) & (r < REQ))
             def _():
                 for n in range(HALVES):
-                    outs[1][n, r - half] = ref[block, n * ROWS : (n + 1) * ROWS]
+                    outs[1][n, r - half] = ref[n * ROWS : (n + 1) * ROWS]
 
 
 def pick(neighbour, arrived):
@@ -152,7 +176,7 @@
         out_shape=[
             jax.ShapeDtypeStruct((HALVES, spans * KNB, ROWS, E), BF16) for first, spans in GROUPS
         ],
-        in_specs=[IN_SMEM] + [IN_VMEM] * CHIPS,
+        in_specs=[IN_SMEM] + [IN_VMEM] * len(arrived),
         out_specs=[IN_VMEM] * len(GROUPS),
         scratch_shapes=[pltpu.SMEM((SLOTS,), jnp.int32)],
         compiler_params=params(),
@@ -274,19 +298,19 @@
         for block in range(2 * CAP):
             r = table[away * 2 * CAP + block]
             low, high = grads[2 * (block // CAP)], grads[2 * (block // CAP) + 1]
-            out = outs[away]
+            out = outgoing(outs, away, block)
 
             @pl.when(r < half)
             def _():
-                out[block] = low[r]
+                out[...] = low[r]
 
             @pl.when((r >= half) & (r < REQ))
             def _():
-                out[block] = high[r - half]
+                out[...] = high[r - half]
 
             @pl.when(r >= REQ)
             def _():
-                out[block] = jnp.zeros((EQ, NTOK), BF16)
+                out[...] = jnp.zeros((EQ, NTOK), BF16)
 
 
 def place(neighbour, sibling_neighbour, grads):
@@ -303,7 +327,7 @@
 
 
 def collect_kernel(rows_ref, *refs):
-    arrived, (out_ref, acc) = refs[:CHIPS], refs[CHIPS:]
+    arrived, (out_ref, acc) = refs[:-2], refs[-2:]
     me = lax.axis_index("seq")
     chip, core = me // 2, lax.rem(me, 2)
     acc[...] = jnp.zeros(acc.shape, F32)
@@ -312,7 +336,7 @@
         for block in range(2 * CAP):
             requester = device + (core if block < CAP else 1 - core)
             row = jnp.clip(rows_ref[requester, block % CAP], 0, STORED - 1)
-            acc[row] += arrived[behind][block].astype(F32)
+            acc[row] += incoming(arrived, behind, block)[...].astype(F32)
     out_ref[...] = acc[...].astype(BF16)
 
 
@@ -320,7 +344,7 @@
     return pl.pallas_call(
         collect_kernel,
         out_shape=jax.ShapeDtypeStruct((STORED, EQ, NTOK), BF16),
-        in_specs=[IN_SMEM] + [IN_VMEM] * CHIPS,
+        in_specs=[IN_SMEM] + [IN_VMEM] * len(arrived),
         out_specs=IN_VMEM,
         scratch_shapes=[pltpu.VMEM((STORED, EQ, NTOK), F32)],
         compiler_params=params(),
@@ -339,6 +363,15 @@
 
 def after(x, *done):
     return lax.optimization_barrier((x,) + done)[0]
+
+
+def exchange_relayed(messages):
+    local, right, *middle, left = messages
+    right, left = ahead(right, 1), ahead(left, CHIPS - 1)
+    middle = [ahead(x, by) for x, by in zip(middle, SENT[2:-1])]
+    first = ahead(right[2 * CAP :], ACROSS - 1)
+    second = ahead(left[2 * CAP :], ACROSS + 1)
+    return [local, right, *middle, left, first, second]
 
 
 def exchange(messages):
@@ -387,7 +420,7 @@
     share = take_share(encoded[0])
     sibling_sources = swap(sources)
     sibling_rows = after(swap(rows), sibling_sources)
-    arrived = exchange(pack_rows(rows, sibling_rows, share, swap(share)))
+    arrived = exchange_relayed(pack_rows(rows, sibling_rows, share, swap(share)))
     picked = pick(sources, arrived)
     low, high = turn(picked[0], 1), turn(picked[0], -1)
     across = [turn(low[0], 1), turn(high[1], -1)]

time: 178 us -> 178 us (level)
  waiting for transfers between devices: 65.9 us -> 61.5 us
  starting transfers between devices: 75.2 us -> 78.9 us
    ppermute x14 -> x15, waiting for transfers between devices: 46.3 us -> 43.1 us  [ahead(): lax.ppermute(x, 'seq', [(i, (i + 2 * by) % N_SEQ) for i in range(N_SEQ)])]
    ppermute x14 -> x15, starting transfers between devices: 45.5 us -> 48.1 us  [ahead(): lax.ppermute(x, 'seq', [(i, (i + 2 * by) % N_SEQ) for i in range(N_SEQ)])]
  transfers between devices with their start and end apart: 33 -> 34, of which waited for: 18 -> 16; matrix products, arithmetic and copies ran while one was open for 0% -> 0% of each run, Pallas kernels for 14% -> 14%
where the time goes in v7:
time: 178 us
  starting transfers between devices  78.9 us (44%)
  waiting for transfers between devices  61.5 us (35%)
  Pallas kernels  33.3 us (19%)
  local copies, waits for them, and re-layouts  2.96 us (2%)
    ppermute x15, starting transfers between devices, ahead(): lax.ppermute(x, 'seq', [(i, (i + 2 * by) % N_SEQ) for i in range(N_SEQ)])  48.1 us
    ppermute x15, waiting for transfers between devices, ahead(): lax.ppermute(x, 'seq', [(i, (i + 2 * by) % N_SEQ) for i in range(N_SEQ)])  43.1 us
    pallas_call x2, Pallas kernels, attention(): pl.pallas_call(functools.partial(attention_kernel, hops), grid=(spans,),...  21.5 us
    ppermute x13, starting transfers between devices, turn(): return lax.ppermute(x, 'tp', [(i, (i + by) % N_TP) for i in range(N_TP)])  15.8 us
    ppermute x13, waiting for transfers between devices, turn(): return lax.ppermute(x, 'tp', [(i, (i + by) % N_TP) for i in range(N_TP)])  15.3 us
    ppermute x5, starting transfers between devices, swap(): return lax.ppermute(x, 'seq', [(i, i ^ 1) for i in range(N_SEQ)])  13.8 us
  transfers between devices with their start and end apart: 34, of which 16 were waited for; matrix products, arithmetic and copies ran while one was open for 0% of the time, Pallas kernels for 14%

profile of v7, /device:TPU:1, one launch (start us, length us, event | category | flops | bytes accessed | tf_op | source)
XLA Modules:
  0.0 177.5 jit_solution(10721998609944360308)
XLA Ops:
  0.7 2.2 %take_share.1.share_ref = bf16[16,32,896]{2,1,0:T(8,128)(2,1)} custom-call(bf16[16,128,896]{2,1,0:T(8,128)(2,1)} %bitcast.24), custom_call_target="tpu_custom_call" | custom-call | bytes 2000000 | tf_op jit(solution)/shard_map/take_share/pallas_call | solution.py:77
  2.9 3.3 %collective-permute-start.2 = (bf16[16,32,896]{2,1,0:T(8,128)(2,1)}, bf16[16,32,896]{2,1,0:T(8,128)(2,1)}, u32[]{:S(2)}, u32[]{:S(2)}) collective-permute-start(bf16[16,32,896]{2,1,0:T(8,128)(2,1)} %take_share.1.share_ref), channel_id=1, source_target_pairs={{0,4},{4,0},{8,12},{12,8},{16,20},{20,16},{24,28},{28,24},{32,36},... | collective-permute-start | bytes 2752520 | tf_op jit(solution)/shard_map/ppermute | solution.py:357
  9.0 3.0 %pack_rows.1 = (bf16[4,32,896]{2,1,0:T(8,128)(2,1)}, bf16[6,32,896]{2,1,0:T(8,128)(2,1)}, bf16[4,32,896]{2,1,0:T(8,128)(2,1)}, bf16[4,32,896]{2,1,0:T(8,128)(2,1...) custom-call(s32[16,2]{1,0:T(8,128)} %copy-done.1, s32[16,2]{1,0:T(8,128)} %copy-done.7, ...), custom_call_target="tpu_custom_call" | custom-call | bytes 3000000 | tf_op jit(solution)/shard_map/pack_rows/pallas_call | solution.py:123
  12.0 3.9 %collective-permute-start.8 = (bf16[6,32,896]{2,1,0:T(8,128)(2,1)}, bf16[6,32,896]{2,1,0:T(8,128)(2,1)S(1)}, u32[]{:S(2)}, u32[]{:S(2)}) collective-permute-start(bf16[6,32,896]{2,1,0:T(8,128)(2,1)} %get-tuple-element.44), channel_id=1, source_target_pairs={{0,56},{4,60},{8,0},{12,4},{16,8},{20,12},{24,16},{28,20},{32,24},... | collective-permute-start | bytes 1032200 | tf_op jit(solution)/shard_map/ppermute | solution.py:361
  15.8 3.5 %collective-permute-start.5 = (bf16[4,32,896]{2,1,0:T(8,128)(2,1)}, bf16[4,32,896]{2,1,0:T(8,128)(2,1)S(1)}, u32[]{:S(2)}, u32[]{:S(2)}) collective-permute-start(bf16[4,32,896]{2,1,0:T(8,128)(2,1)} %get-tuple-element.41), channel_id=1, source_target_pairs={{0,24},{4,28},{8,32},{12,36},{16,40},{20,44},{24,48},{28,52},{32,5... | collective-permute-start | bytes 688136 | tf_op jit(solution)/shard_map/ppermute | solution.py:361
  20.3 3.8 %collective-permute-done.3.refs_1_ = bf16[6,32,896]{2,1,0:T(8,128)(2,1)S(1)} collective-permute-done((bf16[6,32,896]{2,1,0:T(8,128)(2,1)}, bf16[6,32,896]{2,1,0:T(8,128)(2,1)S(1)}, u32[]{:S(2)}, u32[]{:S(2)}) %collective-permute-start.3) | collective-permute-done | bytes 344096 | tf_op jit(solution)/shard_map/ppermute | solution.py:361
  25.7 2.9 %collective-permute-start.9 = (bf16[2,32,896]{2,1,0:T(8,128)(2,1)S(1)}, bf16[2,32,896]{2,1,0:T(8,128)(2,1)S(1)}, u32[]{:S(2)}, u32[]{:S(2)}) collective-permute-start(bf16[2,32,896]{2,1,0:T(8,128)(2,1)S(1)} %slice.16), channel_id=1, source_target_pairs={{0,24},{4,28},{8,32},{12,36},{16,40},{20,44},{24,48},{28,52},{32,5... | collective-permute-start | bytes 344072 | tf_op jit(solution)/shard_map/ppermute | solution.py:361
  28.6 2.0 %collective-permute-done.4.refs_2_ = bf16[4,32,896]{2,1,0:T(8,128)(2,1)S(1)} collective-permute-done((bf16[4,32,896]{2,1,0:T(8,128)(2,1)}, bf16[4,32,896]{2,1,0:T(8,128)(2,1)S(1)}, u32[]{:S(2)}, u32[]{:S(2)}) %collective-permute-start.4) | collective-permute-done | bytes 229408 | tf_op jit(solution)/shard_map/ppermute | solution.py:361
  30.6 6.6 %collective-permute-start.10 = (bf16[2,32,896]{2,1,0:T(8,128)(2,1)S(1)}, bf16[2,32,896]{2,1,0:T(8,128)(2,1)S(1)}, u32[]{:S(2)}, u32[]{:S(2)}) collective-permute-start(bf16[2,32,896]{2,1,0:T(8,128)(2,1)S(1)} %slice.17), channel_id=1, source_target_pairs={{0,40},{4,44},{8,48},{12,52},{16,56},{20,60},{24,0},{28,4},{32,8},... | collective-permute-start | bytes 344072 | tf_op jit(solution)/shard_map/ppermute | solution.py:361
  37.2 11.6 %collective-permute-done.5.refs_3_ = bf16[4,32,896]{2,1,0:T(8,128)(2,1)S(1)} collective-permute-done((bf16[4,32,896]{2,1,0:T(8,128)(2,1)}, bf16[4,32,896]{2,1,0:T(8,128)(2,1)S(1)}, u32[]{:S(2)}, u32[]{:S(2)}) %collective-permute-start.5) | collective-permute-done | bytes 229408 | tf_op jit(solution)/shard_map/ppermute | solution.py:361
  48.8 2.6 %collective-permute-done.7.refs_5_ = bf16[4,32,896]{2,1,0:T(8,128)(2,1)S(1)} collective-permute-done((bf16[4,32,896]{2,1,0:T(8,128)(2,1)}, bf16[4,32,896]{2,1,0:T(8,128)(2,1)S(1)}, u32[]{:S(2)}, u32[]{:S(2)}) %collective-permute-start.7) | collective-permute-done | bytes 229408 | tf_op jit(solution)/shard_map/ppermute | solution.py:361
  51.4 4.4 %collective-permute-done.9.refs_7_ = bf16[2,32,896]{2,1,0:T(8,128)(2,1)S(1)} collective-permute-done((bf16[2,32,896]{2,1,0:T(8,128)(2,1)S(1)}, bf16[2,32,896]{2,1,0:T(8,128)(2,1)S(1)}, u32[]{:S(2)}, u32[]{:S(2)}) %collective-permute-start.9) | collective-permute-done | bytes 114720 | tf_op jit(solution)/shard_map/ppermute | solution.py:361
  60.8 6.9 %collective-permute-done.11.refs_4_ = bf16[2,6,16,896]{3,2,1,0:T(8,128)(2,1)S(1)} collective-permute-done((bf16[2,6,16,896]{3,2,1,0:T(8,128)(2,1)S(1)}, bf16[2,6,16,896]{3,2,1,0:T(8,128)(2,1)S(1)}, u32[]{:S(2)}, u32[]{:S(2)}) %collective-permute-start.11) | collective-permute-done | bytes 344096 | tf_op jit(solution)/shard_map/ppermute | solution.py:388
  67.8 2.7 %collective-permute-start.17 = (bf16[6,16,896]{2,1,0:T(8,128)(2,1)S(1)}, bf16[6,16,896]{2,1,0:T(8,128)(2,1)S(1)}, u32[]{:S(2)}, u32[]{:S(2)}) collective-permute-start(bf16[6,16,896]{2,1,0:T(8,128)(2,1)S(1)} %slice_bitcast_fusion), channel_id=1, source_target_pairs={{0,3},{1,0},{2,1},{3,2},{4,7},{5,4},{6,5},{7,6},{8,11},{9,8},{10,9... | collective-permute-start | bytes 516104 | tf_op jit(solution)/shard_map/ppermute | solution.py:388
  70.6 2.7 %collective-permute-done.13.refs_2_ = bf16[6,16,896]{2,1,0:T(8,128)(2,1)S(1)} collective-permute-done((bf16[6,16,896]{2,1,0:T(8,128)(2,1)S(1)}, bf16[6,16,896]{2,1,0:T(8,128)(2,1)S(1)}, u32[]{:S(2)}, u32[]{:S(2)}) %collective-permute-start.13) | collective-permute-done | bytes 172064 | tf_op jit(solution)/shard_map/ppermute | solution.py:388
  77.5 10.8 %attention.2 = (bf16[384,1024]{1,0:T(8,128)(2,1)}, bf16[384,1024]{1,0:T(8,128)(2,1)S(1)}, bf16[6,224,128]{2,1,0:T(8,128)(2,1)S(1)}, bf16[6,224,128]{2,1,0:T(8,12...) custom-call(bf16[2,6,16,896]{3,2,1,0:T(8,128)(2,1)S(1)} %get-tuple-element.46.refs_0_, ...), custom_call_target="tpu_custom_call" | custom-call | flops 6600000000 | bytes 9500000 | tf_op jit(solution)/shard_map/attention/pallas_call | solution.py:242
  88.9 1.9 %collective-permute-start.20 = (bf16[6,224,128]{2,1,0:T(8,128)(2,1)S(1)}, bf16[6,224,128]{2,1,0:T(8,128)(2,1)S(1)}, u32[]{:S(2)}, u32[]{:S(2)}) collective-permute-start(bf16[6,224,128]{2,1,0:T(8,128)(2,1)S(1)} %get-tuple-element.54), channel_id=1, source_target_pairs={{0,2},{1,3},{2,0},{3,1},{4,6},{5,7},{6,4},{7,5},{8,10},{9,11},{10,... | collective-permute-start | bytes 1032200 | tf_op jit(solution)/shard_map/ppermute | solution.py:388
  90.8 2.0 %collective-permute-start.21 = (bf16[6,224,128]{2,1,0:T(8,128)(2,1)S(1)}, bf16[6,224,128]{2,1,0:T(8,128)(2,1)S(1)}, u32[]{:S(2)}, u32[]{:S(2)}) collective-permute-start(bf16[6,224,128]{2,1,0:T(8,128)(2,1)S(1)} %get-tuple-element.55), channel_id=1, source_target_pairs={{0,3},{1,0},{2,1},{3,2},{4,7},{5,4},{6,5},{7,6},{8,11},{9,8},{10,9... | collective-permute-start | bytes 1032200 | tf_op jit(solution)/shard_map/ppermute | solution.py:388
  92.7 10.7 %attention.3 = (bf16[384,1024]{1,0:T(8,128)(2,1)}, bf16[384,1024]{1,0:T(8,128)(2,1)S(1)}, bf16[6,224,128]{2,1,0:T(8,128)(2,1)S(1)}, bf16[6,224,128]{2,1,0:T(8,12...) custom-call(bf16[2,6,16,896]{3,2,1,0:T(8,128)(2,1)S(1)} %get-tuple-e, ...), custom_call_target="tpu_custom_call", output_to_operand_aliasing={{0}: (8, {}), {1}: (9, {})} | custom-call | flops 6600000000 | bytes 9500000 | tf_op jit(solution)/shard_map/attention/pallas_call | solution.py:242
  103.8 2.5 %collective-permute-start.23 = (bf16[6,224,128]{2,1,0:T(8,128)(2,1)S(1)}, bf16[6,224,128]{2,1,0:T(8,128)(2,1)S(1)}, u32[]{:S(2)}, u32[]{:S(2)}) collective-permute-start(bf16[6,224,128]{2,1,0:T(8,128)(2,1)S(1)} %get-tuple-element.58), channel_id=1, source_target_pairs={{0,2},{1,3},{2,0},{3,1},{4,6},{5,7},{6,4},{7,5},{8,10},{9,11},{10,... | collective-permute-start | bytes 1032200 | tf_op jit(solution)/shard_map/ppermute | solution.py:388
  108.0 5.7 %collective-permute-start.25 = (bf16[6,224,128]{2,1,0:T(8,128)(2,1)S(1)}, bf16[6,224,128]{2,1,0:T(8,128)(2,1)S(1)}, u32[]{:S(2)}, u32[]{:S(2)}) collective-permute-start(bf16[6,224,128]{2,1,0:T(8,128)(2,1)S(1)} %sum_parts.2.refs_0_), channel_id=1, source_target_pairs={{0,4},{4,0},{8,12},{12,8},{16,20},{20,16},{24,28},{28,24},{32,36},... | collective-permute-start | bytes 1032200 | tf_op jit(solution)/shard_map/ppermute | solution.py:357
  113.7 4.4 %collective-permute-done.23.refs_2_ = bf16[6,224,128]{2,1,0:T(8,128)(2,1)S(1)} collective-permute-done((bf16[6,224,128]{2,1,0:T(8,128)(2,1)S(1)}, bf16[6,224,128]{2,1,0:T(8,128)(2,1)S(1)}, u32[]{:S(2)}, u32[]{:S(2)}) %collective-permute-start.23) | collective-permute-done | bytes 344096 | tf_op jit(solution)/shard_map/ppermute | solution.py:388
  119.6 4.2 %collective-permute-start.26 = (bf16[6,224,128]{2,1,0:T(8,128)(2,1)S(1)}, bf16[6,224,128]{2,1,0:T(8,128)(2,1)S(1)}, u32[]{:S(2)}, u32[]{:S(2)}) collective-permute-start(bf16[6,224,128]{2,1,0:T(8,128)(2,1)S(1)} %sum_parts.3.refs_1_), channel_id=1, source_target_pairs={{0,4},{4,0},{8,12},{12,8},{16,20},{20,16},{24,28},{28,24},{32,36},... | collective-permute-start | bytes 1032200 | tf_op jit(solution)/shard_map/ppermute | solution.py:357
  125.1 1.8 %place.1 = (bf16[4,224,128]{2,1,0:T(8,128)(2,1)S(1)}, bf16[4,224,128]{2,1,0:T(8,128)(2,1)S(1)}, bf16[4,224,128]{2,1,0:T(8,128)(2,1)S(1)}, bf16[4,224,128]{2,1,0:...) custom-call(s32[6,2]{1,0:T(8,128)S(1)} %copy.15.neighbour_ref, ...), custom_call_target="tpu_custom_call" | custom-call | bytes 3000000 | tf_op jit(solution)/shard_map/place/pallas_call | solution.py:317
  127.2 4.4 %collective-permute-start.31 = (bf16[4,224,128]{2,1,0:T(8,128)(2,1)S(1)}, bf16[4,224,128]{2,1,0:T(8,128)(2,1)S(1)}, u32[]{:S(2)}, u32[]{:S(2)}) collective-permute-start(bf16[4,224,128]{2,1,0:T(8,128)(2,1)S(1)} %get-tuple-element.67), channel_id=1, source_target_pairs={{0,40},{4,44},{8,48},{12,52},{16,56},{20,60},{24,0},{28,4},{32,8},... | collective-permute-start | bytes 688136 | tf_op jit(solution)/shard_map/ppermute | solution.py:361
  132.7 4.9 %collective-permute-start.30 = (bf16[4,224,128]{2,1,0:T(8,128)(2,1)S(1)}, bf16[4,224,128]{2,1,0:T(8,128)(2,1)S(1)}, u32[]{:S(2)}, u32[]{:S(2)}) collective-permute-start(bf16[4,224,128]{2,1,0:T(8,128)(2,1)S(1)} %get-tuple-element.66), channel_id=1, source_target_pairs={{0,32},{4,36},{8,40},{12,44},{16,48},{20,52},{24,56},{28,60},{32,0... | collective-permute-start | bytes 688136 | tf_op jit(solution)/shard_map/ppermute | solution.py:361
  137.6 7.6 %collective-permute-done.27.refs_3_ = bf16[4,224,128]{2,1,0:T(8,128)(2,1)S(1)} collective-permute-done((bf16[4,224,128]{2,1,0:T(8,128)(2,1)S(1)}, bf16[4,224,128]{2,1,0:T(8,128)(2,1)S(1)}, u32[]{:S(2)}, u32[]{:S(2)}) %collective-permute-start.27) | collective-permute-done | bytes 229408 | tf_op jit(solution)/shard_map/ppermute | solution.py:361
  145.1 15.4 %collective-permute-start.32 = (bf16[4,224,128]{2,1,0:T(8,128)(2,1)S(1)}, bf16[4,224,128]{2,1,0:T(8,128)(2,1)S(1)}, u32[]{:S(2)}, u32[]{:S(2)}) collective-permute-start(bf16[4,224,128]{2,1,0:T(8,128)(2,1)S(1)} %get-tuple-element.68), channel_id=1, source_target_pairs={{0,48},{4,52},{8,56},{12,60},{16,0},{20,4},{24,8},{28,12},{32,16},... | collective-permute-start | bytes 688136 | tf_op jit(solution)/shard_map/ppermute | solution.py:361
  160.6 2.7 %collective-permute-start.33 = (bf16[4,224,128]{2,1,0:T(8,128)(2,1)S(1)}, bf16[4,224,128]{2,1,0:T(8,128)(2,1)S(1)}, u32[]{:S(2)}, u32[]{:S(2)}) collective-permute-start(bf16[4,224,128]{2,1,0:T(8,128)(2,1)S(1)} %get-tuple-element.70), channel_id=1, source_target_pairs={{0,56},{4,60},{8,0},{12,4},{16,8},{20,12},{24,16},{28,20},{32,24},... | collective-permute-start | bytes 688136 | tf_op jit(solution)/shard_map/ppermute | solution.py:361
  164.2 6.2 %collective-permute-done.32.refs_6_ = bf16[4,224,128]{2,1,0:T(8,128)(2,1)S(1)} collective-permute-done((bf16[4,224,128]{2,1,0:T(8,128)(2,1)S(1)}, bf16[4,224,128]{2,1,0:T(8,128)(2,1)S(1)}, u32[]{:S(2)}, u32[]{:S(2)}) %collective-permute-start.32) | collective-permute-done | bytes 229408 | tf_op jit(solution)/shard_map/ppermute | solution.py:361
  172.0 3.3 %collective-permute-done.33.refs_7_ = bf16[4,224,128]{2,1,0:T(8,128)(2,1)S(1)} collective-permute-done((bf16[4,224,128]{2,1,0:T(8,128)(2,1)S(1)}, bf16[4,224,128]{2,1,0:T(8,128)(2,1)S(1)}, u32[]{:S(2)}, u32[]{:S(2)}) %collective-permute-start.33) | collective-permute-done | bytes 229408 | tf_op jit(solution)/shard_map/ppermute | solution.py:361
  175.3 2.2 %collect.1 = bf16[16,224,128]{2,1,0:T(8,128)(2,1)} custom-call(s32[16,2]{1,0:T(8,128)S(1)} %copy-done.2, bf16[4,224,128]{2,1,0:T(8,128)(2,1)S(1)} %get-tuple-element.62.refs_0_, bf16[4,224,128]{2,1,0:T(8,128)(2,1)S(1)} %collective-permute-done.28.refs_1_, bf16[4,224,128]{2,1,0:T(8,128)(2,1)S(1)} %collective-permute-done.29.refs_2_, ...), custom_call_target="tpu_custom_call" | custom-call | bytes 3000000 | tf_op jit(solution)/shard_map/collect/pallas_call | solution.py:344
  (72 shorter events, 23.8 us)
Async XLA Ops:
  2.9 5.8 %collective-permute-start.2 = (bf16[16,32,896]{2,1,0:T(8,128)(2,1)}, bf16[16,32,896]{2,1,0:T(8,128)(2,1)}, u32[]{:S(2)}, u32[]{:S(2)}) collective-permute-start(bf16[16,32,896]{2,1,0:T(8,128)(2,1)} %take_share.1.share_ref), channel_id=1, source_target_pairs={{0,4},{4,0},{8,12},{12,8},{16,20},{20,16},{24,28},{28,24},{32,36},... | collective-permute-start | bytes 2752520 | tf_op jit(solution)/shard_map/ppermute | solution.py:357
  11.9 12.2 %collective-permute-start.3 = (bf16[6,32,896]{2,1,0:T(8,128)(2,1)}, bf16[6,32,896]{2,1,0:T(8,128)(2,1)S(1)}, u32[]{:S(2)}, u32[]{:S(2)}) collective-permute-start(bf16[6,32,896]{2,1,0:T(8,128)(2,1)} %get-tuple-element.39), channel_id=1, source_target_pairs={{0,8},{4,12},{8,16},{12,20},{16,24},{20,28},{24,32},{28,36},{32,40... | collective-permute-start | bytes 1032200 | tf_op jit(solution)/shard_map/ppermute | solution.py:361
  12.0 13.8 %collective-permute-start.8 = (bf16[6,32,896]{2,1,0:T(8,128)(2,1)}, bf16[6,32,896]{2,1,0:T(8,128)(2,1)S(1)}, u32[]{:S(2)}, u32[]{:S(2)}) collective-permute-start(bf16[6,32,896]{2,1,0:T(8,128)(2,1)} %get-tuple-element.44), channel_id=1, source_target_pairs={{0,56},{4,60},{8,0},{12,4},{16,8},{20,12},{24,16},{28,20},{32,24},... | collective-permute-start | bytes 1032200 | tf_op jit(solution)/shard_map/ppermute | solution.py:361
  15.8 14.8 %collective-permute-start.4 = (bf16[4,32,896]{2,1,0:T(8,128)(2,1)}, bf16[4,32,896]{2,1,0:T(8,128)(2,1)S(1)}, u32[]{:S(2)}, u32[]{:S(2)}) collective-permute-start(bf16[4,32,896]{2,1,0:T(8,128)(2,1)} %get-tuple-element.40), channel_id=1, source_target_pairs={{0,16},{4,20},{8,24},{12,28},{16,32},{20,36},{24,40},{28,44},{32,4... | collective-permute-start | bytes 688136 | tf_op jit(solution)/shard_map/ppermute | solution.py:361
  15.8 33.0 %collective-permute-start.5 = (bf16[4,32,896]{2,1,0:T(8,128)(2,1)}, bf16[4,32,896]{2,1,0:T(8,128)(2,1)S(1)}, u32[]{:S(2)}, u32[]{:S(2)}) collective-permute-start(bf16[4,32,896]{2,1,0:T(8,128)(2,1)} %get-tuple-element.41), channel_id=1, source_target_pairs={{0,24},{4,28},{8,32},{12,36},{16,40},{20,44},{24,48},{28,52},{32,5... | collective-permute-start | bytes 688136 | tf_op jit(solution)/shard_map/ppermute | solution.py:361
  19.3 29.4 %collective-permute-start.6 = (bf16[4,32,896]{2,1,0:T(8,128)(2,1)}, bf16[4,32,896]{2,1,0:T(8,128)(2,1)S(1)}, u32[]{:S(2)}, u32[]{:S(2)}) collective-permute-start(bf16[4,32,896]{2,1,0:T(8,128)(2,1)} %get-tuple-element.42), channel_id=1, source_target_pairs={{0,40},{4,44},{8,48},{12,52},{16,56},{20,60},{24,0},{28,4},{32,8},... | collective-permute-start | bytes 688136 | tf_op jit(solution)/shard_map/ppermute | solution.py:361
  24.1 27.2 %collective-permute-start.7 = (bf16[4,32,896]{2,1,0:T(8,128)(2,1)}, bf16[4,32,896]{2,1,0:T(8,128)(2,1)S(1)}, u32[]{:S(2)}, u32[]{:S(2)}) collective-permute-start(bf16[4,32,896]{2,1,0:T(8,128)(2,1)} %get-tuple-element.43), channel_id=1, source_target_pairs={{0,48},{4,52},{8,56},{12,60},{16,0},{20,4},{24,8},{28,12},{32,16},... | collective-permute-start | bytes 688136 | tf_op jit(solution)/shard_map/ppermute | solution.py:361
  25.7 30.0 %collective-permute-start.9 = (bf16[2,32,896]{2,1,0:T(8,128)(2,1)S(1)}, bf16[2,32,896]{2,1,0:T(8,128)(2,1)S(1)}, u32[]{:S(2)}, u32[]{:S(2)}) collective-permute-start(bf16[2,32,896]{2,1,0:T(8,128)(2,1)S(1)} %slice.16), channel_id=1, source_target_pairs={{0,24},{4,28},{8,32},{12,36},{16,40},{20,44},{24,48},{28,52},{32,5... | collective-permute-start | bytes 344072 | tf_op jit(solution)/shard_map/ppermute | solution.py:361
  30.6 25.2 %collective-permute-start.10 = (bf16[2,32,896]{2,1,0:T(8,128)(2,1)S(1)}, bf16[2,32,896]{2,1,0:T(8,128)(2,1)S(1)}, u32[]{:S(2)}, u32[]{:S(2)}) collective-permute-start(bf16[2,32,896]{2,1,0:T(8,128)(2,1)S(1)} %slice.17), channel_id=1, source_target_pairs={{0,40},{4,44},{8,48},{12,52},{16,56},{20,60},{24,0},{28,4},{32,8},... | collective-permute-start | bytes 344072 | tf_op jit(solution)/shard_map/ppermute | solution.py:361
  58.0 9.6 %collective-permute-start.11 = (bf16[2,6,16,896]{3,2,1,0:T(8,128)(2,1)S(1)}, bf16[2,6,16,896]{3,2,1,0:T(8,128)(2,1)S(1)}, u32[]{:S(2)}, u32[]{:S(2)}) collective-permute-start(bf16[2,6,16,896]{3,2,1,0:T(8,128)(2,1)S(1)} %get-tuple-element.46.refs_0_), channel_id=1, source_target_pairs={{0,1},{1,2},{2,3},{3,0},{4,5},{5,6},{6,7},{7,4},{8,9},{9,10},{10,1... | collective-permute-start | bytes 1032200 | tf_op jit(solution)/shard_map/ppermute | solution.py:388
  59.3 8.5 %collective-permute-start.12 = (bf16[2,6,16,896]{3,2,1,0:T(8,128)(2,1)S(1)}, bf16[2,6,16,896]{3,2,1,0:T(8,128)(2,1)S(1)}, u32[]{:S(2)}, u32[]{:S(2)}) collective-permute-start(bf16[2,6,16,896]{3,2,1,0:T(8,128)(2,1)S(1)} %get-tuple-element.46.refs_0_), channel_id=1, source_target_pairs={{0,3},{1,0},{2,1},{3,2},{4,7},{5,4},{6,5},{7,6},{8,11},{9,8},{10,9... | collective-permute-start | bytes 1032200 | tf_op jit(solution)/shard_map/ppermute | solution.py:388
  67.7 5.5 %collective-permute-start.13 = (bf16[6,16,896]{2,1,0:T(8,128)(2,1)S(1)}, bf16[6,16,896]{2,1,0:T(8,128)(2,1)S(1)}, u32[]{:S(2)}, u32[]{:S(2)}) collective-permute-start(bf16[6,16,896]{2,1,0:T(8,128)(2,1)S(1)} %slice_bitcast_fusion.1), channel_id=1, source_target_pairs={{0,1},{1,2},{2,3},{3,0},{4,5},{5,6},{6,7},{7,4},{8,9},{9,10},{10,1... | collective-permute-start | bytes 516104 | tf_op jit(solution)/shard_map/ppermute | solution.py:388
  67.8 8.1 %collective-permute-start.17 = (bf16[6,16,896]{2,1,0:T(8,128)(2,1)S(1)}, bf16[6,16,896]{2,1,0:T(8,128)(2,1)S(1)}, u32[]{:S(2)}, u32[]{:S(2)}) collective-permute-start(bf16[6,16,896]{2,1,0:T(8,128)(2,1)S(1)} %slice_bitcast_fusion), channel_id=1, source_target_pairs={{0,3},{1,0},{2,1},{3,2},{4,7},{5,4},{6,5},{7,6},{8,11},{9,8},{10,9... | collective-permute-start | bytes 516104 | tf_op jit(solution)/shard_map/ppermute | solution.py:388
  73.2 17.5 %collective-permute-start.16 = (bf16[2,6,16,896]{3,2,1,0:T(8,128)(2,1)S(1)}, bf16[2,6,16,896]{3,2,1,0:T(8,128)(2,1)S(1)}, u32[]{:S(2)}, u32[]{:S(2)}) collective-permute-start(bf16[2,6,16,896]{3,2,1,0:T(8,128)(2,1)S(1)} %get-tuple-element.47.refs_0_), channel_id=1, source_target_pairs={{0,1},{1,2},{2,3},{3,0},{4,5},{5,6},{6,7},{7,4},{8,9},{9,10},{10,1... | collective-permute-start | bytes 1032200 | tf_op jit(solution)/shard_map/ppermute | solution.py:388
  73.3 19.5 %collective-permute-start.15 = (bf16[2,6,16,896]{3,2,1,0:T(8,128)(2,1)S(1)}, bf16[2,6,16,896]{3,2,1,0:T(8,128)(2,1)S(1)}, u32[]{:S(2)}, u32[]{:S(2)}) collective-permute-start(bf16[2,6,16,896]{3,2,1,0:T(8,128)(2,1)S(1)} %get-tuple-element.47.refs_0_), channel_id=1, source_target_pairs={{0,2},{1,3},{2,0},{3,1},{4,6},{5,7},{6,4},{7,5},{8,10},{9,11},{10,... | collective-permute-start | bytes 1032200 | tf_op jit(solution)/shard_map/ppermute | solution.py:388
  74.5 18.3 %collective-permute-start.14 = (bf16[2,6,16,896]{3,2,1,0:T(8,128)(2,1)S(1)}, bf16[2,6,16,896]{3,2,1,0:T(8,128)(2,1)S(1)}, u32[]{:S(2)}, u32[]{:S(2)}) collective-permute-start(bf16[2,6,16,896]{3,2,1,0:T(8,128)(2,1)S(1)} %get-tuple-element.47.refs_0_), channel_id=1, source_target_pairs={{0,3},{1,0},{2,1},{3,2},{4,7},{5,4},{6,5},{7,6},{8,11},{9,8},{10,9... | collective-permute-start | bytes 1032200 | tf_op jit(solution)/shard_map/ppermute | solution.py:388
  88.2 18.2 %collective-permute-start.19 = (bf16[6,224,128]{2,1,0:T(8,128)(2,1)S(1)}, bf16[6,224,128]{2,1,0:T(8,128)(2,1)S(1)}, u32[]{:S(2)}, u32[]{:S(2)}) collective-permute-start(bf16[6,224,128]{2,1,0:T(8,128)(2,1)S(1)} %get-tuple-element.53), channel_id=1, source_target_pairs={{0,1},{1,2},{2,3},{3,0},{4,5},{5,6},{6,7},{7,4},{8,9},{9,10},{10,1... | collective-permute-start | bytes 1032200 | tf_op jit(solution)/shard_map/ppermute | solution.py:388
  88.9 17.6 %collective-permute-start.20 = (bf16[6,224,128]{2,1,0:T(8,128)(2,1)S(1)}, bf16[6,224,128]{2,1,0:T(8,128)(2,1)S(1)}, u32[]{:S(2)}, u32[]{:S(2)}) collective-permute-start(bf16[6,224,128]{2,1,0:T(8,128)(2,1)S(1)} %get-tuple-element.54), channel_id=1, source_target_pairs={{0,2},{1,3},{2,0},{3,1},{4,6},{5,7},{6,4},{7,5},{8,10},{9,11},{10,... | collective-permute-start | bytes 1032200 | tf_op jit(solution)/shard_map/ppermute | solution.py:388
  90.8 17.0 %collective-permute-start.21 = (bf16[6,224,128]{2,1,0:T(8,128)(2,1)S(1)}, bf16[6,224,128]{2,1,0:T(8,128)(2,1)S(1)}, u32[]{:S(2)}, u32[]{:S(2)}) collective-permute-start(bf16[6,224,128]{2,1,0:T(8,128)(2,1)S(1)} %get-tuple-element.55), channel_id=1, source_target_pairs={{0,3},{1,0},{2,1},{3,2},{4,7},{5,4},{6,5},{7,6},{8,11},{9,8},{10,9... | collective-permute-start | bytes 1032200 | tf_op jit(solution)/shard_map/ppermute | solution.py:388
  103.5 10.2 %collective-permute-start.22 = (bf16[6,224,128]{2,1,0:T(8,128)(2,1)S(1)}, bf16[6,224,128]{2,1,0:T(8,128)(2,1)S(1)}, u32[]{:S(2)}, u32[]{:S(2)}) collective-permute-start(bf16[6,224,128]{2,1,0:T(8,128)(2,1)S(1)} %get-tuple-element.57), channel_id=1, source_target_pairs={{0,1},{1,2},{2,3},{3,0},{4,5},{5,6},{6,7},{7,4},{8,9},{9,10},{10,1... | collective-permute-start | bytes 1032200 | tf_op jit(solution)/shard_map/ppermute | solution.py:388
  103.8 14.3 %collective-permute-start.23 = (bf16[6,224,128]{2,1,0:T(8,128)(2,1)S(1)}, bf16[6,224,128]{2,1,0:T(8,128)(2,1)S(1)}, u32[]{:S(2)}, u32[]{:S(2)}) collective-permute-start(bf16[6,224,128]{2,1,0:T(8,128)(2,1)S(1)} %get-tuple-element.58), channel_id=1, source_target_pairs={{0,2},{1,3},{2,0},{3,1},{4,6},{5,7},{6,4},{7,5},{8,10},{9,11},{10,... | collective-permute-start | bytes 1032200 | tf_op jit(solution)/shard_map/ppermute | solution.py:388
  106.4 13.1 %collective-permute-start.24 = (bf16[6,224,128]{2,1,0:T(8,128)(2,1)S(1)}, bf16[6,224,128]{2,1,0:T(8,128)(2,1)S(1)}, u32[]{:S(2)}, u32[]{:S(2)}) collective-permute-start(bf16[6,224,128]{2,1,0:T(8,128)(2,1)S(1)} %get-tuple-element.59), channel_id=1, source_target_pairs={{0,3},{1,0},{2,1},{3,2},{4,7},{5,4},{6,5},{7,6},{8,11},{9,8},{10,9... | collective-permute-start | bytes 1032200 | tf_op jit(solution)/shard_map/ppermute | solution.py:388
  106.5 54.1 %collective-permute-start.18 = (bf16[384,1024]{1,0:T(8,128)(2,1)S(1)}, bf16[384,1024]{1,0:T(8,128)(2,1)S(1)}, u32[]{:S(2)}, u32[]{:S(2)}) collective-permute-start(bf16[384,1024]{1,0:T(8,128)(2,1)S(1)} %get-tuple-element.51), channel_id=1, source_target_pairs={{64,0},{128,64},{192,128},{65,1},{129,65},{193,129},{66,2},{130,66... | collective-permute-start | bytes 2359304 | tf_op jit(solution)/shard_map/ppermute | solution.py:393
  108.0 15.9 %collective-permute-start.25 = (bf16[6,224,128]{2,1,0:T(8,128)(2,1)S(1)}, bf16[6,224,128]{2,1,0:T(8,128)(2,1)S(1)}, u32[]{:S(2)}, u32[]{:S(2)}) collective-permute-start(bf16[6,224,128]{2,1,0:T(8,128)(2,1)S(1)} %sum_parts.2.refs_0_), channel_id=1, source_target_pairs={{0,4},{4,0},{8,12},{12,8},{16,20},{20,16},{24,28},{28,24},{32,36},... | collective-permute-start | bytes 1032200 | tf_op jit(solution)/shard_map/ppermute | solution.py:357
  119.6 5.5 %collective-permute-start.26 = (bf16[6,224,128]{2,1,0:T(8,128)(2,1)S(1)}, bf16[6,224,128]{2,1,0:T(8,128)(2,1)S(1)}, u32[]{:S(2)}, u32[]{:S(2)}) collective-permute-start(bf16[6,224,128]{2,1,0:T(8,128)(2,1)S(1)} %sum_parts.3.refs_1_), channel_id=1, source_target_pairs={{0,4},{4,0},{8,12},{12,8},{16,20},{20,16},{24,28},{28,24},{32,36},... | collective-permute-start | bytes 1032200 | tf_op jit(solution)/shard_map/ppermute | solution.py:357
  126.9 18.2 %collective-permute-start.27 = (bf16[4,224,128]{2,1,0:T(8,128)(2,1)S(1)}, bf16[4,224,128]{2,1,0:T(8,128)(2,1)S(1)}, u32[]{:S(2)}, u32[]{:S(2)}) collective-permute-start(bf16[4,224,128]{2,1,0:T(8,128)(2,1)S(1)} %get-tuple-element.60), channel_id=1, source_target_pairs={{0,24},{4,28},{8,32},{12,36},{16,40},{20,44},{24,48},{28,52},{32,5... | collective-permute-start | bytes 688136 | tf_op jit(solution)/shard_map/ppermute | solution.py:361
  127.2 33.4 %collective-permute-start.31 = (bf16[4,224,128]{2,1,0:T(8,128)(2,1)S(1)}, bf16[4,224,128]{2,1,0:T(8,128)(2,1)S(1)}, u32[]{:S(2)}, u32[]{:S(2)}) collective-permute-start(bf16[4,224,128]{2,1,0:T(8,128)(2,1)S(1)} %get-tuple-element.67), channel_id=1, source_target_pairs={{0,40},{4,44},{8,48},{12,52},{16,56},{20,60},{24,0},{28,4},{32,8},... | collective-permute-start | bytes 688136 | tf_op jit(solution)/shard_map/ppermute | solution.py:361
  131.6 32.6 %collective-permute-start.29 = (bf16[4,224,128]{2,1,0:T(8,128)(2,1)S(1)}, bf16[4,224,128]{2,1,0:T(8,128)(2,1)S(1)}, u32[]{:S(2)}, u32[]{:S(2)}) collective-permute-start(bf16[4,224,128]{2,1,0:T(8,128)(2,1)S(1)} %get-tuple-element.65), channel_id=1, source_target_pairs={{0,16},{4,20},{8,24},{12,28},{16,32},{20,36},{24,40},{28,44},{32,4... | collective-permute-start | bytes 688136 | tf_op jit(solution)/shard_map/ppermute | solution.py:361
  132.7 31.5 %collective-permute-start.30 = (bf16[4,224,128]{2,1,0:T(8,128)(2,1)S(1)}, bf16[4,224,128]{2,1,0:T(8,128)(2,1)S(1)}, u32[]{:S(2)}, u32[]{:S(2)}) collective-permute-start(bf16[4,224,128]{2,1,0:T(8,128)(2,1)S(1)} %get-tuple-element.66), channel_id=1, source_target_pairs={{0,32},{4,36},{8,40},{12,44},{16,48},{20,52},{24,56},{28,60},{32,0... | collective-permute-start | bytes 688136 | tf_op jit(solution)/shard_map/ppermute | solution.py:361
  145.1 25.3 %collective-permute-start.32 = (bf16[4,224,128]{2,1,0:T(8,128)(2,1)S(1)}, bf16[4,224,128]{2,1,0:T(8,128)(2,1)S(1)}, u32[]{:S(2)}, u32[]{:S(2)}) collective-permute-start(bf16[4,224,128]{2,1,0:T(8,128)(2,1)S(1)} %get-tuple-element.68), channel_id=1, source_target_pairs={{0,48},{4,52},{8,56},{12,60},{16,0},{20,4},{24,8},{28,12},{32,16},... | collective-permute-start | bytes 688136 | tf_op jit(solution)/shard_map/ppermute | solution.py:361
  160.6 11.4 %collective-permute-start.28 = (bf16[4,224,128]{2,1,0:T(8,128)(2,1)S(1)}, bf16[4,224,128]{2,1,0:T(8,128)(2,1)S(1)}, u32[]{:S(2)}, u32[]{:S(2)}) collective-permute-start(bf16[4,224,128]{2,1,0:T(8,128)(2,1)S(1)} %get-tuple-element.64), channel_id=1, source_target_pairs={{0,8},{4,12},{8,16},{12,20},{16,24},{20,28},{24,32},{28,36},{32,40... | collective-permute-start | bytes 688136 | tf_op jit(solution)/shard_map/ppermute | solution.py:361
  160.6 14.7 %collective-permute-start.33 = (bf16[4,224,128]{2,1,0:T(8,128)(2,1)S(1)}, bf16[4,224,128]{2,1,0:T(8,128)(2,1)S(1)}, u32[]{:S(2)}, u32[]{:S(2)}) collective-permute-start(bf16[4,224,128]{2,1,0:T(8,128)(2,1)S(1)} %get-tuple-element.70), channel_id=1, source_target_pairs={{0,56},{4,60},{8,0},{12,4},{16,8},{20,12},{24,16},{28,20},{32,24},... | collective-permute-start | bytes 688136 | tf_op jit(solution)/shard_map/ppermute | solution.py:361
  (12 other events, 293.9 us)

commit v8 on v7

--- a/solution.py
+++ b/solution.py
@@ -438,6 +438,8 @@
     context, query_grad = held
     passed = section_back(query_grad)
     messages = place(sources, sibling_sources, grads + [swap(grad) for grad in grads])
+    messages = list(messages)
+    messages[6] = after(messages[6], passed)
     returned = exchange(messages)
     encoded_grad = jnp.swapaxes(collect(rows, returned), 1, 2)
     passed = deliver([after(passed, returned[3])])

time: 178 us -> 175 us (0.983)
  starting transfers between devices: 78.9 us -> 66.2 us
  waiting for transfers between devices: 61.5 us -> 71.1 us
    ppermute x15, starting transfers between devices: 48.1 us -> 35.4 us  [ahead(): lax.ppermute(x, 'seq', [(i, (i + 2 * by) % N_SEQ) for i in range(N_SEQ)])]
    ppermute x15, waiting for transfers between devices: 43.1 us -> 52.8 us  [ahead(): lax.ppermute(x, 'seq', [(i, (i + 2 * by) % N_SEQ) for i in range(N_SEQ)])]
  transfers between devices with their start and end apart: 34 -> 34, of which waited for: 16 -> 17; matrix products, arithmetic and copies ran while one was open for 0% -> 0% of each run, Pallas kernels for 14% -> 14%
where the time goes in v8:
time: 175 us; the launch traced here: 174 us
  waiting for transfers between devices  71.1 us (41%)
  starting transfers between devices  66.2 us (38%)
  Pallas kernels  33.3 us (19%)
  local copies, waits for them, and re-layouts  2.96 us (2%)
    ppermute x15, waiting for transfers between devices, ahead(): lax.ppermute(x, 'seq', [(i, (i + 2 * by) % N_SEQ) for i in range(N_SEQ)])  52.8 us
    ppermute x15, starting transfers between devices, ahead(): lax.ppermute(x, 'seq', [(i, (i + 2 * by) % N_SEQ) for i in range(N_SEQ)])  35.4 us
    pallas_call x2, Pallas kernels, attention(): pl.pallas_call(functools.partial(attention_kernel, hops), grid=(spans,),...  21.5 us
    ppermute x13, starting transfers between devices, turn(): return lax.ppermute(x, 'tp', [(i, (i + by) % N_TP) for i in range(N_TP)])  15.8 us
    ppermute x13, waiting for transfers between devices, turn(): return lax.ppermute(x, 'tp', [(i, (i + by) % N_TP) for i in range(N_TP)])  15.3 us
    ppermute x5, starting transfers between devices, swap(): return lax.ppermute(x, 'seq', [(i, i ^ 1) for i in range(N_SEQ)])  13.8 us
  transfers between devices with their start and end apart: 34, of which 17 were waited for; matrix products, arithmetic and copies ran while one was open for 0% of the time, Pallas kernels for 14%

profile of v8, /device:TPU:1, one launch (start us, length us, event | category | flops | bytes accessed | tf_op | source)
XLA Modules:
  0.0 174.4 jit_solution(5133109723735271574)
XLA Ops:
  0.7 2.2 %take_share.1.share_ref = bf16[16,32,896]{2,1,0:T(8,128)(2,1)} custom-call(bf16[16,128,896]{2,1,0:T(8,128)(2,1)} %bitcast.24), custom_call_target="tpu_custom_call" | custom-call | bytes 2000000 | tf_op jit(solution)/shard_map/take_share/pallas_call | solution.py:77
  2.9 3.3 %collective-permute-start.2 = (bf16[16,32,896]{2,1,0:T(8,128)(2,1)}, bf16[16,32,896]{2,1,0:T(8,128)(2,1)}, u32[]{:S(2)}, u32[]{:S(2)}) collective-permute-start(bf16[16,32,896]{2,1,0:T(8,128)(2,1)} %take_share.1.share_ref), channel_id=1, source_target_pairs={{0,4},{4,0},{8,12},{12,8},{16,20},{20,16},{24,28},{28,24},{32,36},... | collective-permute-start | bytes 2752520 | tf_op jit(solution)/shard_map/ppermute | solution.py:357
  9.0 3.0 %pack_rows.1 = (bf16[4,32,896]{2,1,0:T(8,128)(2,1)}, bf16[6,32,896]{2,1,0:T(8,128)(2,1)}, bf16[4,32,896]{2,1,0:T(8,128)(2,1)}, bf16[4,32,896]{2,1,0:T(8,128)(2,1...) custom-call(s32[16,2]{1,0:T(8,128)} %copy-done.1, s32[16,2]{1,0:T(8,128)} %copy-done.7, ...), custom_call_target="tpu_custom_call" | custom-call | bytes 3000000 | tf_op jit(solution)/shard_map/pack_rows/pallas_call | solution.py:123
  12.0 3.9 %collective-permute-start.8 = (bf16[6,32,896]{2,1,0:T(8,128)(2,1)}, bf16[6,32,896]{2,1,0:T(8,128)(2,1)S(1)}, u32[]{:S(2)}, u32[]{:S(2)}) collective-permute-start(bf16[6,32,896]{2,1,0:T(8,128)(2,1)} %get-tuple-element.45), channel_id=1, source_target_pairs={{0,56},{4,60},{8,0},{12,4},{16,8},{20,12},{24,16},{28,20},{32,24},... | collective-permute-start | bytes 1032200 | tf_op jit(solution)/shard_map/ppermute | solution.py:361
  15.8 3.5 %collective-permute-start.5 = (bf16[4,32,896]{2,1,0:T(8,128)(2,1)}, bf16[4,32,896]{2,1,0:T(8,128)(2,1)S(1)}, u32[]{:S(2)}, u32[]{:S(2)}) collective-permute-start(bf16[4,32,896]{2,1,0:T(8,128)(2,1)} %get-tuple-element.42), channel_id=1, source_target_pairs={{0,24},{4,28},{8,32},{12,36},{16,40},{20,44},{24,48},{28,52},{32,5... | collective-permute-start | bytes 688136 | tf_op jit(solution)/shard_map/ppermute | solution.py:361
  20.3 3.8 %collective-permute-done.3.refs_1_ = bf16[6,32,896]{2,1,0:T(8,128)(2,1)S(1)} collective-permute-done((bf16[6,32,896]{2,1,0:T(8,128)(2,1)}, bf16[6,32,896]{2,1,0:T(8,128)(2,1)S(1)}, u32[]{:S(2)}, u32[]{:S(2)}) %collective-permute-start.3) | collective-permute-done | bytes 344096 | tf_op jit(solution)/shard_map/ppermute | solution.py:361
  25.7 2.9 %collective-permute-start.9 = (bf16[2,32,896]{2,1,0:T(8,128)(2,1)S(1)}, bf16[2,32,896]{2,1,0:T(8,128)(2,1)S(1)}, u32[]{:S(2)}, u32[]{:S(2)}) collective-permute-start(bf16[2,32,896]{2,1,0:T(8,128)(2,1)S(1)} %slice.16), channel_id=1, source_target_pairs={{0,24},{4,28},{8,32},{12,36},{16,40},{20,44},{24,48},{28,52},{32,5... | collective-permute-start | bytes 344072 | tf_op jit(solution)/shard_map/ppermute | solution.py:361
  28.6 2.0 %collective-permute-done.4.refs_2_ = bf16[4,32,896]{2,1,0:T(8,128)(2,1)S(1)} collective-permute-done((bf16[4,32,896]{2,1,0:T(8,128)(2,1)}, bf16[4,32,896]{2,1,0:T(8,128)(2,1)S(1)}, u32[]{:S(2)}, u32[]{:S(2)}) %collective-permute-start.4) | collective-permute-done | bytes 229408 | tf_op jit(solution)/shard_map/ppermute | solution.py:361
  30.6 6.6 %collective-permute-start.10 = (bf16[2,32,896]{2,1,0:T(8,128)(2,1)S(1)}, bf16[2,32,896]{2,1,0:T(8,128)(2,1)S(1)}, u32[]{:S(2)}, u32[]{:S(2)}) collective-permute-start(bf16[2,32,896]{2,1,0:T(8,128)(2,1)S(1)} %slice.17), channel_id=1, source_target_pairs={{0,40},{4,44},{8,48},{12,52},{16,56},{20,60},{24,0},{28,4},{32,8},... | collective-permute-start | bytes 344072 | tf_op jit(solution)/shard_map/ppermute | solution.py:361
  37.2 11.6 %collective-permute-done.5.refs_3_ = bf16[4,32,896]{2,1,0:T(8,128)(2,1)S(1)} collective-permute-done((bf16[4,32,896]{2,1,0:T(8,128)(2,1)}, bf16[4,32,896]{2,1,0:T(8,128)(2,1)S(1)}, u32[]{:S(2)}, u32[]{:S(2)}) %collective-permute-start.5) | collective-permute-done | bytes 229408 | tf_op jit(solution)/shard_map/ppermute | solution.py:361
  48.8 2.6 %collective-permute-done.7.refs_5_ = bf16[4,32,896]{2,1,0:T(8,128)(2,1)S(1)} collective-permute-done((bf16[4,32,896]{2,1,0:T(8,128)(2,1)}, bf16[4,32,896]{2,1,0:T(8,128)(2,1)S(1)}, u32[]{:S(2)}, u32[]{:S(2)}) %collective-permute-start.7) | collective-permute-done | bytes 229408 | tf_op jit(solution)/shard_map/ppermute | solution.py:361
  51.4 4.4 %collective-permute-done.9.refs_7_ = bf16[2,32,896]{2,1,0:T(8,128)(2,1)S(1)} collective-permute-done((bf16[2,32,896]{2,1,0:T(8,128)(2,1)S(1)}, bf16[2,32,896]{2,1,0:T(8,128)(2,1)S(1)}, u32[]{:S(2)}, u32[]{:S(2)}) %collective-permute-start.9) | collective-permute-done | bytes 114720 | tf_op jit(solution)/shard_map/ppermute | solution.py:361
  60.8 6.9 %collective-permute-done.11.refs_4_ = bf16[2,6,16,896]{3,2,1,0:T(8,128)(2,1)S(1)} collective-permute-done((bf16[2,6,16,896]{3,2,1,0:T(8,128)(2,1)S(1)}, bf16[2,6,16,896]{3,2,1,0:T(8,128)(2,1)S(1)}, u32[]{:S(2)}, u32[]{:S(2)}) %collective-permute-start.11) | collective-permute-done | bytes 344096 | tf_op jit(solution)/shard_map/ppermute | solution.py:388
  67.8 2.7 %collective-permute-start.17 = (bf16[6,16,896]{2,1,0:T(8,128)(2,1)S(1)}, bf16[6,16,896]{2,1,0:T(8,128)(2,1)S(1)}, u32[]{:S(2)}, u32[]{:S(2)}) collective-permute-start(bf16[6,16,896]{2,1,0:T(8,128)(2,1)S(1)} %slice_bitcast_fusion), channel_id=1, source_target_pairs={{0,3},{1,0},{2,1},{3,2},{4,7},{5,4},{6,5},{7,6},{8,11},{9,8},{10,9... | collective-permute-start | bytes 516104 | tf_op jit(solution)/shard_map/ppermute | solution.py:388
  70.6 2.7 %collective-permute-done.13.refs_2_ = bf16[6,16,896]{2,1,0:T(8,128)(2,1)S(1)} collective-permute-done((bf16[6,16,896]{2,1,0:T(8,128)(2,1)S(1)}, bf16[6,16,896]{2,1,0:T(8,128)(2,1)S(1)}, u32[]{:S(2)}, u32[]{:S(2)}) %collective-permute-start.13) | collective-permute-done | bytes 172064 | tf_op jit(solution)/shard_map/ppermute | solution.py:388
  77.5 10.8 %attention.2 = (bf16[384,1024]{1,0:T(8,128)(2,1)}, bf16[384,1024]{1,0:T(8,128)(2,1)S(1)}, bf16[6,224,128]{2,1,0:T(8,128)(2,1)S(1)}, bf16[6,224,128]{2,1,0:T(8,12...) custom-call(bf16[2,6,16,896]{3,2,1,0:T(8,128)(2,1)S(1)} %get-tuple-element.47.refs_0_, ...), custom_call_target="tpu_custom_call" | custom-call | flops 6600000000 | bytes 9500000 | tf_op jit(solution)/shard_map/attention/pallas_call | solution.py:242
  88.9 1.9 %collective-permute-start.20 = (bf16[6,224,128]{2,1,0:T(8,128)(2,1)S(1)}, bf16[6,224,128]{2,1,0:T(8,128)(2,1)S(1)}, u32[]{:S(2)}, u32[]{:S(2)}) collective-permute-start(bf16[6,224,128]{2,1,0:T(8,128)(2,1)S(1)} %get-tuple-element.55), channel_id=1, source_target_pairs={{0,2},{1,3},{2,0},{3,1},{4,6},{5,7},{6,4},{7,5},{8,10},{9,11},{10,... | collective-permute-start | bytes 1032200 | tf_op jit(solution)/shard_map/ppermute | solution.py:388
  90.8 2.0 %collective-permute-start.21 = (bf16[6,224,128]{2,1,0:T(8,128)(2,1)S(1)}, bf16[6,224,128]{2,1,0:T(8,128)(2,1)S(1)}, u32[]{:S(2)}, u32[]{:S(2)}) collective-permute-start(bf16[6,224,128]{2,1,0:T(8,128)(2,1)S(1)} %get-tuple-element.56), channel_id=1, source_target_pairs={{0,3},{1,0},{2,1},{3,2},{4,7},{5,4},{6,5},{7,6},{8,11},{9,8},{10,9... | collective-permute-start | bytes 1032200 | tf_op jit(solution)/shard_map/ppermute | solution.py:388
  92.7 10.7 %attention.3 = (bf16[384,1024]{1,0:T(8,128)(2,1)}, bf16[384,1024]{1,0:T(8,128)(2,1)S(1)}, bf16[6,224,128]{2,1,0:T(8,128)(2,1)S(1)}, bf16[6,224,128]{2,1,0:T(8,12...) custom-call(bf16[2,6,16,896]{3,2,1,0:T(8,128)(2,1)S(1)} %get-tuple-e, ...), custom_call_target="tpu_custom_call", output_to_operand_aliasing={{0}: (8, {}), {1}: (9, {})} | custom-call | flops 6600000000 | bytes 9500000 | tf_op jit(solution)/shard_map/attention/pallas_call | solution.py:242
  103.8 2.5 %collective-permute-start.23 = (bf16[6,224,128]{2,1,0:T(8,128)(2,1)S(1)}, bf16[6,224,128]{2,1,0:T(8,128)(2,1)S(1)}, u32[]{:S(2)}, u32[]{:S(2)}) collective-permute-start(bf16[6,224,128]{2,1,0:T(8,128)(2,1)S(1)} %get-tuple-element.59), channel_id=1, source_target_pairs={{0,2},{1,3},{2,0},{3,1},{4,6},{5,7},{6,4},{7,5},{8,10},{9,11},{10,... | collective-permute-start | bytes 1032200 | tf_op jit(solution)/shard_map/ppermute | solution.py:388
  108.0 5.7 %collective-permute-start.25 = (bf16[6,224,128]{2,1,0:T(8,128)(2,1)S(1)}, bf16[6,224,128]{2,1,0:T(8,128)(2,1)S(1)}, u32[]{:S(2)}, u32[]{:S(2)}) collective-permute-start(bf16[6,224,128]{2,1,0:T(8,128)(2,1)S(1)} %sum_parts.2.refs_0_), channel_id=1, source_target_pairs={{0,4},{4,0},{8,12},{12,8},{16,20},{20,16},{24,28},{28,24},{32,36},... | collective-permute-start | bytes 1032200 | tf_op jit(solution)/shard_map/ppermute | solution.py:357
  113.7 4.4 %collective-permute-done.23.refs_2_ = bf16[6,224,128]{2,1,0:T(8,128)(2,1)S(1)} collective-permute-done((bf16[6,224,128]{2,1,0:T(8,128)(2,1)S(1)}, bf16[6,224,128]{2,1,0:T(8,128)(2,1)S(1)}, u32[]{:S(2)}, u32[]{:S(2)}) %collective-permute-start.23) | collective-permute-done | bytes 344096 | tf_op jit(solution)/shard_map/ppermute | solution.py:388
  119.6 4.2 %collective-permute-start.26 = (bf16[6,224,128]{2,1,0:T(8,128)(2,1)S(1)}, bf16[6,224,128]{2,1,0:T(8,128)(2,1)S(1)}, u32[]{:S(2)}, u32[]{:S(2)}) collective-permute-start(bf16[6,224,128]{2,1,0:T(8,128)(2,1)S(1)} %sum_parts.3.refs_1_), channel_id=1, source_target_pairs={{0,4},{4,0},{8,12},{12,8},{16,20},{20,16},{24,28},{28,24},{32,36},... | collective-permute-start | bytes 1032200 | tf_op jit(solution)/shard_map/ppermute | solution.py:357
  125.1 1.8 %place.1 = (bf16[4,224,128]{2,1,0:T(8,128)(2,1)S(1)}, bf16[4,224,128]{2,1,0:T(8,128)(2,1)S(1)}, bf16[4,224,128]{2,1,0:T(8,128)(2,1)S(1)}, bf16[4,224,128]{2,1,0:...) custom-call(s32[6,2]{1,0:T(8,128)S(1)} %copy.15.neighbour_ref, ...), custom_call_target="tpu_custom_call" | custom-call | bytes 3000000 | tf_op jit(solution)/shard_map/place/pallas_call | solution.py:317
  127.2 4.4 %collective-permute-start.31 = (bf16[4,224,128]{2,1,0:T(8,128)(2,1)S(1)}, bf16[4,224,128]{2,1,0:T(8,128)(2,1)S(1)}, u32[]{:S(2)}, u32[]{:S(2)}) collective-permute-start(bf16[4,224,128]{2,1,0:T(8,128)(2,1)S(1)} %get-tuple-element.68), channel_id=1, source_target_pairs={{0,40},{4,44},{8,48},{12,52},{16,56},{20,60},{24,0},{28,4},{32,8},... | collective-permute-start | bytes 688136 | tf_op jit(solution)/shard_map/ppermute | solution.py:361
  132.7 4.9 %collective-permute-start.30 = (bf16[4,224,128]{2,1,0:T(8,128)(2,1)S(1)}, bf16[4,224,128]{2,1,0:T(8,128)(2,1)S(1)}, u32[]{:S(2)}, u32[]{:S(2)}) collective-permute-start(bf16[4,224,128]{2,1,0:T(8,128)(2,1)S(1)} %get-tuple-element.67), channel_id=1, source_target_pairs={{0,32},{4,36},{8,40},{12,44},{16,48},{20,52},{24,56},{28,60},{32,0... | collective-permute-start | bytes 688136 | tf_op jit(solution)/shard_map/ppermute | solution.py:361
  138.3 6.9 %collective-permute-done.27.refs_3_ = bf16[4,224,128]{2,1,0:T(8,128)(2,1)S(1)} collective-permute-done((bf16[4,224,128]{2,1,0:T(8,128)(2,1)S(1)}, bf16[4,224,128]{2,1,0:T(8,128)(2,1)S(1)}, u32[]{:S(2)}, u32[]{:S(2)}) %collective-permute-start.27) | collective-permute-done | bytes 229408 | tf_op jit(solution)/shard_map/ppermute | solution.py:361
  145.1 3.5 %collective-permute-start.28 = (bf16[4,224,128]{2,1,0:T(8,128)(2,1)S(1)}, bf16[4,224,128]{2,1,0:T(8,128)(2,1)S(1)}, u32[]{:S(2)}, u32[]{:S(2)}) collective-permute-start(bf16[4,224,128]{2,1,0:T(8,128)(2,1)S(1)} %get-tuple-element.65), channel_id=1, source_target_pairs={{0,8},{4,12},{8,16},{12,20},{16,24},{20,28},{24,32},{28,36},{32,40... | collective-permute-start | bytes 688136 | tf_op jit(solution)/shard_map/ppermute | solution.py:361
  150.7 9.7 %collective-permute-done.29.refs_2_ = bf16[4,224,128]{2,1,0:T(8,128)(2,1)S(1)} collective-permute-done((bf16[4,224,128]{2,1,0:T(8,128)(2,1)S(1)}, bf16[4,224,128]{2,1,0:T(8,128)(2,1)S(1)}, u32[]{:S(2)}, u32[]{:S(2)}) %collective-permute-start.29) | collective-permute-done | bytes 229408 | tf_op jit(solution)/shard_map/ppermute | solution.py:361
  160.4 7.2 %collective-permute-done.32.refs_6_ = bf16[4,224,128]{2,1,0:T(8,128)(2,1)S(1)} collective-permute-done((bf16[4,224,128]{2,1,0:T(8,128)(2,1)S(1)}, bf16[4,224,128]{2,1,0:T(8,128)(2,1)S(1)}, u32[]{:S(2)}, u32[]{:S(2)}) %collective-permute-start.32) | collective-permute-done | bytes 229408 | tf_op jit(solution)/shard_map/ppermute | solution.py:361
  167.7 3.4 %collective-permute-done.28.refs_1_ = bf16[4,224,128]{2,1,0:T(8,128)(2,1)S(1)} collective-permute-done((bf16[4,224,128]{2,1,0:T(8,128)(2,1)S(1)}, bf16[4,224,128]{2,1,0:T(8,128)(2,1)S(1)}, u32[]{:S(2)}, u32[]{:S(2)}) %collective-permute-start.28) | collective-permute-done | bytes 229408 | tf_op jit(solution)/shard_map/ppermute | solution.py:361
  172.3 2.2 %collect.1 = bf16[16,224,128]{2,1,0:T(8,128)(2,1)} custom-call(s32[16,2]{1,0:T(8,128)S(1)} %copy-done.2, bf16[4,224,128]{2,1,0:T(8,128)(2,1)S(1)} %get-tuple-element.63.refs_0_, bf16[4,224,128]{2,1,0:T(8,128)(2,1)S(1)} %collective-permute-done.28.refs_1_, bf16[4,224,128]{2,1,0:T(8,128)(2,1)S(1)} %collective-permute-done.29.refs_2_, ...), custom_call_target="tpu_custom_call" | custom-call | bytes 3000000 | tf_op jit(solution)/shard_map/collect/pallas_call | solution.py:344
  (72 shorter events, 25.3 us)
Async XLA Ops:
  2.9 5.8 %collective-permute-start.2 = (bf16[16,32,896]{2,1,0:T(8,128)(2,1)}, bf16[16,32,896]{2,1,0:T(8,128)(2,1)}, u32[]{:S(2)}, u32[]{:S(2)}) collective-permute-start(bf16[16,32,896]{2,1,0:T(8,128)(2,1)} %take_share.1.share_ref), channel_id=1, source_target_pairs={{0,4},{4,0},{8,12},{12,8},{16,20},{20,16},{24,28},{28,24},{32,36},... | collective-permute-start | bytes 2752520 | tf_op jit(solution)/shard_map/ppermute | solution.py:357
  11.9 12.2 %collective-permute-start.3 = (bf16[6,32,896]{2,1,0:T(8,128)(2,1)}, bf16[6,32,896]{2,1,0:T(8,128)(2,1)S(1)}, u32[]{:S(2)}, u32[]{:S(2)}) collective-permute-start(bf16[6,32,896]{2,1,0:T(8,128)(2,1)} %get-tuple-element.40), channel_id=1, source_target_pairs={{0,8},{4,12},{8,16},{12,20},{16,24},{20,28},{24,32},{28,36},{32,40... | collective-permute-start | bytes 1032200 | tf_op jit(solution)/shard_map/ppermute | solution.py:361
  12.0 13.8 %collective-permute-start.8 = (bf16[6,32,896]{2,1,0:T(8,128)(2,1)}, bf16[6,32,896]{2,1,0:T(8,128)(2,1)S(1)}, u32[]{:S(2)}, u32[]{:S(2)}) collective-permute-start(bf16[6,32,896]{2,1,0:T(8,128)(2,1)} %get-tuple-element.45), channel_id=1, source_target_pairs={{0,56},{4,60},{8,0},{12,4},{16,8},{20,12},{24,16},{28,20},{32,24},... | collective-permute-start | bytes 1032200 | tf_op jit(solution)/shard_map/ppermute | solution.py:361
  15.8 14.8 %collective-permute-start.4 = (bf16[4,32,896]{2,1,0:T(8,128)(2,1)}, bf16[4,32,896]{2,1,0:T(8,128)(2,1)S(1)}, u32[]{:S(2)}, u32[]{:S(2)}) collective-permute-start(bf16[4,32,896]{2,1,0:T(8,128)(2,1)} %get-tuple-element.41), channel_id=1, source_target_pairs={{0,16},{4,20},{8,24},{12,28},{16,32},{20,36},{24,40},{28,44},{32,4... | collective-permute-start | bytes 688136 | tf_op jit(solution)/shard_map/ppermute | solution.py:361
  15.8 33.0 %collective-permute-start.5 = (bf16[4,32,896]{2,1,0:T(8,128)(2,1)}, bf16[4,32,896]{2,1,0:T(8,128)(2,1)S(1)}, u32[]{:S(2)}, u32[]{:S(2)}) collective-permute-start(bf16[4,32,896]{2,1,0:T(8,128)(2,1)} %get-tuple-element.42), channel_id=1, source_target_pairs={{0,24},{4,28},{8,32},{12,36},{16,40},{20,44},{24,48},{28,52},{32,5... | collective-permute-start | bytes 688136 | tf_op jit(solution)/shard_map/ppermute | solution.py:361
  19.3 29.4 %collective-permute-start.6 = (bf16[4,32,896]{2,1,0:T(8,128)(2,1)}, bf16[4,32,896]{2,1,0:T(8,128)(2,1)S(1)}, u32[]{:S(2)}, u32[]{:S(2)}) collective-permute-start(bf16[4,32,896]{2,1,0:T(8,128)(2,1)} %get-tuple-element.43), channel_id=1, source_target_pairs={{0,40},{4,44},{8,48},{12,52},{16,56},{20,60},{24,0},{28,4},{32,8},... | collective-permute-start | bytes 688136 | tf_op jit(solution)/shard_map/ppermute | solution.py:361
  24.1 27.2 %collective-permute-start.7 = (bf16[4,32,896]{2,1,0:T(8,128)(2,1)}, bf16[4,32,896]{2,1,0:T(8,128)(2,1)S(1)}, u32[]{:S(2)}, u32[]{:S(2)}) collective-permute-start(bf16[4,32,896]{2,1,0:T(8,128)(2,1)} %get-tuple-element.44), channel_id=1, source_target_pairs={{0,48},{4,52},{8,56},{12,60},{16,0},{20,4},{24,8},{28,12},{32,16},... | collective-permute-start | bytes 688136 | tf_op jit(solution)/shard_map/ppermute | solution.py:361
  25.7 30.0 %collective-permute-start.9 = (bf16[2,32,896]{2,1,0:T(8,128)(2,1)S(1)}, bf16[2,32,896]{2,1,0:T(8,128)(2,1)S(1)}, u32[]{:S(2)}, u32[]{:S(2)}) collective-permute-start(bf16[2,32,896]{2,1,0:T(8,128)(2,1)S(1)} %slice.16), channel_id=1, source_target_pairs={{0,24},{4,28},{8,32},{12,36},{16,40},{20,44},{24,48},{28,52},{32,5... | collective-permute-start | bytes 344072 | tf_op jit(solution)/shard_map/ppermute | solution.py:361
  30.6 25.2 %collective-permute-start.10 = (bf16[2,32,896]{2,1,0:T(8,128)(2,1)S(1)}, bf16[2,32,896]{2,1,0:T(8,128)(2,1)S(1)}, u32[]{:S(2)}, u32[]{:S(2)}) collective-permute-start(bf16[2,32,896]{2,1,0:T(8,128)(2,1)S(1)} %slice.17), channel_id=1, source_target_pairs={{0,40},{4,44},{8,48},{12,52},{16,56},{20,60},{24,0},{28,4},{32,8},... | collective-permute-start | bytes 344072 | tf_op jit(solution)/shard_map/ppermute | solution.py:361
  58.0 9.6 %collective-permute-start.11 = (bf16[2,6,16,896]{3,2,1,0:T(8,128)(2,1)S(1)}, bf16[2,6,16,896]{3,2,1,0:T(8,128)(2,1)S(1)}, u32[]{:S(2)}, u32[]{:S(2)}) collective-permute-start(bf16[2,6,16,896]{3,2,1,0:T(8,128)(2,1)S(1)} %get-tuple-element.47.refs_0_), channel_id=1, source_target_pairs={{0,1},{1,2},{2,3},{3,0},{4,5},{5,6},{6,7},{7,4},{8,9},{9,10},{10,1... | collective-permute-start | bytes 1032200 | tf_op jit(solution)/shard_map/ppermute | solution.py:388
  59.3 8.5 %collective-permute-start.12 = (bf16[2,6,16,896]{3,2,1,0:T(8,128)(2,1)S(1)}, bf16[2,6,16,896]{3,2,1,0:T(8,128)(2,1)S(1)}, u32[]{:S(2)}, u32[]{:S(2)}) collective-permute-start(bf16[2,6,16,896]{3,2,1,0:T(8,128)(2,1)S(1)} %get-tuple-element.47.refs_0_), channel_id=1, source_target_pairs={{0,3},{1,0},{2,1},{3,2},{4,7},{5,4},{6,5},{7,6},{8,11},{9,8},{10,9... | collective-permute-start | bytes 1032200 | tf_op jit(solution)/shard_map/ppermute | solution.py:388
  67.7 5.5 %collective-permute-start.13 = (bf16[6,16,896]{2,1,0:T(8,128)(2,1)S(1)}, bf16[6,16,896]{2,1,0:T(8,128)(2,1)S(1)}, u32[]{:S(2)}, u32[]{:S(2)}) collective-permute-start(bf16[6,16,896]{2,1,0:T(8,128)(2,1)S(1)} %slice_bitcast_fusion.1), channel_id=1, source_target_pairs={{0,1},{1,2},{2,3},{3,0},{4,5},{5,6},{6,7},{7,4},{8,9},{9,10},{10,1... | collective-permute-start | bytes 516104 | tf_op jit(solution)/shard_map/ppermute | solution.py:388
  67.8 8.1 %collective-permute-start.17 = (bf16[6,16,896]{2,1,0:T(8,128)(2,1)S(1)}, bf16[6,16,896]{2,1,0:T(8,128)(2,1)S(1)}, u32[]{:S(2)}, u32[]{:S(2)}) collective-permute-start(bf16[6,16,896]{2,1,0:T(8,128)(2,1)S(1)} %slice_bitcast_fusion), channel_id=1, source_target_pairs={{0,3},{1,0},{2,1},{3,2},{4,7},{5,4},{6,5},{7,6},{8,11},{9,8},{10,9... | collective-permute-start | bytes 516104 | tf_op jit(solution)/shard_map/ppermute | solution.py:388
  73.2 17.5 %collective-permute-start.16 = (bf16[2,6,16,896]{3,2,1,0:T(8,128)(2,1)S(1)}, bf16[2,6,16,896]{3,2,1,0:T(8,128)(2,1)S(1)}, u32[]{:S(2)}, u32[]{:S(2)}) collective-permute-start(bf16[2,6,16,896]{3,2,1,0:T(8,128)(2,1)S(1)} %get-tuple-element.48.refs_0_), channel_id=1, source_target_pairs={{0,1},{1,2},{2,3},{3,0},{4,5},{5,6},{6,7},{7,4},{8,9},{9,10},{10,1... | collective-permute-start | bytes 1032200 | tf_op jit(solution)/shard_map/ppermute | solution.py:388
  73.3 19.5 %collective-permute-start.15 = (bf16[2,6,16,896]{3,2,1,0:T(8,128)(2,1)S(1)}, bf16[2,6,16,896]{3,2,1,0:T(8,128)(2,1)S(1)}, u32[]{:S(2)}, u32[]{:S(2)}) collective-permute-start(bf16[2,6,16,896]{3,2,1,0:T(8,128)(2,1)S(1)} %get-tuple-element.48.refs_0_), channel_id=1, source_target_pairs={{0,2},{1,3},{2,0},{3,1},{4,6},{5,7},{6,4},{7,5},{8,10},{9,11},{10,... | collective-permute-start | bytes 1032200 | tf_op jit(solution)/shard_map/ppermute | solution.py:388
  74.5 18.3 %collective-permute-start.14 = (bf16[2,6,16,896]{3,2,1,0:T(8,128)(2,1)S(1)}, bf16[2,6,16,896]{3,2,1,0:T(8,128)(2,1)S(1)}, u32[]{:S(2)}, u32[]{:S(2)}) collective-permute-start(bf16[2,6,16,896]{3,2,1,0:T(8,128)(2,1)S(1)} %get-tuple-element.48.refs_0_), channel_id=1, source_target_pairs={{0,3},{1,0},{2,1},{3,2},{4,7},{5,4},{6,5},{7,6},{8,11},{9,8},{10,9... | collective-permute-start | bytes 1032200 | tf_op jit(solution)/shard_map/ppermute | solution.py:388
  88.2 18.2 %collective-permute-start.19 = (bf16[6,224,128]{2,1,0:T(8,128)(2,1)S(1)}, bf16[6,224,128]{2,1,0:T(8,128)(2,1)S(1)}, u32[]{:S(2)}, u32[]{:S(2)}) collective-permute-start(bf16[6,224,128]{2,1,0:T(8,128)(2,1)S(1)} %get-tuple-element.54), channel_id=1, source_target_pairs={{0,1},{1,2},{2,3},{3,0},{4,5},{5,6},{6,7},{7,4},{8,9},{9,10},{10,1... | collective-permute-start | bytes 1032200 | tf_op jit(solution)/shard_map/ppermute | solution.py:388
  88.9 17.6 %collective-permute-start.20 = (bf16[6,224,128]{2,1,0:T(8,128)(2,1)S(1)}, bf16[6,224,128]{2,1,0:T(8,128)(2,1)S(1)}, u32[]{:S(2)}, u32[]{:S(2)}) collective-permute-start(bf16[6,224,128]{2,1,0:T(8,128)(2,1)S(1)} %get-tuple-element.55), channel_id=1, source_target_pairs={{0,2},{1,3},{2,0},{3,1},{4,6},{5,7},{6,4},{7,5},{8,10},{9,11},{10,... | collective-permute-start | bytes 1032200 | tf_op jit(solution)/shard_map/ppermute | solution.py:388
  90.8 17.0 %collective-permute-start.21 = (bf16[6,224,128]{2,1,0:T(8,128)(2,1)S(1)}, bf16[6,224,128]{2,1,0:T(8,128)(2,1)S(1)}, u32[]{:S(2)}, u32[]{:S(2)}) collective-permute-start(bf16[6,224,128]{2,1,0:T(8,128)(2,1)S(1)} %get-tuple-element.56), channel_id=1, source_target_pairs={{0,3},{1,0},{2,1},{3,2},{4,7},{5,4},{6,5},{7,6},{8,11},{9,8},{10,9... | collective-permute-start | bytes 1032200 | tf_op jit(solution)/shard_map/ppermute | solution.py:388
  103.5 10.2 %collective-permute-start.22 = (bf16[6,224,128]{2,1,0:T(8,128)(2,1)S(1)}, bf16[6,224,128]{2,1,0:T(8,128)(2,1)S(1)}, u32[]{:S(2)}, u32[]{:S(2)}) collective-permute-start(bf16[6,224,128]{2,1,0:T(8,128)(2,1)S(1)} %get-tuple-element.58), channel_id=1, source_target_pairs={{0,1},{1,2},{2,3},{3,0},{4,5},{5,6},{6,7},{7,4},{8,9},{9,10},{10,1... | collective-permute-start | bytes 1032200 | tf_op jit(solution)/shard_map/ppermute | solution.py:388
  103.8 14.3 %collective-permute-start.23 = (bf16[6,224,128]{2,1,0:T(8,128)(2,1)S(1)}, bf16[6,224,128]{2,1,0:T(8,128)(2,1)S(1)}, u32[]{:S(2)}, u32[]{:S(2)}) collective-permute-start(bf16[6,224,128]{2,1,0:T(8,128)(2,1)S(1)} %get-tuple-element.59), channel_id=1, source_target_pairs={{0,2},{1,3},{2,0},{3,1},{4,6},{5,7},{6,4},{7,5},{8,10},{9,11},{10,... | collective-permute-start | bytes 1032200 | tf_op jit(solution)/shard_map/ppermute | solution.py:388
  106.4 13.1 %collective-permute-start.24 = (bf16[6,224,128]{2,1,0:T(8,128)(2,1)S(1)}, bf16[6,224,128]{2,1,0:T(8,128)(2,1)S(1)}, u32[]{:S(2)}, u32[]{:S(2)}) collective-permute-start(bf16[6,224,128]{2,1,0:T(8,128)(2,1)S(1)} %get-tuple-element.60), channel_id=1, source_target_pairs={{0,3},{1,0},{2,1},{3,2},{4,7},{5,4},{6,5},{7,6},{8,11},{9,8},{10,9... | collective-permute-start | bytes 1032200 | tf_op jit(solution)/shard_map/ppermute | solution.py:388
  106.5 31.1 %collective-permute-start.18 = (bf16[384,1024]{1,0:T(8,128)(2,1)S(1)}, bf16[384,1024]{1,0:T(8,128)(2,1)S(1)}, u32[]{:S(2)}, u32[]{:S(2)}) collective-permute-start(bf16[384,1024]{1,0:T(8,128)(2,1)S(1)} %get-tuple-element.52), channel_id=1, source_target_pairs={{64,0},{128,64},{192,128},{65,1},{129,65},{193,129},{66,2},{130,66... | collective-permute-start | bytes 2359304 | tf_op jit(solution)/shard_map/ppermute | solution.py:393
  108.0 15.9 %collective-permute-start.25 = (bf16[6,224,128]{2,1,0:T(8,128)(2,1)S(1)}, bf16[6,224,128]{2,1,0:T(8,128)(2,1)S(1)}, u32[]{:S(2)}, u32[]{:S(2)}) collective-permute-start(bf16[6,224,128]{2,1,0:T(8,128)(2,1)S(1)} %sum_parts.2.refs_0_), channel_id=1, source_target_pairs={{0,4},{4,0},{8,12},{12,8},{16,20},{20,16},{24,28},{28,24},{32,36},... | collective-permute-start | bytes 1032200 | tf_op jit(solution)/shard_map/ppermute | solution.py:357
  119.6 5.5 %collective-permute-start.26 = (bf16[6,224,128]{2,1,0:T(8,128)(2,1)S(1)}, bf16[6,224,128]{2,1,0:T(8,128)(2,1)S(1)}, u32[]{:S(2)}, u32[]{:S(2)}) collective-permute-start(bf16[6,224,128]{2,1,0:T(8,128)(2,1)S(1)} %sum_parts.3.refs_1_), channel_id=1, source_target_pairs={{0,4},{4,0},{8,12},{12,8},{16,20},{20,16},{24,28},{28,24},{32,36},... | collective-permute-start | bytes 1032200 | tf_op jit(solution)/shard_map/ppermute | solution.py:357
  126.9 18.2 %collective-permute-start.27 = (bf16[4,224,128]{2,1,0:T(8,128)(2,1)S(1)}, bf16[4,224,128]{2,1,0:T(8,128)(2,1)S(1)}, u32[]{:S(2)}, u32[]{:S(2)}) collective-permute-start(bf16[4,224,128]{2,1,0:T(8,128)(2,1)S(1)} %get-tuple-element.61), channel_id=1, source_target_pairs={{0,24},{4,28},{8,32},{12,36},{16,40},{20,44},{24,48},{28,52},{32,5... | collective-permute-start | bytes 688136 | tf_op jit(solution)/shard_map/ppermute | solution.py:361
  127.2 21.4 %collective-permute-start.31 = (bf16[4,224,128]{2,1,0:T(8,128)(2,1)S(1)}, bf16[4,224,128]{2,1,0:T(8,128)(2,1)S(1)}, u32[]{:S(2)}, u32[]{:S(2)}) collective-permute-start(bf16[4,224,128]{2,1,0:T(8,128)(2,1)S(1)} %get-tuple-element.68), channel_id=1, source_target_pairs={{0,40},{4,44},{8,48},{12,52},{16,56},{20,60},{24,0},{28,4},{32,8},... | collective-permute-start | bytes 688136 | tf_op jit(solution)/shard_map/ppermute | solution.py:361
  131.6 28.8 %collective-permute-start.29 = (bf16[4,224,128]{2,1,0:T(8,128)(2,1)S(1)}, bf16[4,224,128]{2,1,0:T(8,128)(2,1)S(1)}, u32[]{:S(2)}, u32[]{:S(2)}) collective-permute-start(bf16[4,224,128]{2,1,0:T(8,128)(2,1)S(1)} %get-tuple-element.66), channel_id=1, source_target_pairs={{0,16},{4,20},{8,24},{12,28},{16,32},{20,36},{24,40},{28,44},{32,4... | collective-permute-start | bytes 688136 | tf_op jit(solution)/shard_map/ppermute | solution.py:361
  132.7 27.7 %collective-permute-start.30 = (bf16[4,224,128]{2,1,0:T(8,128)(2,1)S(1)}, bf16[4,224,128]{2,1,0:T(8,128)(2,1)S(1)}, u32[]{:S(2)}, u32[]{:S(2)}) collective-permute-start(bf16[4,224,128]{2,1,0:T(8,128)(2,1)S(1)} %get-tuple-element.67), channel_id=1, source_target_pairs={{0,32},{4,36},{8,40},{12,44},{16,48},{20,52},{24,56},{28,60},{32,0... | collective-permute-start | bytes 688136 | tf_op jit(solution)/shard_map/ppermute | solution.py:361
  137.6 30.1 %collective-permute-start.32 = (bf16[4,224,128]{2,1,0:T(8,128)(2,1)S(1)}, bf16[4,224,128]{2,1,0:T(8,128)(2,1)S(1)}, u32[]{:S(2)}, u32[]{:S(2)}) collective-permute-start(bf16[4,224,128]{2,1,0:T(8,128)(2,1)S(1)} %get-tuple-element.70), channel_id=1, source_target_pairs={{0,48},{4,52},{8,56},{12,60},{16,0},{20,4},{24,8},{28,12},{32,16},... | collective-permute-start | bytes 688136 | tf_op jit(solution)/shard_map/ppermute | solution.py:361
  145.1 25.9 %collective-permute-start.28 = (bf16[4,224,128]{2,1,0:T(8,128)(2,1)S(1)}, bf16[4,224,128]{2,1,0:T(8,128)(2,1)S(1)}, u32[]{:S(2)}, u32[]{:S(2)}) collective-permute-start(bf16[4,224,128]{2,1,0:T(8,128)(2,1)S(1)} %get-tuple-element.65), channel_id=1, source_target_pairs={{0,8},{4,12},{8,16},{12,20},{16,24},{20,28},{24,32},{28,36},{32,40... | collective-permute-start | bytes 688136 | tf_op jit(solution)/shard_map/ppermute | solution.py:361
  148.6 23.7 %collective-permute-start.33 = (bf16[4,224,128]{2,1,0:T(8,128)(2,1)S(1)}, bf16[4,224,128]{2,1,0:T(8,128)(2,1)S(1)}, u32[]{:S(2)}, u32[]{:S(2)}) collective-permute-start(bf16[4,224,128]{2,1,0:T(8,128)(2,1)S(1)} %get-tuple-element.72), channel_id=1, source_target_pairs={{0,56},{4,60},{8,0},{12,4},{16,8},{20,12},{24,16},{28,20},{32,24},... | collective-permute-start | bytes 688136 | tf_op jit(solution)/shard_map/ppermute | solution.py:361
  (12 other events, 290.8 us)
